TPU v7x, 32 devices: a whole 2x2x4 slice. The times are simulated.
32 devices in a mesh: rep: 4 (over x, core), shard: 8 (over z, y).
Axes of the slice: x: 2, y: 2, z: 4, core: 2. Of those that a mesh axis runs over, the one named last changes fastest.
Arguments:
- activations: bfloat16 [8, 2048, 1280], P('rep', 'shard'), may hold values from -6 to 6
- cotangent: bfloat16 [8, 2048, 1280], P('rep', 'shard'), may hold values from -6 to 6
- doc_lengths: int32 [8, 16], P('rep'), may hold values from 1 to 1024, 2048 in all within a row
- gain_attn: bfloat16 [1280], P('shard'), may hold values from 0.25 to 1.75
- query_weight: bfloat16 [1280, 1280], P('shard'), may hold values from -0.15625 to 0.15625
- query_bias: bfloat16 [1280], P('shard'), may hold values from -3 to 3
- key_weight: bfloat16 [1280, 1280], P('shard'), may hold values from -0.15625 to 0.15625
- value_weight: bfloat16 [1280, 1280], P('shard'), may hold values from -0.15625 to 0.15625
- value_bias: bfloat16 [1280], P('shard'), may hold values from -3 to 3
- dim_scale: float32 [80], replicated, may hold values from -0.5 to 1.5
- out_weight: bfloat16 [1280, 1280], P('shard'), may hold values from -1 to 1
- gain_mlp: bfloat16 [1280], P('shard'), may hold values from 0.25 to 1.75
- up_weight: bfloat16 [1280, 1280], P('shard'), may hold values from -0.15625 to 0.15625
- down_weight: bfloat16 [1280, 1280], P('shard'), may hold values from -0.15625 to 0.15625
Outputs:
- output: bfloat16 [8, 2048, 1280], P('rep', 'shard')
- input_grad: bfloat16 [8, 2048, 1280], P('rep', 'shard')
- grad_gain_attn: float32 [1280], P('shard')
- grad_query: float32 [1280, 1280], P('shard')
- grad_query_bias: float32 [1280], P('shard')
- grad_key: float32 [1280, 1280], P('shard')
- grad_value: float32 [1280, 1280], P('shard')
- grad_value_bias: float32 [1280], P('shard')
- grad_scale: float32 [80], replicated
- grad_out: float32 [1280, 1280], P('shard')
- grad_gain_mlp: float32 [1280], P('shard')
- grad_up: float32 [1280, 1280], P('shard')
- grad_down: float32 [1280, 1280], P('shard')
Inputs may be any that keep to these rules, and one draw needn't show every extreme that they name: `doc_lengths`: each row of 16 lengths sums to 2048, and its longest document has exactly 1024 tokens.
All inputs are finite; a program needn't handle non-finite values.
Results may differ from a plain program's by a relative error of at most 0.03.
Values may be sent and summed in bfloat16 or wider, within the bound.
No kernel may reach another device: no remote copies, remote signals or barrier semaphores. Data moves between devices by JAX's collectives and lax.ppermute only.
A program may use at most 192 MiB of HBM per device.

v0:
```python
import math

import jax
import jax.numpy as jnp
from jax import lax
from jax.sharding import PartitionSpec as P

HEAD_DIM = 80
BLOCK = 512


NORM_EPS = 1e-06
LOG_BASE = 1.442695041
MASK_FILL = -1e30


def matmul(left_side, right_side):
    return jnp.dot(left_side, right_side, preferred_element_type=jnp.float32)


def norm_apply(values, gain_vec):
    return (
        values * lax.rsqrt(jnp.mean(values * values, axis=-1, keepdims=True) + NORM_EPS) * gain_vec
    )


def norm_back(values, gain_vec, grad_out):
    unused, pull_back = jax.vjp(norm_apply, values, gain_vec)
    return pull_back(grad_out)


def doc_numbers(lengths, total_len):
    doc_ends = jnp.cumsum(lengths, axis=-1)
    places = jnp.arange(total_len, dtype=jnp.int32)
    return jnp.sum((places[None, :, None] >= doc_ends[:, None, :]).astype(jnp.int32), axis=-1)


def block_scores(query_block, key_block, query_docs, key_docs, query_start, key_start):
    scores = jnp.einsum("qhe,khe->hqk", query_block, key_block, preferred_element_type=jnp.float32)
    query_places = query_start + jnp.arange(query_block.shape[0], dtype=jnp.int32)
    key_places = key_start + jnp.arange(key_block.shape[0], dtype=jnp.int32)
    allowed = (query_docs[:, None] == key_docs[None, :]) & (
        key_places[None, :] <= query_places[:, None]
    )
    return (jnp.where(allowed[None], scores, MASK_FILL), allowed[None])


def over_keys(step_fn, start_carry, block_count):

    def advance(carry_state, key_index):
        carry_state = step_fn(key_index, carry_state)
        return (carry_state, None)

    return lax.scan(advance, start_carry, jnp.arange(block_count, dtype=jnp.int32))[0]


def attend_forward(query_seq, key_seq, value_seq, seq_docs):
    length, lane_count = query_seq.shape
    head_count = lane_count // HEAD_DIM
    block_count = length // BLOCK
    block_shape = (block_count, BLOCK, head_count, HEAD_DIM)
    query_blocks = query_seq.reshape(block_shape)
    key_blocks = key_seq.reshape(block_shape)
    value_blocks = value_seq.reshape(block_shape)
    doc_blocks = seq_docs.reshape(block_count, BLOCK)

    def one_block(query_index):
        query_block = query_blocks[query_index]
        query_docs = doc_blocks[query_index]
        query_start = query_index * BLOCK

        def stats_step(key_index, carry_state):
            running_max, running_total = carry_state
            scores, allowed = block_scores(
                query_block,
                key_blocks[key_index],
                query_docs,
                doc_blocks[key_index],
                query_start,
                key_index * BLOCK,
            )
            new_max = jnp.maximum(running_max, jnp.max(scores, axis=-1))
            weighted = jnp.where(allowed, jnp.exp(scores - new_max[..., None]), 0.0)
            return (
                new_max,
                running_total * jnp.exp(running_max - new_max) + jnp.sum(weighted, axis=-1),
            )

        start_stats = (
            jnp.full((head_count, BLOCK), MASK_FILL, jnp.float32),
            jnp.zeros((head_count, BLOCK), jnp.float32),
        )
        top_score, total_weight = over_keys(stats_step, start_stats, block_count)
        log_total = top_score + jnp.log(total_weight)

        def value_step(key_index, mixed_sum):
            scores, allowed = block_scores(
                query_block,
                key_blocks[key_index],
                query_docs,
                doc_blocks[key_index],
                query_start,
                key_index * BLOCK,
            )
            prob_block = jnp.where(allowed, jnp.exp(scores - log_total[..., None]), 0.0).astype(
                jnp.bfloat16
            )
            return mixed_sum + jnp.einsum(
                "hqk,khe->qhe",
                prob_block,
                value_blocks[key_index],
                preferred_element_type=jnp.float32,
            )

        mixed_sum = over_keys(
            value_step, jnp.zeros((BLOCK, head_count, HEAD_DIM), jnp.float32), block_count
        )
        return (mixed_sum.astype(jnp.bfloat16).reshape(BLOCK, lane_count), log_total)

    mixed_blocks, log_totals = lax.map(one_block, jnp.arange(block_count, dtype=jnp.int32))
    return (mixed_blocks.reshape(length, lane_count), log_totals)


def attend_backward(query_seq, key_seq, value_seq, grad_seq, mixed_seq, log_totals, seq_docs):
    length, lane_count = query_seq.shape
    head_count = lane_count // HEAD_DIM
    block_count = length // BLOCK
    block_shape = (block_count, BLOCK, head_count, HEAD_DIM)
    query_blocks = query_seq.reshape(block_shape)
    key_blocks = key_seq.reshape(block_shape)
    value_blocks = value_seq.reshape(block_shape)
    grad_blocks = grad_seq.reshape(block_shape)
    mixed_blocks = mixed_seq.reshape(block_shape)
    doc_blocks = seq_docs.reshape(block_count, BLOCK)

    def one_block(carry_state, query_index):
        key_grads, value_grads = carry_state
        query_block = query_blocks[query_index]
        grad_block = grad_blocks[query_index]
        query_docs = doc_blocks[query_index]
        log_total = log_totals[query_index]
        query_start = query_index * BLOCK
        delta_rows = jnp.einsum(
            "qhe,qhe->hq", grad_block, mixed_blocks[query_index], preferred_element_type=jnp.float32
        )

        def grad_step(key_index, inner_state):
            query_grad, key_acc, value_acc = inner_state
            scores, allowed = block_scores(
                query_block,
                key_blocks[key_index],
                query_docs,
                doc_blocks[key_index],
                query_start,
                key_index * BLOCK,
            )
            prob_block = jnp.where(allowed, jnp.exp(scores - log_total[..., None]), 0.0)
            grad_probs = jnp.einsum(
                "qhe,khe->hqk",
                grad_block,
                value_blocks[key_index],
                preferred_element_type=jnp.float32,
            )
            grad_scores = (prob_block * (grad_probs - delta_rows[..., None])).astype(jnp.bfloat16)
            query_grad = query_grad + jnp.einsum(
                "hqk,khe->qhe",
                grad_scores,
                key_blocks[key_index],
                preferred_element_type=jnp.float32,
            )
            key_acc = key_acc.at[key_index].add(
                jnp.einsum(
                    "hqk,qhe->khe", grad_scores, query_block, preferred_element_type=jnp.float32
                )
            )
            value_acc = value_acc.at[key_index].add(
                jnp.einsum(
                    "hqk,qhe->khe",
                    prob_block.astype(jnp.bfloat16),
                    grad_block,
                    preferred_element_type=jnp.float32,
                )
            )
            return (query_grad, key_acc, value_acc)

        start_inner = (
            jnp.zeros((BLOCK, head_count, HEAD_DIM), jnp.float32),
            key_grads,
            value_grads,
        )
        query_grad, key_grads, value_grads = over_keys(grad_step, start_inner, block_count)
        return ((key_grads, value_grads), query_grad.astype(jnp.bfloat16))

    zero_grads = jnp.zeros(block_shape, jnp.float32)
    (key_grads, value_grads), query_grads = lax.scan(
        one_block, (zero_grads, zero_grads), jnp.arange(block_count, dtype=jnp.int32)
    )
    return (
        query_grads.reshape(length, lane_count),
        key_grads.astype(jnp.bfloat16).reshape(length, lane_count),
        value_grads.astype(jnp.bfloat16).reshape(length, lane_count),
    )


def local(
    activations,
    cotangent,
    doc_lengths,
    gain_attn,
    query_weight,
    query_bias,
    key_weight,
    value_weight,
    value_bias,
    dim_scale,
    out_weight,
    gain_mlp,
    up_weight,
    down_weight,
):
    seq_count, tok_count, model_width = activations.shape
    row_count = seq_count * tok_count
    pieces = lax.axis_size("shard")
    head_total = model_width // HEAD_DIM
    gathered = (
        lax.all_gather(query_weight, "shard", axis=0, tiled=True),
        lax.all_gather(key_weight, "shard", axis=0, tiled=True),
        lax.all_gather(value_weight, "shard", axis=0, tiled=True),
        lax.all_gather(out_weight, "shard", axis=0, tiled=True),
        lax.all_gather(up_weight, "shard", axis=0, tiled=True),
        lax.all_gather(down_weight, "shard", axis=0, tiled=True),
        lax.all_gather(gain_attn, "shard", axis=0, tiled=True),
        lax.all_gather(gain_mlp, "shard", axis=0, tiled=True),
        lax.all_gather(query_bias, "shard", axis=0, tiled=True),
        lax.all_gather(value_bias, "shard", axis=0, tiled=True),
    )
    w_query, w_key, w_value, w_out, w_up, w_down, g_attn, g_mlp, b_query, b_value = gathered
    hidden_in = activations.reshape(row_count, model_width).astype(jnp.float32)
    normed = norm_apply(hidden_in, g_attn.astype(jnp.float32)).astype(jnp.bfloat16)
    query_full = matmul(normed, w_query) + b_query.astype(jnp.float32)
    scale_vec = jnp.tile(LOG_BASE / math.sqrt(HEAD_DIM) * jax.nn.softplus(dim_scale), head_total)
    scaled = (query_full * scale_vec).astype(jnp.bfloat16)
    key_rows = matmul(normed, w_key).astype(jnp.bfloat16)
    value_rows = (matmul(normed, w_value) + b_value.astype(jnp.float32)).astype(jnp.bfloat16)
    token_shape = (seq_count, tok_count, model_width)
    q_heads, k_heads, v_heads = (
        lax.all_to_all(
            scaled.reshape(token_shape), "shard", split_axis=2, concat_axis=1, tiled=True
        ),
        lax.all_to_all(
            key_rows.reshape(token_shape), "shard", split_axis=2, concat_axis=1, tiled=True
        ),
        lax.all_to_all(
            value_rows.reshape(token_shape), "shard", split_axis=2, concat_axis=1, tiled=True
        ),
    )
    seq_docs = doc_numbers(doc_lengths, tok_count * pieces)

    def forward_one(bundle):
        return attend_forward(bundle[0], bundle[1], bundle[2], bundle[3])

    mixed_heads, log_totals = lax.map(forward_one, (q_heads, k_heads, v_heads, seq_docs))
    mixed = lax.all_to_all(mixed_heads, "shard", split_axis=1, concat_axis=2, tiled=True)
    mixed_rows = mixed.reshape(row_count, model_width)
    residual = hidden_in + matmul(mixed_rows, w_out)
    normed_mlp = norm_apply(residual, g_mlp.astype(jnp.float32)).astype(jnp.bfloat16)
    upward = matmul(normed_mlp, w_up)
    activated = jax.nn.silu(upward).astype(jnp.bfloat16)
    output = (residual + matmul(activated, w_down)).astype(jnp.bfloat16)
    backward_set = (
        lax.all_gather(query_weight, "shard", axis=0, tiled=True),
        lax.all_gather(key_weight, "shard", axis=0, tiled=True),
        lax.all_gather(value_weight, "shard", axis=0, tiled=True),
        lax.all_gather(out_weight, "shard", axis=0, tiled=True),
        lax.all_gather(up_weight, "shard", axis=0, tiled=True),
        lax.all_gather(down_weight, "shard", axis=0, tiled=True),
        lax.all_gather(gain_attn, "shard", axis=0, tiled=True),
        lax.all_gather(gain_mlp, "shard", axis=0, tiled=True),
    )
    w_query, w_key, w_value, w_out, w_up, w_down, g_attn, g_mlp = backward_set
    gain_attn32 = g_attn.astype(jnp.float32)
    gain_mlp32 = g_mlp.astype(jnp.float32)
    d_output = cotangent.reshape(row_count, model_width)
    grad_down = jnp.einsum("rf,rd->fd", activated, d_output, preferred_element_type=jnp.float32)
    d_activated = jnp.einsum("rd,fd->rf", d_output, w_down, preferred_element_type=jnp.float32)
    unused, silu_back = jax.vjp(jax.nn.silu, upward)
    d_up = silu_back(d_activated)[0].astype(jnp.bfloat16)
    grad_up = jnp.einsum("rd,rf->df", normed_mlp, d_up, preferred_element_type=jnp.float32)
    d_normed_mlp = jnp.einsum("rf,df->rd", d_up, w_up, preferred_element_type=jnp.float32)
    d_residual_norm, grad_gain_mlp = norm_back(residual, gain_mlp32, d_normed_mlp)
    d_residual = d_output.astype(jnp.float32) + d_residual_norm
    d_proj = d_residual.astype(jnp.bfloat16)
    grad_out = jnp.einsum("rc,rd->cd", mixed_rows, d_proj, preferred_element_type=jnp.float32)
    d_mixed = jnp.einsum("rd,cd->rc", d_proj, w_out, preferred_element_type=jnp.float32).astype(
        jnp.bfloat16
    )
    grad_heads = lax.all_to_all(
        d_mixed.reshape(token_shape), "shard", split_axis=2, concat_axis=1, tiled=True
    )

    def backward_one(bundle):
        return attend_backward(
            bundle[0], bundle[1], bundle[2], bundle[3], bundle[4], bundle[5], bundle[6]
        )

    dq_heads, dk_heads, dv_heads = lax.map(
        backward_one, (q_heads, k_heads, v_heads, grad_heads, mixed_heads, log_totals, seq_docs)
    )
    d_scaled, d_keys, d_values = (
        lax.all_to_all(dq_heads, "shard", split_axis=1, concat_axis=2, tiled=True),
        lax.all_to_all(dk_heads, "shard", split_axis=1, concat_axis=2, tiled=True),
        lax.all_to_all(dv_heads, "shard", split_axis=1, concat_axis=2, tiled=True),
    )
    d_scaled = d_scaled.reshape(row_count, model_width)
    d_keys = d_keys.reshape(row_count, model_width)
    d_values = d_values.reshape(row_count, model_width)
    d_scaled32 = d_scaled.astype(jnp.float32)
    scale_part = jnp.sum(
        (d_scaled32 * query_full).reshape(row_count, head_total, HEAD_DIM), axis=(0, 1)
    )
    scale_part = scale_part * (LOG_BASE / math.sqrt(HEAD_DIM)) * jax.nn.sigmoid(dim_scale)
    d_query = (d_scaled32 * scale_vec).astype(jnp.bfloat16)
    grad_query = jnp.einsum("rc,rd->cd", normed, d_query, preferred_element_type=jnp.float32)
    grad_query_bias = jnp.sum(d_query.astype(jnp.float32), axis=0)
    grad_key = jnp.einsum("rc,rd->cd", normed, d_keys, preferred_element_type=jnp.float32)
    grad_value = jnp.einsum("rc,rd->cd", normed, d_values, preferred_element_type=jnp.float32)
    grad_value_bias = jnp.sum(d_values.astype(jnp.float32), axis=0)
    d_normed = (
        jnp.einsum("rd,cd->rc", d_query, w_query, preferred_element_type=jnp.float32)
        + jnp.einsum("rd,cd->rc", d_keys, w_key, preferred_element_type=jnp.float32)
        + jnp.einsum("rd,cd->rc", d_values, w_value, preferred_element_type=jnp.float32)
    )
    d_hidden_norm, grad_gain_attn = norm_back(hidden_in, gain_attn32, d_normed)
    input_grad = (d_residual + d_hidden_norm).astype(jnp.bfloat16)
    scale_rows = jnp.broadcast_to(scale_part[None, :], (pieces, HEAD_DIM))
    owned = (
        lax.psum_scatter(
            grad_query.astype(jnp.bfloat16), "shard", scatter_dimension=0, tiled=True
        ).astype(jnp.float32),
        lax.psum_scatter(
            grad_key.astype(jnp.bfloat16), "shard", scatter_dimension=0, tiled=True
        ).astype(jnp.float32),
        lax.psum_scatter(
            grad_value.astype(jnp.bfloat16), "shard", scatter_dimension=0, tiled=True
        ).astype(jnp.float32),
        lax.psum_scatter(
            grad_out.astype(jnp.bfloat16), "shard", scatter_dimension=0, tiled=True
        ).astype(jnp.float32),
        lax.psum_scatter(
            grad_up.astype(jnp.bfloat16), "shard", scatter_dimension=0, tiled=True
        ).astype(jnp.float32),
        lax.psum_scatter(
            grad_down.astype(jnp.bfloat16), "shard", scatter_dimension=0, tiled=True
        ).astype(jnp.float32),
        lax.psum_scatter(
            grad_gain_attn.astype(jnp.bfloat16), "shard", scatter_dimension=0, tiled=True
        ).astype(jnp.float32),
        lax.psum_scatter(
            grad_gain_mlp.astype(jnp.bfloat16), "shard", scatter_dimension=0, tiled=True
        ).astype(jnp.float32),
        lax.psum_scatter(
            grad_query_bias.astype(jnp.bfloat16), "shard", scatter_dimension=0, tiled=True
        ).astype(jnp.float32),
        lax.psum_scatter(
            grad_value_bias.astype(jnp.bfloat16), "shard", scatter_dimension=0, tiled=True
        ).astype(jnp.float32),
        lax.psum_scatter(
            scale_rows.astype(jnp.bfloat16), "shard", scatter_dimension=0, tiled=True
        ).astype(jnp.float32),
    )
    totals = (
        lax.psum(owned[0].astype(jnp.bfloat16), "rep").astype(jnp.float32),
        lax.psum(owned[1].astype(jnp.bfloat16), "rep").astype(jnp.float32),
        lax.psum(owned[2].astype(jnp.bfloat16), "rep").astype(jnp.float32),
        lax.psum(owned[3].astype(jnp.bfloat16), "rep").astype(jnp.float32),
        lax.psum(owned[4].astype(jnp.bfloat16), "rep").astype(jnp.float32),
        lax.psum(owned[5].astype(jnp.bfloat16), "rep").astype(jnp.float32),
        lax.psum(owned[6].astype(jnp.bfloat16), "rep").astype(jnp.float32),
        lax.psum(owned[7].astype(jnp.bfloat16), "rep").astype(jnp.float32),
        lax.psum(owned[8].astype(jnp.bfloat16), "rep").astype(jnp.float32),
        lax.psum(owned[9].astype(jnp.bfloat16), "rep").astype(jnp.float32),
        lax.psum(owned[10].astype(jnp.bfloat16), "rep").astype(jnp.float32),
    )
    (
        t_query,
        t_key,
        t_value,
        t_out,
        t_up,
        t_down,
        t_gain_attn,
        t_gain_mlp,
        t_query_bias,
        t_value_bias,
        t_scale,
    ) = totals
    return (
        output.reshape(token_shape),
        input_grad.reshape(token_shape),
        t_gain_attn,
        t_query,
        t_query_bias,
        t_key,
        t_value,
        t_value_bias,
        t_scale.reshape(HEAD_DIM),
        t_out,
        t_gain_mlp,
        t_up,
        t_down,
    )


def solution(mesh):
    in_specs = (
        P("rep", "shard", None),
        P("rep", "shard", None),
        P("rep", None),
        P("shard"),
        P("shard", None),
        P("shard"),
        P("shard", None),
        P("shard", None),
        P("shard"),
        P(),
        P("shard", None),
        P("shard"),
        P("shard", None),
        P("shard", None),
    )
    out_specs = (
        P("rep", "shard", None),
        P("rep", "shard", None),
        P("shard"),
        P("shard", None),
        P("shard"),
        P("shard", None),
        P("shard", None),
        P("shard"),
        P(),
        P("shard", None),
        P("shard"),
        P("shard", None),
        P("shard", None),
    )
    return jax.shard_map(local, mesh=mesh, in_specs=in_specs, out_specs=out_specs, check_vma=False)
```

profile of v0, /device:TPU:9, one launch (start us, length us, event | category | flops | bytes accessed | tf_op | source)
XLA Modules:
  0.0 1752.6 jit_solution(11532711459323993519)
XLA Ops:
  13.9 27.6 %all-reduce.10 = (bf16[1280]{0:T(1024)(128)(2,1)S(1)}, bf16[1280]{0:T(1024)(128)(2,1)S(1)}, bf16[1280]{0:T(1024)(128)(2,1)S(1)}, bf16[1280]{0:T(1024)(128)(2,1)}) all-reduce(bf16[1280]{0:T(1024)(128)(2,1)S(1)} %dynamic-update-slice.6, bf16[1280]{0:T(1024)(128)(2,1)S(1)} %dynamic-update-slice.7, ...), channel_id=1, replica_groups=mesh['rep'=4,'shard'=8] {'shard'}, use_global_device_ids=true, to_apply=%add | all-reduce | flops 5120 | bytes 20480
  42.5 29.9 %all-gather.11.cloned.1.call-done = bf16[1280,1280]{1,0:T(8,128)(2,1)} async-done(((bf16[160,1280]{1,0:T(8,128)(2,1)}), bf16[1280,1280]{1,0:T(8,128)(2,1)}) %all-gather.11.cloned.1.call-update) | async-done | bytes 3276816 | tf_op jit(solution)/shard_map/all_gather | solution.py:228
  84.2 68.6 %all-gather.9.cloned.1.call-done = bf16[1280,1280]{1,0:T(8,128)(2,1)} async-done(((bf16[160,1280]{1,0:T(8,128)(2,1)}), bf16[1280,1280]{1,0:T(8,128)(2,1)}) %all-gather.9.cloned.1.call-update) | async-done | bytes 3276816 | tf_op jit(solution)/shard_map/all_gather | solution.py:227
  166.3 67.6 %all-gather.7.cloned.1.call-done = bf16[1280,1280]{1,0:T(8,128)(2,1)} async-done(((bf16[160,1280]{1,0:T(8,128)(2,1)}), bf16[1280,1280]{1,0:T(8,128)(2,1)}) %all-gather.7.cloned.1.call-update) | async-done | bytes 3276816 | tf_op jit(solution)/shard_map/all_gather | solution.py:226
  255.0 45.0 %all-to-all-done = bf16[2,256,1280]{1,0,2:T(2,128)(2,1)} async-done(((bf16[2,256,1280]{1,0,2:T(2,128)(2,1)}), bf16[2,256,1280]{1,0,2:T(2,128)(2,1)}, u32[]{:S(2)}, u32[]{:S(2)}) %all-to-all-start) | async-done | bytes 1310752 | tf_op jit(solution)/shard_map/all_to_all | solution.py:247
  302.7 332.8 %while.97 = (s32[]{:T(128)}, bf16[2,2048,160]{2,1,0:T(8,128)(2,1)}, f32[2,4,2,512]{3,2,1,0:T(2,128)S(1)}, bf16[2,2048,160]{1,2,0:T(8,128)(2,1)}, s32[2,2048]{1,0...) while((s32[]{:T(128)}, bf16[2,2048,160]{2,1,0:T(8,128)(2,1)}, ...), condition=%wide.region_12.13_spmd, body=%wide.region_3.12_spmd.sunk | while | flops 258727952 | bytes 23116628 | solution.py:262
  307.2 160.3 %while.100 = (s32[]{:T(128)}, bf16[4,512,160]{1,2,0:T(8,128)(2,1)S(1)}, f32[4,2,512]{2,1,0:T(2,128)S(1)}, s32[4]{0:T(128)S(1)}, bf16[4,512,2,80]{1,3,2,0:T(8,128...) while((s32[]{:T(128)}, ...), condition=%wide.region_11.11_spmd, body=%wide.region_4.10_spmd.sunk | while | flops 258727952 | bytes 8239557 | solution.py:120
  310.5 18.6 %while.103 = (s32[]{:T(128)}, f32[2,512]{1,0:T(2,128)S(1)}, f32[2,512]{1,0:T(2,128)S(1)}, s32[1,512]{1,0:T(1,128)S(1)}, s32[4]{0:T(128)S(1)}, /*index=5*/s32[4,5...) while((s32[]{:T(128)}, f32[2,512]{1,0:T(2,128)S(1)}, ...), condition=%wide.region_8.7_spmd.clone, body=%wide.region_5.6_spmd.clone.sunk | while | flops 87824392 | bytes 5378266 | solution.py:54
  329.1 18.1 %while.104 = (s32[]{:T(128)}, f32[512,2,80]{0,2,1:T(8,128)S(1)}, s32[4]{0:T(128)S(1)}, bf16[4,512,2,80]{1,3,2,0:T(8,128)(2,1)S(1)}, s32[1,512]{1,0:T(1,128)S(1)}...) while((s32[]{:T(128)}, f32[512,2,80]{0,2,1:T(8,128)S(1)}, ...), condition=%wide.region_10.9_spmd.clone, body=%wide.region_9.8_spmd.clone.sunk | while | flops 170820608 | bytes 1693404 | solution.py:54
  350.6 18.6 %while.103 = (s32[]{:T(128)}, f32[2,512]{1,0:T(2,128)S(1)}, f32[2,512]{1,0:T(2,128)S(1)}, s32[1,512]{1,0:T(1,128)S(1)}, s32[4]{0:T(128)S(1)}, /*index=5*/s32[4,5...) while((s32[]{:T(128)}, f32[2,512]{1,0:T(2,128)S(1)}, ...), condition=%wide.region_8.7_spmd.clone, body=%wide.region_5.6_spmd.clone.sunk | while | flops 87824392 | bytes 5378266 | solution.py:54
  369.2 18.1 %while.104 = (s32[]{:T(128)}, f32[512,2,80]{0,2,1:T(8,128)S(1)}, s32[4]{0:T(128)S(1)}, bf16[4,512,2,80]{1,3,2,0:T(8,128)(2,1)S(1)}, s32[1,512]{1,0:T(1,128)S(1)}...) while((s32[]{:T(128)}, f32[512,2,80]{0,2,1:T(8,128)S(1)}, ...), condition=%wide.region_10.9_spmd.clone, body=%wide.region_9.8_spmd.clone.sunk | while | flops 170820608 | bytes 1693404 | solution.py:54
  390.6 18.6 %while.103 = (s32[]{:T(128)}, f32[2,512]{1,0:T(2,128)S(1)}, f32[2,512]{1,0:T(2,128)S(1)}, s32[1,512]{1,0:T(1,128)S(1)}, s32[4]{0:T(128)S(1)}, /*index=5*/s32[4,5...) while((s32[]{:T(128)}, f32[2,512]{1,0:T(2,128)S(1)}, ...), condition=%wide.region_8.7_spmd.clone, body=%wide.region_5.6_spmd.clone.sunk | while | flops 87824392 | bytes 5378266 | solution.py:54
  409.2 18.1 %while.104 = (s32[]{:T(128)}, f32[512,2,80]{0,2,1:T(8,128)S(1)}, s32[4]{0:T(128)S(1)}, bf16[4,512,2,80]{1,3,2,0:T(8,128)(2,1)S(1)}, s32[1,512]{1,0:T(1,128)S(1)}...) while((s32[]{:T(128)}, f32[512,2,80]{0,2,1:T(8,128)S(1)}, ...), condition=%wide.region_10.9_spmd.clone, body=%wide.region_9.8_spmd.clone.sunk | while | flops 170820608 | bytes 1693404 | solution.py:54
  430.7 18.6 %while.103 = (s32[]{:T(128)}, f32[2,512]{1,0:T(2,128)S(1)}, f32[2,512]{1,0:T(2,128)S(1)}, s32[1,512]{1,0:T(1,128)S(1)}, s32[4]{0:T(128)S(1)}, /*index=5*/s32[4,5...) while((s32[]{:T(128)}, f32[2,512]{1,0:T(2,128)S(1)}, ...), condition=%wide.region_8.7_spmd.clone, body=%wide.region_5.6_spmd.clone.sunk | while | flops 87824392 | bytes 5378266 | solution.py:54
  449.3 18.1 %while.104 = (s32[]{:T(128)}, f32[512,2,80]{0,2,1:T(8,128)S(1)}, s32[4]{0:T(128)S(1)}, bf16[4,512,2,80]{1,3,2,0:T(8,128)(2,1)S(1)}, s32[1,512]{1,0:T(1,128)S(1)}...) while((s32[]{:T(128)}, f32[512,2,80]{0,2,1:T(8,128)S(1)}, ...), condition=%wide.region_10.9_spmd.clone, body=%wide.region_9.8_spmd.clone.sunk | while | flops 170820608 | bytes 1693404 | solution.py:54
  473.6 160.3 %while.100 = (s32[]{:T(128)}, bf16[4,512,160]{1,2,0:T(8,128)(2,1)S(1)}, f32[4,2,512]{2,1,0:T(2,128)S(1)}, s32[4]{0:T(128)S(1)}, bf16[4,512,2,80]{1,3,2,0:T(8,128...) while((s32[]{:T(128)}, ...), condition=%wide.region_11.11_spmd, body=%wide.region_4.10_spmd.sunk | while | flops 258727952 | bytes 8239557 | solution.py:120
  476.9 18.6 %while.103 = (s32[]{:T(128)}, f32[2,512]{1,0:T(2,128)S(1)}, f32[2,512]{1,0:T(2,128)S(1)}, s32[1,512]{1,0:T(1,128)S(1)}, s32[4]{0:T(128)S(1)}, /*index=5*/s32[4,5...) while((s32[]{:T(128)}, f32[2,512]{1,0:T(2,128)S(1)}, ...), condition=%wide.region_8.7_spmd.clone, body=%wide.region_5.6_spmd.clone.sunk | while | flops 87824392 | bytes 5378266 | solution.py:54
  495.5 18.1 %while.104 = (s32[]{:T(128)}, f32[512,2,80]{0,2,1:T(8,128)S(1)}, s32[4]{0:T(128)S(1)}, bf16[4,512,2,80]{1,3,2,0:T(8,128)(2,1)S(1)}, s32[1,512]{1,0:T(1,128)S(1)}...) while((s32[]{:T(128)}, f32[512,2,80]{0,2,1:T(8,128)S(1)}, ...), condition=%wide.region_10.9_spmd.clone, body=%wide.region_9.8_spmd.clone.sunk | while | flops 170820608 | bytes 1693404 | solution.py:54
  516.9 18.6 %while.103 = (s32[]{:T(128)}, f32[2,512]{1,0:T(2,128)S(1)}, f32[2,512]{1,0:T(2,128)S(1)}, s32[1,512]{1,0:T(1,128)S(1)}, s32[4]{0:T(128)S(1)}, /*index=5*/s32[4,5...) while((s32[]{:T(128)}, f32[2,512]{1,0:T(2,128)S(1)}, ...), condition=%wide.region_8.7_spmd.clone, body=%wide.region_5.6_spmd.clone.sunk | while | flops 87824392 | bytes 5378266 | solution.py:54
  535.5 18.1 %while.104 = (s32[]{:T(128)}, f32[512,2,80]{0,2,1:T(8,128)S(1)}, s32[4]{0:T(128)S(1)}, bf16[4,512,2,80]{1,3,2,0:T(8,128)(2,1)S(1)}, s32[1,512]{1,0:T(1,128)S(1)}...) while((s32[]{:T(128)}, f32[512,2,80]{0,2,1:T(8,128)S(1)}, ...), condition=%wide.region_10.9_spmd.clone, body=%wide.region_9.8_spmd.clone.sunk | while | flops 170820608 | bytes 1693404 | solution.py:54
  557.0 18.6 %while.103 = (s32[]{:T(128)}, f32[2,512]{1,0:T(2,128)S(1)}, f32[2,512]{1,0:T(2,128)S(1)}, s32[1,512]{1,0:T(1,128)S(1)}, s32[4]{0:T(128)S(1)}, /*index=5*/s32[4,5...) while((s32[]{:T(128)}, f32[2,512]{1,0:T(2,128)S(1)}, ...), condition=%wide.region_8.7_spmd.clone, body=%wide.region_5.6_spmd.clone.sunk | while | flops 87824392 | bytes 5378266 | solution.py:54
  575.6 18.1 %while.104 = (s32[]{:T(128)}, f32[512,2,80]{0,2,1:T(8,128)S(1)}, s32[4]{0:T(128)S(1)}, bf16[4,512,2,80]{1,3,2,0:T(8,128)(2,1)S(1)}, s32[1,512]{1,0:T(1,128)S(1)}...) while((s32[]{:T(128)}, f32[512,2,80]{0,2,1:T(8,128)S(1)}, ...), condition=%wide.region_10.9_spmd.clone, body=%wide.region_9.8_spmd.clone.sunk | while | flops 170820608 | bytes 1693404 | solution.py:54
  597.1 18.6 %while.103 = (s32[]{:T(128)}, f32[2,512]{1,0:T(2,128)S(1)}, f32[2,512]{1,0:T(2,128)S(1)}, s32[1,512]{1,0:T(1,128)S(1)}, s32[4]{0:T(128)S(1)}, /*index=5*/s32[4,5...) while((s32[]{:T(128)}, f32[2,512]{1,0:T(2,128)S(1)}, ...), condition=%wide.region_8.7_spmd.clone, body=%wide.region_5.6_spmd.clone.sunk | while | flops 87824392 | bytes 5378266 | solution.py:54
  615.7 18.1 %while.104 = (s32[]{:T(128)}, f32[512,2,80]{0,2,1:T(8,128)S(1)}, s32[4]{0:T(128)S(1)}, bf16[4,512,2,80]{1,3,2,0:T(8,128)(2,1)S(1)}, s32[1,512]{1,0:T(1,128)S(1)}...) while((s32[]{:T(128)}, f32[512,2,80]{0,2,1:T(8,128)S(1)}, ...), condition=%wide.region_10.9_spmd.clone, body=%wide.region_9.8_spmd.clone.sunk | while | flops 170820608 | bytes 1693404 | solution.py:54
  641.3 8.5 all-to-all-start.3
  655.5 40.9 %all-to-all-done.3 = bf16[2,2048,160]{2,0,1:T(2,128)(2,1)S(1)} async-done(((bf16[2,2048,160]{2,0,1:T(2,128)(2,1)}), bf16[2,2048,160]{2,0,1:T(2,128)(2,1)S(1)}, u32[]{:S(2)}, u32[]{:S(2)}) %all-to-all-start.3) | async-done | bytes 1310752 | tf_op jit(solution)/shard_map/all_to_all | solution.py:263
  710.2 7.5 fusion.53
  758.7 27.0 %all-to-all-done.4 = bf16[2,256,1280]{1,0,2:T(2,128)(2,1)S(1)} async-done(((bf16[2,256,1280]{1,0,2:T(2,128)(2,1)}), bf16[2,256,1280]{1,0,2:T(2,128)(2,1)S(1)}, u32[]{:S(2)}, u32[]{:S(2)}) %all-to-all-start.4) | async-done | bytes 1310752 | tf_op jit(solution)/shard_map/all_to_all | solution.py:297
  787.1 523.4 %while.99 = (s32[]{:T(128)}, bf16[2,2048,160]{1,2,0:T(8,128)(2,1)}, bf16[2,2048,160]{1,2,0:T(8,128)(2,1)}, bf16[2,2048,160]{1,2,0:T(8,128)(2,1)}, bf16[2,2048,16...) while((s32[]{:T(128)}, bf16[2,2048,160]{1,2,0:T(8,128)(2,1)}, ...), condition=%wide.region_21.22_spmd, body=%wide.region_15.21_spmd.sunk | while | flops 425443360 | bytes 54217724 | solution.py:306
  802.4 238.0 %while.101 = (s32[]{:T(128)}, f32[4,512,2,80]{1,3,2,0:T(8,128)S(1)}, f32[4,512,2,80]{1,3,2,0:T(8,128)S(1)}, bf16[4,512,2,80]{1,3,2,0:T(8,128)(2,1)}, s32[4]{0:T(...) while((s32[]{:T(128)}, f32[4,512,2,80]{1,3,2,0:T(8,128)S(1)}, ...), condition=%wide.region_20.20_spmd, body=%wide.region_16.19_spmd.sunk | while | flops 424788000 | bytes 15747515 | solution.py:195
  813.0 48.2 %while.102 = (s32[]{:T(128)}, f32[512,2,80]{0,2,1:T(8,128)S(1)}, f32[4,512,2,80]{1,3,2,0:T(8,128)S(1)}, f32[4,512,2,80]{1,3,2,0:T(8,128)S(1)}, s32[4]{0:T(128)},...) while((s32[]{:T(128)}, f32[512,2,80]{0,2,1:T(8,128)S(1)}, ...), condition=%wide.region_19.18_spmd.clone, body=%wide.region_17.17_spmd.clone.sunk | while | flops 424379424 | bytes 13100848 | solution.py:54
  872.5 48.2 %while.102 = (s32[]{:T(128)}, f32[512,2,80]{0,2,1:T(8,128)S(1)}, f32[4,512,2,80]{1,3,2,0:T(8,128)S(1)}, f32[4,512,2,80]{1,3,2,0:T(8,128)S(1)}, s32[4]{0:T(128)},...) while((s32[]{:T(128)}, f32[512,2,80]{0,2,1:T(8,128)S(1)}, ...), condition=%wide.region_19.18_spmd.clone, body=%wide.region_17.17_spmd.clone.sunk | while | flops 424379424 | bytes 13100848 | solution.py:54
  932.1 48.2 %while.102 = (s32[]{:T(128)}, f32[512,2,80]{0,2,1:T(8,128)S(1)}, f32[4,512,2,80]{1,3,2,0:T(8,128)S(1)}, f32[4,512,2,80]{1,3,2,0:T(8,128)S(1)}, s32[4]{0:T(128)},...) while((s32[]{:T(128)}, f32[512,2,80]{0,2,1:T(8,128)S(1)}, ...), condition=%wide.region_19.18_spmd.clone, body=%wide.region_17.17_spmd.clone.sunk | while | flops 424379424 | bytes 13100848 | solution.py:54
  991.5 48.1 %while.102 = (s32[]{:T(128)}, f32[512,2,80]{0,2,1:T(8,128)S(1)}, f32[4,512,2,80]{1,3,2,0:T(8,128)S(1)}, f32[4,512,2,80]{1,3,2,0:T(8,128)S(1)}, s32[4]{0:T(128)},...) while((s32[]{:T(128)}, f32[512,2,80]{0,2,1:T(8,128)S(1)}, ...), condition=%wide.region_19.18_spmd.clone, body=%wide.region_17.17_spmd.clone.sunk | while | flops 424379424 | bytes 13100848 | solution.py:54
  1064.1 237.8 %while.101 = (s32[]{:T(128)}, f32[4,512,2,80]{1,3,2,0:T(8,128)S(1)}, f32[4,512,2,80]{1,3,2,0:T(8,128)S(1)}, bf16[4,512,2,80]{1,3,2,0:T(8,128)(2,1)}, s32[4]{0:T(...) while((s32[]{:T(128)}, f32[4,512,2,80]{1,3,2,0:T(8,128)S(1)}, ...), condition=%wide.region_20.20_spmd, body=%wide.region_16.19_spmd.sunk | while | flops 424788000 | bytes 15747515 | solution.py:195
  1074.7 48.1 %while.102 = (s32[]{:T(128)}, f32[512,2,80]{0,2,1:T(8,128)S(1)}, f32[4,512,2,80]{1,3,2,0:T(8,128)S(1)}, f32[4,512,2,80]{1,3,2,0:T(8,128)S(1)}, s32[4]{0:T(128)},...) while((s32[]{:T(128)}, f32[512,2,80]{0,2,1:T(8,128)S(1)}, ...), condition=%wide.region_19.18_spmd.clone, body=%wide.region_17.17_spmd.clone.sunk | while | flops 424379424 | bytes 13100848 | solution.py:54
  1134.2 48.1 %while.102 = (s32[]{:T(128)}, f32[512,2,80]{0,2,1:T(8,128)S(1)}, f32[4,512,2,80]{1,3,2,0:T(8,128)S(1)}, f32[4,512,2,80]{1,3,2,0:T(8,128)S(1)}, s32[4]{0:T(128)},...) while((s32[]{:T(128)}, f32[512,2,80]{0,2,1:T(8,128)S(1)}, ...), condition=%wide.region_19.18_spmd.clone, body=%wide.region_17.17_spmd.clone.sunk | while | flops 424379424 | bytes 13100848 | solution.py:54
  1193.6 48.1 %while.102 = (s32[]{:T(128)}, f32[512,2,80]{0,2,1:T(8,128)S(1)}, f32[4,512,2,80]{1,3,2,0:T(8,128)S(1)}, f32[4,512,2,80]{1,3,2,0:T(8,128)S(1)}, s32[4]{0:T(128)},...) while((s32[]{:T(128)}, f32[512,2,80]{0,2,1:T(8,128)S(1)}, ...), condition=%wide.region_19.18_spmd.clone, body=%wide.region_17.17_spmd.clone.sunk | while | flops 424379424 | bytes 13100848 | solution.py:54
  1253.1 48.1 %while.102 = (s32[]{:T(128)}, f32[512,2,80]{0,2,1:T(8,128)S(1)}, f32[4,512,2,80]{1,3,2,0:T(8,128)S(1)}, f32[4,512,2,80]{1,3,2,0:T(8,128)S(1)}, s32[4]{0:T(128)},...) while((s32[]{:T(128)}, f32[512,2,80]{0,2,1:T(8,128)S(1)}, ...), condition=%wide.region_19.18_spmd.clone, body=%wide.region_17.17_spmd.clone.sunk | while | flops 424379424 | bytes 13100848 | solution.py:54
  1324.8 45.0 %all-to-all-done.5 = bf16[2,2048,160]{2,0,1:T(2,128)(2,1)S(1)} async-done(((bf16[2,2048,160]{2,0,1:T(2,128)(2,1)}), bf16[2,2048,160]{2,0,1:T(2,128)(2,1)S(1)}, u32[]{:S(2)}, u32[]{:S(2)}) %all-to-all-start.5) | async-done | bytes 1310752 | tf_op jit(solution)/shard_map/all_to_all | solution.py:310
  1387.5 75.1 %all_to_all.126 = bf16[2,2048,160]{2,0,1:T(2,128)(2,1)} all-to-all(bf16[2,2048,160]{2,0,1:T(2,128)(2,1)} %copy.265), channel_id=1, replica_groups=mesh['rep'=4,'shard'=8] {'shard'}, dimensions={1} | all-to-all | bytes 2621440 | tf_op jit(solution)/shard_map/all_to_all | solution.py:312
  1462.6 8.5 copy.266
  1483.7 77.8 %all_to_all.127 = bf16[2,2048,160]{2,0,1:T(2,128)(2,1)} all-to-all(bf16[2,2048,160]{2,0,1:T(2,128)(2,1)} %copy.263), channel_id=1, replica_groups=mesh['rep'=4,'shard'=8] {'shard'}, dimensions={1} | all-to-all | bytes 2621440 | tf_op jit(solution)/shard_map/all_to_all | solution.py:311
  1561.6 8.4 copy.264
  1610.2 66.8 %reduce-scatter.9.cloned.1.call-done = bf16[160,1280]{1,0:T(8,128)(2,1)} async-done(((bf16[1280,1280]{1,0:T(8,128)(2,1)}), bf16[160,1280]{1,0:T(8,128)(2,1)}) %reduce-scatter.9.cloned.1.call-update) | async-done | bytes 409616 | tf_op jit(solution)/shard_map/reduce_scatter | solution.py:340
  1677.1 26.4 %all-reduce.9 = (bf16[1280]{0:T(1024)(128)(2,1)S(1)}, bf16[1280]{0:T(1024)(128)(2,1)S(1)}, bf16[1280]{0:T(1024)(128)(2,1)S(1)}, bf16[8,80]{1,0:T(8,128)(2,1)S(1)}, bf16[1280]{0:T(1024)(128)(2,1)S(1)}) all-reduce(bf16[1280]{0:T(1024)(128)(2,1)S(1)} %get-tuple-element.776, ...), channel_id=2, replica_groups=mesh['rep'=4,'shard'=8] {'shard'}, use_global_device_ids=true, to_apply=%region_24.25.clone | all-reduce | flops 5760 | bytes 23040
  1704.4 12.9 all-reduce.11
  1724.4 13.3 all-reduce.15.cloned.1.call-done
  (1321 shorter events, 782.7 us)
Async XLA Ops:
  7.2 65.2 %all-gather.11.cloned.1.call-start = ((), (), s32[]{:S(2)}) async-start(), calls=%async_computation.16 | async-start | bytes 3686400 | tf_op jit(solution)/shard_map/all_gather | solution.py:228
  8.0 144.8 %all-gather.9.cloned.1.call-start = ((), (), s32[]{:S(2)}) async-start(), calls=%async_computation.15 | async-start | bytes 3686400 | tf_op jit(solution)/shard_map/all_gather | solution.py:227
  8.7 225.2 %all-gather.7.cloned.1.call-start = ((), (), s32[]{:S(2)}) async-start(), calls=%async_computation.14 | async-start | bytes 3686400 | tf_op jit(solution)/shard_map/all_gather | solution.py:226
  9.5 640.7 %all-gather.17.cloned.1.call-start = ((), (), s32[]{:S(2)}) async-start(), calls=%async_computation.19 | async-start | bytes 3686400 | tf_op jit(solution)/shard_map/all_gather | solution.py:231
  11.6 64.6 %copy-start.32 = (f32[512]{0:T(512)}, f32[512]{0:T(512)S(1)}, u32[]{:S(2)}) copy-start(f32[512]{0:T(512)S(1)} %rsqrt.25) | copy-start | bytes 6148
  42.5 33.8 %copy-start.19 = (bf16[512,1280]{1,0:T(8,128)(2,1)}, bf16[512,1280]{1,0:T(8,128)(2,1)S(1)}, u32[]{:S(2)}) copy-start(bf16[512,1280]{1,0:T(8,128)(2,1)S(1)} %fusion.59) | copy-start | bytes 3932164
  78.9 80.8 %all-to-all-start.2 = ((bf16[2,256,1280]{1,0,2:T(2,128)(2,1)}), bf16[2,256,1280]{1,0,2:T(2,128)(2,1)S(1)}, u32[]{:S(2)}, u32[]{:S(2)}) async-start(bf16[2,256,1280]{1,0,2:T(2,128)(2,1)} %copy.249), calls=%async_computation.2 | async-start | bytes 2621440 | tf_op jit(solution)/shard_map/all_to_all | solution.py:253
  83.6 620.7 %all-gather.13.cloned.1.call-start = ((), (), s32[]{:S(2)}) async-start(), calls=%async_computation.17 | async-start | bytes 3686400 | tf_op jit(solution)/shard_map/all_gather | solution.py:229
  157.0 8.7 copy-start.49
  159.7 84.6 %all-to-all-start.1 = ((bf16[2,256,1280]{1,0,2:T(2,128)(2,1)}), bf16[2,256,1280]{1,0,2:T(2,128)(2,1)S(1)}, u32[]{:S(2)}, u32[]{:S(2)}) async-start(bf16[2,256,1280]{1,0,2:T(2,128)(2,1)} %copy.246), calls=%async_computation.1 | async-start | bytes 2621440 | tf_op jit(solution)/shard_map/all_to_all | solution.py:250
  166.3 73.7 %copy-start.34 = (f32[1280]{0:T(1024)}, f32[1280]{0:T(1024)S(1)}, u32[]{:S(2)}) copy-start(f32[1280]{0:T(1024)S(1)} %mul.213) | copy-start | bytes 15364
  244.3 7.6 copy-start.40
  244.3 55.6 %all-to-all-start = ((bf16[2,256,1280]{1,0,2:T(2,128)(2,1)}), bf16[2,256,1280]{1,0,2:T(2,128)(2,1)}, u32[]{:S(2)}, u32[]{:S(2)}) async-start(bf16[2,256,1280]{1,0,2:T(2,128)(2,1)} %copy.243), calls=%async_computation | async-start | bytes 2621440 | tf_op jit(solution)/shard_map/all_to_all | solution.py:247
  251.3 459.0 %all-gather.15.cloned.1.call-start = ((), (), s32[]{:S(2)}) async-start(), calls=%async_computation.18 | async-start | bytes 3686400 | tf_op jit(solution)/shard_map/all_gather | solution.py:230
  641.3 8.8 copy-start.37
  641.3 8.9 copy-start.10
  641.3 55.1 %all-to-all-start.3 = ((bf16[2,2048,160]{2,0,1:T(2,128)(2,1)}), bf16[2,2048,160]{2,0,1:T(2,128)(2,1)S(1)}, u32[]{:S(2)}, u32[]{:S(2)}) async-start(bf16[2,2048,160]{2,0,1:T(2,128)(2,1)} %copy.253), calls=%async_computation.3 | async-start | bytes 4194304 | tf_op jit(solution)/shard_map/all_to_all | solution.py:263
  649.8 960.3 %reduce-scatter.15.cloned.1.call-start = ((), (), s32[]{:S(2)}) async-start(), calls=%async_computation.24 | async-start | bytes 3686400 | tf_op jit(solution)/shard_map/reduce_scatter | solution.py:349
  710.2 8.6 copy-start.5
  722.5 887.6 %reduce-scatter.13.cloned.1.call-start = ((), (), s32[]{:S(2)}) async-start(), calls=%async_computation.23 | async-start | bytes 3686400 | tf_op jit(solution)/shard_map/reduce_scatter | solution.py:346
  740.6 10.0 copy-start.9
  745.0 40.7 %all-to-all-start.4 = ((bf16[2,256,1280]{1,0,2:T(2,128)(2,1)}), bf16[2,256,1280]{1,0,2:T(2,128)(2,1)S(1)}, u32[]{:S(2)}, u32[]{:S(2)}) async-start(bf16[2,256,1280]{1,0,2:T(2,128)(2,1)} %copy.255), calls=%async_computation.4 | async-start | bytes 2621440 | tf_op jit(solution)/shard_map/all_to_all | solution.py:297
  750.6 859.6 %reduce-scatter.17.cloned.1.call-start = ((), (), s32[]{:S(2)}) async-start(), calls=%async_computation.25 | async-start | bytes 3686400 | tf_op jit(solution)/shard_map/reduce_scatter | solution.py:352
  802.4 6.8 copy-start.51
  813.0 48.9 %copy-start.52 = (s32[4]{0:T(128)S(1)}, s32[4]{0:T(128)}, u32[]{:S(2)}) copy-start(s32[4]{0:T(128)} %copy-done.51) | copy-start | bytes 52 | tf_op jit(solution)/shard_map/while/body/eval_jaxpr/while
  872.5 48.9 %copy-start.52 = (s32[4]{0:T(128)S(1)}, s32[4]{0:T(128)}, u32[]{:S(2)}) copy-start(s32[4]{0:T(128)} %copy-done.51) | copy-start | bytes 52 | tf_op jit(solution)/shard_map/while/body/eval_jaxpr/while
  921.4 6.8 copy-start.51
  932.0 48.9 %copy-start.52 = (s32[4]{0:T(128)S(1)}, s32[4]{0:T(128)}, u32[]{:S(2)}) copy-start(s32[4]{0:T(128)} %copy-done.51) | copy-start | bytes 52 | tf_op jit(solution)/shard_map/while/body/eval_jaxpr/while
  980.9 6.8 copy-start.51
  991.5 48.8 %copy-start.52 = (s32[4]{0:T(128)S(1)}, s32[4]{0:T(128)}, u32[]{:S(2)}) copy-start(s32[4]{0:T(128)} %copy-done.51) | copy-start | bytes 52 | tf_op jit(solution)/shard_map/while/body/eval_jaxpr/while
  1064.1 6.8 copy-start.51
  1074.7 48.8 %copy-start.52 = (s32[4]{0:T(128)S(1)}, s32[4]{0:T(128)}, u32[]{:S(2)}) copy-start(s32[4]{0:T(128)} %copy-done.51) | copy-start | bytes 52 | tf_op jit(solution)/shard_map/while/body/eval_jaxpr/while
  1134.2 48.8 %copy-start.52 = (s32[4]{0:T(128)S(1)}, s32[4]{0:T(128)}, u32[]{:S(2)}) copy-start(s32[4]{0:T(128)} %copy-done.51) | copy-start | bytes 52 | tf_op jit(solution)/shard_map/while/body/eval_jaxpr/while
  1183.0 6.8 copy-start.51
  1193.6 48.8 %copy-start.52 = (s32[4]{0:T(128)S(1)}, s32[4]{0:T(128)}, u32[]{:S(2)}) copy-start(s32[4]{0:T(128)} %copy-done.51) | copy-start | bytes 52 | tf_op jit(solution)/shard_map/while/body/eval_jaxpr/while
  1242.4 6.8 copy-start.51
  1253.0 48.8 %copy-start.52 = (s32[4]{0:T(128)S(1)}, s32[4]{0:T(128)}, u32[]{:S(2)}) copy-start(s32[4]{0:T(128)} %copy-done.51) | copy-start | bytes 52 | tf_op jit(solution)/shard_map/while/body/eval_jaxpr/while
  1316.5 6.8 copy-start.2
  1316.5 6.8 copy-start.29
  1316.5 6.8 copy-start.36
  1316.5 53.3 %all-to-all-start.5 = ((bf16[2,2048,160]{2,0,1:T(2,128)(2,1)}), bf16[2,2048,160]{2,0,1:T(2,128)(2,1)S(1)}, u32[]{:S(2)}, u32[]{:S(2)}) async-start(bf16[2,2048,160]{2,0,1:T(2,128)(2,1)} %copy.259), calls=%async_computation.5 | async-start | bytes 4194304 | tf_op jit(solution)/shard_map/all_to_all | solution.py:310
  1323.3 286.9 %reduce-scatter.7.cloned.1.call-start = ((), (), s32[]{:S(2)}) async-start(), calls=%async_computation.20 | async-start | bytes 3686400 | tf_op jit(solution)/shard_map/reduce_scatter | solution.py:337
  1381.5 228.8 %reduce-scatter.11.cloned.1.call-start = ((), (), s32[]{:S(2)}) async-start(), calls=%async_computation.22 | async-start | bytes 3686400 | tf_op jit(solution)/shard_map/reduce_scatter | solution.py:343
  1477.6 199.3 %reduce-scatter.9.cloned.1.call-start = ((), (), s32[]{:S(2)}) async-start(), calls=%async_computation.21 | async-start | bytes 3686400 | tf_op jit(solution)/shard_map/reduce_scatter | solution.py:340
  1576.4 161.3 %all-reduce.15.cloned.1.call-start = ((), (), s32[]{:S(2)}) async-start(), calls=%async_computation.26 | async-start | bytes 4915200 | tf_op jit(solution)/shard_map/psum | solution.py:372
  1610.1 66.9 %copy-start.50 = (f32[80]{0:T(128)S(1)}, f32[80]{0:T(128)}, u32[]{:S(2)}) copy-start(f32[80]{0:T(128)} %param.41) | copy-start | bytes 964
  1610.1 67.0 %copy-start.38 = (bf16[1280]{0:T(1024)(128)(2,1)S(1)}, bf16[1280]{0:T(1024)(128)(2,1)}, u32[]{:S(2)}) copy-start(bf16[1280]{0:T(1024)(128)(2,1)} %get-tuple-element.774) | copy-start | bytes 7684
  1610.1 110.0 %copy-start.31 = (f32[1,2,2,128]{3,1,2,0:T(2,128)S(1)}, f32[1,2,2,128]{3,1,2,0:T(2,128)}, u32[]{:S(2)}) copy-start(f32[1,2,2,128]{3,1,2,0:T(2,128)} %copy-done.30) | copy-start | bytes 6148
  (43 other events, 144.1 us)
Sparse Core Ops, SparseCore 0:
  10.3 62.1 all-gather.10
  74.6 78.1 all-gather.8
  155.0 78.8 all-gather.6
  236.0 78.3 all-gather.16
  316.4 62.3 all-gather.12
  380.9 60.5 all-gather.14
  722.6 93.4 reduce-scatter.14
  820.2 74.9 reduce-scatter.12
  898.8 75.0 reduce-scatter.16
  1381.6 109.5 reduce-scatter.6
  1494.8 103.1 reduce-scatter.10
  1601.9 75.0 reduce-scatter.8
  1679.8 57.9 all-reduce.14
where the time goes:
time: 1770 us; the launch traced here: 1750 us
  waiting for transfers between devices  408 us (23%)
  matrix products  344 us (19%)
  loops' own time  297 us (17%)
  local copies, waits for them, and re-layouts  278 us (16%)
  blocking collectives  220 us (12%)
  other arithmetic  149 us (8%)
  starting transfers between devices  40 us (2%)
    another operation x24, loops' own time, over_keys(): lax.scan(advance, start_carry, jnp.arange(block_count, dtype=jnp.int32))[0]  254 us
    dynamic_slice x112, local copies, waits for them, and re-layouts, attend_forward(): lax.map(one_block, jnp.arange(block_count, dtype=jnp.int32))  85.4 us
    all_to_all x1, blocking collectives, local(): lax.all_to_all(dk_heads, 'shard', split_axis=1, concat_axis=2, tiled=True)  77.8 us
    all_to_all x1, blocking collectives, local(): lax.all_to_all(dv_heads, 'shard', split_axis=1, concat_axis=2, tiled=True)  75.1 us
    dot_general x64, matrix products, block_scores(): jnp.einsum('qhe,khe->hqk', query_block, key_block, preferred_element_type...  72.8 us
    all_gather x1, waiting for transfers between devices, local(): lax.all_gather(key_weight, 'shard', axis=0, tiled=True)  68.6 us
    all_gather x1, waiting for transfers between devices, local(): lax.all_gather(query_weight, 'shard', axis=0, tiled=True)  67.6 us
    reduce_scatter x1, waiting for transfers between devices, local(): lax.psum_scatter(grad_key.astype(jnp.bfloat16), 'shard', scatter_dimensio...  66.8 us
  transfers between devices with their start and end apart: 19, of which 9 were waited for; matrix products, arithmetic and copies ran while one was open for 42% of the time, Pallas kernels for 0%

commit v1 on v0

v1 whole, which is shorter than its diff:
```python
import functools
import math

import jax
import jax.numpy as jnp
from jax import lax
from jax.experimental import pallas as pl
from jax.experimental.pallas import tpu as pltpu
from jax.sharding import PartitionSpec as P

HEAD_DIM = 80
LANES = 128
CORES = 2
NORM_EPS = 1e-06
LOG_BASE = 1.442695041
MASK_FILL = -1e30
AXES = ("rep", "shard")
F32 = jnp.float32
BF16 = jnp.bfloat16


def dot(left, right, left_dim=1, right_dim=0):
    return lax.dot_general(
        left, right, (((left_dim,), (right_dim,)), ((), ())), preferred_element_type=F32
    )


class Place:
    def __init__(self, reps, shards, seqs):
        self.x_size = reps // CORES
        self.a_size = CORES * seqs
        self.b_size = shards // self.a_size
        self.seqs = seqs
        rep, shard = lax.axis_index("rep"), lax.axis_index("shard")
        self.x, self.c = rep // CORES, rep % CORES
        self.a, self.b = shard // self.b_size, shard % self.b_size
        self.shard = shard

    def route(self, move):
        pairs = []
        for x in range(self.x_size):
            for c in range(CORES):
                for a in range(self.a_size):
                    for b in range(self.b_size):
                        pairs.append((self.number(x, c, a, b), self.number(*move(x, c, a, b))))
        return pairs

    def number(self, x, c, a, b):
        return ((x * CORES + c) * self.a_size + a) * self.b_size + b

    def send(self, value, dx=0, dc=0, da=0, db=0):
        return lax.ppermute(
            value,
            AXES,
            self.route(
                lambda x, c, a, b: (
                    (x + dx) % self.x_size,
                    (c + dc) % CORES,
                    (a + da) % self.a_size,
                    (b + db) % self.b_size,
                )
            ),
        )

    def peers(self):
        return [(db, dc) for db in range(self.b_size) for dc in range(CORES)]

    def to_cluster(self, tokens):
        seqs, count, width = tokens.shape
        half = count // CORES
        received = []
        for m in range(self.a_size):
            t = m ^ self.a
            part = lax.dynamic_slice(
                tokens, (t % seqs, (t // seqs) * half, 0), (1, half, width)
            ).reshape(half, width)
            received.append(lax.ppermute(part, AXES, self.route(self._match(m))))
        u = self.a % seqs + seqs * self.c
        return place(received, [m ^ u for m in range(self.a_size)])

    def from_cluster(self, chunks):
        half, width = chunks.shape[1:]
        u = self.a % self.seqs + self.seqs * self.c
        received = []
        for m in range(self.a_size):
            part = lax.dynamic_index_in_dim(chunks, m ^ u, 0, keepdims=False)
            back = [(j, i) for i, j in self.route(self._match(m))]
            received.append(lax.ppermute(part, AXES, back))
        spots = []
        for m in range(self.a_size):
            t = m ^ self.a
            spots.append((t % self.seqs) * CORES + t // self.seqs)
        return place(received, spots).reshape(self.seqs, CORES * half, width)

    def _match(self, m):
        def move(x, c, a, b):
            t = m ^ a
            return x, t // self.seqs, self.seqs * c + t % self.seqs, b

        return move

    def ring(self, value):
        up = self.send(value, da=-1)
        down = self.send(value, da=1)
        cut = value.shape[0] // 2
        far_low = self.send(up[:cut], da=-1)
        far_high = self.send(down[cut:], da=1)
        return [value, up, jnp.concatenate([far_low, far_high]), down]


def place_body(count, spots, *refs):
    pieces, target, sems = refs[:count], refs[count], refs[count + 1]
    copies = [
        pltpu.make_async_copy(pieces[k], target.at[spots[k]], sems.at[k]) for k in range(count)
    ]
    for copy in copies:
        copy.start()
    for copy in copies:
        copy.wait()


def place(pieces, spots):
    count = len(pieces)
    return pl.pallas_call(
        functools.partial(place_body, count),
        out_shape=jax.ShapeDtypeStruct((count, *pieces[0].shape), pieces[0].dtype),
        grid_spec=pltpu.PrefetchScalarGridSpec(
            num_scalar_prefetch=1,
            grid=(1,),
            in_specs=[pl.BlockSpec(memory_space=pltpu.VMEM)] * count,
            out_specs=pl.BlockSpec(memory_space=pl.ANY),
            scratch_shapes=[pltpu.SemaphoreType.DMA((count,))],
        ),
        compiler_params=pltpu.CompilerParams(vmem_limit_bytes=32 * 1024 * 1024),
        name="place",
    )(jnp.stack([jnp.asarray(s, jnp.int32) for s in spots]), *pieces)


def forward_body(heads, block, low, starts, query, key, value, mixed, query_aug, total, top):
    index = pl.program_id(0)
    total[...] = jnp.zeros_like(total)
    top[...] = jnp.full_like(top, MASK_FILL)
    rows = index * block + lax.broadcasted_iota(jnp.int32, (block, block), 0)
    begin = starts[...][:, :1]

    def step(j, carry):
        spot = pl.multiple_of(j * block, block)
        columns = spot + lax.broadcasted_iota(jnp.int32, (block, block), 1)
        bias = jnp.where((columns >= begin) & (columns <= rows), 0.0, MASK_FILL)
        for h in range(heads):
            lanes = slice(h * LANES, (h + 1) * LANES)
            score = dot(query[:, lanes], key[pl.ds(spot, block), lanes], 1, 1) + bias
            old = top[h]
            new = jnp.maximum(old, jnp.max(score, axis=1, keepdims=True))
            weight = jnp.exp(score - jnp.concatenate([new] * (block // LANES), axis=1))
            total[h] = total[h] * jnp.exp(old - new) + dot(
                weight.astype(BF16), value[pl.ds(spot, block), lanes]
            )
            top[h] = new
        return carry

    lax.fori_loop(low[index], index + 1, step, 0)
    lane = lax.broadcasted_iota(jnp.int32, (block, LANES), 1)
    for h in range(heads):
        lanes = slice(h * LANES, (h + 1) * LANES)
        acc = total[h]
        weight_sum = acc[:, HEAD_DIM : HEAD_DIM + 1]
        mixed[:, h * HEAD_DIM : (h + 1) * HEAD_DIM] = (acc / weight_sum)[:, :HEAD_DIM].astype(BF16)
        rest = -(top[h] + jnp.log(weight_sum))
        aug = query[:, lanes].astype(F32)
        for k in range(3):
            term = rest.astype(BF16).astype(F32)
            aug = jnp.where(lane == HEAD_DIM + k, term, aug)
            rest = rest - term
        query_aug[:, lanes] = aug.astype(BF16)


def attend_forward(low, starts, qkv, heads, block):
    length = qkv.shape[0]
    wide = heads * LANES
    return pl.pallas_call(
        functools.partial(forward_body, heads, block),
        out_shape=[
            jax.ShapeDtypeStruct((length, heads * HEAD_DIM), BF16),
            jax.ShapeDtypeStruct((length, wide), BF16),
        ],
        grid_spec=pltpu.PrefetchScalarGridSpec(
            num_scalar_prefetch=1,
            grid=(length // block,),
            in_specs=[
                pl.BlockSpec((block, LANES), lambda i, low: (i, 0)),
                pl.BlockSpec((block, wide), lambda i, low: (i, 0)),
                pl.BlockSpec((length, wide), lambda i, low: (0, 1)),
                pl.BlockSpec((length, wide), lambda i, low: (0, 2)),
            ],
            out_specs=[
                pl.BlockSpec((block, heads * HEAD_DIM), lambda i, low: (i, 0)),
                pl.BlockSpec((block, wide), lambda i, low: (i, 0)),
            ],
            scratch_shapes=[
                pltpu.VMEM((heads, block, LANES), F32),
                pltpu.VMEM((heads, block, LANES), F32),
            ],
        ),
        compiler_params=pltpu.CompilerParams(vmem_limit_bytes=48 * 1024 * 1024),
        name="attend_forward",
    )(low, starts, qkv, qkv, qkv)


def backward_body(
    heads,
    block,
    low,
    starts,
    scale,
    query,
    key,
    value,
    grad,
    mixed,
    grads,
    scale_sum,
    bias_sum,
    grad_aug,
    d_query,
    d_key,
    d_value,
):
    index = pl.num_programs(0) - 1 - pl.program_id(0)
    width = heads * HEAD_DIM

    @pl.when(pl.program_id(0) == 0)
    def clear():
        d_key[...] = jnp.zeros_like(d_key)
        d_value[...] = jnp.zeros_like(d_value)
        scale_sum[...] = jnp.zeros_like(scale_sum)
        bias_sum[...] = jnp.zeros_like(bias_sum)

    lane = lax.broadcasted_iota(jnp.int32, (block, LANES), 1)
    for h in range(heads):
        part = slice(h * HEAD_DIM, (h + 1) * HEAD_DIM)
        grad_h = grad[:, part].astype(F32)
        delta = jnp.sum(grad_h * mixed[:, part].astype(F32), axis=1, keepdims=True)
        aug = jnp.concatenate([grad_h, jnp.zeros((block, LANES - HEAD_DIM), F32)], axis=1)
        high = (-delta).astype(BF16).astype(F32)
        aug = jnp.where(lane == HEAD_DIM, high, aug)
        aug = jnp.where(lane == HEAD_DIM + 1, -delta - high, aug)
        grad_aug[:, h * LANES : (h + 1) * LANES] = aug.astype(BF16)
    d_query[...] = jnp.zeros_like(d_query)
    columns = index * block + lax.broadcasted_iota(jnp.int32, (block, block), 1)
    begin = starts[0:1, :]

    def step(j, carry):
        spot = pl.multiple_of(j * block, block)
        rows = spot + lax.broadcasted_iota(jnp.int32, (block, block), 0)
        allowed = (rows >= begin) & (rows <= columns)
        for h in range(heads):
            lanes = slice(h * LANES, (h + 1) * LANES)
            key_h = key[pl.ds(spot, block), lanes]
            query_h = query[:, lanes]
            grad_h = grad_aug[:, lanes]
            prob = jnp.where(allowed, jnp.exp(dot(key_h, query_h, 1, 1)), 0.0)
            d_prob = dot(value[pl.ds(spot, block), lanes], grad_h, 1, 1)
            d_score = (prob * d_prob).astype(BF16)
            d_value[pl.ds(spot, block), lanes] += dot(prob.astype(BF16), grad_h)
            d_key[pl.ds(spot, block), lanes] += dot(d_score, query_h)
            d_query[:, lanes] += dot(d_score, key_h, 0, 0)
        return carry

    lax.fori_loop(low[index], index + 1, step, 0)
    here = pl.ds(pl.multiple_of(index * block, block), block)
    for h in range(heads):
        lanes = slice(h * LANES, (h + 1) * LANES)
        d_scaled = d_query[:, lanes].astype(BF16).astype(F32)
        scale_sum[...] += jnp.sum(d_scaled * query[:, lanes].astype(F32), axis=0, keepdims=True)
        d_q = (d_scaled * scale[0:1, lanes]).astype(BF16)
        for k, term in enumerate((d_q, d_key[here, lanes], d_value[here, lanes])):
            spot = k * width + h * HEAD_DIM
            term = term.astype(BF16)
            grads[:, spot : spot + HEAD_DIM] = term[:, :HEAD_DIM]
            bias_sum[:, (k * heads + h) * LANES : (k * heads + h + 1) * LANES] += jnp.sum(
                term.astype(F32), axis=0, keepdims=True
            )


def attend_backward(low, starts, scale, query_aug, qkv, grad, mixed, heads, block):
    length = qkv.shape[0]
    wide = heads * LANES
    width = heads * HEAD_DIM
    count = length // block
    return pl.pallas_call(
        functools.partial(backward_body, heads, block),
        out_shape=[
            jax.ShapeDtypeStruct((length, 3 * width), BF16),
            jax.ShapeDtypeStruct((8, LANES), F32),
            jax.ShapeDtypeStruct((8, 3 * wide), F32),
        ],
        grid_spec=pltpu.PrefetchScalarGridSpec(
            num_scalar_prefetch=1,
            grid=(count,),
            in_specs=[
                pl.BlockSpec((8, block), lambda i, low: (0, count - 1 - i)),
                pl.BlockSpec((8, wide), lambda i, low: (0, 0)),
                pl.BlockSpec((block, wide), lambda i, low: (count - 1 - i, 0)),
                pl.BlockSpec((length, wide), lambda i, low: (0, 1)),
                pl.BlockSpec((length, wide), lambda i, low: (0, 2)),
                pl.BlockSpec((block, width), lambda i, low: (count - 1 - i, 0)),
                pl.BlockSpec((block, width), lambda i, low: (count - 1 - i, 0)),
            ],
            out_specs=[
                pl.BlockSpec((block, 3 * width), lambda i, low: (count - 1 - i, 0)),
                pl.BlockSpec((8, LANES), lambda i, low: (0, 0)),
                pl.BlockSpec((8, 3 * wide), lambda i, low: (0, 0)),
            ],
            scratch_shapes=[
                pltpu.VMEM((block, wide), BF16),
                pltpu.VMEM((block, wide), F32),
                pltpu.VMEM((length, wide), F32),
                pltpu.VMEM((length, wide), F32),
            ],
        ),
        compiler_params=pltpu.CompilerParams(vmem_limit_bytes=48 * 1024 * 1024),
        name="attend_backward",
    )(low, starts, scale, query_aug, qkv, qkv, grad, mixed)


def pick(stacked, index):
    return lax.dynamic_index_in_dim(stacked, index, 0, keepdims=False)


def gather_rows(at, pieces, cores):
    rows, width = pieces[0].shape
    split = at.x_size == 2
    if split:
        rows //= 2
        pieces = [pick(p.reshape(2, rows, width), at.x) for p in pieces]
    if cores:
        width //= CORES
        pieces = [pick(p.reshape(rows, CORES, width).swapaxes(0, 1), at.c) for p in pieces]
    near = [pieces[0]] + [at.send(pieces[db], db=db) for db in range(1, at.b_size)]
    rings = [at.ring(p) for p in near]
    found = {}
    for db, ring in enumerate(rings):
        for da, part in enumerate(ring):
            found[(0, da, db)] = part
            if split:
                found[(1, da, db)] = at.send(part, dx=1)
    x_count = 2 if split else 1
    spots, parts = [], []
    for (dx, da, db), part in found.items():
        spot = ((at.a + da) % at.a_size) * at.b_size + (at.b - db) % at.b_size
        spots.append(spot * x_count + ((at.x + dx) % 2 if split else 0))
        parts.append(part)
    whole = place(parts, spots).reshape(-1, width)
    if not cores:
        return whole
    other = at.send(whole, dc=1)
    flip = at.c == 1
    return jnp.concatenate(
        [jnp.where(flip, other, whole), jnp.where(flip, whole, other)], axis=1
    )


def sum_over(at, value, axis, size):
    spot = getattr(at, axis[1])
    total = pick(value, spot).astype(F32)
    for d in range(1, size):
        total = total + at.send(pick(value, (spot + d) % size), **{axis: d}).astype(F32)
    return total


def all_sum(at, value, axis, size):
    total = value
    for d in range(1, size):
        total = total + at.send(value, **{axis: d}).astype(value.dtype)
    return total


def both_cores(at, part):
    other = at.send(part, dc=1)
    flip = at.c == 1
    return jnp.concatenate([jnp.where(flip, other, part), jnp.where(flip, part, other)], axis=1)


def finish_rows(at, part):
    split = at.x_size == 2
    part = sum_over(at, part, "db", at.b_size)
    if not split:
        part = all_sum(at, part.astype(BF16), "dx", at.x_size)
        return part.reshape(-1, part.shape[-1])
    part = part[0].astype(BF16)
    other = at.send(part, dx=1)
    flip = at.x == 1
    return jnp.concatenate([jnp.where(flip, other, part), jnp.where(flip, part, other)], axis=0)


def reduce_full(at, grad):
    rows, width = grad.shape
    split = at.x_size == 2
    x_count = 2 if split else 1
    grad = grad.astype(BF16).reshape(rows, CORES, width // CORES).swapaxes(0, 1)
    part = sum_over(at, grad, "dc", CORES).astype(BF16)
    part = part.reshape(at.a_size, at.b_size, x_count, -1, width // CORES)
    if split:
        part = jnp.moveaxis(part, 2, 0)
        part = sum_over(at, part, "dx", 2).astype(BF16)[:, :, None]
    part = sum_over(at, part, "da", at.a_size).astype(BF16)
    part = finish_rows(at, part)
    return both_cores(at, part).astype(F32)


def reduce_heads(at, grad):
    rows, width = grad.shape
    split = at.x_size == 2
    x_count = 2 if split else 1
    part = grad.astype(BF16).reshape(at.a_size, at.b_size, x_count, -1, width)
    part = sum_over(at, part, "da", at.a_size).astype(BF16)
    if split:
        part = jnp.moveaxis(part, 1, 0)
        part = sum_over(at, part, "dx", 2).astype(BF16)
    else:
        part = all_sum(at, part, "dx", at.x_size)[:, 0]
    pieces, spots = [], []
    for db in range(at.b_size):
        piece = pick(part, (at.b + db) % at.b_size)
        piece = at.send(piece, db=db) if db else piece
        if split:
            other = at.send(piece, dx=1)
            flip = at.x == 1
            piece = jnp.concatenate(
                [jnp.where(flip, other, piece), jnp.where(flip, piece, other)], axis=0
            )
        for dc in range(CORES):
            pieces.append(at.send(piece, dc=dc) if dc else piece)
            spots.append(((at.b - db) % at.b_size) * CORES + (at.c + dc) % CORES)
    stacked = place(pieces, spots)
    count, rows = stacked.shape[:2]
    stacked = stacked.reshape(count, rows, 3, width // 3)
    return stacked.transpose(2, 1, 0, 3).reshape(3, rows, count * width // 3).astype(F32)


def local(
    reps,
    shards,
    activations,
    cotangent,
    doc_lengths,
    gain_attn,
    query_weight,
    query_bias,
    key_weight,
    value_weight,
    value_bias,
    dim_scale,
    out_weight,
    gain_mlp,
    up_weight,
    down_weight,
):
    seqs, tok_count, model = activations.shape
    at = Place(reps, shards, seqs)
    half = tok_count // CORES
    length = tok_count * shards
    peer_count = at.b_size * CORES
    heads = model // HEAD_DIM // peer_count
    width = heads * HEAD_DIM
    wide = heads * LANES
    own_rows = at.a_size * half
    block = min(256, length)
    mine = at.b * CORES + at.c

    vectors = jnp.stack([gain_attn, gain_mlp, query_bias, value_bias])
    vectors = lax.dynamic_update_slice(
        jnp.zeros((4, model), BF16), vectors, (0, at.shard * gain_attn.shape[0])
    )
    vectors = all_sum(at, vectors, "db", at.b_size)
    vectors = all_sum(at, vectors, "da", at.a_size).astype(F32)
    g_attn, g_mlp, b_query, b_value = vectors[0], vectors[1], vectors[2], vectors[3]

    other_lengths = at.send(doc_lengths, dc=1)
    lengths = pick(jnp.where(at.c == at.a // seqs, doc_lengths, other_lengths), at.a % seqs)
    ends = jnp.cumsum(lengths)
    places = jnp.arange(length, dtype=jnp.int32)
    starts = jnp.max(jnp.where(ends[None, :] <= places[:, None], ends[None, :], 0), axis=1)
    starts_row = jnp.broadcast_to(starts[None, :], (8, length))
    starts_col = jnp.broadcast_to(starts[:, None], (length, LANES))
    low = starts[::block] // block

    chunks = at.to_cluster(activations)
    hidden = chunks.reshape(own_rows, model).astype(F32)
    rate_attn = lax.rsqrt(jnp.mean(hidden * hidden, axis=-1, keepdims=True) + NORM_EPS)
    normed_own = (hidden * rate_attn * g_attn).astype(BF16).reshape(at.a_size, half, model)

    stack3 = jnp.stack([query_weight, key_weight, value_weight], axis=1)
    stack3 = stack3.reshape(-1, 3, peer_count, width)
    pieces = [
        lax.dynamic_index_in_dim(
            stack3, ((at.b + db) % at.b_size) * CORES + at.c, 2, keepdims=False
        ).reshape(-1, 3 * width)
        for db in range(at.b_size)
    ]
    w_heads = gather_rows(at, pieces, False)

    parts, spots = [], []
    for db in range(at.b_size):
        near = at.send(normed_own, db=db) if db else normed_own
        for dc in range(CORES):
            part = at.send(near, dc=dc) if dc else near
            for a in range(at.a_size):
                parts.append(part[a])
                spots.append(
                    a * peer_count + ((at.b - db) % at.b_size) * CORES + (at.c + dc) % CORES
                )
    normed = place(parts, spots).reshape(length, model)

    scale_dim = LOG_BASE / math.sqrt(HEAD_DIM) * jax.nn.softplus(dim_scale)
    scale_pad = jnp.tile(jnp.pad(scale_dim, (0, LANES - HEAD_DIM)), heads)
    lane = jnp.arange(LANES)
    ones_key = ((lane >= HEAD_DIM) & (lane < HEAD_DIM + 3)).astype(F32)
    ones_value = ((lane >= HEAD_DIM) & (lane < HEAD_DIM + 2)).astype(F32)

    def pad_heads(vec):
        part = lax.dynamic_slice_in_dim(vec, mine * width, width, 0).reshape(heads, HEAD_DIM)
        return jnp.pad(part, ((0, 0), (0, LANES - HEAD_DIM))).reshape(wide)

    bias_pad = jnp.concatenate(
        [
            pad_heads(b_query),
            jnp.tile(ones_key, heads),
            pad_heads(b_value) + jnp.tile(ones_value, heads),
        ]
    )
    times = jnp.concatenate([scale_pad, jnp.ones((2 * wide,), F32)])
    w_pad = jnp.pad(
        w_heads.reshape(model, 3 * heads, HEAD_DIM), ((0, 0), (0, 0), (0, LANES - HEAD_DIM))
    ).reshape(model, 3 * wide)
    qkv = ((dot(normed, w_pad) + bias_pad) * times).astype(BF16)

    mixed_heads, query_aug = attend_forward(low, starts_col, qkv, heads, block)

    w_out = gather_rows(at, [out_weight] * at.b_size, True)
    w_up = gather_rows(at, [up_weight] * at.b_size, True)
    w_down = gather_rows(at, [down_weight] * at.b_size, True)
    d_out = at.to_cluster(cotangent).reshape(own_rows, model)

    by_peer = mixed_heads.reshape(at.a_size, peer_count, half, width)
    parts, spots = [], []
    for db, dc in at.peers():
        peer = ((at.b + db) % at.b_size) * CORES + (at.c + dc) % CORES
        part = lax.dynamic_index_in_dim(by_peer, peer, 1, keepdims=False)
        part = at.send(part, db=db, dc=dc) if db or dc else part
        parts.append(part.reshape(own_rows, width))
        spots.append(((at.b - db) % at.b_size) * CORES + (at.c + dc) % CORES)
    mixed = place(parts, spots).transpose(1, 0, 2).reshape(own_rows, model)

    residual = hidden + dot(mixed, w_out)
    rate_mlp = lax.rsqrt(jnp.mean(residual * residual, axis=-1, keepdims=True) + NORM_EPS)
    normed_mlp = (residual * rate_mlp * g_mlp).astype(BF16)
    upward = dot(normed_mlp, w_up)
    gate = jax.nn.sigmoid(upward)
    activated = (upward * gate).astype(BF16)
    output = (residual + dot(activated, w_down)).astype(BF16)
    output = at.from_cluster(output.reshape(at.a_size, half, model))

    d_activated = dot(d_out, w_down, 1, 1)
    d_up = (d_activated * gate * (1 + upward * (1 - gate))).astype(BF16)
    d_normed_mlp = dot(d_up, w_up, 1, 1)

    def norm_back(values, rate, gain, grad):
        scaled = grad * gain
        inner = jnp.mean(values * scaled, axis=-1, keepdims=True)
        return (
            rate * scaled - values * (rate * rate * rate * inner),
            jnp.sum(grad * values * rate, axis=0),
        )

    d_norm, grad_gain_mlp = norm_back(residual, rate_mlp, g_mlp, d_normed_mlp)
    d_residual = d_out.astype(F32) + d_norm
    d_proj = d_residual.astype(BF16)
    d_mixed = dot(d_proj, w_out, 1, 1).astype(BF16)

    by_peer = d_mixed.reshape(at.a_size, half, peer_count, width)
    parts, spots = [], []
    for db, dc in at.peers():
        peer = ((at.b + db) % at.b_size) * CORES + (at.c + dc) % CORES
        part = lax.dynamic_index_in_dim(by_peer, peer, 2, keepdims=False)
        part = at.send(part, db=db, dc=dc) if db or dc else part
        source = ((at.b - db) % at.b_size) * CORES + (at.c + dc) % CORES
        for a in range(at.a_size):
            parts.append(part[a])
            spots.append(a * peer_count + source)
    grad_heads = place(parts, spots).reshape(length, width)

    grad_down = reduce_full(at, dot(activated, d_out, 0, 0))
    grad_up = reduce_full(at, dot(normed_mlp, d_up, 0, 0))
    grad_out = reduce_full(at, dot(mixed, d_proj, 0, 0))

    scale_rows = jnp.broadcast_to(scale_pad[None, :], (8, wide))
    d_heads, scale_sum, bias_sum = attend_backward(
        low, starts_row, scale_rows, query_aug, qkv, grad_heads, mixed_heads, heads, block
    )

    partial = dot(d_heads, w_heads, 1, 1).astype(BF16)
    partial = partial.reshape(at.a_size, at.b_size, CORES, half, model)
    partial = sum_over(at, jnp.moveaxis(partial, 2, 0), "dc", CORES).astype(BF16)
    d_normed = sum_over(at, jnp.moveaxis(partial, 1, 0), "db", at.b_size)
    d_normed = d_normed.reshape(own_rows, model)
    d_norm, grad_gain_attn = norm_back(hidden, rate_attn, g_attn, d_normed)
    input_grad = (d_residual + d_norm).astype(BF16)
    input_grad = at.from_cluster(input_grad.reshape(at.a_size, half, model))

    grads = reduce_heads(at, dot(normed, d_heads, 0, 0))

    bias_sum = bias_sum[0].reshape(3, heads, LANES)[:, :, :HEAD_DIM].reshape(3, width)

    def spread(vec):
        return lax.dynamic_update_slice(jnp.zeros((model,), F32), vec, (mine * width,))

    scale_part = jnp.where(scale_dim > 0, scale_sum[0, :HEAD_DIM] / scale_dim, 0.0)
    scale_part = scale_part * (LOG_BASE / math.sqrt(HEAD_DIM)) * jax.nn.sigmoid(dim_scale)
    small = jnp.stack(
        [
            grad_gain_attn,
            grad_gain_mlp,
            spread(bias_sum[0]),
            spread(bias_sum[2]),
            jnp.pad(scale_part, (0, model - HEAD_DIM)),
        ]
    )
    small = all_sum(at, small, "dc", CORES)
    small = all_sum(at, small, "dx", at.x_size)
    small = all_sum(at, small, "db", at.b_size)
    small = all_sum(at, small, "da", at.a_size)
    rows = gain_attn.shape[0]
    owned = lax.dynamic_slice(small, (0, at.shard * rows), (5, rows))
    return (
        output,
        input_grad,
        owned[0],
        grads[0],
        owned[2],
        grads[1],
        grads[2],
        owned[3],
        small[4, :HEAD_DIM],
        grad_out,
        owned[1],
        grad_up,
        grad_down,
    )


def solution(mesh):
    in_specs = (
        P("rep", "shard", None),
        P("rep", "shard", None),
        P("rep", None),
        P("shard"),
        P("shard", None),
        P("shard"),
        P("shard", None),
        P("shard", None),
        P("shard"),
        P(),
        P("shard", None),
        P("shard"),
        P("shard", None),
        P("shard", None),
    )
    out_specs = (
        P("rep", "shard", None),
        P("rep", "shard", None),
        P("shard"),
        P("shard", None),
        P("shard"),
        P("shard", None),
        P("shard", None),
        P("shard"),
        P(),
        P("shard", None),
        P("shard"),
        P("shard", None),
        P("shard", None),
    )
    body = functools.partial(local, mesh.shape["rep"], mesh.shape["shard"])
    return jax.shard_map(body, mesh=mesh, in_specs=in_specs, out_specs=out_specs, check_vma=False)
```

time: 1770 us -> 771 us (0.44)
  loops' own time: 297 us -> 0 us
  matrix products: 344 us -> 55.1 us
  blocking collectives: 220 us -> 0 us
  waiting for transfers between devices: 408 us -> 236 us
  starting transfers between devices: 40 us -> 194 us
  local copies, waits for them, and re-layouts: 278 us -> 135 us
  other arithmetic: 149 us -> 41.6 us
  Pallas kernels: 0 us -> 95.8 us
    another operation x30 -> x0, loops' own time: 297 us -> none  [the longest x24 254 us: over_keys(): lax.scan(advance, start_carry, jnp.arange(block_count, dtype=jnp.int32))[0]]
    dot_general x242 -> x12, matrix products: 344 us -> 55.1 us  [dot(): lax.dot_general(left, right, (((left_dim,), (right_dim,)), ((), ())), pre...]
    ppermute x0 -> x142, waiting for transfers between devices: none -> 236 us  [the longest x126 191 us: send(): lax.ppermute(value, AXES, self.route(lambda x, c, a, b: ((x + dx) % self....]
    ppermute x0 -> x142, starting transfers between devices: none -> 194 us  [the longest x126 146 us: send(): lax.ppermute(value, AXES, self.route(lambda x, c, a, b: ((x + dx) % self....]
    all_gather x6 -> x0, waiting for transfers between devices: 166 us -> none  [the longest x1 68.6 us: local(): lax.all_gather(key_weight, 'shard', axis=0, tiled=True)]
    all_to_all x6 -> x0, waiting for transfers between devices: 158 us -> none  [the longest x1 45 us: local(): lax.all_to_all(dq_heads, 'shard', split_axis=1, concat_axis=2, tiled=True)]
    all_to_all x2 -> x0, blocking collectives: 153 us -> none  [the longest x1 77.8 us: local(): lax.all_to_all(dk_heads, 'shard', split_axis=1, concat_axis=2, tiled=True)]
    dynamic_slice x250 -> x8, local copies, waits for them, and re-layouts: 113 us -> 9.49 us  [the longest x4 7.97 us: local(): part = lax.dynamic_index_in_dim(by_peer, peer, 2, keepdims=False)]
  transfers between devices with their start and end apart: 19 -> 142, of which waited for: 9 -> 40; matrix products, arithmetic and copies ran while one was open for 42% -> 24% of each run, Pallas kernels for 0% -> 12%
where the time goes in v1:
time: 771 us; the launch traced here: 761 us
  waiting for transfers between devices  236 us (31%)
  starting transfers between devices  194 us (25%)
  local copies, waits for them, and re-layouts  135 us (18%)
  Pallas kernels  95.8 us (12%)
  matrix products  55.1 us (7%)
  other arithmetic  41.6 us (5%)
    ppermute x126, waiting for transfers between devices, send(): lax.ppermute(value, AXES, self.route(lambda x, c, a, b: ((x + dx) % self....  191 us
    ppermute x126, starting transfers between devices, send(): lax.ppermute(value, AXES, self.route(lambda x, c, a, b: ((x + dx) % self....  146 us
    dot_general x12, matrix products, dot(): lax.dot_general(left, right, (((left_dim,), (right_dim,)), ((), ())), pre...  55.1 us
    pallas_call x1, Pallas kernels, attend_backward(): pl.pallas_call(functools.partial(backward_body, heads, block), out_shape=...  42.5 us
    ppermute x8, starting transfers between devices, to_cluster(): received.append(lax.ppermute(part, AXES, self.route(self._match(m))))  31.1 us
    pallas_call x1, Pallas kernels, attend_forward(): pl.pallas_call(functools.partial(forward_body, heads, block), out_shape=[...  27.8 us
    ppermute x8, waiting for transfers between devices, from_cluster(): received.append(lax.ppermute(part, AXES, back))  25.9 us
    pallas_call x12, Pallas kernels, place(): pl.pallas_call(functools.partial(place_body, count), out_shape=jax.ShapeD...  25.5 us
  transfers between devices with their start and end apart: 142, of which 40 were waited for; matrix products, arithmetic and copies ran while one was open for 24% of the time, Pallas kernels for 12%

profile of v1, /device:TPU:9, one launch (start us, length us, event | category | flops | bytes accessed | tf_op | source)
XLA Modules:
  0.0 760.7 jit_solution(433422812289964968)
XLA Ops:
  14.9 3.6 pad_maximum_fusion.9
  45.8 4.2 collective-permute-done.71
  94.8 12.9 %collective-permute-start = (bf16[128,1280]{1,0:T(8,128)(2,1)S(1)}, bf16[128,1280]{1,0:T(8,128)(2,1)S(1)}, u32[]{:S(2)}, u32[]{:S(2)}) collective-permute-start(bf16[128,1280]{1,0:T(8,128)(2,1)S(1)} %copy-done.55), channel_id=1, source_target_pairs={{0,0},{1,1},{2,2},{3,3},{4,8},{5,9},{6,10},{7,11},{8,4},{9,5},{10,... | collective-permute-start | bytes 983048 | tf_op jit(solution)/shard_map/ppermute | solution.py:77
  109.6 4.0 collective-permute-start.62
  113.6 6.4 collective-permute-done.62
  121.9 16.0 %collective-permute-done.46 = bf16[40,640]{1,0:T(8,128)(2,1)S(1)} collective-permute-done((bf16[40,640]{1,0:T(8,128)(2,1)S(1)}, bf16[40,640]{1,0:T(8,128)(2,1)S(1)}, u32[]{:S(2)}, u32[]{:S(2)}) %collective-permute-start.46) | collective-permute-done | bytes 51232 | tf_op jit(solution)/shard_map/ppermute | solution.py:52
  161.4 14.4 %collective-permute-start.90 = (bf16[128,1280]{1,0:T(8,128)(2,1)S(1)}, bf16[128,1280]{1,0:T(8,128)(2,1)S(1)}, u32[]{:S(2)}, u32[]{:S(2)}) collective-permute-start(bf16[128,1280]{1,0:T(8,128)(2,1)S(1)} %get-tuple-element.69), channel_id=1, source_target_pairs={{0,0},{1,1},{2,2},{3,3},{4,8},{5,9},{6,10},{7,11},{8,4},{9,5},{10,... | collective-permute-start | bytes 983048 | tf_op jit(solution)/shard_map/ppermute | solution.py:77
  183.5 15.0 %collective-permute-done.91.refs_1_ = bf16[128,1280]{1,0:T(8,128)(2,1)S(1)} collective-permute-done((bf16[128,1280]{1,0:T(8,128)(2,1)S(1)}, bf16[128,1280]{1,0:T(8,128)(2,1)S(1)}, u32[]{:S(2)}, u32[]{:S(2)}) %collective-permute-start.91) | collective-permute-done | bytes 327712 | tf_op jit(solution)/shard_map/ppermute | solution.py:77
  228.2 4.5 place.14
  234.3 6.4 copy.91
  240.7 7.1 reshape_reshape.11
  256.6 3.9 broadcast_select_fusion.1
  264.4 10.5 %multiply_convert_fusion.query.key.value = bf16[2048,1536]{1,0:T(8,128)(2,1)} fusion(bf16[2048,1280]{1,0:T(8,128)(2,1)S(1)} %bitcast.396, bf16[1280,1536]{0,1:T(8,128)(2,1)S(1)} %bitcast.434, f32[1536]{0:T(1024)S(1)} %concatenate.67, f32[1536]{0:T(1024)S(1)} %pad_maximum_fusion.15), kind=kOutput, calls=%fused_computation | convolution fusion | flops 8062500864 | bytes 15478784 | tf_op jit(solution)/shard_map/dot_general | solution.py:23
  275.2 27.8 %attend_forward.1 = (bf16[2048,320]{1,0:T(8,128)(2,1)S(1)}, bf16[2048,512]{1,0:T(8,128)(2,1)S(1)}) custom-call(s32[8]{0:T(128)S(1)} %and_select_fusion.low, s32[2048,128]{1,0:T(8,128)S(1)} %broadcast_in_dim.20.starts, bf16[2048,1536]{1,0:T(8,128)(2,1)} %multiply_convert_fusion.query.key.value, bf16[2048,1536]{1,0:T(8,128)(2,1)} %multiply_convert_fusion.query.key.value, ...), custom_call_target="tpu_custom_call" | custom-call | tf_op jit(solution)/shard_map/attend_forward/pallas_call | solution.py:181
  305.5 4.0 broadcast_select_fusion.3
  309.4 4.2 collective-permute-done.30
  313.7 9.0 %collective-permute-done.31 = bf16[4,128,320]{2,1,0:T(8,128)(2,1)S(1)} collective-permute-done((bf16[4,128,320]{2,1,0:T(8,128)(2,1)S(1)}, bf16[4,128,320]{2,1,0:T(8,128)(2,1)S(1)}, u32[]{:S(2)}, u32[]{:S(2)}) %collective-permute-start.31) | collective-permute-done | bytes 327712 | tf_op jit(solution)/shard_map/ppermute | solution.py:52
  327.9 4.6 multiply_reduce_fusion.2
  346.6 3.7 convolution_convert_fusion.2
  350.3 3.7 convolution_convert_fusion.1
  354.0 3.8 convolution_convert_fusion
  358.8 3.8 collective-permute-start.86
  362.7 4.9 reshape.588
  367.6 5.6 constant_dynamic-slice_fusion.12
  386.9 3.5 copy.106
  390.4 3.5 copy.128
  393.9 3.5 copy.108
  397.4 3.5 copy.129
  404.5 3.5 copy.131
  414.5 42.5 %attend_backward.1 = (bf16[2048,960]{1,0:T(8,128)(2,1)}, f32[8,128]{1,0:T(8,128)S(1)}, f32[8,1536]{1,0:T(8,128)S(1)}) custom-call(s32[8]{0:T(128)S(1)} %and_select_fusion.low, s32[8,2048]{1,0:T(8,128)S(1)} %broadcast_in_dim.22.starts, f32[8,512]{1,0:T(8,128)S(1)} %broadcast_in_dim.23.scale, bf16[2048,512]{1,0:T(8,128)(2,1)S(1)} %copy-done.9, ...), custom_call_target="tpu_custom_call" | custom-call | tf_op jit(solution)/shard_map/attend_backward/pallas_call | solution.py:291
  457.0 9.2 %convolution_convert_fusion.4 = bf16[1280,960]{0,1:T(8,128)(2,1)} fusion(bf16[2048,1280]{1,0:T(8,128)(2,1)S(1)} %bitcast.399, bf16[2048,960]{1,0:T(8,128)(2,1)} %get-tuple-element.20), kind=kOutput, calls=%fused_computation.7 | convolution fusion | flops 5034393600 | bytes 11632640 | tf_op jit(solution)/shard_map/dot_general | solution.py:23
  466.2 4.5 copy.101
  477.9 7.5 convolution_convert_fusion.3
  485.4 4.8 collective-permute-done.111
  490.5 28.1 %collective-permute-done.110 = bf16[2,2,80,960]{3,2,1,0:T(8,128)(2,1)S(1)} collective-permute-done((bf16[2,2,80,960]{3,2,1,0:T(8,128)(2,1)S(1)}, bf16[2,2,80,960]{3,2,1,0:T(8,128)(2,1)S(1)}, u32[]{:S(2)}, u32[]{:S(2)}) %collective-permute-start.110) | collective-permute-done | bytes 614432 | tf_op jit(solution)/shard_map/ppermute | solution.py:52
  519.6 16.6 %collective-permute-done.109 = bf16[2,2,80,960]{3,2,1,0:T(8,128)(2,1)S(1)} collective-permute-done((bf16[2,2,80,960]{3,2,1,0:T(8,128)(2,1)S(1)}, bf16[2,2,80,960]{3,2,1,0:T(8,128)(2,1)S(1)}, u32[]{:S(2)}, u32[]{:S(2)}) %collective-permute-start.109) | collective-permute-done | bytes 614432 | tf_op jit(solution)/shard_map/ppermute | solution.py:52
  542.4 4.8 collective-permute-done.112
  562.5 5.3 collective-permute-done.116
  580.7 3.7 reshape.587
  584.4 8.3 %fusion.60 = (f32[1,160,4,320]{3,0,1,2:T(1,128)}, f32[1,160,4,320]{3,0,1,2:T(1,128)}, f32[1,160,4,320]{3,0,1,2:T(1,128)S(1)}) fusion(f32[3,160,4,320]{3,0,1,2:T(4,128)} %bitcast.423), kind=kLoop, calls=%fused_computation.289 | loop fusion | bytes 4915200 | tf_op jit(solution)/shard_map/slice | solution.py:643
  614.0 14.1 %collective-permute-done.135 = bf16[4,2,80,640]{3,2,1,0:T(8,128)(2,1)} collective-permute-done((bf16[4,2,80,640]{3,2,1,0:T(8,128)(2,1)}, bf16[4,2,80,640]{3,2,1,0:T(8,128)(2,1)}, u32[]{:S(2)}, u32[]{:S(2)}) %collective-permute-start.135) | collective-permute-done | bytes 819232 | tf_op jit(solution)/shard_map/ppermute | solution.py:52
  637.4 8.4 %collective-permute-done.129 = bf16[2,1,80,640]{3,2,1,0:T(8,128)(2,1)S(1)} collective-permute-done((bf16[2,1,80,640]{3,2,1,0:T(8,128)(2,1)S(1)}, bf16[2,1,80,640]{3,2,1,0:T(8,128)(2,1)S(1)}, u32[]{:S(2)}, u32[]{:S(2)}) %collective-permute-start.129) | collective-permute-done | bytes 204832 | tf_op jit(solution)/shard_map/ppermute | solution.py:52
  647.9 10.0 %collective-permute-done.128 = bf16[2,1,80,640]{3,2,1,0:T(8,128)(2,1)S(1)} collective-permute-done((bf16[2,1,80,640]{3,2,1,0:T(8,128)(2,1)S(1)}, bf16[2,1,80,640]{3,2,1,0:T(8,128)(2,1)S(1)}, u32[]{:S(2)}, u32[]{:S(2)}) %collective-permute-start.128) | collective-permute-done | bytes 204832 | tf_op jit(solution)/shard_map/ppermute | solution.py:52
  662.3 4.4 collective-permute-done.136
  684.2 23.2 %collective-permute-done.98 = bf16[4,128,1280]{2,1,0:T(8,128)(2,1)S(1)} collective-permute-done((bf16[4,128,1280]{2,1,0:T(8,128)(2,1)S(1)}, bf16[4,128,1280]{2,1,0:T(8,128)(2,1)S(1)}, u32[]{:S(2)}, u32[]{:S(2)}) %collective-permute-start.98) | collective-permute-done | bytes 1310752 | tf_op jit(solution)/shard_map/ppermute | solution.py:52
  724.2 6.3 collective-permute-start.99
  735.0 15.1 %collective-permute-done.99.refs_0_ = bf16[128,1280]{1,0:T(8,128)(2,1)S(1)} collective-permute-done((bf16[128,1280]{1,0:T(8,128)(2,1)S(1)}, bf16[128,1280]{1,0:T(8,128)(2,1)S(1)}, u32[]{:S(2)}, u32[]{:S(2)}) %collective-permute-start.99) | collective-permute-done | bytes 327712 | tf_op jit(solution)/shard_map/ppermute | solution.py:88
  750.1 7.3 collective-permute-done.100.refs_1_
  (624 shorter events, 331.9 us)
Async XLA Ops:
  2.0 33.9 %collective-permute-start.33 = (bf16[80,640]{1,0:T(8,128)(2,1)S(1)}, bf16[80,640]{1,0:T(8,128)(2,1)S(1)}, u32[]{:S(2)}, u32[]{:S(2)}) collective-permute-start(bf16[80,640]{1,0:T(8,128)(2,1)S(1)} %bitcast.401), channel_id=1, source_target_pairs={{0,6},{1,7},{2,0},{3,1},{4,2},{5,3},{6,4},{7,5},{8,14},{9,15},{10,... | collective-permute-start | bytes 307208 | tf_op jit(solution)/shard_map/ppermute | solution.py:52
  2.1 33.9 %collective-permute-start.36 = (bf16[80,640]{1,0:T(8,128)(2,1)S(1)}, bf16[80,640]{1,0:T(8,128)(2,1)S(1)}, u32[]{:S(2)}, u32[]{:S(2)}) collective-permute-start(bf16[80,640]{1,0:T(8,128)(2,1)S(1)} %bitcast.402), channel_id=1, source_target_pairs={{0,2},{1,3},{2,4},{3,5},{4,6},{5,7},{6,0},{7,1},{8,10},{9,11},{10,... | collective-permute-start | bytes 307208 | tf_op jit(solution)/shard_map/ppermute | solution.py:52
  3.5 21.5 %collective-permute-start.4 = (s32[2,16]{1,0:T(2,128)}, s32[2,16]{1,0:T(2,128)S(1)}, u32[]{:S(2)}, u32[]{:S(2)}) collective-permute-start(s32[2,16]{1,0:T(2,128)} %param.16), channel_id=1, source_target_pairs={{0,8},{1,9},{2,10},{3,11},{4,12},{5,13},{6,14},{7,15},{8,0},{9,1},... | collective-permute-start | bytes 392 | tf_op jit(solution)/shard_map/ppermute | solution.py:52
  39.3 18.7 %collective-permute-start.13 = (bf16[80,960]{1,0:T(8,128)(2,1)S(1)}, bf16[80,960]{1,0:T(8,128)(2,1)S(1)}, u32[]{:S(2)}, u32[]{:S(2)}) collective-permute-start(bf16[80,960]{1,0:T(8,128)(2,1)S(1)} %dynamic-slice_bitcast_fusion.39.refs_0_), channel_id=1, source_target_pairs={{0,6},{1,7},{2,0},{3,1},{4,2},{5,3},{6,4},{7,5},{8,14},{9,15},{10,... | collective-permute-start | bytes 460808 | tf_op jit(solution)/shard_map/ppermute | solution.py:52
  42.6 21.4 %collective-permute-start.16 = (bf16[80,960]{1,0:T(8,128)(2,1)S(1)}, bf16[80,960]{1,0:T(8,128)(2,1)S(1)}, u32[]{:S(2)}, u32[]{:S(2)}) collective-permute-start(bf16[80,960]{1,0:T(8,128)(2,1)S(1)} %dynamic-slice_bitcast_fusion.39.refs_0_), channel_id=1, source_target_pairs={{0,2},{1,3},{2,4},{3,5},{4,6},{5,7},{6,0},{7,1},{8,10},{9,11},{10,... | collective-permute-start | bytes 460808 | tf_op jit(solution)/shard_map/ppermute | solution.py:52
  94.8 47.0 %collective-permute-start = (bf16[128,1280]{1,0:T(8,128)(2,1)S(1)}, bf16[128,1280]{1,0:T(8,128)(2,1)S(1)}, u32[]{:S(2)}, u32[]{:S(2)}) collective-permute-start(bf16[128,1280]{1,0:T(8,128)(2,1)S(1)} %copy-done.55), channel_id=1, source_target_pairs={{0,0},{1,1},{2,2},{3,3},{4,8},{5,9},{6,10},{7,11},{8,4},{9,5},{10,... | collective-permute-start | bytes 983048 | tf_op jit(solution)/shard_map/ppermute | solution.py:77
  107.7 34.9 %collective-permute-start.1 = (bf16[128,1280]{1,0:T(8,128)(2,1)S(1)}, bf16[128,1280]{1,0:T(8,128)(2,1)S(1)}, u32[]{:S(2)}, u32[]{:S(2)}) collective-permute-start(bf16[128,1280]{1,0:T(8,128)(2,1)S(1)} %get-tuple-element.92), channel_id=1, source_target_pairs={{0,2},{1,3},{2,0},{3,1},{4,10},{5,11},{6,8},{7,9},{8,6},{9,7},{10,... | collective-permute-start | bytes 983048 | tf_op jit(solution)/shard_map/ppermute | solution.py:77
  108.8 34.4 %collective-permute-start.2 = (bf16[128,1280]{1,0:T(8,128)(2,1)S(1)}, bf16[128,1280]{1,0:T(8,128)(2,1)S(1)}, u32[]{:S(2)}, u32[]{:S(2)}) collective-permute-start(bf16[128,1280]{1,0:T(8,128)(2,1)S(1)} %get-tuple-element.94), channel_id=1, source_target_pairs={{0,8},{1,9},{2,10},{3,11},{4,0},{5,1},{6,2},{7,3},{8,12},{9,13},{1... | collective-permute-start | bytes 983048 | tf_op jit(solution)/shard_map/ppermute | solution.py:77
  108.8 35.2 %collective-permute-start.3 = (bf16[128,1280]{1,0:T(8,128)(2,1)S(1)}, bf16[128,1280]{1,0:T(8,128)(2,1)S(1)}, u32[]{:S(2)}, u32[]{:S(2)}) collective-permute-start(bf16[128,1280]{1,0:T(8,128)(2,1)S(1)} %get-tuple-element.91), channel_id=1, source_target_pairs={{0,10},{1,11},{2,8},{3,9},{4,2},{5,3},{6,0},{7,1},{8,14},{9,15},{1... | collective-permute-start | bytes 983048 | tf_op jit(solution)/shard_map/ppermute | solution.py:77
  155.7 20.1 %collective-permute-start.48 = (bf16[80,640]{1,0:T(8,128)(2,1)S(1)}, bf16[80,640]{1,0:T(8,128)(2,1)S(1)}, u32[]{:S(2)}, u32[]{:S(2)}) collective-permute-start(bf16[80,640]{1,0:T(8,128)(2,1)S(1)} %collective-permute-done.45.refs_14_), channel_id=1, source_target_pairs={{0,16},{1,17},{2,18},{3,19},{4,20},{5,21},{6,22},{7,23},{8,24},{9,... | collective-permute-start | bytes 307208 | tf_op jit(solution)/shard_map/ppermute | solution.py:52
  161.4 21.8 %collective-permute-start.90 = (bf16[128,1280]{1,0:T(8,128)(2,1)S(1)}, bf16[128,1280]{1,0:T(8,128)(2,1)S(1)}, u32[]{:S(2)}, u32[]{:S(2)}) collective-permute-start(bf16[128,1280]{1,0:T(8,128)(2,1)S(1)} %get-tuple-element.69), channel_id=1, source_target_pairs={{0,0},{1,1},{2,2},{3,3},{4,8},{5,9},{6,10},{7,11},{8,4},{9,5},{10,... | collective-permute-start | bytes 983048 | tf_op jit(solution)/shard_map/ppermute | solution.py:77
  175.8 22.7 %collective-permute-start.91 = (bf16[128,1280]{1,0:T(8,128)(2,1)S(1)}, bf16[128,1280]{1,0:T(8,128)(2,1)S(1)}, u32[]{:S(2)}, u32[]{:S(2)}) collective-permute-start(bf16[128,1280]{1,0:T(8,128)(2,1)S(1)} %get-tuple-element.68), channel_id=1, source_target_pairs={{0,2},{1,3},{2,0},{3,1},{4,10},{5,11},{6,8},{7,9},{8,6},{9,7},{10,... | collective-permute-start | bytes 983048 | tf_op jit(solution)/shard_map/ppermute | solution.py:77
  175.9 25.0 %collective-permute-start.92 = (bf16[128,1280]{1,0:T(8,128)(2,1)S(1)}, bf16[128,1280]{1,0:T(8,128)(2,1)S(1)}, u32[]{:S(2)}, u32[]{:S(2)}) collective-permute-start(bf16[128,1280]{1,0:T(8,128)(2,1)S(1)} %get-tuple-element.70), channel_id=1, source_target_pairs={{0,8},{1,9},{2,10},{3,11},{4,0},{5,1},{6,2},{7,3},{8,12},{9,13},{1... | collective-permute-start | bytes 983048 | tf_op jit(solution)/shard_map/ppermute | solution.py:77
  176.0 28.4 %collective-permute-start.93 = (bf16[128,1280]{1,0:T(8,128)(2,1)S(1)}, bf16[128,1280]{1,0:T(8,128)(2,1)S(1)}, u32[]{:S(2)}, u32[]{:S(2)}) collective-permute-start(bf16[128,1280]{1,0:T(8,128)(2,1)S(1)} %get-tuple-element.67), channel_id=1, source_target_pairs={{0,10},{1,11},{2,8},{3,9},{4,2},{5,3},{6,0},{7,1},{8,14},{9,15},{1... | collective-permute-start | bytes 983048 | tf_op jit(solution)/shard_map/ppermute | solution.py:77
  182.2 22.1 %collective-permute-start.47 = (bf16[80,640]{1,0:T(8,128)(2,1)S(1)}, bf16[80,640]{1,0:T(8,128)(2,1)S(1)}, u32[]{:S(2)}, u32[]{:S(2)}) collective-permute-start(bf16[80,640]{1,0:T(8,128)(2,1)S(1)} %constant_dynamic-update-slice_fusion.6.refs_12_), channel_id=1, source_target_pairs={{0,16},{1,17},{2,18},{3,19},{4,20},{5,21},{6,22},{7,23},{8,24},{9,... | collective-permute-start | bytes 307208 | tf_op jit(solution)/shard_map/ppermute | solution.py:52
  183.2 66.7 %collective-permute-start.10 = (bf16[4,128,1280]{2,1,0:T(8,128)(2,1)}, bf16[4,128,1280]{2,1,0:T(8,128)(2,1)}, u32[]{:S(2)}, u32[]{:S(2)}) collective-permute-start(bf16[4,128,1280]{2,1,0:T(8,128)(2,1)} %fusion.13), channel_id=1, source_target_pairs={{0,1},{1,0},{2,3},{3,2},{4,5},{5,4},{6,7},{7,6},{8,9},{9,8},{10,11... | collective-permute-start | bytes 3932168 | tf_op jit(solution)/shard_map/ppermute | solution.py:52
  204.4 47.4 %collective-permute-start.9 = (bf16[4,128,1280]{2,1,0:T(8,128)(2,1)}, bf16[4,128,1280]{2,1,0:T(8,128)(2,1)}, u32[]{:S(2)}, u32[]{:S(2)}) collective-permute-start(bf16[4,128,1280]{2,1,0:T(8,128)(2,1)} %fusion.13), channel_id=1, source_target_pairs={{0,8},{1,9},{2,10},{3,11},{4,12},{5,13},{6,14},{7,15},{8,0},{9,1},... | collective-permute-start | bytes 3932168 | tf_op jit(solution)/shard_map/ppermute | solution.py:52
  214.6 38.5 %collective-permute-start.49 = (bf16[1280,640]{1,0:T(8,128)(2,1)S(1)}, bf16[1280,640]{1,0:T(8,128)(2,1)}, u32[]{:S(2)}, u32[]{:S(2)}) collective-permute-start(bf16[1280,640]{1,0:T(8,128)(2,1)S(1)} %bitcast.390), channel_id=1, source_target_pairs={{0,8},{1,9},{2,10},{3,11},{4,12},{5,13},{6,14},{7,15},{8,0},{9,1},... | collective-permute-start | bytes 4915208 | tf_op jit(solution)/shard_map/ppermute | solution.py:52
  226.6 30.0 %collective-permute-start.85 = (bf16[1280,640]{1,0:T(8,128)(2,1)}, bf16[1280,640]{1,0:T(8,128)(2,1)}, u32[]{:S(2)}, u32[]{:S(2)}) collective-permute-start(bf16[1280,640]{1,0:T(8,128)(2,1)} %bitcast.82), channel_id=1, source_target_pairs={{0,8},{1,9},{2,10},{3,11},{4,12},{5,13},{6,14},{7,15},{8,0},{9,1},... | collective-permute-start | bytes 4915208 | tf_op jit(solution)/shard_map/ppermute | solution.py:52
  228.1 77.3 %collective-permute-start.67 = (bf16[1280,640]{1,0:T(8,128)(2,1)}, bf16[1280,640]{1,0:T(8,128)(2,1)}, u32[]{:S(2)}, u32[]{:S(2)}) collective-permute-start(bf16[1280,640]{1,0:T(8,128)(2,1)} %bitcast.80), channel_id=1, source_target_pairs={{0,8},{1,9},{2,10},{3,11},{4,12},{5,13},{6,14},{7,15},{8,0},{9,1},... | collective-permute-start | bytes 4915208 | tf_op jit(solution)/shard_map/ppermute | solution.py:52
  303.9 18.8 %collective-permute-start.31 = (bf16[4,128,320]{2,1,0:T(8,128)(2,1)S(1)}, bf16[4,128,320]{2,1,0:T(8,128)(2,1)S(1)}, u32[]{:S(2)}, u32[]{:S(2)}) collective-permute-start(bf16[4,128,320]{2,1,0:T(8,128)(2,1)S(1)} %get-tuple-element.59), channel_id=1, source_target_pairs={{0,9},{1,8},{2,11},{3,10},{4,13},{5,12},{6,15},{7,14},{8,1},{9,0},... | collective-permute-start | bytes 983048 | tf_op jit(solution)/shard_map/ppermute | solution.py:52
  358.8 192.8 %collective-permute-start.86 = (bf16[128,1280]{1,0:T(8,128)(2,1)}, bf16[128,1280]{1,0:T(8,128)(2,1)}, u32[]{:S(2)}, u32[]{:S(2)}) collective-permute-start(bf16[128,1280]{1,0:T(8,128)(2,1)} %get-tuple-element.74), channel_id=1, source_target_pairs={{0,0},{1,1},{2,2},{3,3},{8,4},{9,5},{10,6},{11,7},{4,8},{5,9},{6,1... | collective-permute-start | bytes 983048 | tf_op jit(solution)/shard_map/ppermute | solution.py:88
  362.6 190.6 %collective-permute-start.87 = (bf16[128,1280]{1,0:T(8,128)(2,1)}, bf16[128,1280]{1,0:T(8,128)(2,1)}, u32[]{:S(2)}, u32[]{:S(2)}) collective-permute-start(bf16[128,1280]{1,0:T(8,128)(2,1)} %get-tuple-element.73), channel_id=1, source_target_pairs={{2,0},{3,1},{0,2},{1,3},{10,4},{11,5},{8,6},{9,7},{6,8},{7,9},{4,1... | collective-permute-start | bytes 983048 | tf_op jit(solution)/shard_map/ppermute | solution.py:88
  373.9 34.1 %collective-permute-start.94 = (bf16[4,128,320]{2,1,0:T(8,128)(2,1)}, bf16[4,128,320]{2,1,0:T(8,128)(2,1)}, u32[]{:S(2)}, u32[]{:S(2)}) collective-permute-start(bf16[4,128,320]{2,1,0:T(8,128)(2,1)} %bitcast.379), channel_id=1, source_target_pairs={{0,8},{1,9},{2,10},{3,11},{4,12},{5,13},{6,14},{7,15},{8,0},{9,1},... | collective-permute-start | bytes 983048 | tf_op jit(solution)/shard_map/ppermute | solution.py:52
  374.8 34.5 %collective-permute-start.95 = (bf16[4,128,320]{2,1,0:T(8,128)(2,1)}, bf16[4,128,320]{2,1,0:T(8,128)(2,1)}, u32[]{:S(2)}, u32[]{:S(2)}) collective-permute-start(bf16[4,128,320]{2,1,0:T(8,128)(2,1)} %bitcast.378), channel_id=1, source_target_pairs={{0,1},{1,0},{2,3},{3,2},{4,5},{5,4},{6,7},{7,6},{8,9},{9,8},{10,11... | collective-permute-start | bytes 983048 | tf_op jit(solution)/shard_map/ppermute | solution.py:52
  385.1 25.2 %collective-permute-start.96 = (bf16[4,128,320]{2,1,0:T(8,128)(2,1)}, bf16[4,128,320]{2,1,0:T(8,128)(2,1)}, u32[]{:S(2)}, u32[]{:S(2)}) collective-permute-start(bf16[4,128,320]{2,1,0:T(8,128)(2,1)} %bitcast.377), channel_id=1, source_target_pairs={{0,9},{1,8},{2,11},{3,10},{4,13},{5,12},{6,15},{7,14},{8,1},{9,0},... | collective-permute-start | bytes 983048 | tf_op jit(solution)/shard_map/ppermute | solution.py:52
  474.5 44.1 %collective-permute-start.110 = (bf16[2,2,80,960]{3,2,1,0:T(8,128)(2,1)S(1)}, bf16[2,2,80,960]{3,2,1,0:T(8,128)(2,1)S(1)}, u32[]{:S(2)}, u32[]{:S(2)}) collective-permute-start(bf16[2,2,80,960]{3,2,1,0:T(8,128)(2,1)S(1)} %get-tuple-element.49), channel_id=1, source_target_pairs={{0,4},{1,5},{2,6},{3,7},{4,0},{5,1},{6,2},{7,3},{8,12},{9,13},{10,... | collective-permute-start | bytes 1843208 | tf_op jit(solution)/shard_map/ppermute | solution.py:52
  476.2 60.0 %collective-permute-start.109 = (bf16[2,2,80,960]{3,2,1,0:T(8,128)(2,1)S(1)}, bf16[2,2,80,960]{3,2,1,0:T(8,128)(2,1)S(1)}, u32[]{:S(2)}, u32[]{:S(2)}) collective-permute-start(bf16[2,2,80,960]{3,2,1,0:T(8,128)(2,1)S(1)} %get-tuple-element.47), channel_id=1, source_target_pairs={{0,2},{1,3},{2,4},{3,5},{4,6},{5,7},{6,0},{7,1},{8,10},{9,11},{10,... | collective-permute-start | bytes 1843208 | tf_op jit(solution)/shard_map/ppermute | solution.py:52
  490.1 63.2 %collective-permute-start.88 = (bf16[128,1280]{1,0:T(8,128)(2,1)}, bf16[128,1280]{1,0:T(8,128)(2,1)S(1)}, u32[]{:S(2)}, u32[]{:S(2)}) collective-permute-start(bf16[128,1280]{1,0:T(8,128)(2,1)} %get-tuple-element.72), channel_id=1, source_target_pairs={{8,0},{9,1},{10,2},{11,3},{0,4},{1,5},{2,6},{3,7},{12,8},{13,9},{1... | collective-permute-start | bytes 983048 | tf_op jit(solution)/shard_map/ppermute | solution.py:88
  518.6 50.4 %collective-permute-start.118 = (bf16[1280,640]{1,0:T(8,128)(2,1)}, bf16[1280,640]{1,0:T(8,128)(2,1)}, u32[]{:S(2)}, u32[]{:S(2)}) collective-permute-start(bf16[1280,640]{1,0:T(8,128)(2,1)} %bitcast.158), channel_id=1, source_target_pairs={{0,8},{1,9},{2,10},{3,11},{4,12},{5,13},{6,14},{7,15},{8,0},{9,1},... | collective-permute-start | bytes 4915208 | tf_op jit(solution)/shard_map/ppermute | solution.py:52
  551.7 21.6 %collective-permute-start.126 = (bf16[1280,640]{1,0:T(8,128)(2,1)}, bf16[1280,640]{1,0:T(8,128)(2,1)}, u32[]{:S(2)}, u32[]{:S(2)}) collective-permute-start(bf16[1280,640]{1,0:T(8,128)(2,1)} %bitcast.439), channel_id=1, source_target_pairs={{0,8},{1,9},{2,10},{3,11},{4,12},{5,13},{6,14},{7,15},{8,0},{9,1},... | collective-permute-start | bytes 4915208 | tf_op jit(solution)/shard_map/ppermute | solution.py:52
  557.1 19.3 %collective-permute-start.134 = (bf16[1280,640]{1,0:T(8,128)(2,1)}, bf16[1280,640]{1,0:T(8,128)(2,1)S(1)}, u32[]{:S(2)}, u32[]{:S(2)}) collective-permute-start(bf16[1280,640]{1,0:T(8,128)(2,1)} %bitcast.438), channel_id=1, source_target_pairs={{0,8},{1,9},{2,10},{3,11},{4,12},{5,13},{6,14},{7,15},{8,0},{9,1},... | collective-permute-start | bytes 4915208 | tf_op jit(solution)/shard_map/ppermute | solution.py:52
  562.2 113.7 %collective-permute-start.97 = (bf16[4,2,128,1280]{3,2,0,1:T(8,128)(2,1)}, bf16[4,2,128,1280]{3,2,0,1:T(8,128)(2,1)}, u32[]{:S(2)}, u32[]{:S(2)}) collective-permute-start(bf16[4,2,128,1280]{3,2,0,1:T(8,128)(2,1)} %bitcast.376), channel_id=1, source_target_pairs={{0,8},{1,9},{2,10},{3,11},{4,12},{5,13},{6,14},{7,15},{8,0},{9,1},... | collective-permute-start | bytes 7864328 | tf_op jit(solution)/shard_map/ppermute | solution.py:52
  573.3 30.5 %collective-permute-start.119 = (bf16[4,2,80,640]{3,2,1,0:T(8,128)(2,1)}, bf16[4,2,80,640]{3,2,1,0:T(8,128)(2,1)}, u32[]{:S(2)}, u32[]{:S(2)}) collective-permute-start(bf16[4,2,80,640]{3,2,1,0:T(8,128)(2,1)} %dynamic-slice_bitcast_fusion.3), channel_id=1, source_target_pairs={{0,16},{1,17},{2,18},{3,19},{4,20},{5,21},{6,22},{7,23},{8,24},{9,... | collective-permute-start | bytes 2457608 | tf_op jit(solution)/shard_map/ppermute | solution.py:52
  576.4 34.2 %collective-permute-start.127 = (bf16[4,2,80,640]{3,2,1,0:T(8,128)(2,1)}, bf16[4,2,80,640]{3,2,1,0:T(8,128)(2,1)}, u32[]{:S(2)}, u32[]{:S(2)}) collective-permute-start(bf16[4,2,80,640]{3,2,1,0:T(8,128)(2,1)} %dynamic-slice_bitcast_fusion.2), channel_id=1, source_target_pairs={{0,16},{1,17},{2,18},{3,19},{4,20},{5,21},{6,22},{7,23},{8,24},{9,... | collective-permute-start | bytes 2457608 | tf_op jit(solution)/shard_map/ppermute | solution.py:52
  579.3 48.8 %collective-permute-start.135 = (bf16[4,2,80,640]{3,2,1,0:T(8,128)(2,1)}, bf16[4,2,80,640]{3,2,1,0:T(8,128)(2,1)}, u32[]{:S(2)}, u32[]{:S(2)}) collective-permute-start(bf16[4,2,80,640]{3,2,1,0:T(8,128)(2,1)} %dynamic-slice_bitcast_fusion.1), channel_id=1, source_target_pairs={{0,16},{1,17},{2,18},{3,19},{4,20},{5,21},{6,22},{7,23},{8,24},{9,... | collective-permute-start | bytes 2457608 | tf_op jit(solution)/shard_map/ppermute | solution.py:52
  605.5 25.9 %collective-permute-start.122 = (bf16[2,1,80,640]{3,2,0,1:T(8,128)(2,1)S(1)}, bf16[2,1,80,640]{3,2,0,1:T(8,128)(2,1)S(1)}, u32[]{:S(2)}, u32[]{:S(2)}) collective-permute-start(bf16[2,1,80,640]{3,2,0,1:T(8,128)(2,1)S(1)} %get-tuple-element.102), channel_id=1, source_target_pairs={{0,6},{1,7},{2,0},{3,1},{4,2},{5,3},{6,4},{7,5},{8,14},{9,15},{10,... | collective-permute-start | bytes 614408 | tf_op jit(solution)/shard_map/ppermute | solution.py:52
  607.3 25.5 %collective-permute-start.121 = (bf16[2,1,80,640]{3,2,0,1:T(8,128)(2,1)S(1)}, bf16[2,1,80,640]{3,2,0,1:T(8,128)(2,1)S(1)}, u32[]{:S(2)}, u32[]{:S(2)}) collective-permute-start(bf16[2,1,80,640]{3,2,0,1:T(8,128)(2,1)S(1)} %get-tuple-element.103), channel_id=1, source_target_pairs={{0,4},{1,5},{2,6},{3,7},{4,0},{5,1},{6,2},{7,3},{8,12},{9,13},{10,... | collective-permute-start | bytes 614408 | tf_op jit(solution)/shard_map/ppermute | solution.py:52
  610.6 23.6 %collective-permute-start.120 = (bf16[2,1,80,640]{3,2,0,1:T(8,128)(2,1)S(1)}, bf16[2,1,80,640]{3,2,0,1:T(8,128)(2,1)S(1)}, u32[]{:S(2)}, u32[]{:S(2)}) collective-permute-start(bf16[2,1,80,640]{3,2,0,1:T(8,128)(2,1)S(1)} %get-tuple-element.101), channel_id=1, source_target_pairs={{0,2},{1,3},{2,4},{3,5},{4,6},{5,7},{6,0},{7,1},{8,10},{9,11},{10,... | collective-permute-start | bytes 614408 | tf_op jit(solution)/shard_map/ppermute | solution.py:52
  632.8 25.1 %collective-permute-start.128 = (bf16[2,1,80,640]{3,2,1,0:T(8,128)(2,1)S(1)}, bf16[2,1,80,640]{3,2,1,0:T(8,128)(2,1)S(1)}, u32[]{:S(2)}, u32[]{:S(2)}) collective-permute-start(bf16[2,1,80,640]{3,2,1,0:T(8,128)(2,1)S(1)} %get-tuple-element.98), channel_id=1, source_target_pairs={{0,2},{1,3},{2,4},{3,5},{4,6},{5,7},{6,0},{7,1},{8,10},{9,11},{10,... | collective-permute-start | bytes 614408 | tf_op jit(solution)/shard_map/ppermute | solution.py:52
  634.1 27.4 %collective-permute-start.138 = (bf16[2,1,80,640]{3,2,1,0:T(8,128)(2,1)S(1)}, bf16[2,1,80,640]{3,2,1,0:T(8,128)(2,1)S(1)}, u32[]{:S(2)}, u32[]{:S(2)}) collective-permute-start(bf16[2,1,80,640]{3,2,1,0:T(8,128)(2,1)S(1)} %get-tuple-element.96), channel_id=1, source_target_pairs={{0,6},{1,7},{2,0},{3,1},{4,2},{5,3},{6,4},{7,5},{8,14},{9,15},{10,... | collective-permute-start | bytes 614408 | tf_op jit(solution)/shard_map/ppermute | solution.py:52
  634.4 27.8 %collective-permute-start.137 = (bf16[2,1,80,640]{3,2,1,0:T(8,128)(2,1)S(1)}, bf16[2,1,80,640]{3,2,1,0:T(8,128)(2,1)S(1)}, u32[]{:S(2)}, u32[]{:S(2)}) collective-permute-start(bf16[2,1,80,640]{3,2,1,0:T(8,128)(2,1)S(1)} %get-tuple-element.97), channel_id=1, source_target_pairs={{0,4},{1,5},{2,6},{3,7},{4,0},{5,1},{6,2},{7,3},{8,12},{9,13},{10,... | collective-permute-start | bytes 614408 | tf_op jit(solution)/shard_map/ppermute | solution.py:52
  645.8 20.8 %collective-permute-start.136 = (bf16[2,1,80,640]{3,2,1,0:T(8,128)(2,1)S(1)}, bf16[2,1,80,640]{3,2,1,0:T(8,128)(2,1)S(1)}, u32[]{:S(2)}, u32[]{:S(2)}) collective-permute-start(bf16[2,1,80,640]{3,2,1,0:T(8,128)(2,1)S(1)} %get-tuple-element.95), channel_id=1, source_target_pairs={{0,2},{1,3},{2,4},{3,5},{4,6},{5,7},{6,0},{7,1},{8,10},{9,11},{10,... | collective-permute-start | bytes 614408 | tf_op jit(solution)/shard_map/ppermute | solution.py:52
  678.3 29.1 %collective-permute-start.98 = (bf16[4,128,1280]{2,1,0:T(8,128)(2,1)S(1)}, bf16[4,128,1280]{2,1,0:T(8,128)(2,1)S(1)}, u32[]{:S(2)}, u32[]{:S(2)}) collective-permute-start(bf16[4,128,1280]{2,1,0:T(8,128)(2,1)S(1)} %dynamic-slice_bitcast_fusion), channel_id=1, source_target_pairs={{0,1},{1,0},{2,3},{3,2},{4,5},{5,4},{6,7},{7,6},{8,9},{9,8},{10,11... | collective-permute-start | bytes 3932168 | tf_op jit(solution)/shard_map/ppermute | solution.py:52
  724.2 25.8 %collective-permute-start.99 = (bf16[128,1280]{1,0:T(8,128)(2,1)S(1)}, bf16[128,1280]{1,0:T(8,128)(2,1)S(1)}, u32[]{:S(2)}, u32[]{:S(2)}) collective-permute-start(bf16[128,1280]{1,0:T(8,128)(2,1)S(1)} %get-tuple-element.66), channel_id=1, source_target_pairs={{0,0},{1,1},{2,2},{3,3},{8,4},{9,5},{10,6},{11,7},{4,8},{5,9},{6,1... | collective-permute-start | bytes 983048 | tf_op jit(solution)/shard_map/ppermute | solution.py:88
  730.5 26.8 %collective-permute-start.100 = (bf16[128,1280]{1,0:T(8,128)(2,1)S(1)}, bf16[128,1280]{1,0:T(8,128)(2,1)S(1)}, u32[]{:S(2)}, u32[]{:S(2)}) collective-permute-start(bf16[128,1280]{1,0:T(8,128)(2,1)S(1)} %get-tuple-element.65), channel_id=1, source_target_pairs={{2,0},{3,1},{0,2},{1,3},{10,4},{11,5},{8,6},{9,7},{6,8},{7,9},{4,1... | collective-permute-start | bytes 983048 | tf_op jit(solution)/shard_map/ppermute | solution.py:88
  730.6 26.7 %collective-permute-start.101 = (bf16[128,1280]{1,0:T(8,128)(2,1)S(1)}, bf16[128,1280]{1,0:T(8,128)(2,1)S(1)}, u32[]{:S(2)}, u32[]{:S(2)}) collective-permute-start(bf16[128,1280]{1,0:T(8,128)(2,1)S(1)} %get-tuple-element.64), channel_id=1, source_target_pairs={{8,0},{9,1},{10,2},{11,3},{0,4},{1,5},{2,6},{3,7},{12,8},{13,9},{1... | collective-permute-start | bytes 983048 | tf_op jit(solution)/shard_map/ppermute | solution.py:88
  730.7 27.9 %collective-permute-start.102 = (bf16[128,1280]{1,0:T(8,128)(2,1)S(1)}, bf16[128,1280]{1,0:T(8,128)(2,1)S(1)}, u32[]{:S(2)}, u32[]{:S(2)}) collective-permute-start(bf16[128,1280]{1,0:T(8,128)(2,1)S(1)} %get-tuple-element.63), channel_id=1, source_target_pairs={{10,0},{11,1},{8,2},{9,3},{2,4},{3,5},{0,6},{1,7},{14,8},{15,9},{1... | collective-permute-start | bytes 983048 | tf_op jit(solution)/shard_map/ppermute | solution.py:88
  (165 other events, 2442.6 us)

commit v2 on v1

v2 whole, which is shorter than its diff:
```python
import functools
import math

import jax
import jax.numpy as jnp
from jax import lax
from jax.experimental import pallas as pl
from jax.experimental.pallas import tpu as pltpu
from jax.sharding import PartitionSpec as P

HEAD_DIM = 80
LANES = 128
CORES = 2
NORM_EPS = 1e-06
LOG_BASE = 1.442695041
MASK_FILL = -1e30
AXES = ("rep", "shard")
F32 = jnp.float32
BF16 = jnp.bfloat16


def dot(left, right, left_dim=1, right_dim=0):
    return lax.dot_general(
        left, right, (((left_dim,), (right_dim,)), ((), ())), preferred_element_type=F32
    )


class Place:
    def __init__(self, reps, shards, seqs):
        self.x_size = reps // CORES
        self.x_split = 2 if self.x_size == 2 else 1
        self.a_size = CORES * seqs
        self.b_size = shards // self.a_size
        self.even = self.x_size == 2 and self.b_size == 2
        self.peer_count = self.b_size * CORES
        self.seqs = seqs
        rep, shard = lax.axis_index("rep"), lax.axis_index("shard")
        self.x, self.c = rep // CORES, rep % CORES
        self.a, self.b = shard // self.b_size, shard % self.b_size
        self.shard = shard

    def route(self, move):
        pairs = []
        for x in range(self.x_size):
            for c in range(CORES):
                for a in range(self.a_size):
                    for b in range(self.b_size):
                        pairs.append((self.number(x, c, a, b), self.number(*move(x, c, a, b))))
        return pairs

    def number(self, x, c, a, b):
        return ((x * CORES + c) * self.a_size + a) * self.b_size + b

    def send(self, value, dx=0, dc=0, da=0, db=0):
        return lax.ppermute(
            value,
            AXES,
            self.route(
                lambda x, c, a, b: (
                    (x + dx) % self.x_size,
                    (c + dc) % CORES,
                    (a + da) % self.a_size,
                    (b + db) % self.b_size,
                )
            ),
        )

    def peers(self):
        return [(db, dc) for db in range(self.b_size) for dc in range(CORES)]

    def source(self, db, dc):
        return ((self.b - db) % self.b_size) * CORES + (self.c + dc) % CORES

    def to_cluster(self, tokens):
        seqs, count, width = tokens.shape
        half = count // CORES
        halves = tokens.reshape(seqs, CORES, half, width)
        shape = (seqs, half, width)
        moves = []
        for i in range(seqs):
            moves += [(0, (i, self.c), 0, i), (0, (i, 1 - self.c), 1, i)]
        own, give = shuffle([halves], [(shape, BF16)] * 2, moves)
        got = self.send(give, dc=1)
        after = yield
        parts = route_parts(self, own, got, after or ())
        received = [parts[0]] + [self.send(parts[d], da=d) for d in range(1, self.a_size)]
        moves = [(d, None, 0, (self.a - d) % self.a_size) for d in range(self.a_size)]
        after = yield
        yield shuffle(received, [((self.a_size, half, width), BF16)], moves, after or ())[0]

    def from_cluster(self, chunks):
        half, width = chunks.shape[1:]
        picks = [(0, (self.a + d) % self.a_size, d, None) for d in range(self.a_size)]
        parts = shuffle([chunks], [((half, width), BF16)] * self.a_size, picks)
        received = [parts[0]] + [self.send(parts[d], da=d) for d in range(1, self.a_size)]
        yield
        own, give = route_back(self, received)
        got = self.send(give, dc=1)
        moves = []
        for i in range(self.seqs):
            moves += [(0, i, 0, i * CORES + self.c), (1, i, 0, i * CORES + 1 - self.c)]
        yield
        whole = shuffle([own, got], [((self.a_size, half, width), BF16)], moves)[0]
        yield whole.reshape(self.seqs, CORES * half, width)

    def send_back(self, part, m):
        return lax.ppermute(part, AXES, [(j, i) for i, j in self.route(self._match(m))])

    def place_back(self, received):
        half, width = received[0].shape
        moves = []
        for m in range(self.a_size):
            t = m ^ self.a
            moves.append((m, None, 0, (t % self.seqs) * CORES + t // self.seqs))
        whole = shuffle(received, [((self.a_size, half, width), BF16)], moves)[0]
        return whole.reshape(self.seqs, CORES * half, width)

    def _match(self, m):
        def move(x, c, a, b):
            t = m ^ a
            return x, t // self.seqs, self.seqs * c + t % self.seqs, b

        return move


VMEM = pl.BlockSpec(memory_space=pltpu.VMEM)
ANY = pl.BlockSpec(memory_space=pl.ANY)


LAST = []
SCALE = 0.25
COST = {
    "project": 14.5,
    "attend_forward": 26.0,
    "middle": 20.0,
    "outer": 7.0,
    "outer_give": 0.1,
    "attend_backward": 25.0,
    "heads_outer": 5.5,
    "back_project": 3.5,
    "pad_weights": 3.5,
    "norm_back": 3.0,
    "finish_heads": 4.0,
    "finish_full": 3.5,
}


def call(name, body, scalars, inputs, outputs, grid=(1,), scratch=(), after=(), vmem=40):
    deps = [*LAST[-1:], *after]
    count, skip = len(inputs), len(deps)

    def run(spots, *refs):
        body(spots, *refs[:count], *refs[count + skip :])

    results = pl.pallas_call(
        run,
        out_shape=[jax.ShapeDtypeStruct(shape, kind) for shape, kind, _ in outputs],
        grid_spec=pltpu.PrefetchScalarGridSpec(
            num_scalar_prefetch=1,
            grid=grid,
            in_specs=[spec for _, spec in inputs] + [ANY] * skip,
            out_specs=[spec for _, _, spec in outputs],
            scratch_shapes=list(scratch),
        ),
        cost_estimate=pl.CostEstimate(
            flops=int(COST.get(name, 1.5) * SCALE * 1.1e9),
            bytes_accessed=int(COST.get(name, 1.5) * SCALE * 3.3e6),
            transcendentals=0,
        ),
        compiler_params=pltpu.CompilerParams(vmem_limit_bytes=vmem * 1024 * 1024),
        name=name,
    )(scalars_of(scalars), *[value for value, _ in inputs], *deps)
    LAST.append(results[0])
    return results


def scalars_of(values):
    if isinstance(values, (list, tuple)):
        return jnp.stack([jnp.asarray(v, jnp.int32) for v in values])
    return values


def shuffle_body(moves, counts, spots, *refs):
    sources, targets, sems = refs[: counts[0]], refs[counts[0] : -1], refs[-1]
    copies, n = [], 0
    for src, src_rank, dst, dst_rank in moves:
        ends = []
        for ref, rank in ((sources[src], src_rank), (targets[dst], dst_rank)):
            ends.append(ref.at[tuple(spots[n + k] for k in range(rank))] if rank else ref)
            n += rank
        copies.append(pltpu.make_async_copy(*ends, sems.at[len(copies)]))
    for copy in copies:
        copy.start()
    for copy in copies:
        copy.wait()


def shuffle(sources, shapes, moves, after=()):
    spots, shape_of = [], []
    for src, src_spot, dst, dst_spot in moves:
        ranks = []
        for spot in (src_spot, dst_spot):
            spot = () if spot is None else spot if isinstance(spot, tuple) else (spot,)
            ranks.append(len(spot))
            spots += spot
        shape_of.append((src, ranks[0], dst, ranks[1]))
    return call(
        "shuffle",
        functools.partial(shuffle_body, shape_of, (len(sources), len(shapes))),
        spots or [0],
        [(source, VMEM) for source in sources],
        [(*shape, ANY) for shape in shapes],
        scratch=[pltpu.SemaphoreType.DMA((len(moves),))],
        after=after,
    )


def route_parts_body(seqs, info, own, got, *outs):
    for d, out in enumerate(outs):
        target = info[1 + d]

        @pl.when(target // seqs == info[0])
        def near():
            out[...] = own[target % seqs]

        @pl.when(target // seqs != info[0])
        def far():
            out[...] = got[target % seqs]


def route_parts(at, own, got, after=()):
    return call(
        "route_parts",
        functools.partial(route_parts_body, at.seqs),
        [at.c, *ahead(at.a, at.a_size)],
        [(own, VMEM), (got, VMEM)],
        [(own.shape[1:], BF16, VMEM)] * at.a_size,
        after=after,
    )


def route_back_body(seqs, info, *refs):
    parts, own, give = refs[:-2], refs[-2], refs[-1]
    for d, part in enumerate(parts):
        source = info[1 + d]

        @pl.when(source // seqs == info[0])
        def near():
            own[source % seqs] = part[...]

        @pl.when(source // seqs != info[0])
        def far():
            give[source % seqs] = part[...]


def route_back(at, parts):
    shape = (at.seqs, *parts[0].shape)
    return call(
        "route_back",
        functools.partial(route_back_body, at.seqs),
        [at.c, *[(at.a - d) % at.a_size for d in range(at.a_size)]],
        [(part, VMEM) for part in parts],
        [(shape, BF16, VMEM)] * 2,
    )


def add_body(counts, spots, *refs):
    terms = sum(counts)
    ins, outs, n = refs[:terms], refs[terms:], 0
    for count, out in zip(counts, outs):
        total = ins[n][...].astype(F32)
        for k in range(1, count):
            total = total + ins[n + k][...].astype(F32)
        out[...] = total.reshape(out.shape).astype(out.dtype)
        n += count


def add_blocks(groups):
    spots, inputs, outputs = [], [], []
    for terms in groups:
        for value, dim, index in terms:
            block = [1 if k == dim else size for k, size in enumerate(value.shape)]

            def spot(i, s, dim=dim, n=len(spots), rank=value.ndim):
                return tuple(s[n] if k == dim else 0 for k in range(rank))

            spots.append(index)
            inputs.append((value, pl.BlockSpec(tuple(block), spot)))
        shape = tuple(size for k, size in enumerate(value.shape) if k != dim)
        outputs.append((shape, BF16, VMEM))
    return call(
        "add_blocks",
        functools.partial(add_body, [len(terms) for terms in groups]),
        spots,
        inputs,
        outputs,
    )


def later(value, *done):
    return lax.optimization_barrier((value, *done))[0]


def pick(stacked, index, axis=0):
    return lax.dynamic_index_in_dim(stacked, index, axis, keepdims=False)


def ring_gather(at, piece):
    up = at.send(piece, da=-1)
    down = at.send(piece, da=1)
    cut = max(1, piece.shape[0] // 2)
    far = [at.send(up[:cut], da=-1), at.send(down[cut:], da=1)]
    yield
    shape = (3, *piece.shape)
    yield shuffle([piece, up, down], [(shape, BF16)], [(k, None, 0, k) for k in range(3)])[0]
    moves = []
    for k in range(piece.shape[0]):
        moves.append((0, k, 0, k) if k < cut else (1, k - cut, 0, k))
    yield shuffle(far, [(piece.shape, BF16)], moves)[0]


def by_order(own, others, axis_size, spot):
    moves = [(d, None, 0, (spot - d) % axis_size) for d in range(axis_size)]
    return shuffle([own, *others], [((axis_size, *own.shape), own.dtype)], moves)[0]


def heads_part_body(count, groups, info, query, key, value, vectors, *outs):
    width = query.shape[1] // count // groups
    rows = outs[0].shape[0]
    down = pl.ds(pl.multiple_of(info[len(outs)] * rows, rows), rows)
    for n, out in enumerate(outs):
        for peer in range(count):

            @pl.when(info[n] == peer)
            def copy():
                for g in range(groups):
                    for k, source in enumerate((query, key, value)):
                        spot = (g * 3 + k) * width
                        first = (peer * groups + g) * width
                        out[:, spot : spot + width] = source[down, first : first + width]

        out[:, 3 * groups * width :] = vectors[down, :]


def heads_parts(at, weights, vectors, groups):
    rows, model = weights[0].shape
    count = at.peer_count
    shape = (rows // at.x_split, 3 * model // count + vectors.shape[1])
    targets = [((at.b + db) % at.b_size) * CORES + at.c for db in range(at.b_size)]
    return call(
        "heads_parts",
        functools.partial(heads_part_body, count, groups),
        [*targets, at.x if at.x_split == 2 else 0],
        [(w, VMEM) for w in (*weights, vectors)],
        [(shape, BF16, VMEM)] * at.b_size,
    )


def quarter_body(info, *refs):
    out, sem = refs[3], refs[4]
    rows, half = out.shape[1:]
    down = pl.ds(pl.multiple_of(info[0] * rows, rows), rows)
    right = pl.ds(pl.multiple_of(info[1] * half, half), half)
    copies = [pltpu.make_async_copy(refs[w].at[down, right], out.at[w], sem.at[w]) for w in range(3)]
    for copy in copies:
        copy.start()
    for copy in copies:
        copy.wait()


def quarter_of(at, weights, after):
    rows, model = weights[0].shape
    return call(
        "quarter",
        quarter_body,
        [at.x if at.x_split == 2 else 0, at.c],
        [(w, VMEM) for w in weights],
        [((3, rows // at.x_split, model // CORES), BF16, ANY)],
        scratch=[pltpu.SemaphoreType.DMA((3,))],
        after=after,
    )[0]


def pad_body(heads, groups, x_split, info, *refs):
    sources, outs = refs[: 2 * x_split], refs[2 * x_split :]
    compact, (padded, vectors) = outs[:groups], outs[groups:]
    b_size, rows, width = sources[1].shape
    used = 3 * heads * HEAD_DIM
    part = heads // groups
    padded[...] = jnp.zeros_like(padded)
    for n in range(x_split):
        for a in range(4):
            for b in range(b_size):
                piece = sources[2 * n][a, b] if a < 3 else sources[2 * n + 1][b]
                spot = (info[1 + a] * b_size + b) * x_split
                spot = (spot + (info[0] ^ n if x_split == 2 else 0)) * rows
                spot = pl.ds(pl.multiple_of(spot, rows), rows)
                for g in range(groups):
                    step = used // groups
                    compact[g][spot, :] = piece[:, g * step : (g + 1) * step]
                vectors[spot, :] = piece[:, used:]
                for k in range(3):
                    for h in range(heads):
                        first = (((h // part) * 3 + k) * part + h % part) * HEAD_DIM
                        lane = (k * heads + h) * LANES
                        padded[spot, lane : lane + HEAD_DIM] = piece[:, first : first + HEAD_DIM]


def pad_weights(at, sources, heads, groups, after):
    b_size, rows, width = sources[1].shape
    total = at.a_size * b_size * rows * at.x_split
    used = 3 * heads * HEAD_DIM
    return call(
        "pad_weights",
        functools.partial(pad_body, heads, groups, at.x_split),
        [at.x, at.a, (at.a + 1) % 4, (at.a + 3) % 4, (at.a + 2) % 4],
        [(source, VMEM) for source in sources],
        [
            *[((total, used // groups), BF16, VMEM)] * groups,
            ((total, 3 * heads * LANES), BF16, VMEM),
            ((total, width - used), BF16, VMEM),
        ],
        after=after,
    )


def project_body(count, spots, *refs):
    tokens, (gain, weight, bias, times, qkv, normed) = refs[:count], refs[count:]
    rows = tokens[0].shape[1]
    for p in range(count):
        value = tokens[p][0].astype(F32)
        rate = lax.rsqrt(jnp.mean(value * value, axis=-1, keepdims=True) + NORM_EPS)
        spot = pl.multiple_of(spots[p] * rows, rows)
        normed[pl.ds(spot, rows), :] = (value * rate * gain[...]).astype(BF16)
    step = qkv.shape[1] // 3
    for k in range(3):
        lanes = slice(k * step, (k + 1) * step)
        acc = dot(normed[...], weight[:, lanes])
        qkv[:, lanes] = ((acc + bias[:, lanes]) * times[:, lanes]).astype(BF16)


def project(at, parts, gain, weight, bias, times):
    a_size, half, model = parts[0].shape
    count = len(parts)
    cols = weight.shape[1]
    fixed = lambda a, s: (0, 0)
    return call(
        "project",
        functools.partial(project_body, count),
        [at.source(db, dc) for db, dc in at.peers()],
        [(part, pl.BlockSpec((1, half, model), lambda a, s: (a, 0, 0))) for part in parts]
        + [
            (gain, pl.BlockSpec((1, model), fixed)),
            (weight, pl.BlockSpec((model, cols), fixed)),
            (bias, pl.BlockSpec((1, cols), fixed)),
            (times, pl.BlockSpec((1, cols), fixed)),
        ],
        [
            (
                (a_size * count * half, cols),
                BF16,
                pl.BlockSpec((count * half, cols), lambda a, s: (a, 0)),
            ),
            (
                (a_size * count * half, model),
                BF16,
                pl.BlockSpec((count * half, model), lambda a, s: (a, 0)),
            ),
        ],
        grid=(a_size,),
    )


def forward_body(heads, block, info, starts, query, key, value, mixed, query_aug, total, top):
    index = pl.program_id(0)
    half = block // CORES
    core = info[pl.num_programs(0) + 1]
    total[...] = jnp.zeros_like(total)
    top[...] = jnp.full_like(top, MASK_FILL)
    rows = index * block + lax.broadcasted_iota(jnp.int32, (block, block), 0)
    begin = starts[...][:, :1]

    def step(j, carry):
        spot = pl.multiple_of(j * block, block)
        columns = spot + lax.broadcasted_iota(jnp.int32, (block, block), 1)
        bias = jnp.where((columns >= begin) & (columns <= rows), 0.0, MASK_FILL)
        for h in range(heads):
            lanes = slice(h * LANES, (h + 1) * LANES)
            score = dot(query[:, lanes], key[pl.ds(spot, block), lanes], 1, 1) + bias
            old = top[h]
            new = jnp.maximum(old, jnp.max(score, axis=1, keepdims=True))
            weight = jnp.exp(score - jnp.concatenate([new] * (block // LANES), axis=1))
            total[h] = total[h] * jnp.exp(old - new) + dot(
                weight.astype(BF16), value[pl.ds(spot, block), lanes]
            )
            top[h] = new
        return carry

    lax.fori_loop(info[index], index + 1, step, 0)
    lane = lax.broadcasted_iota(jnp.int32, (block, LANES), 1)
    for h in range(heads):
        lanes = slice(h * LANES, (h + 1) * LANES)
        acc = total[h]
        weight_sum = acc[:, HEAD_DIM : HEAD_DIM + 1]
        result = (acc / weight_sum)[:, :HEAD_DIM].astype(BF16)
        for k in range(CORES):
            mixed[0, core ^ k, 0, :, h * HEAD_DIM : (h + 1) * HEAD_DIM] = result[
                k * half : (k + 1) * half
            ]
        rest = -(top[h] + jnp.log(weight_sum))
        aug = query[:, lanes].astype(F32)
        for k in range(3):
            term = rest.astype(BF16).astype(F32)
            aug = jnp.where(lane == HEAD_DIM + k, term, aug)
            rest = rest - term
        query_aug[:, lanes] = aug.astype(BF16)


def attend_forward(at, info, starts, qkv, heads, block):
    length = qkv.shape[0]
    wide = heads * LANES
    width = heads * HEAD_DIM
    count = length // block
    b_size = at.b_size
    return call(
        "attend_forward",
        functools.partial(forward_body, heads, block),
        info,
        [
            (starts, pl.BlockSpec((block, LANES), lambda i, s: (i, 0))),
            (qkv, pl.BlockSpec((block, wide), lambda i, s: (i, 0))),
            (qkv, pl.BlockSpec((length, wide), lambda i, s: (0, 1))),
            (qkv, pl.BlockSpec((length, wide), lambda i, s: (0, 2))),
        ],
        [
            (
                (b_size, CORES, at.a_size, block // CORES, width),
                BF16,
                pl.BlockSpec(
                    (1, CORES, 1, block // CORES, width),
                    lambda i, s: ((i + b_size - s[count]) % b_size, 0, i // b_size, 0, 0),
                ),
            ),
            ((length, wide), BF16, pl.BlockSpec((block, wide), lambda i, s: (i, 0))),
        ],
        grid=(count,),
        scratch=[
            pltpu.VMEM((heads, block, LANES), F32),
            pltpu.VMEM((heads, block, LANES), F32),
        ],
    )


def backward_body(
    heads,
    first,
    block,
    count,
    info,
    starts,
    scale,
    query,
    key,
    value,
    mixed,
    *rest,
):
    grad_refs = rest[:count]
    grads, scale_sum, bias_sum, grad, grad_aug, d_query, d_key, d_value = rest[count:]
    index = pl.num_programs(0) - 1 - pl.program_id(0)
    b_own, core = info[pl.num_programs(0)], info[pl.num_programs(0) + 1]
    b_size = count // CORES
    width = heads * HEAD_DIM

    @pl.when(pl.program_id(0) == 0)
    def clear():
        d_key[...] = jnp.zeros_like(d_key)
        d_value[...] = jnp.zeros_like(d_value)
        scale_sum[...] = jnp.zeros_like(scale_sum)
        bias_sum[...] = jnp.zeros_like(bias_sum)

    half = block // CORES
    lane = lax.broadcasted_iota(jnp.int32, (half, LANES), 1)
    for k in range(CORES):
        peer = ((b_own + b_size - index % b_size) % b_size) * CORES + (core ^ k)
        for p in range(count):

            @pl.when(peer == p)
            def fetch():
                grad[...] = grad_refs[p][index // b_size]

        for h in range(heads):
            part = slice((first + h) * HEAD_DIM, (first + h + 1) * HEAD_DIM)
            grad_h = grad[:, part].astype(F32)
            mixed_h = mixed[0, core ^ k, 0, :, part].astype(F32)
            delta = jnp.sum(grad_h * mixed_h, axis=1, keepdims=True)
            aug = jnp.concatenate([grad_h, jnp.zeros((half, LANES - HEAD_DIM), F32)], axis=1)
            high = (-delta).astype(BF16).astype(F32)
            aug = jnp.where(lane == HEAD_DIM, high, aug)
            aug = jnp.where(lane == HEAD_DIM + 1, -delta - high, aug)
            grad_aug[k * half : (k + 1) * half, h * LANES : (h + 1) * LANES] = aug.astype(BF16)
    d_query[...] = jnp.zeros_like(d_query)
    columns = index * block + lax.broadcasted_iota(jnp.int32, (block, block), 1)
    begin = starts[0:1, :]

    def step(j, carry):
        spot = pl.multiple_of(j * block, block)
        rows = spot + lax.broadcasted_iota(jnp.int32, (block, block), 0)
        allowed = (rows >= begin) & (rows <= columns)
        for h in range(heads):
            lanes = slice(h * LANES, (h + 1) * LANES)
            key_h = key[pl.ds(spot, block), lanes]
            query_h = query[:, lanes]
            grad_h = grad_aug[:, lanes]
            prob = jnp.where(allowed, jnp.exp(dot(key_h, query_h, 1, 1)), 0.0)
            d_prob = dot(value[pl.ds(spot, block), lanes], grad_h, 1, 1)
            d_score = (prob * d_prob).astype(BF16)
            d_value[pl.ds(spot, block), lanes] += dot(prob.astype(BF16), grad_h)
            d_key[pl.ds(spot, block), lanes] += dot(d_score, query_h)
            d_query[:, lanes] += dot(d_score, key_h, 0, 0)
        return carry

    lax.fori_loop(info[index], index + 1, step, 0)
    here = pl.ds(pl.multiple_of(index * block, block), block)
    for h in range(heads):
        lanes = slice(h * LANES, (h + 1) * LANES)
        d_scaled = d_query[:, lanes].astype(BF16).astype(F32)
        scale_sum[...] += jnp.sum(d_scaled * query[:, lanes].astype(F32), axis=0, keepdims=True)
        d_q = (d_scaled * scale[0:1, lanes]).astype(BF16)
        for k, term in enumerate((d_q, d_key[here, lanes], d_value[here, lanes])):
            spot = k * width + h * HEAD_DIM
            term = term.astype(BF16)
            grads[:, spot : spot + HEAD_DIM] = term[:, :HEAD_DIM]
            bias_sum[:, (k * heads + h) * LANES : (k * heads + h + 1) * LANES] += jnp.sum(
                term.astype(F32), axis=0, keepdims=True
            )


def attend_backward(
    at, info, starts, scale, query_aug, qkv, grads, mixed, heads, groups, group, block
):
    length = qkv.shape[0]
    wide = heads * LANES
    width = heads * HEAD_DIM
    count = length // block
    b_size = at.b_size
    half = block // CORES

    def mixed_spot(i, s):
        i = count - 1 - i
        return (i + b_size - s[count]) % b_size, 0, i // b_size, 0, 0

    fixed = lambda i, s: (0, 0)
    return call(
        "attend_backward",
        functools.partial(backward_body, heads, group * heads, block, len(grads)),
        info,
        [
            (starts, pl.BlockSpec((8, block), lambda i, s: (0, count - 1 - i))),
            (scale, pl.BlockSpec((8, wide), fixed)),
            (query_aug, pl.BlockSpec((block, wide), lambda i, s: (count - 1 - i, group))),
            (qkv, pl.BlockSpec((length, wide), lambda i, s: (0, groups + group))),
            (qkv, pl.BlockSpec((length, wide), lambda i, s: (0, 2 * groups + group))),
            (mixed, pl.BlockSpec((1, CORES, 1, half, mixed.shape[4]), mixed_spot)),
        ]
        + [(grad, VMEM) for grad in grads],
        [
            (
                (length, 3 * width),
                BF16,
                pl.BlockSpec((block, 3 * width), lambda i, s: (count - 1 - i, 0)),
            ),
            ((8, LANES), F32, pl.BlockSpec((8, LANES), fixed)),
            ((8, 3 * wide), F32, pl.BlockSpec((8, 3 * wide), fixed)),
        ],
        grid=(count,),
        scratch=[
            pltpu.VMEM((half, mixed.shape[4]), BF16),
            pltpu.VMEM((block, wide), BF16),
            pltpu.VMEM((block, wide), F32),
            pltpu.VMEM((length, wide), F32),
            pltpu.VMEM((length, wide), F32),
        ],
    )


def concat_body(info, *refs):
    parts, out = refs[:-1], refs[-1]
    width = parts[0].shape[1]
    for p, part in enumerate(parts):
        out[:, p * width : (p + 1) * width] = part[...]


def concat(parts, after):
    rows, width = parts[0].shape
    return call(
        "concat",
        concat_body,
        [0],
        [(part, VMEM) for part in parts],
        [((rows, width * len(parts)), BF16, VMEM)],
        after=after,
    )[0]


def middle_body(count, source_count, moves, info, *refs):
    mixed, tokens, d_out, gain = refs[:4]
    sources = refs[4 : 4 + source_count]
    outs = refs[4 + source_count :]
    output, d_residual, d_proj, normed, activated, d_up = outs[:6]
    d_parts = outs[6:-4]
    weights, sems = outs[-4:-1], outs[-1]
    w_out, w_up, w_down = weights
    rows, half = sources[0].shape[2:]
    width = d_parts[0].shape[1]

    def copies(w):
        for n, (src, s, k) in enumerate(moves):
            if k == w:
                down = pl.ds(pl.multiple_of(info[2 * n] * rows, rows), rows)
                right = pl.ds(pl.multiple_of(info[2 * n + 1] * half, half), half)
                yield pltpu.make_async_copy(
                    sources[src].at[s, w], weights[w].at[down, right], sems.at[n]
                )

    def arrived(w):
        @pl.when(pl.program_id(0) == 0)
        def wait():
            for copy in copies(w):
                copy.wait()

    @pl.when(pl.program_id(0) == 0)
    def start():
        for w in range(3):
            for copy in copies(w):
                copy.start()

    arrived(0)
    residual = tokens[...].astype(F32) + dot(mixed[...], w_out[...])
    rate = lax.rsqrt(jnp.mean(residual * residual, axis=-1, keepdims=True) + NORM_EPS)
    normed[...] = (residual * rate * gain[...]).astype(BF16)
    arrived(1)
    upward = dot(normed[...], w_up[...])
    gate = 1.0 / (1.0 + jnp.exp(-upward))
    activated[...] = (upward * gate).astype(BF16)
    arrived(2)
    output[...] = (residual + dot(activated[...], w_down[...])).astype(BF16)
    d_activated = dot(d_out[...], w_down[...], 1, 1)
    d_up[...] = (d_activated * gate * (1 + upward * (1 - gate))).astype(BF16)
    scaled = dot(d_up[...], w_up[...], 1, 1) * gain[...]
    inner = jnp.mean(residual * scaled, axis=-1, keepdims=True)
    d_norm = rate * scaled - residual * (rate * rate * rate * inner)
    d_total = d_out[...].astype(F32) + d_norm
    d_residual[...] = d_total
    d_proj[...] = d_total.astype(BF16)
    d_mixed = dot(d_proj[...], w_out[...], 1, 1).astype(BF16)
    for p in range(count):
        d_parts[p][...] = d_mixed[:, p * width : (p + 1) * width]


def middle(at, mixed, tokens, d_out, gain, sources):
    count = at.peer_count
    rows, model = tokens.shape
    width = model // count
    arrays = list(sources.values())
    a_size, _, piece, half = arrays[0].shape
    group = model // at.peer_count // piece
    moves, spots = [], []
    for n, (dx, db, dc) in enumerate(sources):
        for a in range(a_size):
            for w in range(3):
                row = a * at.b_size + (at.b - db) % at.b_size
                if at.x_split == 2:
                    row = row * 2 + (at.x + dx) % 2
                if w == 0:
                    peer, rest = row // group, row % group
                    far = (at.b - peer // CORES) % at.b_size
                    row = (far * CORES + ((peer % CORES) ^ at.c)) * group + rest
                moves.append((n, a, w))
                spots += [row, (at.c + dc) % CORES]
    block = min(256, rows)
    row = lambda i, s: (i, 0)
    rows_of = pl.BlockSpec((block, model), row)
    part = pl.BlockSpec((block, width), row)
    types = [BF16, F32, BF16, BF16, BF16, BF16]
    return call(
        "middle",
        functools.partial(middle_body, count, len(arrays), moves),
        spots,
        [(mixed, rows_of), (tokens, rows_of), (d_out, rows_of)]
        + [(gain, pl.BlockSpec(gain.shape, lambda i, s: (0, 0)))]
        + [(source, ANY) for source in arrays],
        [((rows, model), kind, rows_of) for kind in types]
        + [((rows, width), BF16, part)] * count,
        grid=(rows // block,),
        scratch=[pltpu.VMEM((model, model), BF16)] * 3
        + [pltpu.SemaphoreType.DMA((len(moves),))],
    )


def outer_body(count, split, add, info, *refs):
    pairs, rest = refs[:6], refs[6:]
    for w in range(3):

        @pl.when(pl.program_id(0) == w)
        def product():
            value = dot(pairs[2 * w][...], pairs[2 * w + 1][...], 0, 0)
            target = rest[-1] if split else rest[-1].at[0]
            width = value.shape[0] // count
            for p in range(count):
                spot = p * width
                if w == 0:
                    spot = pl.multiple_of(info[3 + p] * width, width)
                part = value[p * width : (p + 1) * width]
                if add:
                    part = part + rest[0][0, pl.ds(spot, width)].astype(F32)
                target[pl.ds(spot, width)] = part.astype(BF16)

    if split:
        keep_x, give_x, keep_b, give_b, total = rest[1:]
        pairs_a, b_size, rows = keep_x.shape[1:4]
        for k in range(pairs_a):
            for b in range(b_size):
                for half, out in ((info[1], keep_x), (1 - info[1], give_x)):
                    spot = pl.multiple_of((k * b_size + b) * 2 * rows + half * rows, rows)
                    out[0, k, b] = total[pl.ds(spot, rows)]
            for b, out in ((info[2], keep_b), (1 - info[2], give_b)):
                for half in range(2):
                    spot = (((k + pairs_a) * b_size) * 2 + half) * rows + b * 2 * rows
                    out[0, k, half] = total[pl.ds(pl.multiple_of(spot, rows), rows)]


def outer(at, pairs, cols, add=None, after=()):
    rows, model = pairs[0][0].shape
    half = model // CORES
    count = at.peer_count
    split = add is not None and at.even
    info = [cols, at.x if at.even else 0, at.b, *[at.source(db, dc) for db, dc in at.peers()]]
    inputs = []
    for left, right in pairs:
        inputs.append((left, pl.BlockSpec((rows, model), lambda w, s: (0, 0))))
        inputs.append((right, pl.BlockSpec((rows, half), lambda w, s: (0, s[0]))))
    block = pl.BlockSpec((1, model, half), lambda w, s: (w, 0, 0))
    outputs = [((3, model, half), BF16, block)]
    scratch = []
    if add is not None:
        inputs.append((add, block))
    if split:
        shape = (at.a_size // 2, 2, model // at.a_size // 4, half)
        part = pl.BlockSpec((1, *shape), lambda w, s: (w, 0, 0, 0, 0))
        outputs = [((3, *shape), BF16, part)] * 4
        scratch = [pltpu.VMEM((model, half), BF16)]
    return call(
        "outer_give" if add is None else "outer",
        functools.partial(outer_body, count, split, add is not None),
        info,
        inputs,
        outputs,
        grid=(3,),
        scratch=scratch,
        after=after,
        vmem=60,
    )


def give_body(groups, info, *refs):
    grads, weights, out = refs[:groups], refs[groups : 2 * groups], refs[-1]
    value = back_product(grads, weights)
    out[...] = value.astype(BF16).reshape(out.shape)


def back_product(grads, weights):
    total = 0.0
    for grad, weight in zip(grads, weights):
        total = total + dot(grad[...].reshape(-1, grad.shape[-1]), weight[...], 1, 1)
    return total


def keep_body(groups, info, *refs):
    grads, weights, got = refs[:groups], refs[groups : 2 * groups], refs[2 * groups]
    outs = refs[2 * groups + 1 :]
    pairs, b_size, half = got.shape[:3]
    value = back_product(grads, weights).reshape(got.shape) + got[...].astype(F32)
    for b in range(b_size):
        for n, out in enumerate(outs):

            @pl.when(info[2 + n] == b)
            def copy():
                out[...] = value[:, b].astype(out.dtype)


def back_project(at, grads, weights, half, which, got=None):
    model = weights[0].shape[0]
    pair = at.a_size // 2
    groups = len(grads)
    width = grads[0].shape[1]
    shape = (pair, at.b_size, half, model)
    grads = [g.reshape(at.a_size, at.b_size, CORES, half, width) for g in grads]
    block = pl.BlockSpec((pair, at.b_size, 1, half, width), lambda i, s: (s[0], 0, s[1], 0, 0))
    core = at.c if got is not None else 1 - at.c
    inputs = [(g, block) for g in grads]
    inputs += [(weight, VMEM) for weight in weights]
    if got is None:
        body, outputs = give_body, [(shape, BF16, VMEM)]
    else:
        body = keep_body
        inputs.append((got, VMEM))
        outputs = [((pair, half, model), F32 if db == 0 else BF16, VMEM) for db in range(at.b_size)]
    return call(
        "back_project",
        functools.partial(body, groups),
        [which ^ core, core, *ahead(at.b, at.b_size)],
        inputs,
        outputs,
    )


def norm_back_body(count, info, *refs):
    own, others = refs[0], refs[1:count]
    tokens, d_residual, gain = refs[count : count + 3]
    for n, out in enumerate(refs[count + 3 :]):
        k = info[1 + n]
        grad = own[k]
        for other in others:
            grad = grad + other[k].astype(F32)
        value = tokens[k].astype(F32)
        rate = lax.rsqrt(jnp.mean(value * value, axis=-1, keepdims=True) + NORM_EPS)
        scaled = grad * gain[...]
        inner = jnp.mean(value * scaled, axis=-1, keepdims=True)
        d_norm = rate * scaled - value * (rate * rate * rate * inner)
        out[...] = (d_residual[k] + d_norm).astype(BF16)


def norm_back(at, terms, chunks, d_residual, gain, which):
    pair, half, model = terms[0].shape
    block = pl.BlockSpec((pair, half, model), lambda i, s: (s[0], 0, 0))
    order = [k ^ (at.a % pair) for k in range(pair)]
    return call(
        "norm_back",
        functools.partial(norm_back_body, len(terms)),
        [which ^ at.c, *order],
        [(t, VMEM) for t in terms] + [(chunks, block), (d_residual, block), (gain, VMEM)],
        [((half, model), BF16, VMEM)] * pair,
    )


def heads_outer_body(steps, info, normed, grads, extra, *rest):
    outs, acc = rest[:-1], rest[-1]
    value = dot(normed[...], grads[...], 0, 0)

    @pl.when(pl.program_id(0) == 0)
    def first():
        acc[...] = value

    @pl.when(pl.program_id(0) != 0)
    def later():
        acc[...] += value

    @pl.when(pl.program_id(0) == steps - 1)
    def last():
        used = acc.shape[1]
        pairs, b_size, rows = outs[0].shape[:3]
        split = len(outs)
        for n, out in enumerate(outs):
            for s in range(pairs * b_size):
                spot = (s * split + (info[0] ^ n if split == 2 else 0)) * rows
                spot = pl.ds(pl.multiple_of(spot, rows), rows)
                out[s // b_size, s % b_size, :, :used] = acc[spot, :].astype(BF16)
                out[s // b_size, s % b_size, :, used:] = extra[spot, :]


def heads_outer(at, normed, grads, extra):
    length, model = normed.shape
    used = grads.shape[1]
    block = min(512, length)
    steps = length // block
    rows = model // at.a_size // at.b_size // at.x_split
    shape = (at.a_size, at.b_size, rows, used + extra.shape[1])
    return call(
        "heads_outer",
        functools.partial(heads_outer_body, steps),
        [at.x],
        [
            (normed, pl.BlockSpec((block, model), lambda i, s: (i, 0))),
            (grads, pl.BlockSpec((block, used), lambda i, s: (i, 0))),
            (extra, pl.BlockSpec(extra.shape, lambda i, s: (0, 0))),
        ],
        [(shape, BF16, pl.BlockSpec(shape, lambda i, s: (0, 0, 0, 0)))] * at.x_split,
        grid=(steps,),
        scratch=[pltpu.VMEM((model, used), F32)],
    )


def all_sum(at, value, axis, size):
    total = value
    for d in range(1, size):
        total = total + at.send(value, **{axis: d}).astype(value.dtype)
    return total


def ahead(spot, size):
    return [(spot + d) % size for d in range(size)]


def cat_body(info, first, first_got, second, second_got, out):
    pair = first.shape[1]
    out[:, :pair] = (first[...].astype(F32) + first_got[...].astype(F32)).astype(BF16)
    out[:, pair:] = (second[...].astype(F32) + second_got[...].astype(F32)).astype(BF16)


class FullReduce:
    def __init__(self, at, parts):
        self.at = at
        if at.even:
            keep_x, give_x, keep_b, give_b = parts
            self.first = keep_x, at.send(give_x, dx=1)
            self.second = keep_b, at.send(give_b, db=1)
        else:
            self.part = parts[0].reshape(3, at.a_size, at.b_size, -1, parts[0].shape[-1])

    def next(self):
        at = self.at
        if not at.even:
            return
        groups = [[(t, 2, b) for t in self.first] for b in ahead(at.b, 2)]
        groups += [[(t, 2, x) for t in self.second] for x in ahead(at.x, 2)]
        keep_b, give_b, keep_x, give_x = add_blocks(groups)
        self.first = keep_b, at.send(give_b, db=1)
        self.second = keep_x, at.send(give_x, dx=1)

    def over_a(self):
        at = self.at
        part = None
        if at.even:
            shape = self.first[0].shape
            part = call(
                "cat",
                cat_body,
                [0],
                [(t, VMEM) for t in (*self.first, *self.second)],
                [((3, at.a_size, *shape[2:]), BF16, VMEM)],
            )[0]
        else:
            part = self.part
        parts = add_blocks([[(part, 1, a)] for a in ahead(at.a, at.a_size)])
        self.got = [parts[0]] + [at.send(parts[d], da=d) for d in range(1, at.a_size)]

    def end(self):
        at = self.at
        if at.even:
            part = add_blocks([[(t[None], 0, 0) for t in self.got]])[0]
            far = at.send(part, dx=1)
            return [part, far, at.send(part, dc=1), at.send(far, dc=1)]
        parts = add_blocks([[(t, 1, b) for t in self.got] for b in ahead(at.b, at.b_size)])
        got = [parts[0]] + [at.send(parts[d], db=d) for d in range(1, at.b_size)]
        part = add_blocks([[(t[None], 0, 0) for t in got]])[0]
        part = all_sum(at, part, "dx", at.x_size)
        return [part, at.send(part, dc=1)]


class HeadsReduce:
    def __init__(self, at, parts):
        self.at = at
        self.got = [parts[0]]
        if at.x_split == 2:
            self.got.append(at.send(parts[1], dx=1))

    def over_a(self):
        at = self.at
        parts = add_blocks([[(t, 0, a) for t in self.got] for a in ahead(at.a, at.a_size)])
        self.got = [parts[0]] + [at.send(parts[d], da=d) for d in range(1, at.a_size)]
        return parts

    def to_peers(self):
        at = self.at
        if at.x_split == 1:
            total = add_blocks([[(t[None], 0, 0) for t in self.got]])[0]
            self.got = [all_sum(at, total, "dx", at.x_size)]
        parts = add_blocks([[(t, 0, b) for t in self.got] for b in ahead(at.b, at.b_size)])
        parts = [
            at.send(parts[db], db=db, dc=dc) if db or dc else parts[0] for db, dc in at.peers()
        ]
        if at.x_split == 1:
            return [parts]
        return [parts, at.send(jnp.stack(parts), dx=1)]


def in_order(info, refs, split, half, core, spot):
    near = [r[spot] for r in refs]
    if split == 2:
        near = [jnp.where(info[0] == half, near[2 * k], near[2 * k + 1]) for k in range(2)]
    return jnp.where(info[1] == core, near[0], near[1])


def finish_full_body(split, info, *refs):
    count = CORES * split
    parts, (weight, gain), outs = refs[:count], refs[count : count + 2], refs[count + 2 :]
    rows, half = parts[0].shape[1:]
    for x in range(split):
        spot = slice(x * rows, (x + 1) * rows)
        for w in range(3):
            for c in range(CORES):
                outs[w][spot, c * half : (c + 1) * half] = in_order(
                    info, parts, split, x, c, w
                ).astype(F32)
    total = jnp.sum(outs[1][...] * weight[...].astype(F32), axis=1, keepdims=True)
    outs[3][...] = total / gain[...].astype(F32)


def finish_full(at, parts, weight, gain, after):
    rows, model = weight.shape
    return call(
        "finish_full",
        functools.partial(finish_full_body, 2 if at.even else 1),
        [at.x, at.c],
        [(p, VMEM) for p in parts] + [(weight, VMEM), (gain[:, None], VMEM)],
        [((rows, model), F32, VMEM)] * 3 + [((rows, 1), F32, VMEM)],
        after=after,
    )


def finish_heads_body(count, groups, split, info, *refs):
    parts, refs = refs[: groups * count], refs[groups * count :]
    far, refs = refs[: groups * (split - 1)], refs[groups * (split - 1) :]
    weights, gain, outs = refs[:3], refs[3], refs[4:]
    few = outs[4].shape[1]
    rows, width = parts[0].shape
    width = (width - few) // 3
    for n in range(split):
        down = pl.ds(pl.multiple_of((info[count] ^ n if split == 2 else 0) * rows, rows), rows)
        total = jnp.zeros((rows, few), F32)
        for p in range(count):
            for g in range(groups):
                source = far[g].at[p] if n else parts[g * count + p]
                total = total + source[:, 3 * width :].astype(F32)
                for peer in range(count):

                    @pl.when(info[p] == peer)
                    def copy():
                        for k in range(3):
                            spot = (peer * groups + g) * width
                            piece = source[:, k * width : (k + 1) * width]
                            outs[k][down, spot : spot + width] = piece.astype(F32)

        outs[4][down, :] = total
    total = jnp.zeros(outs[3].shape, F32)
    for k in range(3):
        total = total + jnp.sum(outs[k][...] * weights[k][...].astype(F32), axis=1, keepdims=True)
    outs[3][...] = total / gain[...].astype(F32)


def finish_heads(at, parts, weights, gain, few):
    rows, model = weights[0].shape
    flat = [part for group in parts for part in group[0]]
    flat += [group[1] for group in parts if at.x_split == 2]
    return call(
        "finish_heads",
        functools.partial(finish_heads_body, at.peer_count, len(parts), at.x_split),
        [*[at.source(db, dc) for db, dc in at.peers()], at.x],
        [(p, VMEM) for p in flat] + [(w, VMEM) for w in weights] + [(gain[:, None], VMEM)],
        [((rows, model), F32, VMEM)] * 3 + [((rows, 1), F32, VMEM), ((rows, few), F32, VMEM)],
    )


def local(
    reps,
    shards,
    activations,
    cotangent,
    doc_lengths,
    gain_attn,
    query_weight,
    query_bias,
    key_weight,
    value_weight,
    value_bias,
    dim_scale,
    out_weight,
    gain_mlp,
    up_weight,
    down_weight,
):
    seqs, tok_count, model = activations.shape
    at = Place(reps, shards, seqs)
    half = tok_count // CORES
    length = tok_count * shards
    peer_count = at.peer_count
    heads = model // HEAD_DIM // peer_count
    width = heads * HEAD_DIM
    wide = heads * LANES
    own_rows = at.a_size * half
    rows = gain_attn.shape[0]
    groups = 2
    block = CORES * half
    mine = at.b * CORES + at.c

    LAST.clear()
    stage = at.to_cluster(activations)
    next(stage)
    vectors = jnp.stack([gain_attn, gain_mlp, query_bias, value_bias], axis=1)
    own, *sent = heads_parts(at, (query_weight, key_weight, value_weight), vectors, groups)
    sent = [at.send(part, db=db + 1) for db, part in enumerate(sent)]
    next(stage)
    near = by_order(own, sent, at.b_size, at.b)
    ring = ring_gather(at, near)
    next(ring)
    chunks = next(stage)
    nears = [at.send(chunks, db=db) if db else chunks for db in range(at.b_size)]
    most = next(ring)
    sources = [most, None]
    if at.x_split == 2:
        sources += [at.send(most, dx=1), None]
    far = next(ring)
    parts = []
    for near in nears:
        parts += [near, at.send(later(near, far), dc=1)]
    sources[1] = far
    if at.x_split == 2:
        sources[3] = at.send(far, dx=1)
    quarter = quarter_of(at, (out_weight, up_weight, down_weight), parts[1:])
    stage = at.to_cluster(cotangent)
    next(stage)
    pieces = [quarter] + [at.send(quarter, da=d) for d in range(1, at.a_size)]
    *w_heads, w_pad, vectors = pad_weights(
        at, sources, heads, groups, parts[1:]
    )
    moves = [(d, None, 0, (at.a - d) % at.a_size) for d in range(at.a_size)]
    quarter = shuffle(pieces, [((at.a_size, *quarter.shape), BF16)], moves)[0]
    others = {(0, 0, 0): quarter, (0, 0, 1): at.send(quarter, dc=1)}
    for db in range(1, at.b_size):
        others[(0, db, 0)] = at.send(quarter, db=db)
    if at.x_split == 2:
        others[(1, 0, 0)] = at.send(quarter, dx=1)
    vectors = vectors.T.astype(F32)
    g_attn, g_mlp, b_query, b_value = vectors[0], vectors[1], vectors[2], vectors[3]

    other_lengths = at.send(doc_lengths, dc=1)
    lengths = pick(jnp.where(at.c == at.a // seqs, doc_lengths, other_lengths), at.a % seqs)
    ends = jnp.cumsum(lengths)
    places = jnp.arange(length, dtype=jnp.int32)
    starts = jnp.max(jnp.where(ends[None, :] <= places[:, None], ends[None, :], 0), axis=1)
    starts_row = jnp.broadcast_to(starts[None, :], (8, length))
    starts_col = jnp.broadcast_to(starts[:, None], (length, LANES))
    info = jnp.concatenate([starts[::block] // block, jnp.stack([at.b, at.c])]).astype(jnp.int32)

    scale_dim = LOG_BASE / math.sqrt(HEAD_DIM) * jax.nn.softplus(dim_scale)
    scale_pad = jnp.tile(jnp.pad(scale_dim, (0, LANES - HEAD_DIM)), heads)
    lane = jnp.arange(LANES)
    ones_key = ((lane >= HEAD_DIM) & (lane < HEAD_DIM + 3)).astype(F32)
    ones_value = ((lane >= HEAD_DIM) & (lane < HEAD_DIM + 2)).astype(F32)

    def pad_heads(vec):
        part = lax.dynamic_slice_in_dim(vec, mine * width, width, 0).reshape(heads, HEAD_DIM)
        return jnp.pad(part, ((0, 0), (0, LANES - HEAD_DIM))).reshape(wide)

    bias_pad = jnp.concatenate(
        [
            pad_heads(b_query),
            jnp.tile(ones_key, heads),
            pad_heads(b_value) + jnp.tile(ones_value, heads),
        ]
    )
    times = jnp.concatenate([scale_pad, jnp.ones((2 * wide,), F32)])
    qkv, normed = project(at, parts, g_attn[None], w_pad, bias_pad[None], times[None])

    part_heads = heads // groups
    part_width = part_heads * HEAD_DIM
    stage.send([others[(0, db, 0)] for db in range(1, at.b_size)] + [others[(0, 0, 1)]])
    soon = []
    if at.x_split == 2:
        for db in range(1, at.b_size):
            others[(1, db, 0)] = at.send(later(others[(0, db, 0)], qkv), dx=1)
            soon.append(others[(1, db, 0)])
        others[(1, 0, 1)] = at.send(later(others[(1, 0, 0)], qkv), dc=1)
        soon.append(others[(1, 0, 1)])
    mixed_rel, query_aug = attend_forward(at, info, starts_col, qkv, heads, block)
    parts = []
    for db, dc in at.peers():
        part = mixed_rel[db, dc].reshape(own_rows, width)
        parts.append(at.send(part, db=db, dc=dc) if db or dc else part)
    d_out = stage.send(soon).reshape(own_rows, model)
    last = []
    for dx, db, dc in list(others):
        if (dx, db, 1) not in others:
            others[(dx, db, 1)] = at.send(later(others[(dx, db, 0)], d_out), dc=1)
            last.append(others[(dx, db, 1)])
    mixed = concat(parts, last)
    tokens = chunks.reshape(own_rows, model)
    output, d_residual, d_proj, normed_mlp, activated, d_up, *d_parts = middle(
        at, mixed, tokens, d_out, g_mlp[None], others
    )

    grads = []
    for (db, dc), part in zip(at.peers(), d_parts):
        part = at.send(part, db=db, dc=dc) if db or dc else part
        grads.append(part.reshape(at.a_size, half, width))

    pairs = [(mixed, d_proj), (normed_mlp, d_up), (activated, d_out)]
    give = outer(at, pairs, 1 - at.c)[0]
    full = FullReduce(at, outer(at, pairs, at.c, at.send(give, dc=1), grads))

    scale_rows = jnp.broadcast_to(scale_pad[None, : part_heads * LANES], (8, part_heads * LANES))
    zeros = jnp.zeros((model,), F32)

    def backward(g):
        d_heads, scale_sum, bias_sum = attend_backward(
            at,
            info,
            starts_row,
            scale_rows,
            query_aug,
            qkv,
            grads,
            mixed_rel,
            part_heads,
            groups,
            g,
            block,
        )
        bias_sum = bias_sum[0].reshape(3, part_heads, LANES)[:, :, :HEAD_DIM]
        bias_sum = bias_sum.reshape(3, part_width)
        spot = (mine * groups + g) * part_width
        scale_sum = jnp.pad(scale_sum[0, :HEAD_DIM], (0, rows - HEAD_DIM))
        extra = [
            lax.dynamic_update_slice(zeros, bias_sum[0], (spot,)),
            lax.dynamic_update_slice(zeros, bias_sum[2], (spot,)),
            jnp.tile(scale_sum, shards),
        ]
        return d_heads, jnp.stack(extra, axis=1).astype(BF16)

    stage = at.from_cluster(output.reshape(at.a_size, half, model))
    next(stage)
    d_first, extra_first = backward(0)
    full.next()
    next(stage)
    reduce_first = HeadsReduce(at, heads_outer(at, normed, d_first, extra_first))
    output = next(stage)
    full.over_a()
    d_second, extra_second = backward(1)
    full_parts = full.end()
    reduce_first.over_a()

    d_heads = [d_first, d_second]
    gives = [back_project(at, d_heads, w_heads, half, which)[0] for which in range(2)]
    keeps = []
    for which in range(2):
        terms = back_project(at, d_heads, w_heads, half, which, at.send(gives[which], dc=1))
        keeps.append([terms[0]] + [at.send(terms[db], db=db) for db in range(1, at.b_size)])
    first = reduce_first.to_peers()
    reduce_second = HeadsReduce(at, heads_outer(at, normed, d_second, extra_second))
    residual_chunks = d_residual.reshape(at.a_size, half, model)
    received = []

    def back(which):
        sent = norm_back(at, keeps[which], chunks, residual_chunks, g_attn[None], which)
        for k, part in enumerate(sent):
            received.append(at.send_back(part, which * len(sent) + k))

    back(0)
    *grads_full, grad_gain_mlp = finish_full(at, full_parts, up_weight, gain_mlp, first[0][1:])
    back(1)
    reduce_second.over_a()
    input_grad = at.place_back(received)
    second = reduce_second.to_peers()
    weights = (query_weight, key_weight, value_weight)
    *grads_heads, grad_gain_attn, few = finish_heads(at, [first, second], weights, gain_attn, 3)
    grad_scale = few[:HEAD_DIM, 2] / scale_dim * (LOG_BASE / math.sqrt(HEAD_DIM))
    grad_scale = grad_scale * jax.nn.sigmoid(dim_scale)
    return (
        output,
        input_grad,
        grad_gain_attn[:, 0],
        grads_heads[0],
        few[:, 0],
        grads_heads[1],
        grads_heads[2],
        few[:, 1],
        grad_scale,
        grads_full[0],
        grad_gain_mlp[:, 0],
        grads_full[1],
        grads_full[2],
    )


def solution(mesh):
    in_specs = (
        P("rep", "shard", None),
        P("rep", "shard", None),
        P("rep", None),
        P("shard"),
        P("shard", None),
        P("shard"),
        P("shard", None),
        P("shard", None),
        P("shard"),
        P(),
        P("shard", None),
        P("shard"),
        P("shard", None),
        P("shard", None),
    )
    out_specs = (
        P("rep", "shard", None),
        P("rep", "shard", None),
        P("shard"),
        P("shard", None),
        P("shard"),
        P("shard", None),
        P("shard", None),
        P("shard"),
        P(),
        P("shard", None),
        P("shard"),
        P("shard", None),
        P("shard", None),
    )
    body = functools.partial(local, mesh.shape["rep"], mesh.shape["shard"])
    return jax.shard_map(body, mesh=mesh, in_specs=in_specs, out_specs=out_specs, check_vma=False)
```

time: 771 us -> 518 us (0.67)
  starting transfers between devices: 194 us -> 69.2 us
  Pallas kernels: 95.8 us -> 204 us
  waiting for transfers between devices: 236 us -> 164 us
  local copies, waits for them, and re-layouts: 135 us -> 63.2 us
  matrix products: 55.1 us -> 0 us
  other arithmetic: 41.6 us -> 5.6 us
    pallas_call x14 -> x43, Pallas kernels: 95.8 us -> 204 us  [call(): pl.pallas_call(run, out_shape=[jax.ShapeDtypeStruct(shape, kind) for shap...]
    ppermute x126 -> x70, starting transfers between devices: 146 us -> 62.6 us  [send(): lax.ppermute(value, AXES, self.route(lambda x, c, a, b: ((x + dx) % self....]
    ppermute x126 -> x70, waiting for transfers between devices: 191 us -> 131 us  [send(): lax.ppermute(value, AXES, self.route(lambda x, c, a, b: ((x + dx) % self....]
    dot_general x12 -> x0, matrix products: 55.1 us -> none  [dot(): lax.dot_general(left, right, (((left_dim,), (right_dim,)), ((), ())), pre...]
    ppermute x16 -> x4, starting transfers between devices: 47.5 us -> 6.57 us  [send_back(): lax.ppermute(part, AXES, [(j, i) for i, j in self.route(self._match(m))])]
    another operation x37, local copies, waits for them, and re-layouts: 37.6 us -> 4.52 us  [the longest x12 2.28 us: scalars_of(): return jnp.stack([jnp.asarray(v, jnp.int32) for v in values])]
    unnamed x160 -> x205, local copies, waits for them, and re-layouts: 22.6 us -> 54.6 us
    convert_element_type x22 -> x0, other arithmetic: 21.9 us -> none  [the longest x3 4.48 us: reduce_full(): part = sum_over(at, grad, 'dc', CORES).astype(BF16)]
  transfers between devices with their start and end apart: 142 -> 74, of which waited for: 40 -> 26; matrix products, arithmetic and copies ran while one was open for 24% -> 2% of each run, Pallas kernels for 12% -> 29%
where the time goes in v2:
time: 518 us; the launch traced here: 509 us
  Pallas kernels  204 us (39%)
  waiting for transfers between devices  164 us (32%)
  starting transfers between devices  69.2 us (13%)
  local copies, waits for them, and re-layouts  63.2 us (12%)
  other arithmetic  5.6 us (1%)
    pallas_call x43, Pallas kernels, call(): pl.pallas_call(run, out_shape=[jax.ShapeDtypeStruct(shape, kind) for shap...  204 us
    ppermute x70, waiting for transfers between devices, send(): lax.ppermute(value, AXES, self.route(lambda x, c, a, b: ((x + dx) % self....  131 us
    ppermute x70, starting transfers between devices, send(): lax.ppermute(value, AXES, self.route(lambda x, c, a, b: ((x + dx) % self....  62.6 us
    unnamed x205, local copies, waits for them, and re-layouts  54.6 us
    ppermute x4, waiting for transfers between devices, send_back(): lax.ppermute(part, AXES, [(j, i) for i, j in self.route(self._match(m))])  33.1 us
  transfers between devices with their start and end apart: 74, of which 26 were waited for; matrix products, arithmetic and copies ran while one was open for 2% of the time, Pallas kernels for 29%

profile of v2, /device:TPU:9, one launch (start us, length us, event | category | flops | bytes accessed | tf_op | source)
XLA Modules:
  0.0 508.9 jit_solution(3840891795484091416)
XLA Ops:
  12.4 3.1 collective-permute-done.5.refs_1_
  16.5 19.8 %collective-permute-done.3.refs_2_ = bf16[128,1280]{1,0:T(8,128)(2,1)S(1)} collective-permute-done((bf16[128,1280]{1,0:T(8,128)(2,1)S(1)}, bf16[128,1280]{1,0:T(8,128)(2,1)S(1)}, u32[]{:S(2)}, u32[]{:S(2)}) %collective-permute-start.3) | collective-permute-done | bytes 327712 | tf_op jit(solution)/shard_map/ppermute | solution.py:55
  36.3 2.5 collective-permute-done.4.refs_3_
  42.6 8.4 %collective-permute-done.6.refs_1_ = bf16[2,80,964]{2,1,0:T(8,128)(2,1)S(1)} collective-permute-done((bf16[2,80,964]{2,1,0:T(8,128)(2,1)S(1)}, bf16[2,80,964]{2,1,0:T(8,128)(2,1)S(1)}, u32[]{:S(2)}, u32[]{:S(2)}) %collective-permute-start.6) | collective-permute-done | bytes 308512 | tf_op jit(solution)/shard_map/ppermute | solution.py:55
  51.1 7.2 %collective-permute-done.8.refs_2_ = bf16[2,80,964]{2,1,0:T(8,128)(2,1)S(1)} collective-permute-done((bf16[2,80,964]{2,1,0:T(8,128)(2,1)S(1)}, bf16[2,80,964]{2,1,0:T(8,128)(2,1)S(1)}, u32[]{:S(2)}, u32[]{:S(2)}) %collective-permute-start.8) | collective-permute-done | bytes 308512 | tf_op jit(solution)/shard_map/ppermute | solution.py:55
  58.3 2.9 collective-permute-start.9
  66.8 3.0 collective-permute-done.11.refs_5_.refs_6_.refs_2_
  80.2 21.1 %collective-permute-done.14.refs_3_ = bf16[2,80,964]{2,1,0:T(8,128)(2,1)} collective-permute-done((bf16[2,80,964]{2,1,0:T(8,128)(2,1)S(1)}, bf16[2,80,964]{2,1,0:T(8,128)(2,1)}, u32[]{:S(2)}, u32[]{:S(2)}) %collective-permute-start.14) | collective-permute-done | bytes 308512 | tf_op jit(solution)/shard_map/ppermute | solution.py:55
  101.3 4.6 pad_weights.1
  109.1 2.9 shuffle.17.refs_8_.refs_4_
  118.9 14.5 %project.1 = (bf16[2048,1536]{1,0:T(8,128)(2,1)}, bf16[2048,1280]{1,0:T(8,128)(2,1)}) custom-call(s32[4]{0:T(128)S(1)} %pad_add_fusion.2.spots, bf16[4,128,1280]{2,1,0:T(8,128)(2,1)S(1)} %shuffle.13.refs_3_.refs_0_.refs_2_, bf16[4,128,1280]{2,1,0:T(8,128)(2,1)} %collective-permute-done.10.refs_4_.refs_5_.refs_1_, ...), custom_call_target="tpu_custom_call" | custom-call | flops 3987500032 | bytes 11962500 | tf_op jit(solution)/shard_map/project/pallas_call | solution.py:155
  133.4 6.1 %collective-permute-done.28.refs_7_ = bf16[4,3,80,640]{3,2,1,0:T(8,128)(2,1)} collective-permute-done((bf16[4,3,80,640]{3,2,1,0:T(8,128)(2,1)}, bf16[4,3,80,640]{3,2,1,0:T(8,128)(2,1)}, u32[]{:S(2)}, u32[]{:S(2)}) %collective-permute-start.28) | collective-permute-done | bytes 1228832 | tf_op jit(solution)/shard_map/ppermute | solution.py:55
  143.5 2.8 copy-done.21
  151.3 26.0 %attend_forward.1 = (bf16[2,2,4,128,320]{4,3,2,1,0:T(8,128)(2,1)S(1)}, bf16[2048,512]{1,0:T(8,128)(2,1)S(1)}) custom-call(s32[10]{0:T(128)S(1)} %pad_add_fusion.1.spots, s32[2048,128]{1,0:T(8,128)S(1)} %broadcast_in_dim.58.refs_0_, bf16[2048,1536]{1,0:T(8,128)(2,1)S(1)} %copy-done.22, bf16[2048,1536]{1,0:T(8,128)(2,1)S(1)} %copy-done.22, ...), custom_call_target="tpu_custom_call" | custom-call | flops 7150000128 | bytes 21450000 | tf_op jit(solution)/shard_map/attend_forward/pallas_call | solution.py:155
  187.6 8.4 %collective-permute-done.22.refs_2_ = bf16[512,320]{1,0:T(8,128)(2,1)} collective-permute-done((bf16[512,320]{1,0:T(8,128)(2,1)}, bf16[512,320]{1,0:T(8,128)(2,1)}, u32[]{:S(2)}, u32[]{:S(2)}) %collective-permute-start.22) | collective-permute-done | bytes 327712 | tf_op jit(solution)/shard_map/ppermute | solution.py:55
  196.0 8.6 %collective-permute-done.23.refs_3_ = bf16[512,320]{1,0:T(8,128)(2,1)} collective-permute-done((bf16[512,320]{1,0:T(8,128)(2,1)}, bf16[512,320]{1,0:T(8,128)(2,1)}, u32[]{:S(2)}, u32[]{:S(2)}) %collective-permute-start.23) | collective-permute-done | bytes 327712 | tf_op jit(solution)/shard_map/ppermute | solution.py:55
  207.3 19.2 %middle.1 = (bf16[512,1280]{1,0:T(8,128)(2,1)S(1)}, f32[512,1280]{1,0:T(8,128)}, bf16[512,1280]{1,0:T(8,128)(2,1)S(1)}, bf16[512,1280]{1,0:T(8,128)(2,1)}, bf16[...) custom-call(s32[192]{0:T(256)S(1)} %stack.276.spots, ...), custom_call_target="tpu_custom_call" | custom-call | flops 5500000256 | bytes 16500000 | tf_op jit(solution)/shard_map/middle/pallas_call | solution.py:155
  229.3 8.5 %outer_give.1.refs_7_ = bf16[3,1280,640]{2,1,0:T(8,128)(2,1)} custom-call(s32[7]{0:T(128)} %stack.302.spots, bf16[512,1280]{1,0:T(8,128)(2,1)} %copy-done.15, bf16[512,1280]{1,0:T(8,128)(2,1)} %copy-done.30, bf16[512,1280]{1,0:T(8,128)(2,1)} %get-tuple-element.135.refs_2_, bf16[512,1280]{1,0:T(8,128)(2,1)} %get-tuple-element.136.refs_3_, ...), custom_call_target="tpu_custom_call" | custom-call | flops 27500000 | bytes 82500 | tf_op jit(solution)/shard_map/outer_give/pallas_call | solution.py:155
  242.9 6.1 %collective-permute-done.34 = bf16[512,320]{1,0:T(8,128)(2,1)S(1)} collective-permute-done((bf16[512,320]{1,0:T(8,128)(2,1)}, bf16[512,320]{1,0:T(8,128)(2,1)S(1)}, u32[]{:S(2)}, u32[]{:S(2)}) %collective-permute-start.34) | collective-permute-done | bytes 327712 | tf_op jit(solution)/shard_map/ppermute | solution.py:55
  249.0 8.8 %collective-permute-done.35 = bf16[512,320]{1,0:T(8,128)(2,1)S(1)} collective-permute-done((bf16[512,320]{1,0:T(8,128)(2,1)S(1)}, bf16[512,320]{1,0:T(8,128)(2,1)S(1)}, u32[]{:S(2)}, u32[]{:S(2)}) %collective-permute-start.35) | collective-permute-done | bytes 327712 | tf_op jit(solution)/shard_map/ppermute | solution.py:55
  258.6 9.9 %outer.1 = (bf16[3,2,2,80,640]{4,3,2,1,0:T(8,128)(2,1)}, bf16[3,2,2,80,640]{4,3,2,1,0:T(8,128)(2,1)}, bf16[3,2,2,80,640]{4,3,2,1,0:T(8,128)(2,1)}, bf16[3,2,2,80,640]{4,3,2,1,0:T(8,128)(2,1)}) custom-call(s32[7]{0:T(128)} %stack.301.spots, bf16[512,1280]{1,0:T(8,128)(2,1)} %copy-done.15, bf16[512,1280]{1,0:T(8,128)(2,1)} %copy-done.30, ...), custom_call_target="tpu_custom_call" | custom-call | flops 1924999936 | bytes 5775000 | tf_op jit(solution)/shard_map/outer/pallas_call | solution.py:155
  273.7 3.0 collective-permute-start.37
  276.8 2.8 copy-done.23
  283.2 24.1 %attend_backward.2 = (bf16[2048,480]{1,0:T(8,128)(2,1)S(1)}, f32[8,128]{1,0:T(8,128)S(1)}, f32[8,768]{1,0:T(8,128)S(1)}) custom-call(s32[10]{0:T(128)S(1)} %pad_add_fusion.1.spots, s32[8,2048]{1,0:T(8,128)S(1)} %broadcast_in_dim.61.refs_0_, f32[8,256]{1,0:T(8,128)S(1)} %broadcast_in_dim.63.refs_1_, bf16[2048,512]{1,0:T(8,128)(2,1)S(1)} %copy-done.88, ...), custom_call_target="tpu_custom_call" | custom-call | flops 6874999808 | bytes 20625000 | tf_op jit(solution)/shard_map/attend_backward/pallas_call | solution.py:155
  307.4 2.8 add_blocks.7
  317.7 2.5 copy-done.13
  322.2 5.6 %heads_outer.2 = (bf16[4,2,80,483]{3,2,1,0:T(8,128)(2,1)S(1)}, bf16[4,2,80,483]{3,2,1,0:T(8,128)(2,1)}) custom-call(s32[1]{0:T(128)} %bitcast.54.spots, bf16[2048,1280]{1,0:T(8,128)(2,1)S(1)} %copy-done.13, bf16[2048,480]{1,0:T(8,128)(2,1)S(1)} %get-tuple-element.151.refs_8_.refs_1_, bf16[1280,3]{1,0:T(8,128)(2,1)S(1)} %copy-done.49, ...), custom_call_target="tpu_custom_call" | custom-call | flops 1512499968 | bytes 4537500 | tf_op jit(solution)/shard_map/heads_outer/pallas_call | solution.py:155
  329.1 3.0 shuffle.20.refs_4_
  339.2 25.1 %attend_backward.3 = (bf16[2048,480]{1,0:T(8,128)(2,1)S(1)}, f32[8,128]{1,0:T(8,128)S(1)}, f32[8,768]{1,0:T(8,128)S(1)}) custom-call(s32[10]{0:T(128)S(1)} %pad_add_fusion.1.spots, s32[8,2048]{1,0:T(8,128)S(1)} %broadcast_in_dim.61.refs_0_, f32[8,256]{1,0:T(8,128)S(1)} %broadcast_in_dim.63.refs_1_, bf16[2048,512]{1,0:T(8,128)(2,1)S(1)} %copy-done.89, ...), custom_call_target="tpu_custom_call" | custom-call | flops 6874999808 | bytes 20625000 | tf_op jit(solution)/shard_map/attend_backward/pallas_call | solution.py:155
  368.6 3.2 back_project.4.refs_4_
  375.8 3.2 back_project.5.refs_5_
  380.3 2.7 collective-permute-start.51
  385.9 4.4 back_project.6
  399.4 4.7 back_project.7
  405.8 5.4 %collective-permute-done.52.refs_3_.refs_7_ = bf16[2,80,483]{2,1,0:T(8,128)(2,1)S(1)} collective-permute-done((bf16[2,80,483]{2,1,0:T(8,128)(2,1)}, bf16[2,80,483]{2,1,0:T(8,128)(2,1)S(1)}, u32[]{:S(2)}, u32[]{:S(2)}) %collective-permute-start.52) | collective-permute-done | bytes 154592 | tf_op jit(solution)/shard_map/ppermute | solution.py:55
  415.1 2.5 copy-done.14
  417.6 4.8 heads_outer.3
  426.6 3.0 norm_back.2
  431.1 3.3 finish_full.1
  437.4 3.9 collective-permute-start.54
  444.0 2.5 collective-permute-done.63.refs_2_
  446.5 24.2 %collective-permute-done.64.refs_3_ = bf16[128,1280]{1,0:T(8,128)(2,1)S(1)} collective-permute-done((bf16[128,1280]{1,0:T(8,128)(2,1)S(1)}, bf16[128,1280]{1,0:T(8,128)(2,1)S(1)}, u32[]{:S(2)}, u32[]{:S(2)}) %collective-permute-start.64) | collective-permute-done | bytes 327712 | tf_op jit(solution)/shard_map/ppermute | solution.py:107
  470.8 6.4 %collective-permute-done.55.refs_1_ = bf16[128,1280]{1,0:T(8,128)(2,1)S(1)} collective-permute-done((bf16[128,1280]{1,0:T(8,128)(2,1)}, bf16[128,1280]{1,0:T(8,128)(2,1)S(1)}, u32[]{:S(2)}, u32[]{:S(2)}) %collective-permute-start.55) | collective-permute-done | bytes 327712 | tf_op jit(solution)/shard_map/ppermute | solution.py:107
  482.5 2.9 collective-permute-start.71
  486.7 2.5 collective-permute-done.71.refs_7_
  491.1 4.0 collective-permute-done.72.refs_8_
  495.1 7.0 %collective-permute-done.73.refs_9_ = bf16[4,80,483]{2,1,0:T(8,128)(2,1)S(1)} collective-permute-done((bf16[4,80,483]{2,1,0:T(8,128)(2,1)}, bf16[4,80,483]{2,1,0:T(8,128)(2,1)S(1)}, u32[]{:S(2)}, u32[]{:S(2)}) %collective-permute-start.73) | collective-permute-done | bytes 309152 | tf_op jit(solution)/shard_map/ppermute | solution.py:55
  502.2 4.1 finish_heads.1
  (453 shorter events, 148.7 us)
Async XLA Ops:
  8.5 27.8 %collective-permute-start.3 = (bf16[128,1280]{1,0:T(8,128)(2,1)S(1)}, bf16[128,1280]{1,0:T(8,128)(2,1)S(1)}, u32[]{:S(2)}, u32[]{:S(2)}) collective-permute-start(bf16[128,1280]{1,0:T(8,128)(2,1)S(1)} %get-tuple-element.113), channel_id=1, source_target_pairs={{0,4},{1,5},{2,6},{3,7},{4,0},{5,1},{6,2},{7,3},{8,12},{9,13},{10,... | collective-permute-start | bytes 983048 | tf_op jit(solution)/shard_map/ppermute | solution.py:55
  9.6 29.2 %collective-permute-start.4 = (bf16[128,1280]{1,0:T(8,128)(2,1)S(1)}, bf16[128,1280]{1,0:T(8,128)(2,1)S(1)}, u32[]{:S(2)}, u32[]{:S(2)}) collective-permute-start(bf16[128,1280]{1,0:T(8,128)(2,1)S(1)} %get-tuple-element.114), channel_id=1, source_target_pairs={{0,6},{1,7},{2,0},{3,1},{4,2},{5,3},{6,4},{7,5},{8,14},{9,15},{10,... | collective-permute-start | bytes 983048 | tf_op jit(solution)/shard_map/ppermute | solution.py:55
  39.8 30.0 %collective-permute-start.11 = (bf16[4,128,1280]{2,1,0:T(8,128)(2,1)S(1)}, bf16[4,128,1280]{2,1,0:T(8,128)(2,1)}, u32[]{:S(2)}, u32[]{:S(2)}) collective-permute-start(bf16[4,128,1280]{2,1,0:T(8,128)(2,1)S(1)} %shuffle.13.refs_3_.refs_0_.refs_2_), channel_id=1, source_target_pairs={{0,1},{1,0},{2,3},{3,2},{4,5},{5,4},{6,7},{7,6},{8,9},{9,8},{10,11... | collective-permute-start | bytes 3932168 | tf_op jit(solution)/shard_map/ppermute | solution.py:55
  41.1 17.1 %collective-permute-start.8 = (bf16[2,80,964]{2,1,0:T(8,128)(2,1)S(1)}, bf16[2,80,964]{2,1,0:T(8,128)(2,1)S(1)}, u32[]{:S(2)}, u32[]{:S(2)}) collective-permute-start(bf16[2,80,964]{2,1,0:T(8,128)(2,1)S(1)} %shuffle.12.refs_4_.refs_0_), channel_id=1, source_target_pairs={{0,2},{1,3},{2,4},{3,5},{4,6},{5,7},{6,0},{7,1},{8,10},{9,11},{10,... | collective-permute-start | bytes 925448 | tf_op jit(solution)/shard_map/ppermute | solution.py:55
  71.3 30.0 %collective-permute-start.13 = (bf16[3,2,80,964]{3,2,1,0:T(8,128)(2,1)S(1)}, bf16[3,2,80,964]{3,2,1,0:T(8,128)(2,1)}, u32[]{:S(2)}, u32[]{:S(2)}) collective-permute-start(bf16[3,2,80,964]{3,2,1,0:T(8,128)(2,1)S(1)} %shuffle.14.refs_2_.refs_0_), channel_id=1, source_target_pairs={{0,16},{1,17},{2,18},{3,19},{4,20},{5,21},{6,22},{7,23},{8,24},{9,... | collective-permute-start | bytes 2776328 | tf_op jit(solution)/shard_map/ppermute | solution.py:55
  72.5 28.7 %collective-permute-start.14 = (bf16[2,80,964]{2,1,0:T(8,128)(2,1)S(1)}, bf16[2,80,964]{2,1,0:T(8,128)(2,1)}, u32[]{:S(2)}, u32[]{:S(2)}) collective-permute-start(bf16[2,80,964]{2,1,0:T(8,128)(2,1)S(1)} %shuffle.15.refs_3_.refs_1_), channel_id=1, source_target_pairs={{0,16},{1,17},{2,18},{3,19},{4,20},{5,21},{6,22},{7,23},{8,24},{9,... | collective-permute-start | bytes 925448 | tf_op jit(solution)/shard_map/ppermute | solution.py:55
  76.5 32.6 %collective-permute-start.15 = (bf16[3,80,640]{2,1,0:T(8,128)(2,1)}, bf16[3,80,640]{2,1,0:T(8,128)(2,1)}, u32[]{:S(2)}, u32[]{:S(2)}) collective-permute-start(bf16[3,80,640]{2,1,0:T(8,128)(2,1)} %quarter.1.refs_1_.refs_0_), channel_id=1, source_target_pairs={{0,2},{1,3},{2,4},{3,5},{4,6},{5,7},{6,0},{7,1},{8,10},{9,11},{10,... | collective-permute-start | bytes 921608 | tf_op jit(solution)/shard_map/ppermute | solution.py:55
  76.6 32.5 %collective-permute-start.16 = (bf16[3,80,640]{2,1,0:T(8,128)(2,1)}, bf16[3,80,640]{2,1,0:T(8,128)(2,1)}, u32[]{:S(2)}, u32[]{:S(2)}) collective-permute-start(bf16[3,80,640]{2,1,0:T(8,128)(2,1)} %quarter.1.refs_1_.refs_0_), channel_id=1, source_target_pairs={{0,4},{1,5},{2,6},{3,7},{4,0},{5,1},{6,2},{7,3},{8,12},{9,13},{10,... | collective-permute-start | bytes 921608 | tf_op jit(solution)/shard_map/ppermute | solution.py:55
  78.0 31.1 %collective-permute-start.17 = (bf16[3,80,640]{2,1,0:T(8,128)(2,1)}, bf16[3,80,640]{2,1,0:T(8,128)(2,1)}, u32[]{:S(2)}, u32[]{:S(2)}) collective-permute-start(bf16[3,80,640]{2,1,0:T(8,128)(2,1)} %quarter.1.refs_1_.refs_0_), channel_id=1, source_target_pairs={{0,6},{1,7},{2,0},{3,1},{4,2},{5,3},{6,4},{7,5},{8,14},{9,15},{10,... | collective-permute-start | bytes 921608 | tf_op jit(solution)/shard_map/ppermute | solution.py:55
  111.9 27.5 %collective-permute-start.28 = (bf16[4,3,80,640]{3,2,1,0:T(8,128)(2,1)}, bf16[4,3,80,640]{3,2,1,0:T(8,128)(2,1)}, u32[]{:S(2)}, u32[]{:S(2)}) collective-permute-start(bf16[4,3,80,640]{3,2,1,0:T(8,128)(2,1)} %shuffle.17.refs_8_.refs_4_), channel_id=1, source_target_pairs={{0,16},{1,17},{2,18},{3,19},{4,20},{5,21},{6,22},{7,23},{8,24},{9,... | collective-permute-start | bytes 3686408 | tf_op jit(solution)/shard_map/ppermute | solution.py:55
  113.2 28.5 %collective-permute-start.19 = (bf16[4,3,80,640]{3,2,1,0:T(8,128)(2,1)}, bf16[4,3,80,640]{3,2,1,0:T(8,128)(2,1)}, u32[]{:S(2)}, u32[]{:S(2)}) collective-permute-start(bf16[4,3,80,640]{3,2,1,0:T(8,128)(2,1)} %shuffle.17.refs_8_.refs_4_), channel_id=1, source_target_pairs={{0,1},{1,0},{2,3},{3,2},{4,5},{5,4},{6,7},{7,6},{8,9},{9,8},{10,11... | collective-permute-start | bytes 3686408 | tf_op jit(solution)/shard_map/ppermute | solution.py:55
  114.8 28.8 %collective-permute-start.20 = (bf16[4,3,80,640]{3,2,1,0:T(8,128)(2,1)}, bf16[4,3,80,640]{3,2,1,0:T(8,128)(2,1)}, u32[]{:S(2)}, u32[]{:S(2)}) collective-permute-start(bf16[4,3,80,640]{3,2,1,0:T(8,128)(2,1)} %shuffle.17.refs_8_.refs_4_), channel_id=1, source_target_pairs={{0,8},{1,9},{2,10},{3,11},{4,12},{5,13},{6,14},{7,15},{8,0},{9,1},... | collective-permute-start | bytes 3686408 | tf_op jit(solution)/shard_map/ppermute | solution.py:55
  116.7 26.8 %collective-permute-start.18 = (bf16[2,128,1280]{2,1,0:T(8,128)(2,1)}, bf16[2,128,1280]{2,1,0:T(8,128)(2,1)}, u32[]{:S(2)}, u32[]{:S(2)}) collective-permute-start(bf16[2,128,1280]{2,1,0:T(8,128)(2,1)} %get-tuple-element.123), channel_id=1, source_target_pairs={{0,8},{1,9},{2,10},{3,11},{4,12},{5,13},{6,14},{7,15},{8,0},{9,1},... | collective-permute-start | bytes 1966088 | tf_op jit(solution)/shard_map/ppermute | solution.py:55
  139.5 39.1 %collective-permute-start.29 = (bf16[4,3,80,640]{3,2,1,0:T(8,128)(2,1)}, bf16[4,3,80,640]{3,2,1,0:T(8,128)(2,1)S(1)}, u32[]{:S(2)}, u32[]{:S(2)}) collective-permute-start(bf16[4,3,80,640]{3,2,1,0:T(8,128)(2,1)} %collective-permute-done.28.refs_7_), channel_id=1, source_target_pairs={{0,8},{1,9},{2,10},{3,11},{4,12},{5,13},{6,14},{7,15},{8,0},{9,1},... | collective-permute-start | bytes 3686408 | tf_op jit(solution)/shard_map/ppermute | solution.py:55
  141.8 37.9 %collective-permute-start.27 = (bf16[4,3,80,640]{3,2,1,0:T(8,128)(2,1)}, bf16[4,3,80,640]{3,2,1,0:T(8,128)(2,1)}, u32[]{:S(2)}, u32[]{:S(2)}) collective-permute-start(bf16[4,3,80,640]{3,2,1,0:T(8,128)(2,1)} %collective-permute-done.19.refs_3_.refs_6_), channel_id=1, source_target_pairs={{0,16},{1,17},{2,18},{3,19},{4,20},{5,21},{6,22},{7,23},{8,24},{9,... | collective-permute-start | bytes 3686408 | tf_op jit(solution)/shard_map/ppermute | solution.py:55
  148.3 30.2 %collective-permute-start.24 = (bf16[128,1280]{1,0:T(8,128)(2,1)S(1)}, bf16[128,1280]{1,0:T(8,128)(2,1)S(1)}, u32[]{:S(2)}, u32[]{:S(2)}) collective-permute-start(bf16[128,1280]{1,0:T(8,128)(2,1)S(1)} %get-tuple-element.126), channel_id=1, source_target_pairs={{0,2},{1,3},{2,4},{3,5},{4,6},{5,7},{6,0},{7,1},{8,10},{9,11},{10,... | collective-permute-start | bytes 983048 | tf_op jit(solution)/shard_map/ppermute | solution.py:55
  148.4 30.2 %collective-permute-start.25 = (bf16[128,1280]{1,0:T(8,128)(2,1)S(1)}, bf16[128,1280]{1,0:T(8,128)(2,1)S(1)}, u32[]{:S(2)}, u32[]{:S(2)}) collective-permute-start(bf16[128,1280]{1,0:T(8,128)(2,1)S(1)} %get-tuple-element.127), channel_id=1, source_target_pairs={{0,4},{1,5},{2,6},{3,7},{4,0},{5,1},{6,2},{7,3},{8,12},{9,13},{10,... | collective-permute-start | bytes 983048 | tf_op jit(solution)/shard_map/ppermute | solution.py:55
  149.1 29.5 %collective-permute-start.26 = (bf16[128,1280]{1,0:T(8,128)(2,1)S(1)}, bf16[128,1280]{1,0:T(8,128)(2,1)S(1)}, u32[]{:S(2)}, u32[]{:S(2)}) collective-permute-start(bf16[128,1280]{1,0:T(8,128)(2,1)S(1)} %get-tuple-element.128), channel_id=1, source_target_pairs={{0,6},{1,7},{2,0},{3,1},{4,2},{5,3},{6,4},{7,5},{8,14},{9,15},{10,... | collective-permute-start | bytes 983048 | tf_op jit(solution)/shard_map/ppermute | solution.py:55
  182.0 22.6 %collective-permute-start.31 = (bf16[4,3,80,640]{3,2,1,0:T(8,128)(2,1)}, bf16[4,3,80,640]{3,2,1,0:T(8,128)(2,1)}, u32[]{:S(2)}, u32[]{:S(2)}) collective-permute-start(bf16[4,3,80,640]{3,2,1,0:T(8,128)(2,1)} %collective-permute-done.27.refs_5_.refs_8_), channel_id=1, source_target_pairs={{0,8},{1,9},{2,10},{3,11},{4,12},{5,13},{6,14},{7,15},{8,0},{9,1},... | collective-permute-start | bytes 3686408 | tf_op jit(solution)/shard_map/ppermute | solution.py:55
  183.4 21.2 %collective-permute-start.30 = (bf16[4,3,80,640]{3,2,1,0:T(8,128)(2,1)}, bf16[4,3,80,640]{3,2,1,0:T(8,128)(2,1)}, u32[]{:S(2)}, u32[]{:S(2)}) collective-permute-start(bf16[4,3,80,640]{3,2,1,0:T(8,128)(2,1)} %collective-permute-done.19.refs_3_.refs_6_), channel_id=1, source_target_pairs={{0,8},{1,9},{2,10},{3,11},{4,12},{5,13},{6,14},{7,15},{8,0},{9,1},... | collective-permute-start | bytes 3686408 | tf_op jit(solution)/shard_map/ppermute | solution.py:55
  186.3 18.3 %collective-permute-start.23 = (bf16[512,320]{1,0:T(8,128)(2,1)}, bf16[512,320]{1,0:T(8,128)(2,1)}, u32[]{:S(2)}, u32[]{:S(2)}) collective-permute-start(bf16[512,320]{1,0:T(8,128)(2,1)} %bitcast.67), channel_id=1, source_target_pairs={{0,9},{1,8},{2,11},{3,10},{4,13},{5,12},{6,15},{7,14},{8,1},{9,0},... | collective-permute-start | bytes 983048 | tf_op jit(solution)/shard_map/ppermute | solution.py:55
  237.8 20.0 %collective-permute-start.32 = (bf16[3,1280,640]{2,1,0:T(8,128)(2,1)}, bf16[3,1280,640]{2,1,0:T(8,128)(2,1)}, u32[]{:S(2)}, u32[]{:S(2)}) collective-permute-start(bf16[3,1280,640]{2,1,0:T(8,128)(2,1)} %outer_give.1.refs_7_), channel_id=1, source_target_pairs={{0,8},{1,9},{2,10},{3,11},{4,12},{5,13},{6,14},{7,15},{8,0},{9,1},... | collective-permute-start | bytes 14745608 | tf_op jit(solution)/shard_map/ppermute | solution.py:55
  239.6 18.2 %collective-permute-start.35 = (bf16[512,320]{1,0:T(8,128)(2,1)S(1)}, bf16[512,320]{1,0:T(8,128)(2,1)S(1)}, u32[]{:S(2)}, u32[]{:S(2)}) collective-permute-start(bf16[512,320]{1,0:T(8,128)(2,1)S(1)} %get-tuple-element.141), channel_id=1, source_target_pairs={{0,9},{1,8},{2,11},{3,10},{4,13},{5,12},{6,15},{7,14},{8,1},{9,0},... | collective-permute-start | bytes 983048 | tf_op jit(solution)/shard_map/ppermute | solution.py:55
  268.5 38.8 %collective-permute-start.39 = (bf16[3,2,2,80,640]{4,3,2,1,0:T(8,128)(2,1)}, bf16[3,2,2,80,640]{4,3,2,1,0:T(8,128)(2,1)S(1)}, u32[]{:S(2)}, u32[]{:S(2)}) collective-permute-start(bf16[3,2,2,80,640]{4,3,2,1,0:T(8,128)(2,1)} %get-tuple-element.147), channel_id=1, source_target_pairs={{0,16},{1,17},{2,18},{3,19},{4,20},{5,21},{6,22},{7,23},{8,24},{9,... | collective-permute-start | bytes 3686408 | tf_op jit(solution)/shard_map/ppermute | solution.py:55
  269.7 37.6 %collective-permute-start.40 = (bf16[3,2,2,80,640]{4,3,2,1,0:T(8,128)(2,1)}, bf16[3,2,2,80,640]{4,3,2,1,0:T(8,128)(2,1)S(1)}, u32[]{:S(2)}, u32[]{:S(2)}) collective-permute-start(bf16[3,2,2,80,640]{4,3,2,1,0:T(8,128)(2,1)} %get-tuple-element.149), channel_id=1, source_target_pairs={{0,1},{1,0},{2,3},{3,2},{4,5},{5,4},{6,7},{7,6},{8,9},{9,8},{10,11... | collective-permute-start | bytes 3686408 | tf_op jit(solution)/shard_map/ppermute | solution.py:55
  273.3 36.9 %collective-permute-start.36 = (bf16[128,1280]{1,0:T(8,128)(2,1)S(1)}, bf16[128,1280]{1,0:T(8,128)(2,1)S(1)}, u32[]{:S(2)}, u32[]{:S(2)}) collective-permute-start(bf16[128,1280]{1,0:T(8,128)(2,1)S(1)} %get-tuple-element.144), channel_id=1, source_target_pairs={{0,2},{1,3},{2,4},{3,5},{4,6},{5,7},{6,0},{7,1},{8,10},{9,11},{10,... | collective-permute-start | bytes 983048 | tf_op jit(solution)/shard_map/ppermute | solution.py:55
  273.7 36.5 %collective-permute-start.37 = (bf16[128,1280]{1,0:T(8,128)(2,1)S(1)}, bf16[128,1280]{1,0:T(8,128)(2,1)S(1)}, u32[]{:S(2)}, u32[]{:S(2)}) collective-permute-start(bf16[128,1280]{1,0:T(8,128)(2,1)S(1)} %get-tuple-element.145), channel_id=1, source_target_pairs={{0,4},{1,5},{2,6},{3,7},{4,0},{5,1},{6,2},{7,3},{8,12},{9,13},{10,... | collective-permute-start | bytes 983048 | tf_op jit(solution)/shard_map/ppermute | solution.py:55
  276.8 33.5 %collective-permute-start.38 = (bf16[128,1280]{1,0:T(8,128)(2,1)S(1)}, bf16[128,1280]{1,0:T(8,128)(2,1)S(1)}, u32[]{:S(2)}, u32[]{:S(2)}) collective-permute-start(bf16[128,1280]{1,0:T(8,128)(2,1)S(1)} %get-tuple-element.146), channel_id=1, source_target_pairs={{0,6},{1,7},{2,0},{3,1},{4,2},{5,3},{6,4},{7,5},{8,14},{9,15},{10,... | collective-permute-start | bytes 983048 | tf_op jit(solution)/shard_map/ppermute | solution.py:55
  312.7 16.4 %collective-permute-start.41 = (bf16[2,128,1280]{2,1,0:T(8,128)(2,1)}, bf16[2,128,1280]{2,1,0:T(8,128)(2,1)}, u32[]{:S(2)}, u32[]{:S(2)}) collective-permute-start(bf16[2,128,1280]{2,1,0:T(8,128)(2,1)} %get-tuple-element.154), channel_id=1, source_target_pairs={{0,8},{1,9},{2,10},{3,11},{4,12},{5,13},{6,14},{7,15},{8,0},{9,1},... | collective-permute-start | bytes 1966088 | tf_op jit(solution)/shard_map/ppermute | solution.py:55
  313.9 18.2 %collective-permute-start.42 = (bf16[3,2,80,640]{3,2,1,0:T(8,128)(2,1)}, bf16[3,2,80,640]{3,2,1,0:T(8,128)(2,1)}, u32[]{:S(2)}, u32[]{:S(2)}) collective-permute-start(bf16[3,2,80,640]{3,2,1,0:T(8,128)(2,1)} %get-tuple-element.159), channel_id=1, source_target_pairs={{0,1},{1,0},{2,3},{3,2},{4,5},{5,4},{6,7},{7,6},{8,9},{9,8},{10,11... | collective-permute-start | bytes 1843208 | tf_op jit(solution)/shard_map/ppermute | solution.py:55
  314.2 17.9 %collective-permute-start.43 = (bf16[3,2,80,640]{3,2,1,0:T(8,128)(2,1)}, bf16[3,2,80,640]{3,2,1,0:T(8,128)(2,1)}, u32[]{:S(2)}, u32[]{:S(2)}) collective-permute-start(bf16[3,2,80,640]{3,2,1,0:T(8,128)(2,1)} %get-tuple-element.161), channel_id=1, source_target_pairs={{0,16},{1,17},{2,18},{3,19},{4,20},{5,21},{6,22},{7,23},{8,24},{9,... | collective-permute-start | bytes 1843208 | tf_op jit(solution)/shard_map/ppermute | solution.py:55
  327.9 38.6 %collective-permute-start.44 = (bf16[4,2,80,483]{3,2,1,0:T(8,128)(2,1)}, bf16[4,2,80,483]{3,2,1,0:T(8,128)(2,1)S(1)}, u32[]{:S(2)}, u32[]{:S(2)}) collective-permute-start(bf16[4,2,80,483]{3,2,1,0:T(8,128)(2,1)} %get-tuple-element.165), channel_id=1, source_target_pairs={{0,16},{1,17},{2,18},{3,19},{4,20},{5,21},{6,22},{7,23},{8,24},{9,... | collective-permute-start | bytes 1854728 | tf_op jit(solution)/shard_map/ppermute | solution.py:55
  336.0 28.4 %collective-permute-start.45 = (bf16[3,80,640]{2,1,0:T(8,128)(2,1)S(1)}, bf16[3,80,640]{2,1,0:T(8,128)(2,1)S(1)}, u32[]{:S(2)}, u32[]{:S(2)}) collective-permute-start(bf16[3,80,640]{2,1,0:T(8,128)(2,1)S(1)} %get-tuple-element.166), channel_id=1, source_target_pairs={{0,2},{1,3},{2,4},{3,5},{4,6},{5,7},{6,0},{7,1},{8,10},{9,11},{10,... | collective-permute-start | bytes 921608 | tf_op jit(solution)/shard_map/ppermute | solution.py:55
  337.6 26.8 %collective-permute-start.46 = (bf16[3,80,640]{2,1,0:T(8,128)(2,1)S(1)}, bf16[3,80,640]{2,1,0:T(8,128)(2,1)S(1)}, u32[]{:S(2)}, u32[]{:S(2)}) collective-permute-start(bf16[3,80,640]{2,1,0:T(8,128)(2,1)S(1)} %get-tuple-element.167), channel_id=1, source_target_pairs={{0,4},{1,5},{2,6},{3,7},{4,0},{5,1},{6,2},{7,3},{8,12},{9,13},{10,... | collective-permute-start | bytes 921608 | tf_op jit(solution)/shard_map/ppermute | solution.py:55
  339.2 26.5 %collective-permute-start.47 = (bf16[3,80,640]{2,1,0:T(8,128)(2,1)S(1)}, bf16[3,80,640]{2,1,0:T(8,128)(2,1)S(1)}, u32[]{:S(2)}, u32[]{:S(2)}) collective-permute-start(bf16[3,80,640]{2,1,0:T(8,128)(2,1)S(1)} %get-tuple-element.168), channel_id=1, source_target_pairs={{0,6},{1,7},{2,0},{3,1},{4,2},{5,3},{6,4},{7,5},{8,14},{9,15},{10,... | collective-permute-start | bytes 921608 | tf_op jit(solution)/shard_map/ppermute | solution.py:55
  379.5 25.7 %collective-permute-start.57 = (bf16[3,80,640]{2,1,0:T(8,128)(2,1)}, bf16[3,80,640]{2,1,0:T(8,128)(2,1)}, u32[]{:S(2)}, u32[]{:S(2)}) collective-permute-start(bf16[3,80,640]{2,1,0:T(8,128)(2,1)} %copy-done.51), channel_id=1, source_target_pairs={{0,16},{1,17},{2,18},{3,19},{4,20},{5,21},{6,22},{7,23},{8,24},{9,... | collective-permute-start | bytes 921608 | tf_op jit(solution)/shard_map/ppermute | solution.py:55
  379.8 25.4 %collective-permute-start.50 = (bf16[2,80,483]{2,1,0:T(8,128)(2,1)}, bf16[2,80,483]{2,1,0:T(8,128)(2,1)}, u32[]{:S(2)}, u32[]{:S(2)}) collective-permute-start(bf16[2,80,483]{2,1,0:T(8,128)(2,1)} %copy-done.86), channel_id=1, source_target_pairs={{0,2},{1,3},{2,4},{3,5},{4,6},{5,7},{6,0},{7,1},{8,10},{9,11},{10,... | collective-permute-start | bytes 463688 | tf_op jit(solution)/shard_map/ppermute | solution.py:55
  380.3 24.9 %collective-permute-start.51 = (bf16[2,80,483]{2,1,0:T(8,128)(2,1)}, bf16[2,80,483]{2,1,0:T(8,128)(2,1)}, u32[]{:S(2)}, u32[]{:S(2)}) collective-permute-start(bf16[2,80,483]{2,1,0:T(8,128)(2,1)} %copy-done.85), channel_id=1, source_target_pairs={{0,4},{1,5},{2,6},{3,7},{4,0},{5,1},{6,2},{7,3},{8,12},{9,13},{10,... | collective-permute-start | bytes 463688 | tf_op jit(solution)/shard_map/ppermute | solution.py:55
  391.4 33.7 %collective-permute-start.49 = (bf16[2,128,1280]{2,1,0:T(8,128)(2,1)}, bf16[2,128,1280]{2,1,0:T(8,128)(2,1)}, u32[]{:S(2)}, u32[]{:S(2)}) collective-permute-start(bf16[2,128,1280]{2,1,0:T(8,128)(2,1)} %get-tuple-element.171), channel_id=1, source_target_pairs={{0,1},{1,0},{2,3},{3,2},{4,5},{5,4},{6,7},{7,6},{8,9},{9,8},{10,11... | collective-permute-start | bytes 1966088 | tf_op jit(solution)/shard_map/ppermute | solution.py:55
  393.5 30.2 %collective-permute-start.58 = (bf16[3,80,640]{2,1,0:T(8,128)(2,1)}, bf16[3,80,640]{2,1,0:T(8,128)(2,1)}, u32[]{:S(2)}, u32[]{:S(2)}) collective-permute-start(bf16[3,80,640]{2,1,0:T(8,128)(2,1)} %copy-done.51), channel_id=1, source_target_pairs={{0,8},{1,9},{2,10},{3,11},{4,12},{5,13},{6,14},{7,15},{8,0},{9,1},... | collective-permute-start | bytes 921608 | tf_op jit(solution)/shard_map/ppermute | solution.py:55
  405.2 19.6 %collective-permute-start.59 = (bf16[3,80,640]{2,1,0:T(8,128)(2,1)}, bf16[3,80,640]{2,1,0:T(8,128)(2,1)}, u32[]{:S(2)}, u32[]{:S(2)}) collective-permute-start(bf16[3,80,640]{2,1,0:T(8,128)(2,1)} %collective-permute-done.57.refs_1_), channel_id=1, source_target_pairs={{0,8},{1,9},{2,10},{3,11},{4,12},{5,13},{6,14},{7,15},{8,0},{9,1},... | collective-permute-start | bytes 921608 | tf_op jit(solution)/shard_map/ppermute | solution.py:55
  405.3 29.1 %collective-permute-start.56 = (bf16[2,128,1280]{2,1,0:T(8,128)(2,1)}, bf16[2,128,1280]{2,1,0:T(8,128)(2,1)S(1)}, u32[]{:S(2)}, u32[]{:S(2)}) collective-permute-start(bf16[2,128,1280]{2,1,0:T(8,128)(2,1)} %get-tuple-element.183), channel_id=1, source_target_pairs={{0,1},{1,0},{2,3},{3,2},{4,5},{5,4},{6,7},{7,6},{8,9},{9,8},{10,11... | collective-permute-start | bytes 1966088 | tf_op jit(solution)/shard_map/ppermute | solution.py:55
  422.4 20.9 %collective-permute-start.65 = (bf16[4,2,80,483]{3,2,1,0:T(8,128)(2,1)S(1)}, bf16[4,2,80,483]{3,2,1,0:T(8,128)(2,1)S(1)}, u32[]{:S(2)}, u32[]{:S(2)}) collective-permute-start(bf16[4,2,80,483]{3,2,1,0:T(8,128)(2,1)S(1)} %get-tuple-element.188), channel_id=1, source_target_pairs={{0,16},{1,17},{2,18},{3,19},{4,20},{5,21},{6,22},{7,23},{8,24},{9,... | collective-permute-start | bytes 1854728 | tf_op jit(solution)/shard_map/ppermute | solution.py:55
  436.7 34.0 %collective-permute-start.64 = (bf16[128,1280]{1,0:T(8,128)(2,1)S(1)}, bf16[128,1280]{1,0:T(8,128)(2,1)S(1)}, u32[]{:S(2)}, u32[]{:S(2)}) collective-permute-start(bf16[128,1280]{1,0:T(8,128)(2,1)S(1)} %get-tuple-element.187), channel_id=1, source_target_pairs={{10,0},{11,1},{8,2},{9,3},{2,4},{3,5},{0,6},{1,7},{14,8},{15,9},{1... | collective-permute-start | bytes 983048 | tf_op jit(solution)/shard_map/ppermute | solution.py:107
  437.4 33.5 %collective-permute-start.54 = (bf16[128,1280]{1,0:T(8,128)(2,1)}, bf16[128,1280]{1,0:T(8,128)(2,1)S(1)}, u32[]{:S(2)}, u32[]{:S(2)}) collective-permute-start(bf16[128,1280]{1,0:T(8,128)(2,1)} %get-tuple-element.181.refs_6_), channel_id=1, source_target_pairs={{0,0},{1,1},{2,2},{3,3},{8,4},{9,5},{10,6},{11,7},{4,8},{5,9},{6,1... | collective-permute-start | bytes 983048 | tf_op jit(solution)/shard_map/ppermute | solution.py:107
  441.3 36.0 %collective-permute-start.55 = (bf16[128,1280]{1,0:T(8,128)(2,1)}, bf16[128,1280]{1,0:T(8,128)(2,1)S(1)}, u32[]{:S(2)}, u32[]{:S(2)}) collective-permute-start(bf16[128,1280]{1,0:T(8,128)(2,1)} %get-tuple-element.182), channel_id=1, source_target_pairs={{2,0},{3,1},{0,2},{1,3},{10,4},{11,5},{8,6},{9,7},{6,8},{7,9},{4,1... | collective-permute-start | bytes 983048 | tf_op jit(solution)/shard_map/ppermute | solution.py:107
  443.9 34.9 %collective-permute-start.66 = (bf16[2,80,483]{2,1,0:T(8,128)(2,1)S(1)}, bf16[2,80,483]{2,1,0:T(8,128)(2,1)S(1)}, u32[]{:S(2)}, u32[]{:S(2)}) collective-permute-start(bf16[2,80,483]{2,1,0:T(8,128)(2,1)S(1)} %get-tuple-element.190), channel_id=1, source_target_pairs={{0,2},{1,3},{2,4},{3,5},{4,6},{5,7},{6,0},{7,1},{8,10},{9,11},{10,... | collective-permute-start | bytes 463688 | tf_op jit(solution)/shard_map/ppermute | solution.py:55
  446.5 33.5 %collective-permute-start.67 = (bf16[2,80,483]{2,1,0:T(8,128)(2,1)S(1)}, bf16[2,80,483]{2,1,0:T(8,128)(2,1)S(1)}, u32[]{:S(2)}, u32[]{:S(2)}) collective-permute-start(bf16[2,80,483]{2,1,0:T(8,128)(2,1)S(1)} %get-tuple-element.191), channel_id=1, source_target_pairs={{0,4},{1,5},{2,6},{3,7},{4,0},{5,1},{6,2},{7,3},{8,12},{9,13},{10,... | collective-permute-start | bytes 463688 | tf_op jit(solution)/shard_map/ppermute | solution.py:55
  (128 other events, 871.1 us)

commit v3 on v2

--- a/solution.py
+++ b/solution.py
@@ -71,7 +71,7 @@
     def source(self, db, dc):
         return ((self.b - db) % self.b_size) * CORES + (self.c + dc) % CORES
 
-    def to_cluster(self, tokens):
+    def to_cluster(self, tokens, after=()):
         seqs, count, width = tokens.shape
         half = count // CORES
         halves = tokens.reshape(seqs, CORES, half, width)
@@ -79,7 +79,7 @@
         moves = []
         for i in range(seqs):
             moves += [(0, (i, self.c), 0, i), (0, (i, 1 - self.c), 1, i)]
-        own, give = shuffle([halves], [(shape, BF16)] * 2, moves)
+        own, give = shuffle([halves], [(shape, BF16)] * 2, moves, after)
         got = self.send(give, dc=1)
         after = yield
         parts = route_parts(self, own, got, after or ())
@@ -129,9 +129,21 @@
 
 LAST = []
 SCALE = 0.25
+SIZE = {
+    "project": 28,
+    "attend_forward": 24,
+    "middle": 48,
+    "outer": 60,
+    "outer_give": 60,
+    "attend_backward": 24,
+    "heads_outer": 24,
+    "back_project": 20,
+    "finish_heads": 16,
+    "finish_full": 16,
+}
 COST = {
     "project": 14.5,
-    "attend_forward": 26.0,
+    "attend_forward": 12.0,
     "middle": 20.0,
     "outer": 7.0,
     "outer_give": 0.1,
@@ -145,7 +157,7 @@
 }
 
 
-def call(name, body, scalars, inputs, outputs, grid=(1,), scratch=(), after=(), vmem=40):
+def call(name, body, scalars, inputs, outputs, grid=(1,), scratch=(), after=(), vmem=0):
     deps = [*LAST[-1:], *after]
     count, skip = len(inputs), len(deps)
 
@@ -167,7 +179,7 @@
             bytes_accessed=int(COST.get(name, 1.5) * SCALE * 3.3e6),
             transcendentals=0,
         ),
-        compiler_params=pltpu.CompilerParams(vmem_limit_bytes=vmem * 1024 * 1024),
+        compiler_params=pltpu.CompilerParams(vmem_limit_bytes=(vmem or SIZE.get(name, 12)) * 1024 * 1024),
         name=name,
     )(scalars_of(scalars), *[value for value, _ in inputs], *deps)
     LAST.append(results[0])
@@ -275,7 +287,7 @@
         n += count
 
 
-def add_blocks(groups):
+def add_blocks(groups, after=()):
     spots, inputs, outputs = [], [], []
     for terms in groups:
         for value, dim, index in terms:
@@ -294,6 +306,7 @@
         spots,
         inputs,
         outputs,
+        after=after,
     )
 
 
@@ -303,20 +316,6 @@
 
 def pick(stacked, index, axis=0):
     return lax.dynamic_index_in_dim(stacked, index, axis, keepdims=False)
-
-
-def ring_gather(at, piece):
-    up = at.send(piece, da=-1)
-    down = at.send(piece, da=1)
-    cut = max(1, piece.shape[0] // 2)
-    far = [at.send(up[:cut], da=-1), at.send(down[cut:], da=1)]
-    yield
-    shape = (3, *piece.shape)
-    yield shuffle([piece, up, down], [(shape, BF16)], [(k, None, 0, k) for k in range(3)])[0]
-    moves = []
-    for k in range(piece.shape[0]):
-        moves.append((0, k, 0, k) if k < cut else (1, k - cut, 0, k))
-    yield shuffle(far, [(piece.shape, BF16)], moves)[0]
 
 
 def by_order(own, others, axis_size, spot):
@@ -381,19 +380,20 @@
     )[0]
 
 
-def pad_body(heads, groups, x_split, info, *refs):
-    sources, outs = refs[: 2 * x_split], refs[2 * x_split :]
+def pad_body(heads, groups, a_size, info, *refs):
+    split = (len(refs) - groups - 2) // a_size
+    sources, outs = refs[: split * a_size], refs[split * a_size :]
     compact, (padded, vectors) = outs[:groups], outs[groups:]
-    b_size, rows, width = sources[1].shape
+    b_size, rows, width = sources[0].shape
     used = 3 * heads * HEAD_DIM
     part = heads // groups
     padded[...] = jnp.zeros_like(padded)
-    for n in range(x_split):
-        for a in range(4):
+    for n in range(split):
+        for d in range(a_size):
             for b in range(b_size):
-                piece = sources[2 * n][a, b] if a < 3 else sources[2 * n + 1][b]
-                spot = (info[1 + a] * b_size + b) * x_split
-                spot = (spot + (info[0] ^ n if x_split == 2 else 0)) * rows
+                piece = sources[n * a_size + d][b]
+                spot = (info[1 + d] * b_size + b) * split
+                spot = (spot + (info[0] ^ n if split == 2 else 0)) * rows
                 spot = pl.ds(pl.multiple_of(spot, rows), rows)
                 for g in range(groups):
                     step = used // groups
@@ -407,13 +407,13 @@
 
 
 def pad_weights(at, sources, heads, groups, after):
-    b_size, rows, width = sources[1].shape
-    total = at.a_size * b_size * rows * at.x_split
+    b_size, rows, width = sources[0].shape
+    total = len(sources) * b_size * rows
     used = 3 * heads * HEAD_DIM
     return call(
         "pad_weights",
-        functools.partial(pad_body, heads, groups, at.x_split),
-        [at.x, at.a, (at.a + 1) % 4, (at.a + 3) % 4, (at.a + 2) % 4],
+        functools.partial(pad_body, heads, groups, at.a_size),
+        [at.x, *[(at.a - d) % at.a_size for d in range(at.a_size)]],
         [(source, VMEM) for source in sources],
         [
             *[((total, used // groups), BF16, VMEM)] * groups,
@@ -421,6 +421,7 @@
             ((total, width - used), BF16, VMEM),
         ],
         after=after,
+        vmem=16,
     )
 
 
@@ -484,16 +485,22 @@
         spot = pl.multiple_of(j * block, block)
         columns = spot + lax.broadcasted_iota(jnp.int32, (block, block), 1)
         bias = jnp.where((columns >= begin) & (columns <= rows), 0.0, MASK_FILL)
+        lanes = [slice(h * LANES, (h + 1) * LANES) for h in range(heads)]
+        scores = [dot(query[:, l], key[pl.ds(spot, block), l], 1, 1) + bias for l in lanes]
+        olds = [top[h] for h in range(heads)]
+        news = [
+            jnp.maximum(old, jnp.max(score, axis=1, keepdims=True))
+            for old, score in zip(olds, scores)
+        ]
+        weights = [
+            jnp.exp(score - jnp.concatenate([new] * (block // LANES), axis=1)).astype(BF16)
+            for score, new in zip(scores, news)
+        ]
         for h in range(heads):
-            lanes = slice(h * LANES, (h + 1) * LANES)
-            score = dot(query[:, lanes], key[pl.ds(spot, block), lanes], 1, 1) + bias
-            old = top[h]
-            new = jnp.maximum(old, jnp.max(score, axis=1, keepdims=True))
-            weight = jnp.exp(score - jnp.concatenate([new] * (block // LANES), axis=1))
-            total[h] = total[h] * jnp.exp(old - new) + dot(
-                weight.astype(BF16), value[pl.ds(spot, block), lanes]
+            total[h] = total[h] * jnp.exp(olds[h] - news[h]) + dot(
+                weights[h], value[pl.ds(spot, block), lanes[h]]
             )
-            top[h] = new
+            top[h] = news[h]
         return carry
 
     lax.fori_loop(info[index], index + 1, step, 0)
@@ -607,17 +614,20 @@
         spot = pl.multiple_of(j * block, block)
         rows = spot + lax.broadcasted_iota(jnp.int32, (block, block), 0)
         allowed = (rows >= begin) & (rows <= columns)
-        for h in range(heads):
-            lanes = slice(h * LANES, (h + 1) * LANES)
-            key_h = key[pl.ds(spot, block), lanes]
-            query_h = query[:, lanes]
-            grad_h = grad_aug[:, lanes]
-            prob = jnp.where(allowed, jnp.exp(dot(key_h, query_h, 1, 1)), 0.0)
-            d_prob = dot(value[pl.ds(spot, block), lanes], grad_h, 1, 1)
-            d_score = (prob * d_prob).astype(BF16)
-            d_value[pl.ds(spot, block), lanes] += dot(prob.astype(BF16), grad_h)
-            d_key[pl.ds(spot, block), lanes] += dot(d_score, query_h)
-            d_query[:, lanes] += dot(d_score, key_h, 0, 0)
+        lanes = [slice(h * LANES, (h + 1) * LANES) for h in range(heads)]
+        keys = [key[pl.ds(spot, block), l] for l in lanes]
+        queries = [query[:, l] for l in lanes]
+        grads_of = [grad_aug[:, l] for l in lanes]
+        scores = [dot(k, q, 1, 1) for k, q in zip(keys, queries)]
+        d_probs = [
+            dot(value[pl.ds(spot, block), l], g, 1, 1) for l, g in zip(lanes, grads_of)
+        ]
+        probs = [jnp.where(allowed, jnp.exp(score), 0.0) for score in scores]
+        d_scores = [(prob * d_prob).astype(BF16) for prob, d_prob in zip(probs, d_probs)]
+        for h, l in enumerate(lanes):
+            d_value[pl.ds(spot, block), l] += dot(probs[h].astype(BF16), grads_of[h])
+            d_key[pl.ds(spot, block), l] += dot(d_scores[h], queries[h])
+            d_query[:, l] += dot(d_scores[h], keys[h], 0, 0)
         return carry
 
     lax.fori_loop(info[index], index + 1, step, 0)
@@ -859,7 +869,6 @@
         grid=(3,),
         scratch=scratch,
         after=after,
-        vmem=60,
     )
 
 
@@ -1002,10 +1011,18 @@
     return [(spot + d) % size for d in range(size)]
 
 
-def cat_body(info, first, first_got, second, second_got, out):
+def cat_body(info, first, first_got, second, second_got, *outs):
     pair = first.shape[1]
-    out[:, :pair] = (first[...].astype(F32) + first_got[...].astype(F32)).astype(BF16)
-    out[:, pair:] = (second[...].astype(F32) + second_got[...].astype(F32)).astype(BF16)
+    for d, out in enumerate(outs):
+        spot = info[d] % pair
+
+        @pl.when(info[d] < pair)
+        def low():
+            out[...] = (first[:, spot].astype(F32) + first_got[:, spot].astype(F32)).astype(BF16)
+
+        @pl.when(info[d] >= pair)
+        def high():
+            out[...] = (second[:, spot].astype(F32) + second_got[:, spot].astype(F32)).astype(BF16)
 
 
 class FullReduce:
@@ -1030,19 +1047,17 @@
 
     def over_a(self):
         at = self.at
-        part = None
         if at.even:
             shape = self.first[0].shape
-            part = call(
+            parts = call(
                 "cat",
                 cat_body,
-                [0],
+                ahead(at.a, at.a_size),
                 [(t, VMEM) for t in (*self.first, *self.second)],
-                [((3, at.a_size, *shape[2:]), BF16, VMEM)],
-            )[0]
+                [((3, *shape[2:]), BF16, VMEM)] * at.a_size,
+            )
         else:
-            part = self.part
-        parts = add_blocks([[(part, 1, a)] for a in ahead(at.a, at.a_size)])
+            parts = add_blocks([[(self.part, 1, a)] for a in ahead(at.a, at.a_size)])
         self.got = [parts[0]] + [at.send(parts[d], da=d) for d in range(1, at.a_size)]
 
     def end(self):
@@ -1071,18 +1086,34 @@
         self.got = [parts[0]] + [at.send(parts[d], da=d) for d in range(1, at.a_size)]
         return parts
 
-    def to_peers(self):
+    def by_b(self, after=()):
         at = self.at
         if at.x_split == 1:
             total = add_blocks([[(t[None], 0, 0) for t in self.got]])[0]
             self.got = [all_sum(at, total, "dx", at.x_size)]
-        parts = add_blocks([[(t, 0, b) for t in self.got] for b in ahead(at.b, at.b_size)])
-        parts = [
-            at.send(parts[db], db=db, dc=dc) if db or dc else parts[0] for db, dc in at.peers()
-        ]
-        if at.x_split == 1:
-            return [parts]
-        return [parts, at.send(jnp.stack(parts), dx=1)]
+        groups = [[(t, 0, b) for t in self.got] for b in ahead(at.b, at.b_size)]
+        return add_blocks(groups, after)
+
+
+def side_body(groups, info, *refs):
+    for n, out in enumerate(refs[-(len(refs) // (groups + 1)) :]):
+        for g in range(groups):
+            out[g] = refs[n * groups + g][...]
+
+
+def to_peers(at, groups):
+    shape = (len(groups), *groups[0][0].shape)
+    parts = call(
+        "side",
+        functools.partial(side_body, len(groups)),
+        [0],
+        [(group[b], VMEM) for b in range(at.b_size) for group in groups],
+        [(shape, BF16, VMEM)] * at.b_size,
+    )
+    parts = [at.send(parts[db], db=db, dc=dc) if db or dc else parts[0] for db, dc in at.peers()]
+    if at.x_split == 1:
+        return [parts]
+    return [parts, at.send(jnp.stack(parts), dx=1)]
 
 
 def in_order(info, refs, split, half, core, spot):
@@ -1119,19 +1150,19 @@
     )
 
 
-def finish_heads_body(count, groups, split, info, *refs):
-    parts, refs = refs[: groups * count], refs[groups * count :]
-    far, refs = refs[: groups * (split - 1)], refs[groups * (split - 1) :]
+def finish_heads_body(count, split, info, *refs):
+    parts, refs = refs[:count], refs[count:]
+    far, refs = refs[: split - 1], refs[split - 1 :]
     weights, gain, outs = refs[:3], refs[3], refs[4:]
     few = outs[4].shape[1]
-    rows, width = parts[0].shape
+    groups, rows, width = parts[0].shape
     width = (width - few) // 3
     for n in range(split):
         down = pl.ds(pl.multiple_of((info[count] ^ n if split == 2 else 0) * rows, rows), rows)
         total = jnp.zeros((rows, few), F32)
         for p in range(count):
             for g in range(groups):
-                source = far[g].at[p] if n else parts[g * count + p]
+                source = far[0].at[p, g] if n else parts[p].at[g]
                 total = total + source[:, 3 * width :].astype(F32)
                 for peer in range(count):
 
@@ -1151,11 +1182,10 @@
 
 def finish_heads(at, parts, weights, gain, few):
     rows, model = weights[0].shape
-    flat = [part for group in parts for part in group[0]]
-    flat += [group[1] for group in parts if at.x_split == 2]
+    flat = [*parts[0], *parts[1:]]
     return call(
         "finish_heads",
-        functools.partial(finish_heads_body, at.peer_count, len(parts), at.x_split),
+        functools.partial(finish_heads_body, at.peer_count, at.x_split),
         [*[at.source(db, dc) for db, dc in at.peers()], at.x],
         [(p, VMEM) for p in flat] + [(w, VMEM) for w in weights] + [(gain[:, None], VMEM)],
         [((rows, model), F32, VMEM)] * 3 + [((rows, 1), F32, VMEM), ((rows, few), F32, VMEM)],
@@ -1202,35 +1232,23 @@
     sent = [at.send(part, db=db + 1) for db, part in enumerate(sent)]
     next(stage)
     near = by_order(own, sent, at.b_size, at.b)
-    ring = ring_gather(at, near)
-    next(ring)
+    sources = [near] + [at.send(near, da=d) for d in range(1, at.a_size)]
+    if at.x_split == 2:
+        sources += [at.send(source, dx=1) for source in sources]
     chunks = next(stage)
-    nears = [at.send(chunks, db=db) if db else chunks for db in range(at.b_size)]
-    most = next(ring)
-    sources = [most, None]
+    parts = []
+    early = sources[1 : at.a_size]
     if at.x_split == 2:
-        sources += [at.send(most, dx=1), None]
-    far = next(ring)
-    parts = []
-    for near in nears:
-        parts += [near, at.send(later(near, far), dc=1)]
-    sources[1] = far
-    if at.x_split == 2:
-        sources[3] = at.send(far, dx=1)
-    quarter = quarter_of(at, (out_weight, up_weight, down_weight), parts[1:])
-    stage = at.to_cluster(cotangent)
+        early = [sources[2], sources[at.a_size + 1], sources[at.a_size + 3]]
+    for db in range(at.b_size):
+        near = at.send(chunks, db=db) if db else chunks
+        ready = later(near, *early) if db else near
+        parts += [near, at.send(ready, dc=1)]
+    stage = at.to_cluster(cotangent, sources[at.a_size : at.a_size + 1])
     next(stage)
+    quarter = quarter_of(at, (out_weight, up_weight, down_weight), sources[1 : at.a_size])
     pieces = [quarter] + [at.send(quarter, da=d) for d in range(1, at.a_size)]
-    *w_heads, w_pad, vectors = pad_weights(
-        at, sources, heads, groups, parts[1:]
-    )
-    moves = [(d, None, 0, (at.a - d) % at.a_size) for d in range(at.a_size)]
-    quarter = shuffle(pieces, [((at.a_size, *quarter.shape), BF16)], moves)[0]
-    others = {(0, 0, 0): quarter, (0, 0, 1): at.send(quarter, dc=1)}
-    for db in range(1, at.b_size):
-        others[(0, db, 0)] = at.send(quarter, db=db)
-    if at.x_split == 2:
-        others[(1, 0, 0)] = at.send(quarter, dx=1)
+    *w_heads, w_pad, vectors = pad_weights(at, sources, heads, groups, parts[1:])
     vectors = vectors.T.astype(F32)
     g_attn, g_mlp, b_query, b_value = vectors[0], vectors[1], vectors[2], vectors[3]
 
@@ -1265,26 +1283,27 @@
 
     part_heads = heads // groups
     part_width = part_heads * HEAD_DIM
-    stage.send([others[(0, db, 0)] for db in range(1, at.b_size)] + [others[(0, 0, 1)]])
-    soon = []
+    moves = [(d, None, 0, (at.a - d) % at.a_size) for d in range(at.a_size)]
+    quarter = shuffle(pieces, [((at.a_size, *quarter.shape), BF16)], moves)[0]
+    others = {(0, 0, 0): quarter, (0, 0, 1): at.send(quarter, dc=1)}
+    for db in range(1, at.b_size):
+        others[(0, db, 0)] = at.send(quarter, db=db)
+    if at.x_split == 2:
+        others[(1, 0, 0)] = at.send(quarter, dx=1)
+    stage.send([others[(0, 0, 1)]])
+    mixed_rel, query_aug = attend_forward(at, info, starts_col, qkv, heads, block)
+    d_out = next(stage).reshape(own_rows, model)
     if at.x_split == 2:
         for db in range(1, at.b_size):
-            others[(1, db, 0)] = at.send(later(others[(0, db, 0)], qkv), dx=1)
-            soon.append(others[(1, db, 0)])
-        others[(1, 0, 1)] = at.send(later(others[(1, 0, 0)], qkv), dc=1)
-        soon.append(others[(1, 0, 1)])
-    mixed_rel, query_aug = attend_forward(at, info, starts_col, qkv, heads, block)
+            others[(1, db, 0)] = at.send(later(others[(0, db, 0)], d_out), dx=1)
     parts = []
     for db, dc in at.peers():
-        part = mixed_rel[db, dc].reshape(own_rows, width)
+        part = later(mixed_rel[db, dc], d_out).reshape(own_rows, width)
         parts.append(at.send(part, db=db, dc=dc) if db or dc else part)
-    d_out = stage.send(soon).reshape(own_rows, model)
-    last = []
+    mixed = concat(parts, [])
     for dx, db, dc in list(others):
         if (dx, db, 1) not in others:
-            others[(dx, db, 1)] = at.send(later(others[(dx, db, 0)], d_out), dc=1)
-            last.append(others[(dx, db, 1)])
-    mixed = concat(parts, last)
+            others[(dx, db, 1)] = at.send(later(others[(dx, db, 0)], mixed), dc=1)
     tokens = chunks.reshape(own_rows, model)
     output, d_residual, d_proj, normed_mlp, activated, d_up, *d_parts = middle(
         at, mixed, tokens, d_out, g_mlp[None], others
@@ -1331,39 +1350,44 @@
     stage = at.from_cluster(output.reshape(at.a_size, half, model))
     next(stage)
     d_first, extra_first = backward(0)
+    next(stage)
     full.next()
-    next(stage)
     reduce_first = HeadsReduce(at, heads_outer(at, normed, d_first, extra_first))
-    output = next(stage)
     full.over_a()
     d_second, extra_second = backward(1)
     full_parts = full.end()
     reduce_first.over_a()
 
     d_heads = [d_first, d_second]
-    gives = [back_project(at, d_heads, w_heads, half, which)[0] for which in range(2)]
-    keeps = []
-    for which in range(2):
-        terms = back_project(at, d_heads, w_heads, half, which, at.send(gives[which], dc=1))
+    keeps, received = [], []
+    residual_chunks = d_residual.reshape(at.a_size, half, model)
+
+    def give(which):
+        return at.send(back_project(at, d_heads, w_heads, half, which)[0], dc=1)
+
+    def keep(which, got):
+        terms = back_project(at, d_heads, w_heads, half, which, got)
         keeps.append([terms[0]] + [at.send(terms[db], db=db) for db in range(1, at.b_size)])
-    first = reduce_first.to_peers()
-    reduce_second = HeadsReduce(at, heads_outer(at, normed, d_second, extra_second))
-    residual_chunks = d_residual.reshape(at.a_size, half, model)
-    received = []
 
     def back(which):
         sent = norm_back(at, keeps[which], chunks, residual_chunks, g_attn[None], which)
         for k, part in enumerate(sent):
             received.append(at.send_back(part, which * len(sent) + k))
 
+    got = give(0)
+    reduce_second = HeadsReduce(at, heads_outer(at, normed, d_second, extra_second))
+    first = reduce_first.by_b(full_parts[1:2])
+    keep(0, got)
+    keep(1, give(1))
+    reduce_second.over_a()
     back(0)
-    *grads_full, grad_gain_mlp = finish_full(at, full_parts, up_weight, gain_mlp, first[0][1:])
+    parts = to_peers(at, [first, reduce_second.by_b()])
     back(1)
-    reduce_second.over_a()
+    *grads_full, grad_gain_mlp = finish_full(at, full_parts, up_weight, gain_mlp, [])
+    output = next(stage)
     input_grad = at.place_back(received)
-    second = reduce_second.to_peers()
     weights = (query_weight, key_weight, value_weight)
-    *grads_heads, grad_gain_attn, few = finish_heads(at, [first, second], weights, gain_attn, 3)
+    *grads_heads, grad_gain_attn, few = finish_heads(at, parts, weights, gain_attn, 3)
     grad_scale = few[:HEAD_DIM, 2] / scale_dim * (LOG_BASE / math.sqrt(HEAD_DIM))
     grad_scale = grad_scale * jax.nn.sigmoid(dim_scale)
     return (

time: 518 us -> 492 us (0.950)
  waiting for transfers between devices: 164 us -> 145 us
  Pallas kernels: 204 us -> 191 us
  local copies, waits for them, and re-layouts: 63.2 us -> 70.9 us
    ppermute x4, waiting for transfers between devices: 33.1 us -> 13 us  [send_back(): lax.ppermute(part, AXES, [(j, i) for i, j in self.route(self._match(m))])]
    pallas_call x43 -> x41, Pallas kernels: 204 us -> 191 us  [call(): pl.pallas_call(run, out_shape=[jax.ShapeDtypeStruct(shape, kind) for shap...]
    unnamed x205 -> x265, local copies, waits for them, and re-layouts: 54.6 us -> 62.4 us
    ppermute x70 -> x67, waiting for transfers between devices: 131 us -> 132 us  [send(): lax.ppermute(value, AXES, self.route(lambda x, c, a, b: ((x + dx) % self....]
    ppermute x70 -> x67, starting transfers between devices: 62.6 us -> 62.8 us  [send(): lax.ppermute(value, AXES, self.route(lambda x, c, a, b: ((x + dx) % self....]
  transfers between devices with their start and end apart: 74 -> 71, of which waited for: 26 -> 31; matrix products, arithmetic and copies ran while one was open for 2% -> 2% of each run, Pallas kernels for 29% -> 26%
where the time goes in v3:
time: 492 us; the launch traced here: 483 us
  Pallas kernels  191 us (39%)
  waiting for transfers between devices  145 us (29%)
  local copies, waits for them, and re-layouts  70.9 us (14%)
  starting transfers between devices  69.8 us (14%)
    pallas_call x41, Pallas kernels, call(): pl.pallas_call(run, out_shape=[jax.ShapeDtypeStruct(shape, kind) for shap...  191 us
    ppermute x67, waiting for transfers between devices, send(): lax.ppermute(value, AXES, self.route(lambda x, c, a, b: ((x + dx) % self....  132 us
    ppermute x67, starting transfers between devices, send(): lax.ppermute(value, AXES, self.route(lambda x, c, a, b: ((x + dx) % self....  62.8 us
    unnamed x265, local copies, waits for them, and re-layouts  62.4 us
    ppermute x4, waiting for transfers between devices, send_back(): lax.ppermute(part, AXES, [(j, i) for i, j in self.route(self._match(m))])  13 us
  transfers between devices with their start and end apart: 71, of which 31 were waited for; matrix products, arithmetic and copies ran while one was open for 2% of the time, Pallas kernels for 26%

profile of v3, /device:TPU:9, one launch (start us, length us, event | category | flops | bytes accessed | tf_op | source)
XLA Modules:
  0.0 483.2 jit_solution(680133301514709082)
XLA Ops:
  13.0 3.1 collective-permute-done.5.refs_1_
  17.1 20.0 %collective-permute-done.3.refs_2_ = bf16[128,1280]{1,0:T(8,128)(2,1)S(1)} collective-permute-done((bf16[128,1280]{1,0:T(8,128)(2,1)S(1)}, bf16[128,1280]{1,0:T(8,128)(2,1)S(1)}, u32[]{:S(2)}, u32[]{:S(2)}) %collective-permute-start.3) | collective-permute-done | bytes 327712 | tf_op jit(solution)/shard_map/ppermute | solution.py:55
  47.5 5.8 %collective-permute-done.9.refs_4_.refs_1_ = bf16[2,80,964]{2,1,0:T(8,128)(2,1)S(1)} collective-permute-done((bf16[2,80,964]{2,1,0:T(8,128)(2,1)S(1)}, bf16[2,80,964]{2,1,0:T(8,128)(2,1)S(1)}, u32[]{:S(2)}, u32[]{:S(2)}) %collective-permute-start.9) | collective-permute-done | bytes 308512 | tf_op jit(solution)/shard_map/ppermute | solution.py:55
  54.4 8.4 %collective-permute-done.11.refs_6_.refs_3_ = bf16[2,80,964]{2,1,0:T(8,128)(2,1)S(1)} collective-permute-done((bf16[2,80,964]{2,1,0:T(8,128)(2,1)S(1)}, bf16[2,80,964]{2,1,0:T(8,128)(2,1)S(1)}, u32[]{:S(2)}, u32[]{:S(2)}) %collective-permute-start.11) | collective-permute-done | bytes 308512 | tf_op jit(solution)/shard_map/ppermute | solution.py:55
  65.0 7.3 %collective-permute-done.8.refs_5_.refs_2_ = bf16[2,80,964]{2,1,0:T(8,128)(2,1)S(1)} collective-permute-done((bf16[2,80,964]{2,1,0:T(8,128)(2,1)S(1)}, bf16[2,80,964]{2,1,0:T(8,128)(2,1)S(1)}, u32[]{:S(2)}, u32[]{:S(2)}) %collective-permute-start.8) | collective-permute-done | bytes 308512 | tf_op jit(solution)/shard_map/ppermute | solution.py:55
  77.0 7.7 %collective-permute-done.14.refs_2_.refs_4_ = bf16[2,80,964]{2,1,0:T(8,128)(2,1)S(1)} collective-permute-done((bf16[2,80,964]{2,1,0:T(8,128)(2,1)S(1)}, bf16[2,80,964]{2,1,0:T(8,128)(2,1)S(1)}, u32[]{:S(2)}, u32[]{:S(2)}) %collective-permute-start.14) | collective-permute-done | bytes 308512 | tf_op jit(solution)/shard_map/ppermute | solution.py:55
  89.4 4.0 collective-permute-start.18
  98.0 4.3 pad_weights.1
  109.6 13.0 %project.1 = (bf16[2048,1536]{1,0:T(8,128)(2,1)S(1)}, bf16[2048,1280]{1,0:T(8,128)(2,1)S(1)}) custom-call(s32[4]{0:T(128)S(1)} %pad_add_fusion.2.spots, bf16[4,128,1280]{2,1,0:T(8,128)(2,1)S(1)} %shuffle.11.refs_1_.refs_0_.refs_2_, bf16[4,128,1280]{2,1,0:T(8,128)(2,1)} %collective-permute-done.6.refs_9_.refs_1_, ...), custom_call_target="tpu_custom_call" | custom-call | flops 3987500032 | bytes 11962500 | tf_op jit(solution)/shard_map/project/pallas_call | solution.py:167
  122.6 2.4 copy-done.15
  125.1 3.6 shuffle.13.refs_2_.refs_4_
  140.8 2.8 copy-done.1
  143.6 21.3 %attend_forward.1 = (bf16[2,2,4,128,320]{4,3,2,1,0:T(8,128)(2,1)S(1)}, bf16[2048,512]{1,0:T(8,128)(2,1)S(1)}) custom-call(s32[10]{0:T(128)S(1)} %pad_add_fusion.1.spots, s32[2048,128]{1,0:T(8,128)S(1)} %broadcast_in_dim.58.refs_0_, bf16[2048,1536]{1,0:T(8,128)(2,1)S(1)} %copy-done.1, bf16[2048,1536]{1,0:T(8,128)(2,1)S(1)} %copy-done.1, ...), custom_call_target="tpu_custom_call" | custom-call | flops 3300000000 | bytes 9900000 | tf_op jit(solution)/shard_map/attend_forward/pallas_call | solution.py:167
  172.1 8.8 %collective-permute-done.26.refs_3_ = bf16[512,320]{1,0:T(8,128)(2,1)S(1)} collective-permute-done((bf16[512,320]{1,0:T(8,128)(2,1)S(1)}, bf16[512,320]{1,0:T(8,128)(2,1)S(1)}, u32[]{:S(2)}, u32[]{:S(2)}) %collective-permute-start.26) | collective-permute-done | bytes 327712 | tf_op jit(solution)/shard_map/ppermute | solution.py:55
  181.0 8.9 %collective-permute-done.25.refs_2_ = bf16[512,320]{1,0:T(8,128)(2,1)S(1)} collective-permute-done((bf16[512,320]{1,0:T(8,128)(2,1)S(1)}, bf16[512,320]{1,0:T(8,128)(2,1)S(1)}, u32[]{:S(2)}, u32[]{:S(2)}) %collective-permute-start.25) | collective-permute-done | bytes 327712 | tf_op jit(solution)/shard_map/ppermute | solution.py:55
  191.8 4.3 collective-permute-done.29.refs_8_
  200.8 19.8 %middle.1 = (bf16[512,1280]{1,0:T(8,128)(2,1)}, f32[512,1280]{1,0:T(8,128)}, bf16[512,1280]{1,0:T(8,128)(2,1)}, bf16[512,1280]{1,0:T(8,128)(2,1)}, bf16[512,1280...) custom-call(s32[192]{0:T(256)S(1)} %stack.264.spots, ...), custom_call_target="tpu_custom_call" | custom-call | flops 5500000256 | bytes 16500000 | tf_op jit(solution)/shard_map/middle/pallas_call | solution.py:167
  221.3 8.5 %outer_give.1.refs_7_ = bf16[3,1280,640]{2,1,0:T(8,128)(2,1)} custom-call(s32[7]{0:T(128)} %stack.289.spots, bf16[512,1280]{1,0:T(8,128)(2,1)} %copy-done.22, bf16[512,1280]{1,0:T(8,128)(2,1)} %get-tuple-element.142.refs_1_, bf16[512,1280]{1,0:T(8,128)(2,1)} %get-tuple-element.143.refs_2_, bf16[512,1280]{1,0:T(8,128)(2,1)} %get-tuple-element.144.refs_3_, ...), custom_call_target="tpu_custom_call" | custom-call | flops 27500000 | bytes 82500 | tf_op jit(solution)/shard_map/outer_give/pallas_call | solution.py:167
  233.3 2.9 collective-permute-done.34
  236.1 4.7 collective-permute-done.35
  240.8 9.0 %collective-permute-done.36 = bf16[512,320]{1,0:T(8,128)(2,1)S(1)} collective-permute-done((bf16[512,320]{1,0:T(8,128)(2,1)S(1)}, bf16[512,320]{1,0:T(8,128)(2,1)S(1)}, u32[]{:S(2)}, u32[]{:S(2)}) %collective-permute-start.36) | collective-permute-done | bytes 327712 | tf_op jit(solution)/shard_map/ppermute | solution.py:55
  250.5 10.0 %outer.1 = (bf16[3,2,2,80,640]{4,3,2,1,0:T(8,128)(2,1)}, bf16[3,2,2,80,640]{4,3,2,1,0:T(8,128)(2,1)}, bf16[3,2,2,80,640]{4,3,2,1,0:T(8,128)(2,1)}, bf16[3,2,2,80,640]{4,3,2,1,0:T(8,128)(2,1)}) custom-call(s32[7]{0:T(128)} %stack.288.spots, bf16[512,1280]{1,0:T(8,128)(2,1)} %copy-done.22, bf16[512,1280]{1,0:T(8,128)(2,1)} %get-tuple-element.142.refs_1_, ...), custom_call_target="tpu_custom_call" | custom-call | flops 1924999936 | bytes 5775000 | tf_op jit(solution)/shard_map/outer/pallas_call | solution.py:167
  267.2 2.8 copy-done.2
  273.6 20.5 %attend_backward.2 = (bf16[2048,480]{1,0:T(8,128)(2,1)S(1)}, f32[8,128]{1,0:T(8,128)S(1)}, f32[8,768]{1,0:T(8,128)S(1)}) custom-call(s32[10]{0:T(128)S(1)} %pad_add_fusion.1.spots, s32[8,2048]{1,0:T(8,128)S(1)} %broadcast_in_dim.61.refs_0_, f32[8,256]{1,0:T(8,128)S(1)} %broadcast_in_dim.63.refs_1_, bf16[2048,512]{1,0:T(8,128)(2,1)S(1)} %copy-done.104, ...), custom_call_target="tpu_custom_call" | custom-call | flops 6874999808 | bytes 20625000 | tf_op jit(solution)/shard_map/attend_backward/pallas_call | solution.py:167
  299.5 3.6 add_blocks.6
  309.6 2.5 copy-done.16
  314.1 4.8 heads_outer.2
  320.8 2.4 cat.1
  325.7 21.5 %attend_backward.3 = (bf16[2048,480]{1,0:T(8,128)(2,1)S(1)}, f32[8,128]{1,0:T(8,128)S(1)}, f32[8,768]{1,0:T(8,128)S(1)}) custom-call(s32[10]{0:T(128)S(1)} %pad_add_fusion.1.spots, s32[8,2048]{1,0:T(8,128)S(1)} %broadcast_in_dim.61.refs_0_, f32[8,256]{1,0:T(8,128)S(1)} %broadcast_in_dim.63.refs_1_, bf16[2048,512]{1,0:T(8,128)(2,1)S(1)} %copy-done.105, ...), custom_call_target="tpu_custom_call" | custom-call | flops 6874999808 | bytes 20625000 | tf_op jit(solution)/shard_map/attend_backward/pallas_call | solution.py:167
  347.9 3.8 collective-permute-done.47
  355.1 3.2 back_project.4.refs_3_
  365.7 2.5 copy-done.17
  369.2 5.6 %heads_outer.3 = (bf16[4,2,80,483]{3,2,1,0:T(8,128)(2,1)S(1)}, bf16[4,2,80,483]{3,2,1,0:T(8,128)(2,1)}) custom-call(s32[1]{0:T(128)} %bitcast.54.spots, bf16[2048,1280]{1,0:T(8,128)(2,1)S(1)} %copy-done.17, bf16[2048,480]{1,0:T(8,128)(2,1)S(1)} %copy-done.7, bf16[1280,3]{1,0:T(8,128)(2,1)S(1)} %copy-done.46, bf16[2,2,128,1280]{3,2,1,0:T(8,128)(2,1)} %back_project.4.refs_3_), custom_call_target="tpu_custom_call" | custom-call | flops 1512499968 | bytes 4537500 | tf_op jit(solution)/shard_map/heads_outer/pallas_call | solution.py:167
  379.6 4.7 back_project.5
  384.2 3.2 back_project.6.refs_5_
  393.8 3.6 back_project.7
  397.4 7.2 %collective-permute-done.58.refs_1_.refs_3_.refs_5_.refs_7_ = bf16[4,2,80,483]{3,2,1,0:T(8,128)(2,1)} collective-permute-done((bf16[4,2,80,483]{3,2,1,0:T(8,128)(2,1)}, bf16[4,2,80,483]{3,2,1,0:T(8,128)(2,1)}, u32[]{:S(2)}, u32[]{:S(2)}) %collective-permute-start.58) | collective-permute-done | bytes 618272 | tf_op jit(solution)/shard_map/ppermute | solution.py:55
  411.6 2.9 norm_back.2
  414.6 5.8 %collective-permute-done.60.refs_2_.refs_6_ = bf16[2,80,483]{2,1,0:T(8,128)(2,1)S(1)} collective-permute-done((bf16[2,80,483]{2,1,0:T(8,128)(2,1)S(1)}, bf16[2,80,483]{2,1,0:T(8,128)(2,1)S(1)}, u32[]{:S(2)}, u32[]{:S(2)}) %collective-permute-start.60) | collective-permute-done | bytes 154592 | tf_op jit(solution)/shard_map/ppermute | solution.py:55
  420.3 2.6 collective-permute-done.61.refs_3_.refs_7_
  426.1 3.8 collective-permute-done.68.refs_2_
  435.9 3.8 collective-permute-start.63
  443.1 3.2 collective-permute-start.66
  448.9 3.1 finish_full.1
  455.5 10.2 %collective-permute-done.64.refs_1_ = bf16[128,1280]{1,0:T(8,128)(2,1)S(1)} collective-permute-done((bf16[128,1280]{1,0:T(8,128)(2,1)}, bf16[128,1280]{1,0:T(8,128)(2,1)S(1)}, u32[]{:S(2)}, u32[]{:S(2)}) %collective-permute-start.64) | collective-permute-done | bytes 327712 | tf_op jit(solution)/shard_map/ppermute | solution.py:107
  466.4 2.8 collective-permute-done.66.refs_3_
  471.5 2.6 shuffle.17.refs_9_
  475.5 5.1 %finish_heads.1 = (f32[160,1280]{1,0:T(8,128)}, f32[160,1280]{1,0:T(8,128)}, f32[160,1280]{1,0:T(8,128)}, f32[160,1]{1,0:T(8,128)S(1)}, f32[160,3]{1,0:T(8,128)S(1)}) custom-call(s32[5]{0:T(128)S(1)} %stack.317.spots, bf16[2,80,483]{2,1,0:T(8,128)(2,1)S(1)} %get-tuple-element.199.refs_5_.refs_0_, bf16[2,80,483]{2,1,0:T(8,128)(2,1)S(1)} %copy-done.96, ...), custom_call_target="tpu_custom_call" | custom-call | flops 1100000000 | bytes 3300000 | tf_op jit(solution)/shard_map/finish_heads/pallas_call | solution.py:167
  (501 shorter events, 162.4 us)
Async XLA Ops:
  9.2 28.0 %collective-permute-start.3 = (bf16[128,1280]{1,0:T(8,128)(2,1)S(1)}, bf16[128,1280]{1,0:T(8,128)(2,1)S(1)}, u32[]{:S(2)}, u32[]{:S(2)}) collective-permute-start(bf16[128,1280]{1,0:T(8,128)(2,1)S(1)} %get-tuple-element.118), channel_id=1, source_target_pairs={{0,4},{1,5},{2,6},{3,7},{4,0},{5,1},{6,2},{7,3},{8,12},{9,13},{10,... | collective-permute-start | bytes 983048 | tf_op jit(solution)/shard_map/ppermute | solution.py:55
  10.2 29.4 %collective-permute-start.4 = (bf16[128,1280]{1,0:T(8,128)(2,1)S(1)}, bf16[128,1280]{1,0:T(8,128)(2,1)S(1)}, u32[]{:S(2)}, u32[]{:S(2)}) collective-permute-start(bf16[128,1280]{1,0:T(8,128)(2,1)S(1)} %get-tuple-element.119), channel_id=1, source_target_pairs={{0,6},{1,7},{2,0},{3,1},{4,2},{5,3},{6,4},{7,5},{8,14},{9,15},{10,... | collective-permute-start | bytes 983048 | tf_op jit(solution)/shard_map/ppermute | solution.py:55
  43.4 30.5 %collective-permute-start.7 = (bf16[4,128,1280]{2,1,0:T(8,128)(2,1)S(1)}, bf16[4,128,1280]{2,1,0:T(8,128)(2,1)}, u32[]{:S(2)}, u32[]{:S(2)}) collective-permute-start(bf16[4,128,1280]{2,1,0:T(8,128)(2,1)S(1)} %shuffle.11.refs_1_.refs_0_.refs_2_), channel_id=1, source_target_pairs={{0,1},{1,0},{2,3},{3,2},{4,5},{5,4},{6,7},{7,6},{8,9},{9,8},{10,11... | collective-permute-start | bytes 3932168 | tf_op jit(solution)/shard_map/ppermute | solution.py:55
  44.7 18.2 %collective-permute-start.11 = (bf16[2,80,964]{2,1,0:T(8,128)(2,1)S(1)}, bf16[2,80,964]{2,1,0:T(8,128)(2,1)S(1)}, u32[]{:S(2)}, u32[]{:S(2)}) collective-permute-start(bf16[2,80,964]{2,1,0:T(8,128)(2,1)S(1)} %shuffle.10.refs_4_.refs_0_), channel_id=1, source_target_pairs={{0,6},{1,7},{2,0},{3,1},{4,2},{5,3},{6,4},{7,5},{8,14},{9,15},{10,... | collective-permute-start | bytes 925448 | tf_op jit(solution)/shard_map/ppermute | solution.py:55
  46.1 26.2 %collective-permute-start.8 = (bf16[2,80,964]{2,1,0:T(8,128)(2,1)S(1)}, bf16[2,80,964]{2,1,0:T(8,128)(2,1)S(1)}, u32[]{:S(2)}, u32[]{:S(2)}) collective-permute-start(bf16[2,80,964]{2,1,0:T(8,128)(2,1)S(1)} %shuffle.10.refs_4_.refs_0_), channel_id=1, source_target_pairs={{0,4},{1,5},{2,6},{3,7},{4,0},{5,1},{6,2},{7,3},{8,12},{9,13},{10,... | collective-permute-start | bytes 925448 | tf_op jit(solution)/shard_map/ppermute | solution.py:55
  53.2 19.1 %collective-permute-start.10 = (bf16[2,80,964]{2,1,0:T(8,128)(2,1)S(1)}, bf16[2,80,964]{2,1,0:T(8,128)(2,1)S(1)}, u32[]{:S(2)}, u32[]{:S(2)}) collective-permute-start(bf16[2,80,964]{2,1,0:T(8,128)(2,1)S(1)} %collective-permute-done.9.refs_4_.refs_1_), channel_id=1, source_target_pairs={{0,16},{1,17},{2,18},{3,19},{4,20},{5,21},{6,22},{7,23},{8,24},{9,... | collective-permute-start | bytes 925448 | tf_op jit(solution)/shard_map/ppermute | solution.py:55
  64.1 31.0 %collective-permute-start.6 = (bf16[4,128,1280]{2,1,0:T(8,128)(2,1)S(1)}, bf16[4,128,1280]{2,1,0:T(8,128)(2,1)}, u32[]{:S(2)}, u32[]{:S(2)}) collective-permute-start(bf16[4,128,1280]{2,1,0:T(8,128)(2,1)S(1)} %shuffle.11.refs_1_.refs_0_.refs_2_), channel_id=1, source_target_pairs={{0,8},{1,9},{2,10},{3,11},{4,12},{5,13},{6,14},{7,15},{8,0},{9,1},... | collective-permute-start | bytes 3932168 | tf_op jit(solution)/shard_map/ppermute | solution.py:55
  73.8 21.2 %collective-permute-start.13 = (bf16[4,128,1280]{2,1,0:T(8,128)(2,1)}, bf16[4,128,1280]{2,1,0:T(8,128)(2,1)}, u32[]{:S(2)}, u32[]{:S(2)}) collective-permute-start(bf16[4,128,1280]{2,1,0:T(8,128)(2,1)} %collective-permute-done.7.refs_10_.refs_2_), channel_id=1, source_target_pairs={{0,8},{1,9},{2,10},{3,11},{4,12},{5,13},{6,14},{7,15},{8,0},{9,1},... | collective-permute-start | bytes 3932168 | tf_op jit(solution)/shard_map/ppermute | solution.py:55
  76.6 16.8 %collective-permute-start.15 = (bf16[2,80,964]{2,1,0:T(8,128)(2,1)S(1)}, bf16[2,80,964]{2,1,0:T(8,128)(2,1)}, u32[]{:S(2)}, u32[]{:S(2)}) collective-permute-start(bf16[2,80,964]{2,1,0:T(8,128)(2,1)S(1)} %collective-permute-done.8.refs_5_.refs_2_), channel_id=1, source_target_pairs={{0,16},{1,17},{2,18},{3,19},{4,20},{5,21},{6,22},{7,23},{8,24},{9,... | collective-permute-start | bytes 925448 | tf_op jit(solution)/shard_map/ppermute | solution.py:55
  88.0 37.0 %collective-permute-start.17 = (bf16[3,80,640]{2,1,0:T(8,128)(2,1)S(1)}, bf16[3,80,640]{2,1,0:T(8,128)(2,1)}, u32[]{:S(2)}, u32[]{:S(2)}) collective-permute-start(bf16[3,80,640]{2,1,0:T(8,128)(2,1)S(1)} %quarter.1.refs_8_.refs_0_), channel_id=1, source_target_pairs={{0,2},{1,3},{2,4},{3,5},{4,6},{5,7},{6,0},{7,1},{8,10},{9,11},{10,... | collective-permute-start | bytes 921608 | tf_op jit(solution)/shard_map/ppermute | solution.py:55
  89.4 35.6 %collective-permute-start.18 = (bf16[3,80,640]{2,1,0:T(8,128)(2,1)S(1)}, bf16[3,80,640]{2,1,0:T(8,128)(2,1)}, u32[]{:S(2)}, u32[]{:S(2)}) collective-permute-start(bf16[3,80,640]{2,1,0:T(8,128)(2,1)S(1)} %quarter.1.refs_8_.refs_0_), channel_id=1, source_target_pairs={{0,4},{1,5},{2,6},{3,7},{4,0},{5,1},{6,2},{7,3},{8,12},{9,13},{10,... | collective-permute-start | bytes 921608 | tf_op jit(solution)/shard_map/ppermute | solution.py:55
  93.4 31.6 %collective-permute-start.19 = (bf16[3,80,640]{2,1,0:T(8,128)(2,1)S(1)}, bf16[3,80,640]{2,1,0:T(8,128)(2,1)}, u32[]{:S(2)}, u32[]{:S(2)}) collective-permute-start(bf16[3,80,640]{2,1,0:T(8,128)(2,1)S(1)} %quarter.1.refs_8_.refs_0_), channel_id=1, source_target_pairs={{0,6},{1,7},{2,0},{3,1},{4,2},{5,3},{6,4},{7,5},{8,14},{9,15},{10,... | collective-permute-start | bytes 921608 | tf_op jit(solution)/shard_map/ppermute | solution.py:55
  129.9 38.2 %collective-permute-start.27 = (bf16[4,3,80,640]{3,2,1,0:T(8,128)(2,1)}, bf16[4,3,80,640]{3,2,1,0:T(8,128)(2,1)}, u32[]{:S(2)}, u32[]{:S(2)}) collective-permute-start(bf16[4,3,80,640]{3,2,1,0:T(8,128)(2,1)} %shuffle.13.refs_2_.refs_4_), channel_id=1, source_target_pairs={{0,1},{1,0},{2,3},{3,2},{4,5},{5,4},{6,7},{7,6},{8,9},{9,8},{10,11... | collective-permute-start | bytes 3686408 | tf_op jit(solution)/shard_map/ppermute | solution.py:55
  135.5 29.4 %collective-permute-start.21 = (bf16[128,1280]{1,0:T(8,128)(2,1)S(1)}, bf16[128,1280]{1,0:T(8,128)(2,1)S(1)}, u32[]{:S(2)}, u32[]{:S(2)}) collective-permute-start(bf16[128,1280]{1,0:T(8,128)(2,1)S(1)} %get-tuple-element.130), channel_id=1, source_target_pairs={{0,2},{1,3},{2,4},{3,5},{4,6},{5,7},{6,0},{7,1},{8,10},{9,11},{10,... | collective-permute-start | bytes 983048 | tf_op jit(solution)/shard_map/ppermute | solution.py:55
  136.3 28.6 %collective-permute-start.22 = (bf16[128,1280]{1,0:T(8,128)(2,1)S(1)}, bf16[128,1280]{1,0:T(8,128)(2,1)S(1)}, u32[]{:S(2)}, u32[]{:S(2)}) collective-permute-start(bf16[128,1280]{1,0:T(8,128)(2,1)S(1)} %get-tuple-element.131), channel_id=1, source_target_pairs={{0,4},{1,5},{2,6},{3,7},{4,0},{5,1},{6,2},{7,3},{8,12},{9,13},{10,... | collective-permute-start | bytes 983048 | tf_op jit(solution)/shard_map/ppermute | solution.py:55
  138.7 28.4 %collective-permute-start.23 = (bf16[128,1280]{1,0:T(8,128)(2,1)S(1)}, bf16[128,1280]{1,0:T(8,128)(2,1)S(1)}, u32[]{:S(2)}, u32[]{:S(2)}) collective-permute-start(bf16[128,1280]{1,0:T(8,128)(2,1)S(1)} %get-tuple-element.132), channel_id=1, source_target_pairs={{0,6},{1,7},{2,0},{3,1},{4,2},{5,3},{6,4},{7,5},{8,14},{9,15},{10,... | collective-permute-start | bytes 983048 | tf_op jit(solution)/shard_map/ppermute | solution.py:55
  139.2 52.0 %collective-permute-start.28 = (bf16[4,3,80,640]{3,2,1,0:T(8,128)(2,1)}, bf16[4,3,80,640]{3,2,1,0:T(8,128)(2,1)}, u32[]{:S(2)}, u32[]{:S(2)}) collective-permute-start(bf16[4,3,80,640]{3,2,1,0:T(8,128)(2,1)} %shuffle.13.refs_2_.refs_4_), channel_id=1, source_target_pairs={{0,16},{1,17},{2,18},{3,19},{4,20},{5,21},{6,22},{7,23},{8,24},{9,... | collective-permute-start | bytes 3686408 | tf_op jit(solution)/shard_map/ppermute | solution.py:55
  168.1 28.0 %collective-permute-start.29 = (bf16[4,3,80,640]{3,2,1,0:T(8,128)(2,1)}, bf16[4,3,80,640]{3,2,1,0:T(8,128)(2,1)}, u32[]{:S(2)}, u32[]{:S(2)}) collective-permute-start(bf16[4,3,80,640]{3,2,1,0:T(8,128)(2,1)} %collective-permute-done.27.refs_6_), channel_id=1, source_target_pairs={{0,16},{1,17},{2,18},{3,19},{4,20},{5,21},{6,22},{7,23},{8,24},{9,... | collective-permute-start | bytes 3686408 | tf_op jit(solution)/shard_map/ppermute | solution.py:55
  171.1 18.7 %collective-permute-start.25 = (bf16[512,320]{1,0:T(8,128)(2,1)S(1)}, bf16[512,320]{1,0:T(8,128)(2,1)S(1)}, u32[]{:S(2)}, u32[]{:S(2)}) collective-permute-start(bf16[512,320]{1,0:T(8,128)(2,1)S(1)} %bitcast.162), channel_id=1, source_target_pairs={{0,1},{1,0},{2,3},{3,2},{4,5},{5,4},{6,7},{7,6},{8,9},{9,8},{10,11... | collective-permute-start | bytes 983048 | tf_op jit(solution)/shard_map/ppermute | solution.py:55
  172.1 17.7 %collective-permute-start.24 = (bf16[512,320]{1,0:T(8,128)(2,1)S(1)}, bf16[512,320]{1,0:T(8,128)(2,1)S(1)}, u32[]{:S(2)}, u32[]{:S(2)}) collective-permute-start(bf16[512,320]{1,0:T(8,128)(2,1)S(1)} %bitcast.161), channel_id=1, source_target_pairs={{0,8},{1,9},{2,10},{3,11},{4,12},{5,13},{6,14},{7,15},{8,0},{9,1},... | collective-permute-start | bytes 983048 | tf_op jit(solution)/shard_map/ppermute | solution.py:55
  229.8 20.0 %collective-permute-start.33 = (bf16[3,1280,640]{2,1,0:T(8,128)(2,1)}, bf16[3,1280,640]{2,1,0:T(8,128)(2,1)}, u32[]{:S(2)}, u32[]{:S(2)}) collective-permute-start(bf16[3,1280,640]{2,1,0:T(8,128)(2,1)} %outer_give.1.refs_7_), channel_id=1, source_target_pairs={{0,8},{1,9},{2,10},{3,11},{4,12},{5,13},{6,14},{7,15},{8,0},{9,1},... | collective-permute-start | bytes 14745608 | tf_op jit(solution)/shard_map/ppermute | solution.py:55
  230.8 19.0 %collective-permute-start.36 = (bf16[512,320]{1,0:T(8,128)(2,1)S(1)}, bf16[512,320]{1,0:T(8,128)(2,1)S(1)}, u32[]{:S(2)}, u32[]{:S(2)}) collective-permute-start(bf16[512,320]{1,0:T(8,128)(2,1)S(1)} %get-tuple-element.149), channel_id=1, source_target_pairs={{0,9},{1,8},{2,11},{3,10},{4,13},{5,12},{6,15},{7,14},{8,1},{9,0},... | collective-permute-start | bytes 983048 | tf_op jit(solution)/shard_map/ppermute | solution.py:55
  260.5 38.9 %collective-permute-start.41 = (bf16[3,2,2,80,640]{4,3,2,1,0:T(8,128)(2,1)}, bf16[3,2,2,80,640]{4,3,2,1,0:T(8,128)(2,1)}, u32[]{:S(2)}, u32[]{:S(2)}) collective-permute-start(bf16[3,2,2,80,640]{4,3,2,1,0:T(8,128)(2,1)} %get-tuple-element.159), channel_id=1, source_target_pairs={{0,16},{1,17},{2,18},{3,19},{4,20},{5,21},{6,22},{7,23},{8,24},{9,... | collective-permute-start | bytes 3686408 | tf_op jit(solution)/shard_map/ppermute | solution.py:55
  261.8 37.7 %collective-permute-start.42 = (bf16[3,2,2,80,640]{4,3,2,1,0:T(8,128)(2,1)}, bf16[3,2,2,80,640]{4,3,2,1,0:T(8,128)(2,1)}, u32[]{:S(2)}, u32[]{:S(2)}) collective-permute-start(bf16[3,2,2,80,640]{4,3,2,1,0:T(8,128)(2,1)} %get-tuple-element.161), channel_id=1, source_target_pairs={{0,1},{1,0},{2,3},{3,2},{4,5},{5,4},{6,7},{7,6},{8,9},{9,8},{10,11... | collective-permute-start | bytes 3686408 | tf_op jit(solution)/shard_map/ppermute | solution.py:55
  265.3 29.0 %collective-permute-start.37 = (bf16[128,1280]{1,0:T(8,128)(2,1)}, bf16[128,1280]{1,0:T(8,128)(2,1)}, u32[]{:S(2)}, u32[]{:S(2)}) collective-permute-start(bf16[128,1280]{1,0:T(8,128)(2,1)} %get-tuple-element.152), channel_id=1, source_target_pairs={{0,2},{1,3},{2,4},{3,5},{4,6},{5,7},{6,0},{7,1},{8,10},{9,11},{10,... | collective-permute-start | bytes 983048 | tf_op jit(solution)/shard_map/ppermute | solution.py:55
  265.3 29.0 %collective-permute-start.38 = (bf16[128,1280]{1,0:T(8,128)(2,1)}, bf16[128,1280]{1,0:T(8,128)(2,1)}, u32[]{:S(2)}, u32[]{:S(2)}) collective-permute-start(bf16[128,1280]{1,0:T(8,128)(2,1)} %get-tuple-element.153), channel_id=1, source_target_pairs={{0,4},{1,5},{2,6},{3,7},{4,0},{5,1},{6,2},{7,3},{8,12},{9,13},{10,... | collective-permute-start | bytes 983048 | tf_op jit(solution)/shard_map/ppermute | solution.py:55
  265.9 29.6 %collective-permute-start.39 = (bf16[128,1280]{1,0:T(8,128)(2,1)}, bf16[128,1280]{1,0:T(8,128)(2,1)}, u32[]{:S(2)}, u32[]{:S(2)}) collective-permute-start(bf16[128,1280]{1,0:T(8,128)(2,1)} %get-tuple-element.154), channel_id=1, source_target_pairs={{0,6},{1,7},{2,0},{3,1},{4,2},{5,3},{6,4},{7,5},{8,14},{9,15},{10,... | collective-permute-start | bytes 983048 | tf_op jit(solution)/shard_map/ppermute | solution.py:55
  304.8 15.4 %collective-permute-start.43 = (bf16[3,2,80,640]{3,2,1,0:T(8,128)(2,1)}, bf16[3,2,80,640]{3,2,1,0:T(8,128)(2,1)}, u32[]{:S(2)}, u32[]{:S(2)}) collective-permute-start(bf16[3,2,80,640]{3,2,1,0:T(8,128)(2,1)} %get-tuple-element.163), channel_id=1, source_target_pairs={{0,1},{1,0},{2,3},{3,2},{4,5},{5,4},{6,7},{7,6},{8,9},{9,8},{10,11... | collective-permute-start | bytes 1843208 | tf_op jit(solution)/shard_map/ppermute | solution.py:55
  305.8 14.9 %collective-permute-start.44 = (bf16[3,2,80,640]{3,2,1,0:T(8,128)(2,1)}, bf16[3,2,80,640]{3,2,1,0:T(8,128)(2,1)}, u32[]{:S(2)}, u32[]{:S(2)}) collective-permute-start(bf16[3,2,80,640]{3,2,1,0:T(8,128)(2,1)} %get-tuple-element.165), channel_id=1, source_target_pairs={{0,16},{1,17},{2,18},{3,19},{4,20},{5,21},{6,22},{7,23},{8,24},{9,... | collective-permute-start | bytes 1843208 | tf_op jit(solution)/shard_map/ppermute | solution.py:55
  318.9 33.5 %collective-permute-start.51 = (bf16[4,2,80,483]{3,2,1,0:T(8,128)(2,1)S(1)}, bf16[4,2,80,483]{3,2,1,0:T(8,128)(2,1)S(1)}, u32[]{:S(2)}, u32[]{:S(2)}) collective-permute-start(bf16[4,2,80,483]{3,2,1,0:T(8,128)(2,1)S(1)} %get-tuple-element.176), channel_id=1, source_target_pairs={{0,16},{1,17},{2,18},{3,19},{4,20},{5,21},{6,22},{7,23},{8,24},{9,... | collective-permute-start | bytes 1854728 | tf_op jit(solution)/shard_map/ppermute | solution.py:55
  323.2 24.1 %collective-permute-start.45 = (bf16[3,80,640]{2,1,0:T(8,128)(2,1)S(1)}, bf16[3,80,640]{2,1,0:T(8,128)(2,1)S(1)}, u32[]{:S(2)}, u32[]{:S(2)}) collective-permute-start(bf16[3,80,640]{2,1,0:T(8,128)(2,1)S(1)} %get-tuple-element.171), channel_id=1, source_target_pairs={{0,2},{1,3},{2,4},{3,5},{4,6},{5,7},{6,0},{7,1},{8,10},{9,11},{10,... | collective-permute-start | bytes 921608 | tf_op jit(solution)/shard_map/ppermute | solution.py:55
  323.2 24.6 %collective-permute-start.46 = (bf16[3,80,640]{2,1,0:T(8,128)(2,1)S(1)}, bf16[3,80,640]{2,1,0:T(8,128)(2,1)S(1)}, u32[]{:S(2)}, u32[]{:S(2)}) collective-permute-start(bf16[3,80,640]{2,1,0:T(8,128)(2,1)S(1)} %get-tuple-element.172), channel_id=1, source_target_pairs={{0,4},{1,5},{2,6},{3,7},{4,0},{5,1},{6,2},{7,3},{8,12},{9,13},{10,... | collective-permute-start | bytes 921608 | tf_op jit(solution)/shard_map/ppermute | solution.py:55
  324.2 27.4 %collective-permute-start.47 = (bf16[3,80,640]{2,1,0:T(8,128)(2,1)S(1)}, bf16[3,80,640]{2,1,0:T(8,128)(2,1)S(1)}, u32[]{:S(2)}, u32[]{:S(2)}) collective-permute-start(bf16[3,80,640]{2,1,0:T(8,128)(2,1)S(1)} %get-tuple-element.173), channel_id=1, source_target_pairs={{0,6},{1,7},{2,0},{3,1},{4,2},{5,3},{6,4},{7,5},{8,14},{9,15},{10,... | collective-permute-start | bytes 921608 | tf_op jit(solution)/shard_map/ppermute | solution.py:55
  358.3 21.2 %collective-permute-start.52 = (bf16[2,2,128,1280]{3,2,1,0:T(8,128)(2,1)}, bf16[2,2,128,1280]{3,2,1,0:T(8,128)(2,1)}, u32[]{:S(2)}, u32[]{:S(2)}) collective-permute-start(bf16[2,2,128,1280]{3,2,1,0:T(8,128)(2,1)} %back_project.4.refs_3_), channel_id=1, source_target_pairs={{0,8},{1,9},{2,10},{3,11},{4,12},{5,13},{6,14},{7,15},{8,0},{9,1},... | collective-permute-start | bytes 3932168 | tf_op jit(solution)/shard_map/ppermute | solution.py:55
  360.0 17.2 %collective-permute-start.48 = (bf16[3,80,640]{2,1,0:T(8,128)(2,1)}, bf16[3,80,640]{2,1,0:T(8,128)(2,1)}, u32[]{:S(2)}, u32[]{:S(2)}) collective-permute-start(bf16[3,80,640]{2,1,0:T(8,128)(2,1)} %copy-done.55), channel_id=1, source_target_pairs={{0,16},{1,17},{2,18},{3,19},{4,20},{5,21},{6,22},{7,23},{8,24},{9,... | collective-permute-start | bytes 921608 | tf_op jit(solution)/shard_map/ppermute | solution.py:55
  360.3 14.5 %collective-permute-start.53 = (bf16[2,80,483]{2,1,0:T(8,128)(2,1)}, bf16[2,80,483]{2,1,0:T(8,128)(2,1)}, u32[]{:S(2)}, u32[]{:S(2)}) collective-permute-start(bf16[2,80,483]{2,1,0:T(8,128)(2,1)} %copy-done.116), channel_id=1, source_target_pairs={{0,2},{1,3},{2,4},{3,5},{4,6},{5,7},{6,0},{7,1},{8,10},{9,11},{10,... | collective-permute-start | bytes 463688 | tf_op jit(solution)/shard_map/ppermute | solution.py:55
  361.7 15.5 %collective-permute-start.55 = (bf16[2,80,483]{2,1,0:T(8,128)(2,1)}, bf16[2,80,483]{2,1,0:T(8,128)(2,1)}, u32[]{:S(2)}, u32[]{:S(2)}) collective-permute-start(bf16[2,80,483]{2,1,0:T(8,128)(2,1)} %copy-done.114), channel_id=1, source_target_pairs={{0,6},{1,7},{2,0},{3,1},{4,2},{5,3},{6,4},{7,5},{8,14},{9,15},{10,... | collective-permute-start | bytes 463688 | tf_op jit(solution)/shard_map/ppermute | solution.py:55
  387.9 16.7 %collective-permute-start.58 = (bf16[4,2,80,483]{3,2,1,0:T(8,128)(2,1)}, bf16[4,2,80,483]{3,2,1,0:T(8,128)(2,1)}, u32[]{:S(2)}, u32[]{:S(2)}) collective-permute-start(bf16[4,2,80,483]{3,2,1,0:T(8,128)(2,1)} %get-tuple-element.189), channel_id=1, source_target_pairs={{0,16},{1,17},{2,18},{3,19},{4,20},{5,21},{6,22},{7,23},{8,24},{9,... | collective-permute-start | bytes 1854728 | tf_op jit(solution)/shard_map/ppermute | solution.py:55
  389.1 20.6 %collective-permute-start.62 = (bf16[2,128,1280]{2,1,0:T(8,128)(2,1)}, bf16[2,128,1280]{2,1,0:T(8,128)(2,1)}, u32[]{:S(2)}, u32[]{:S(2)}) collective-permute-start(bf16[2,128,1280]{2,1,0:T(8,128)(2,1)} %get-tuple-element.194), channel_id=1, source_target_pairs={{0,1},{1,0},{2,3},{3,2},{4,5},{5,4},{6,7},{7,6},{8,9},{9,8},{10,11... | collective-permute-start | bytes 1966088 | tf_op jit(solution)/shard_map/ppermute | solution.py:55
  407.8 15.2 %collective-permute-start.61 = (bf16[2,80,483]{2,1,0:T(8,128)(2,1)S(1)}, bf16[2,80,483]{2,1,0:T(8,128)(2,1)S(1)}, u32[]{:S(2)}, u32[]{:S(2)}) collective-permute-start(bf16[2,80,483]{2,1,0:T(8,128)(2,1)S(1)} %get-tuple-element.193), channel_id=1, source_target_pairs={{0,6},{1,7},{2,0},{3,1},{4,2},{5,3},{6,4},{7,5},{8,14},{9,15},{10,... | collective-permute-start | bytes 463688 | tf_op jit(solution)/shard_map/ppermute | solution.py:55
  409.2 26.7 %collective-permute-start.57 = (bf16[2,128,1280]{2,1,0:T(8,128)(2,1)S(1)}, bf16[2,128,1280]{2,1,0:T(8,128)(2,1)S(1)}, u32[]{:S(2)}, u32[]{:S(2)}) collective-permute-start(bf16[2,128,1280]{2,1,0:T(8,128)(2,1)S(1)} %get-tuple-element.187), channel_id=1, source_target_pairs={{0,1},{1,0},{2,3},{3,2},{4,5},{5,4},{6,7},{7,6},{8,9},{9,8},{10,11... | collective-permute-start | bytes 1966088 | tf_op jit(solution)/shard_map/ppermute | solution.py:55
  409.7 31.8 %collective-permute-start.40 = (bf16[2,128,1280]{2,1,0:T(8,128)(2,1)S(1)}, bf16[2,128,1280]{2,1,0:T(8,128)(2,1)S(1)}, u32[]{:S(2)}, u32[]{:S(2)}) collective-permute-start(bf16[2,128,1280]{2,1,0:T(8,128)(2,1)S(1)} %copy-done.108), channel_id=1, source_target_pairs={{0,8},{1,9},{2,10},{3,11},{4,12},{5,13},{6,14},{7,15},{8,0},{9,1},... | collective-permute-start | bytes 1966088 | tf_op jit(solution)/shard_map/ppermute | solution.py:55
  425.9 15.7 %collective-permute-start.49 = (bf16[3,80,640]{2,1,0:T(8,128)(2,1)S(1)}, bf16[3,80,640]{2,1,0:T(8,128)(2,1)S(1)}, u32[]{:S(2)}, u32[]{:S(2)}) collective-permute-start(bf16[3,80,640]{2,1,0:T(8,128)(2,1)S(1)} %copy-done.56), channel_id=1, source_target_pairs={{0,8},{1,9},{2,10},{3,11},{4,12},{5,13},{6,14},{7,15},{8,0},{9,1},... | collective-permute-start | bytes 921608 | tf_op jit(solution)/shard_map/ppermute | solution.py:55
  434.6 39.5 %collective-permute-start.70 = (bf16[4,2,80,483]{3,2,1,0:T(8,128)(2,1)}, bf16[4,2,80,483]{3,2,1,0:T(8,128)(2,1)}, u32[]{:S(2)}, u32[]{:S(2)}) collective-permute-start(bf16[4,2,80,483]{3,2,1,0:T(8,128)(2,1)} %pad_maximum_fusion), channel_id=1, source_target_pairs={{0,16},{1,17},{2,18},{3,19},{4,20},{5,21},{6,22},{7,23},{8,24},{9,... | collective-permute-start | bytes 1854728 | tf_op jit(solution)/shard_map/ppermute | solution.py:55
  435.9 19.5 %collective-permute-start.63 = (bf16[128,1280]{1,0:T(8,128)(2,1)}, bf16[128,1280]{1,0:T(8,128)(2,1)S(1)}, u32[]{:S(2)}, u32[]{:S(2)}) collective-permute-start(bf16[128,1280]{1,0:T(8,128)(2,1)} %get-tuple-element.195.refs_8_), channel_id=1, source_target_pairs={{0,0},{1,1},{2,2},{3,3},{8,4},{9,5},{10,6},{11,7},{4,8},{5,9},{6,1... | collective-permute-start | bytes 983048 | tf_op jit(solution)/shard_map/ppermute | solution.py:107
  441.5 24.1 %collective-permute-start.64 = (bf16[128,1280]{1,0:T(8,128)(2,1)}, bf16[128,1280]{1,0:T(8,128)(2,1)S(1)}, u32[]{:S(2)}, u32[]{:S(2)}) collective-permute-start(bf16[128,1280]{1,0:T(8,128)(2,1)} %get-tuple-element.202), channel_id=1, source_target_pairs={{2,0},{3,1},{0,2},{1,3},{10,4},{11,5},{8,6},{9,7},{6,8},{7,9},{4,1... | collective-permute-start | bytes 983048 | tf_op jit(solution)/shard_map/ppermute | solution.py:107
  442.4 23.3 %collective-permute-start.65 = (bf16[128,1280]{1,0:T(8,128)(2,1)}, bf16[128,1280]{1,0:T(8,128)(2,1)S(1)}, u32[]{:S(2)}, u32[]{:S(2)}) collective-permute-start(bf16[128,1280]{1,0:T(8,128)(2,1)} %get-tuple-element.200.refs_6_), channel_id=1, source_target_pairs={{8,0},{9,1},{10,2},{11,3},{0,4},{1,5},{2,6},{3,7},{12,8},{13,9},{1... | collective-permute-start | bytes 983048 | tf_op jit(solution)/shard_map/ppermute | solution.py:107
  443.1 26.1 %collective-permute-start.66 = (bf16[128,1280]{1,0:T(8,128)(2,1)}, bf16[128,1280]{1,0:T(8,128)(2,1)}, u32[]{:S(2)}, u32[]{:S(2)}) collective-permute-start(bf16[128,1280]{1,0:T(8,128)(2,1)} %get-tuple-element.203), channel_id=1, source_target_pairs={{10,0},{11,1},{8,2},{9,3},{2,4},{3,5},{0,6},{1,7},{14,8},{15,9},{1... | collective-permute-start | bytes 983048 | tf_op jit(solution)/shard_map/ppermute | solution.py:107
  (155 other events, 1026.1 us)

commit v4 on v3

--- a/solution.py
+++ b/solution.py
@@ -940,7 +940,7 @@
         out[...] = (d_residual[k] + d_norm).astype(BF16)
 
 
-def norm_back(at, terms, chunks, d_residual, gain, which):
+def norm_back(at, terms, chunks, d_residual, gain, which, after):
     pair, half, model = terms[0].shape
     block = pl.BlockSpec((pair, half, model), lambda i, s: (s[0], 0, 0))
     order = [k ^ (at.a % pair) for k in range(pair)]
@@ -950,6 +950,7 @@
         [which ^ at.c, *order],
         [(t, VMEM) for t in terms] + [(chunks, block), (d_residual, block), (gain, VMEM)],
         [((half, model), BF16, VMEM)] * pair,
+        after=after,
     )
 
 
@@ -1370,7 +1371,9 @@
         keeps.append([terms[0]] + [at.send(terms[db], db=db) for db in range(1, at.b_size)])
 
     def back(which):
-        sent = norm_back(at, keeps[which], chunks, residual_chunks, g_attn[None], which)
+        sent = norm_back(
+            at, keeps[which], chunks, residual_chunks, g_attn[None], which, received[:]
+        )
         for k, part in enumerate(sent):
             received.append(at.send_back(part, which * len(sent) + k))
 
@@ -1379,15 +1382,16 @@
     first = reduce_first.by_b(full_parts[1:2])
     keep(0, got)
     keep(1, give(1))
+    *grads_full, grad_gain_mlp = finish_full(at, full_parts, up_weight, gain_mlp, [])
+    output = next(stage)
     reduce_second.over_a()
     back(0)
-    parts = to_peers(at, [first, reduce_second.by_b()])
+    second = reduce_second.by_b(keeps[1][1:])
     back(1)
-    *grads_full, grad_gain_mlp = finish_full(at, full_parts, up_weight, gain_mlp, [])
-    output = next(stage)
-    input_grad = at.place_back(received)
+    parts = to_peers(at, [first, second])
     weights = (query_weight, key_weight, value_weight)
     *grads_heads, grad_gain_attn, few = finish_heads(at, parts, weights, gain_attn, 3)
+    input_grad = at.place_back(received)
     grad_scale = few[:HEAD_DIM, 2] / scale_dim * (LOG_BASE / math.sqrt(HEAD_DIM))
     grad_scale = grad_scale * jax.nn.sigmoid(dim_scale)
     return (

time: 492 us -> 495 us (level)
  waiting for transfers between devices: 145 us -> 154 us
    ppermute x67, waiting for transfers between devices: 132 us -> 154 us  [send(): lax.ppermute(value, AXES, self.route(lambda x, c, a, b: ((x + dx) % self....]
    ppermute x4, waiting for transfers between devices: 13 us -> 0.01 us  [send_back(): lax.ppermute(part, AXES, [(j, i) for i, j in self.route(self._match(m))])]
    unnamed x265 -> x233, local copies, waits for them, and re-layouts: 62.4 us -> 57.5 us
  transfers between devices with their start and end apart: 71 -> 71, of which waited for: 31 -> 27; matrix products, arithmetic and copies ran while one was open for 2% -> 3% of each run, Pallas kernels for 26% -> 27%
where the time goes in v4:
time: 495 us; the launch traced here: 486 us
  Pallas kernels  194 us (39%)
  waiting for transfers between devices  154 us (31%)
  local copies, waits for them, and re-layouts  66 us (13%)
  starting transfers between devices  64.9 us (13%)
    pallas_call x41, Pallas kernels, call(): pl.pallas_call(run, out_shape=[jax.ShapeDtypeStruct(shape, kind) for shap...  194 us
    ppermute x67, waiting for transfers between devices, send(): lax.ppermute(value, AXES, self.route(lambda x, c, a, b: ((x + dx) % self....  154 us
    ppermute x67, starting transfers between devices, send(): lax.ppermute(value, AXES, self.route(lambda x, c, a, b: ((x + dx) % self....  58.7 us
    unnamed x233, local copies, waits for them, and re-layouts  57.5 us
  transfers between devices with their start and end apart: 71, of which 27 were waited for; matrix products, arithmetic and copies ran while one was open for 3% of the time, Pallas kernels for 27%

profile of v4, /device:TPU:9, one launch (start us, length us, event | category | flops | bytes accessed | tf_op | source)
XLA Modules:
  0.0 485.6 jit_solution(18349625582906962033)
XLA Ops:
  13.2 3.4 collective-permute-done.5.refs_1_
  18.5 18.9 %collective-permute-done.3.refs_2_ = bf16[128,1280]{1,0:T(8,128)(2,1)S(1)} collective-permute-done((bf16[128,1280]{1,0:T(8,128)(2,1)S(1)}, bf16[128,1280]{1,0:T(8,128)(2,1)S(1)}, u32[]{:S(2)}, u32[]{:S(2)}) %collective-permute-start.3) | collective-permute-done | bytes 327712 | tf_op jit(solution)/shard_map/ppermute | solution.py:55
  37.4 2.4 collective-permute-done.4.refs_3_
  44.4 6.4 %collective-permute-done.9.refs_4_.refs_1_ = bf16[2,80,964]{2,1,0:T(8,128)(2,1)S(1)} collective-permute-done((bf16[2,80,964]{2,1,0:T(8,128)(2,1)S(1)}, bf16[2,80,964]{2,1,0:T(8,128)(2,1)S(1)}, u32[]{:S(2)}, u32[]{:S(2)}) %collective-permute-start.9) | collective-permute-done | bytes 308512 | tf_op jit(solution)/shard_map/ppermute | solution.py:55
  51.9 7.7 %collective-permute-done.11.refs_6_.refs_3_ = bf16[2,80,964]{2,1,0:T(8,128)(2,1)S(1)} collective-permute-done((bf16[2,80,964]{2,1,0:T(8,128)(2,1)S(1)}, bf16[2,80,964]{2,1,0:T(8,128)(2,1)S(1)}, u32[]{:S(2)}, u32[]{:S(2)}) %collective-permute-start.11) | collective-permute-done | bytes 308512 | tf_op jit(solution)/shard_map/ppermute | solution.py:55
  61.7 8.1 %collective-permute-done.8.refs_5_.refs_2_ = bf16[2,80,964]{2,1,0:T(8,128)(2,1)S(1)} collective-permute-done((bf16[2,80,964]{2,1,0:T(8,128)(2,1)S(1)}, bf16[2,80,964]{2,1,0:T(8,128)(2,1)S(1)}, u32[]{:S(2)}, u32[]{:S(2)}) %collective-permute-start.8) | collective-permute-done | bytes 308512 | tf_op jit(solution)/shard_map/ppermute | solution.py:55
  74.5 7.7 %collective-permute-done.14.refs_2_.refs_4_ = bf16[2,80,964]{2,1,0:T(8,128)(2,1)S(1)} collective-permute-done((bf16[2,80,964]{2,1,0:T(8,128)(2,1)S(1)}, bf16[2,80,964]{2,1,0:T(8,128)(2,1)S(1)}, u32[]{:S(2)}, u32[]{:S(2)}) %collective-permute-start.14) | collective-permute-done | bytes 308512 | tf_op jit(solution)/shard_map/ppermute | solution.py:55
  87.0 4.0 collective-permute-start.18
  94.9 4.3 pad_weights.1
  106.6 13.0 %project.1 = (bf16[2048,1536]{1,0:T(8,128)(2,1)S(1)}, bf16[2048,1280]{1,0:T(8,128)(2,1)S(1)}) custom-call(s32[4]{0:T(128)S(1)} %pad_add_fusion.2.spots, bf16[4,128,1280]{2,1,0:T(8,128)(2,1)S(1)} %shuffle.11.refs_1_.refs_0_.refs_2_, bf16[4,128,1280]{2,1,0:T(8,128)(2,1)} %collective-permute-done.6.refs_9_.refs_1_, ...), custom_call_target="tpu_custom_call" | custom-call | flops 3987500032 | bytes 11962500 | tf_op jit(solution)/shard_map/project/pallas_call | solution.py:167
  119.6 2.4 copy-done.15
  122.0 3.7 shuffle.13.refs_2_.refs_4_
  138.2 2.8 copy-done.1
  141.0 21.2 %attend_forward.1 = (bf16[2,2,4,128,320]{4,3,2,1,0:T(8,128)(2,1)S(1)}, bf16[2048,512]{1,0:T(8,128)(2,1)S(1)}) custom-call(s32[10]{0:T(128)S(1)} %pad_add_fusion.1.spots, s32[2048,128]{1,0:T(8,128)S(1)} %broadcast_in_dim.58.refs_0_, bf16[2048,1536]{1,0:T(8,128)(2,1)S(1)} %copy-done.1, bf16[2048,1536]{1,0:T(8,128)(2,1)S(1)} %copy-done.1, ...), custom_call_target="tpu_custom_call" | custom-call | flops 3300000000 | bytes 9900000 | tf_op jit(solution)/shard_map/attend_forward/pallas_call | solution.py:167
  169.3 8.4 %collective-permute-done.26.refs_3_ = bf16[512,320]{1,0:T(8,128)(2,1)S(1)} collective-permute-done((bf16[512,320]{1,0:T(8,128)(2,1)S(1)}, bf16[512,320]{1,0:T(8,128)(2,1)S(1)}, u32[]{:S(2)}, u32[]{:S(2)}) %collective-permute-start.26) | collective-permute-done | bytes 327712 | tf_op jit(solution)/shard_map/ppermute | solution.py:55
  177.7 9.1 %collective-permute-done.25.refs_2_ = bf16[512,320]{1,0:T(8,128)(2,1)S(1)} collective-permute-done((bf16[512,320]{1,0:T(8,128)(2,1)S(1)}, bf16[512,320]{1,0:T(8,128)(2,1)S(1)}, u32[]{:S(2)}, u32[]{:S(2)}) %collective-permute-start.25) | collective-permute-done | bytes 327712 | tf_op jit(solution)/shard_map/ppermute | solution.py:55
  188.7 4.0 collective-permute-done.29.refs_8_
  197.7 19.8 %middle.1 = (bf16[512,1280]{1,0:T(8,128)(2,1)}, f32[512,1280]{1,0:T(8,128)}, bf16[512,1280]{1,0:T(8,128)(2,1)}, bf16[512,1280]{1,0:T(8,128)(2,1)}, bf16[512,1280...) custom-call(s32[192]{0:T(256)S(1)} %stack.264.spots, ...), custom_call_target="tpu_custom_call" | custom-call | flops 5500000256 | bytes 16500000 | tf_op jit(solution)/shard_map/middle/pallas_call | solution.py:167
  218.3 8.5 %outer_give.1.refs_7_ = bf16[3,1280,640]{2,1,0:T(8,128)(2,1)} custom-call(s32[7]{0:T(128)} %stack.289.spots, bf16[512,1280]{1,0:T(8,128)(2,1)} %copy-done.22, bf16[512,1280]{1,0:T(8,128)(2,1)} %get-tuple-element.142.refs_1_, bf16[512,1280]{1,0:T(8,128)(2,1)} %get-tuple-element.143.refs_2_, bf16[512,1280]{1,0:T(8,128)(2,1)} %get-tuple-element.144.refs_3_, ...), custom_call_target="tpu_custom_call" | custom-call | flops 27500000 | bytes 82500 | tf_op jit(solution)/shard_map/outer_give/pallas_call | solution.py:167
  230.2 2.7 collective-permute-done.34
  232.9 4.9 %collective-permute-done.35 = bf16[512,320]{1,0:T(8,128)(2,1)S(1)} collective-permute-done((bf16[512,320]{1,0:T(8,128)(2,1)}, bf16[512,320]{1,0:T(8,128)(2,1)S(1)}, u32[]{:S(2)}, u32[]{:S(2)}) %collective-permute-start.35) | collective-permute-done | bytes 327712 | tf_op jit(solution)/shard_map/ppermute | solution.py:55
  237.8 8.9 %collective-permute-done.36 = bf16[512,320]{1,0:T(8,128)(2,1)S(1)} collective-permute-done((bf16[512,320]{1,0:T(8,128)(2,1)}, bf16[512,320]{1,0:T(8,128)(2,1)S(1)}, u32[]{:S(2)}, u32[]{:S(2)}) %collective-permute-start.36) | collective-permute-done | bytes 327712 | tf_op jit(solution)/shard_map/ppermute | solution.py:55
  247.5 10.0 %outer.1 = (bf16[3,2,2,80,640]{4,3,2,1,0:T(8,128)(2,1)}, bf16[3,2,2,80,640]{4,3,2,1,0:T(8,128)(2,1)}, bf16[3,2,2,80,640]{4,3,2,1,0:T(8,128)(2,1)}, bf16[3,2,2,80,640]{4,3,2,1,0:T(8,128)(2,1)}) custom-call(s32[7]{0:T(128)} %stack.288.spots, bf16[512,1280]{1,0:T(8,128)(2,1)} %copy-done.22, bf16[512,1280]{1,0:T(8,128)(2,1)} %get-tuple-element.142.refs_1_, ...), custom_call_target="tpu_custom_call" | custom-call | flops 1924999936 | bytes 5775000 | tf_op jit(solution)/shard_map/outer/pallas_call | solution.py:167
  265.0 2.8 copy-done.2
  271.4 20.5 %attend_backward.2 = (bf16[2048,480]{1,0:T(8,128)(2,1)S(1)}, f32[8,128]{1,0:T(8,128)S(1)}, f32[8,768]{1,0:T(8,128)S(1)}) custom-call(s32[10]{0:T(128)S(1)} %pad_add_fusion.1.spots, s32[8,2048]{1,0:T(8,128)S(1)} %broadcast_in_dim.61.refs_0_, f32[8,256]{1,0:T(8,128)S(1)} %broadcast_in_dim.63.refs_1_, bf16[2048,512]{1,0:T(8,128)(2,1)S(1)} %copy-done.95, ...), custom_call_target="tpu_custom_call" | custom-call | flops 6874999808 | bytes 20625000 | tf_op jit(solution)/shard_map/attend_backward/pallas_call | solution.py:167
  294.4 2.9 route_back.1
  297.3 3.6 add_blocks.6
  307.9 2.5 copy-done.16
  312.5 4.8 heads_outer.2
  318.5 2.4 cat.1
  322.7 21.5 %attend_backward.3 = (bf16[2048,480]{1,0:T(8,128)(2,1)S(1)}, f32[8,128]{1,0:T(8,128)S(1)}, f32[8,768]{1,0:T(8,128)S(1)}) custom-call(s32[10]{0:T(128)S(1)} %pad_add_fusion.1.spots, s32[8,2048]{1,0:T(8,128)S(1)} %broadcast_in_dim.61.refs_0_, f32[8,256]{1,0:T(8,128)S(1)} %broadcast_in_dim.63.refs_1_, bf16[2048,512]{1,0:T(8,128)(2,1)S(1)} %copy-done.96, ...), custom_call_target="tpu_custom_call" | custom-call | flops 6874999808 | bytes 20625000 | tf_op jit(solution)/shard_map/attend_backward/pallas_call | solution.py:167
  345.9 4.2 collective-permute-done.47
  354.3 3.2 back_project.4.refs_3_
  364.7 2.5 copy-done.17
  368.2 5.6 %heads_outer.3 = (bf16[4,2,80,483]{3,2,1,0:T(8,128)(2,1)S(1)}, bf16[4,2,80,483]{3,2,1,0:T(8,128)(2,1)}) custom-call(s32[1]{0:T(128)} %bitcast.54.spots, bf16[2048,1280]{1,0:T(8,128)(2,1)S(1)} %copy-done.17, bf16[2048,480]{1,0:T(8,128)(2,1)S(1)} %copy-done.7, bf16[1280,3]{1,0:T(8,128)(2,1)S(1)} %copy-done.46, bf16[2,2,128,1280]{3,2,1,0:T(8,128)(2,1)} %back_project.4.refs_3_), custom_call_target="tpu_custom_call" | custom-call | flops 1512499968 | bytes 4537500 | tf_op jit(solution)/shard_map/heads_outer/pallas_call | solution.py:167
  373.8 2.4 collective-permute-done.55.refs_3_.refs_7_
  378.0 4.7 back_project.5
  382.7 3.2 back_project.6.refs_5_
  392.7 4.4 back_project.7
  401.1 3.4 finish_full.1
  405.6 2.7 shuffle.16.refs_8_
  412.1 2.3 norm_back.2
  414.3 4.2 collective-permute-start.59
  420.3 23.3 %collective-permute-done.63.refs_2_.refs_6_ = bf16[2,80,483]{2,1,0:T(8,128)(2,1)S(1)} collective-permute-done((bf16[2,80,483]{2,1,0:T(8,128)(2,1)S(1)}, bf16[2,80,483]{2,1,0:T(8,128)(2,1)S(1)}, u32[]{:S(2)}, u32[]{:S(2)}) %collective-permute-start.63) | collective-permute-done | bytes 154592 | tf_op jit(solution)/shard_map/ppermute | solution.py:55
  450.0 4.1 collective-permute-done.68.refs_2_
  454.0 3.7 collective-permute-done.69.refs_3_
  461.6 13.5 %collective-permute-done.70.refs_4_ = bf16[4,2,80,483]{3,2,1,0:T(8,128)(2,1)} collective-permute-done((bf16[4,2,80,483]{3,2,1,0:T(8,128)(2,1)}, bf16[4,2,80,483]{3,2,1,0:T(8,128)(2,1)}, u32[]{:S(2)}, u32[]{:S(2)}) %collective-permute-start.70) | collective-permute-done | bytes 618272 | tf_op jit(solution)/shard_map/ppermute | solution.py:55
  475.1 5.1 %finish_heads.1 = (f32[160,1280]{1,0:T(8,128)}, f32[160,1280]{1,0:T(8,128)}, f32[160,1280]{1,0:T(8,128)}, f32[160,1]{1,0:T(8,128)S(1)}, f32[160,3]{1,0:T(8,128)S(1)}) custom-call(s32[5]{0:T(128)S(1)} %stack.317.spots, bf16[2,80,483]{2,1,0:T(8,128)(2,1)S(1)} %get-tuple-element.203.refs_0_.refs_9_, bf16[2,80,483]{2,1,0:T(8,128)(2,1)S(1)} %collective-permute-done.67.refs_1_, ...), custom_call_target="tpu_custom_call" | custom-call | flops 1100000000 | bytes 3300000 | tf_op jit(solution)/shard_map/finish_heads/pallas_call | solution.py:167
  (469 shorter events, 147.5 us)
Async XLA Ops:
  9.3 28.1 %collective-permute-start.3 = (bf16[128,1280]{1,0:T(8,128)(2,1)S(1)}, bf16[128,1280]{1,0:T(8,128)(2,1)S(1)}, u32[]{:S(2)}, u32[]{:S(2)}) collective-permute-start(bf16[128,1280]{1,0:T(8,128)(2,1)S(1)} %get-tuple-element.118), channel_id=1, source_target_pairs={{0,4},{1,5},{2,6},{3,7},{4,0},{5,1},{6,2},{7,3},{8,12},{9,13},{10,... | collective-permute-start | bytes 983048 | tf_op jit(solution)/shard_map/ppermute | solution.py:55
  10.3 29.5 %collective-permute-start.4 = (bf16[128,1280]{1,0:T(8,128)(2,1)S(1)}, bf16[128,1280]{1,0:T(8,128)(2,1)S(1)}, u32[]{:S(2)}, u32[]{:S(2)}) collective-permute-start(bf16[128,1280]{1,0:T(8,128)(2,1)S(1)} %get-tuple-element.119), channel_id=1, source_target_pairs={{0,6},{1,7},{2,0},{3,1},{4,2},{5,3},{6,4},{7,5},{8,14},{9,15},{10,... | collective-permute-start | bytes 983048 | tf_op jit(solution)/shard_map/ppermute | solution.py:55
  40.8 30.5 %collective-permute-start.7 = (bf16[4,128,1280]{2,1,0:T(8,128)(2,1)S(1)}, bf16[4,128,1280]{2,1,0:T(8,128)(2,1)}, u32[]{:S(2)}, u32[]{:S(2)}) collective-permute-start(bf16[4,128,1280]{2,1,0:T(8,128)(2,1)S(1)} %shuffle.11.refs_1_.refs_0_.refs_2_), channel_id=1, source_target_pairs={{0,1},{1,0},{2,3},{3,2},{4,5},{5,4},{6,7},{7,6},{8,9},{9,8},{10,11... | collective-permute-start | bytes 3932168 | tf_op jit(solution)/shard_map/ppermute | solution.py:55
  42.1 17.5 %collective-permute-start.11 = (bf16[2,80,964]{2,1,0:T(8,128)(2,1)S(1)}, bf16[2,80,964]{2,1,0:T(8,128)(2,1)S(1)}, u32[]{:S(2)}, u32[]{:S(2)}) collective-permute-start(bf16[2,80,964]{2,1,0:T(8,128)(2,1)S(1)} %shuffle.10.refs_4_.refs_0_), channel_id=1, source_target_pairs={{0,6},{1,7},{2,0},{3,1},{4,2},{5,3},{6,4},{7,5},{8,14},{9,15},{10,... | collective-permute-start | bytes 925448 | tf_op jit(solution)/shard_map/ppermute | solution.py:55
  43.6 26.2 %collective-permute-start.8 = (bf16[2,80,964]{2,1,0:T(8,128)(2,1)S(1)}, bf16[2,80,964]{2,1,0:T(8,128)(2,1)S(1)}, u32[]{:S(2)}, u32[]{:S(2)}) collective-permute-start(bf16[2,80,964]{2,1,0:T(8,128)(2,1)S(1)} %shuffle.10.refs_4_.refs_0_), channel_id=1, source_target_pairs={{0,4},{1,5},{2,6},{3,7},{4,0},{5,1},{6,2},{7,3},{8,12},{9,13},{10,... | collective-permute-start | bytes 925448 | tf_op jit(solution)/shard_map/ppermute | solution.py:55
  50.7 19.1 %collective-permute-start.10 = (bf16[2,80,964]{2,1,0:T(8,128)(2,1)S(1)}, bf16[2,80,964]{2,1,0:T(8,128)(2,1)S(1)}, u32[]{:S(2)}, u32[]{:S(2)}) collective-permute-start(bf16[2,80,964]{2,1,0:T(8,128)(2,1)S(1)} %collective-permute-done.9.refs_4_.refs_1_), channel_id=1, source_target_pairs={{0,16},{1,17},{2,18},{3,19},{4,20},{5,21},{6,22},{7,23},{8,24},{9,... | collective-permute-start | bytes 925448 | tf_op jit(solution)/shard_map/ppermute | solution.py:55
  60.8 31.1 %collective-permute-start.6 = (bf16[4,128,1280]{2,1,0:T(8,128)(2,1)S(1)}, bf16[4,128,1280]{2,1,0:T(8,128)(2,1)}, u32[]{:S(2)}, u32[]{:S(2)}) collective-permute-start(bf16[4,128,1280]{2,1,0:T(8,128)(2,1)S(1)} %shuffle.11.refs_1_.refs_0_.refs_2_), channel_id=1, source_target_pairs={{0,8},{1,9},{2,10},{3,11},{4,12},{5,13},{6,14},{7,15},{8,0},{9,1},... | collective-permute-start | bytes 3932168 | tf_op jit(solution)/shard_map/ppermute | solution.py:55
  71.3 20.7 %collective-permute-start.13 = (bf16[4,128,1280]{2,1,0:T(8,128)(2,1)}, bf16[4,128,1280]{2,1,0:T(8,128)(2,1)}, u32[]{:S(2)}, u32[]{:S(2)}) collective-permute-start(bf16[4,128,1280]{2,1,0:T(8,128)(2,1)} %collective-permute-done.7.refs_10_.refs_2_), channel_id=1, source_target_pairs={{0,8},{1,9},{2,10},{3,11},{4,12},{5,13},{6,14},{7,15},{8,0},{9,1},... | collective-permute-start | bytes 3932168 | tf_op jit(solution)/shard_map/ppermute | solution.py:55
  74.0 17.0 %collective-permute-start.15 = (bf16[2,80,964]{2,1,0:T(8,128)(2,1)S(1)}, bf16[2,80,964]{2,1,0:T(8,128)(2,1)}, u32[]{:S(2)}, u32[]{:S(2)}) collective-permute-start(bf16[2,80,964]{2,1,0:T(8,128)(2,1)S(1)} %collective-permute-done.8.refs_5_.refs_2_), channel_id=1, source_target_pairs={{0,16},{1,17},{2,18},{3,19},{4,20},{5,21},{6,22},{7,23},{8,24},{9,... | collective-permute-start | bytes 925448 | tf_op jit(solution)/shard_map/ppermute | solution.py:55
  86.3 35.6 %collective-permute-start.17 = (bf16[3,80,640]{2,1,0:T(8,128)(2,1)S(1)}, bf16[3,80,640]{2,1,0:T(8,128)(2,1)}, u32[]{:S(2)}, u32[]{:S(2)}) collective-permute-start(bf16[3,80,640]{2,1,0:T(8,128)(2,1)S(1)} %quarter.1.refs_8_.refs_0_), channel_id=1, source_target_pairs={{0,2},{1,3},{2,4},{3,5},{4,6},{5,7},{6,0},{7,1},{8,10},{9,11},{10,... | collective-permute-start | bytes 921608 | tf_op jit(solution)/shard_map/ppermute | solution.py:55
  87.0 34.9 %collective-permute-start.18 = (bf16[3,80,640]{2,1,0:T(8,128)(2,1)S(1)}, bf16[3,80,640]{2,1,0:T(8,128)(2,1)}, u32[]{:S(2)}, u32[]{:S(2)}) collective-permute-start(bf16[3,80,640]{2,1,0:T(8,128)(2,1)S(1)} %quarter.1.refs_8_.refs_0_), channel_id=1, source_target_pairs={{0,4},{1,5},{2,6},{3,7},{4,0},{5,1},{6,2},{7,3},{8,12},{9,13},{10,... | collective-permute-start | bytes 921608 | tf_op jit(solution)/shard_map/ppermute | solution.py:55
  91.1 30.9 %collective-permute-start.19 = (bf16[3,80,640]{2,1,0:T(8,128)(2,1)S(1)}, bf16[3,80,640]{2,1,0:T(8,128)(2,1)}, u32[]{:S(2)}, u32[]{:S(2)}) collective-permute-start(bf16[3,80,640]{2,1,0:T(8,128)(2,1)S(1)} %quarter.1.refs_8_.refs_0_), channel_id=1, source_target_pairs={{0,6},{1,7},{2,0},{3,1},{4,2},{5,3},{6,4},{7,5},{8,14},{9,15},{10,... | collective-permute-start | bytes 921608 | tf_op jit(solution)/shard_map/ppermute | solution.py:55
  126.8 38.1 %collective-permute-start.27 = (bf16[4,3,80,640]{3,2,1,0:T(8,128)(2,1)}, bf16[4,3,80,640]{3,2,1,0:T(8,128)(2,1)}, u32[]{:S(2)}, u32[]{:S(2)}) collective-permute-start(bf16[4,3,80,640]{3,2,1,0:T(8,128)(2,1)} %shuffle.13.refs_2_.refs_4_), channel_id=1, source_target_pairs={{0,1},{1,0},{2,3},{3,2},{4,5},{5,4},{6,7},{7,6},{8,9},{9,8},{10,11... | collective-permute-start | bytes 3686408 | tf_op jit(solution)/shard_map/ppermute | solution.py:55
  132.4 29.9 %collective-permute-start.21 = (bf16[128,1280]{1,0:T(8,128)(2,1)S(1)}, bf16[128,1280]{1,0:T(8,128)(2,1)S(1)}, u32[]{:S(2)}, u32[]{:S(2)}) collective-permute-start(bf16[128,1280]{1,0:T(8,128)(2,1)S(1)} %get-tuple-element.130), channel_id=1, source_target_pairs={{0,2},{1,3},{2,4},{3,5},{4,6},{5,7},{6,0},{7,1},{8,10},{9,11},{10,... | collective-permute-start | bytes 983048 | tf_op jit(solution)/shard_map/ppermute | solution.py:55
  134.0 28.3 %collective-permute-start.22 = (bf16[128,1280]{1,0:T(8,128)(2,1)S(1)}, bf16[128,1280]{1,0:T(8,128)(2,1)S(1)}, u32[]{:S(2)}, u32[]{:S(2)}) collective-permute-start(bf16[128,1280]{1,0:T(8,128)(2,1)S(1)} %get-tuple-element.131), channel_id=1, source_target_pairs={{0,4},{1,5},{2,6},{3,7},{4,0},{5,1},{6,2},{7,3},{8,12},{9,13},{10,... | collective-permute-start | bytes 983048 | tf_op jit(solution)/shard_map/ppermute | solution.py:55
  136.2 27.8 %collective-permute-start.23 = (bf16[128,1280]{1,0:T(8,128)(2,1)S(1)}, bf16[128,1280]{1,0:T(8,128)(2,1)S(1)}, u32[]{:S(2)}, u32[]{:S(2)}) collective-permute-start(bf16[128,1280]{1,0:T(8,128)(2,1)S(1)} %get-tuple-element.132), channel_id=1, source_target_pairs={{0,6},{1,7},{2,0},{3,1},{4,2},{5,3},{6,4},{7,5},{8,14},{9,15},{10,... | collective-permute-start | bytes 983048 | tf_op jit(solution)/shard_map/ppermute | solution.py:55
  136.7 51.5 %collective-permute-start.28 = (bf16[4,3,80,640]{3,2,1,0:T(8,128)(2,1)}, bf16[4,3,80,640]{3,2,1,0:T(8,128)(2,1)}, u32[]{:S(2)}, u32[]{:S(2)}) collective-permute-start(bf16[4,3,80,640]{3,2,1,0:T(8,128)(2,1)} %shuffle.13.refs_2_.refs_4_), channel_id=1, source_target_pairs={{0,16},{1,17},{2,18},{3,19},{4,20},{5,21},{6,22},{7,23},{8,24},{9,... | collective-permute-start | bytes 3686408 | tf_op jit(solution)/shard_map/ppermute | solution.py:55
  165.0 27.7 %collective-permute-start.29 = (bf16[4,3,80,640]{3,2,1,0:T(8,128)(2,1)}, bf16[4,3,80,640]{3,2,1,0:T(8,128)(2,1)}, u32[]{:S(2)}, u32[]{:S(2)}) collective-permute-start(bf16[4,3,80,640]{3,2,1,0:T(8,128)(2,1)} %collective-permute-done.27.refs_6_), channel_id=1, source_target_pairs={{0,16},{1,17},{2,18},{3,19},{4,20},{5,21},{6,22},{7,23},{8,24},{9,... | collective-permute-start | bytes 3686408 | tf_op jit(solution)/shard_map/ppermute | solution.py:55
  168.3 18.5 %collective-permute-start.25 = (bf16[512,320]{1,0:T(8,128)(2,1)S(1)}, bf16[512,320]{1,0:T(8,128)(2,1)S(1)}, u32[]{:S(2)}, u32[]{:S(2)}) collective-permute-start(bf16[512,320]{1,0:T(8,128)(2,1)S(1)} %bitcast.162), channel_id=1, source_target_pairs={{0,1},{1,0},{2,3},{3,2},{4,5},{5,4},{6,7},{7,6},{8,9},{9,8},{10,11... | collective-permute-start | bytes 983048 | tf_op jit(solution)/shard_map/ppermute | solution.py:55
  169.3 17.5 %collective-permute-start.24 = (bf16[512,320]{1,0:T(8,128)(2,1)S(1)}, bf16[512,320]{1,0:T(8,128)(2,1)S(1)}, u32[]{:S(2)}, u32[]{:S(2)}) collective-permute-start(bf16[512,320]{1,0:T(8,128)(2,1)S(1)} %bitcast.161), channel_id=1, source_target_pairs={{0,8},{1,9},{2,10},{3,11},{4,12},{5,13},{6,14},{7,15},{8,0},{9,1},... | collective-permute-start | bytes 983048 | tf_op jit(solution)/shard_map/ppermute | solution.py:55
  226.8 20.0 %collective-permute-start.33 = (bf16[3,1280,640]{2,1,0:T(8,128)(2,1)}, bf16[3,1280,640]{2,1,0:T(8,128)(2,1)}, u32[]{:S(2)}, u32[]{:S(2)}) collective-permute-start(bf16[3,1280,640]{2,1,0:T(8,128)(2,1)} %outer_give.1.refs_7_), channel_id=1, source_target_pairs={{0,8},{1,9},{2,10},{3,11},{4,12},{5,13},{6,14},{7,15},{8,0},{9,1},... | collective-permute-start | bytes 14745608 | tf_op jit(solution)/shard_map/ppermute | solution.py:55
  227.9 18.8 %collective-permute-start.36 = (bf16[512,320]{1,0:T(8,128)(2,1)}, bf16[512,320]{1,0:T(8,128)(2,1)S(1)}, u32[]{:S(2)}, u32[]{:S(2)}) collective-permute-start(bf16[512,320]{1,0:T(8,128)(2,1)} %get-tuple-element.149), channel_id=1, source_target_pairs={{0,9},{1,8},{2,11},{3,10},{4,13},{5,12},{6,15},{7,14},{8,1},{9,0},... | collective-permute-start | bytes 983048 | tf_op jit(solution)/shard_map/ppermute | solution.py:55
  257.5 39.7 %collective-permute-start.41 = (bf16[3,2,2,80,640]{4,3,2,1,0:T(8,128)(2,1)}, bf16[3,2,2,80,640]{4,3,2,1,0:T(8,128)(2,1)}, u32[]{:S(2)}, u32[]{:S(2)}) collective-permute-start(bf16[3,2,2,80,640]{4,3,2,1,0:T(8,128)(2,1)} %get-tuple-element.159), channel_id=1, source_target_pairs={{0,16},{1,17},{2,18},{3,19},{4,20},{5,21},{6,22},{7,23},{8,24},{9,... | collective-permute-start | bytes 3686408 | tf_op jit(solution)/shard_map/ppermute | solution.py:55
  258.7 38.5 %collective-permute-start.42 = (bf16[3,2,2,80,640]{4,3,2,1,0:T(8,128)(2,1)}, bf16[3,2,2,80,640]{4,3,2,1,0:T(8,128)(2,1)}, u32[]{:S(2)}, u32[]{:S(2)}) collective-permute-start(bf16[3,2,2,80,640]{4,3,2,1,0:T(8,128)(2,1)} %get-tuple-element.161), channel_id=1, source_target_pairs={{0,1},{1,0},{2,3},{3,2},{4,5},{5,4},{6,7},{7,6},{8,9},{9,8},{10,11... | collective-permute-start | bytes 3686408 | tf_op jit(solution)/shard_map/ppermute | solution.py:55
  262.4 29.7 %collective-permute-start.37 = (bf16[128,1280]{1,0:T(8,128)(2,1)}, bf16[128,1280]{1,0:T(8,128)(2,1)}, u32[]{:S(2)}, u32[]{:S(2)}) collective-permute-start(bf16[128,1280]{1,0:T(8,128)(2,1)} %get-tuple-element.152), channel_id=1, source_target_pairs={{0,2},{1,3},{2,4},{3,5},{4,6},{5,7},{6,0},{7,1},{8,10},{9,11},{10,... | collective-permute-start | bytes 983048 | tf_op jit(solution)/shard_map/ppermute | solution.py:55
  262.5 29.6 %collective-permute-start.38 = (bf16[128,1280]{1,0:T(8,128)(2,1)}, bf16[128,1280]{1,0:T(8,128)(2,1)}, u32[]{:S(2)}, u32[]{:S(2)}) collective-permute-start(bf16[128,1280]{1,0:T(8,128)(2,1)} %get-tuple-element.153), channel_id=1, source_target_pairs={{0,4},{1,5},{2,6},{3,7},{4,0},{5,1},{6,2},{7,3},{8,12},{9,13},{10,... | collective-permute-start | bytes 983048 | tf_op jit(solution)/shard_map/ppermute | solution.py:55
  263.8 29.6 %collective-permute-start.39 = (bf16[128,1280]{1,0:T(8,128)(2,1)}, bf16[128,1280]{1,0:T(8,128)(2,1)}, u32[]{:S(2)}, u32[]{:S(2)}) collective-permute-start(bf16[128,1280]{1,0:T(8,128)(2,1)} %get-tuple-element.154), channel_id=1, source_target_pairs={{0,6},{1,7},{2,0},{3,1},{4,2},{5,3},{6,4},{7,5},{8,14},{9,15},{10,... | collective-permute-start | bytes 983048 | tf_op jit(solution)/shard_map/ppermute | solution.py:55
  302.6 15.4 %collective-permute-start.43 = (bf16[3,2,80,640]{3,2,1,0:T(8,128)(2,1)}, bf16[3,2,80,640]{3,2,1,0:T(8,128)(2,1)}, u32[]{:S(2)}, u32[]{:S(2)}) collective-permute-start(bf16[3,2,80,640]{3,2,1,0:T(8,128)(2,1)} %get-tuple-element.163), channel_id=1, source_target_pairs={{0,1},{1,0},{2,3},{3,2},{4,5},{5,4},{6,7},{7,6},{8,9},{9,8},{10,11... | collective-permute-start | bytes 1843208 | tf_op jit(solution)/shard_map/ppermute | solution.py:55
  303.6 14.9 %collective-permute-start.44 = (bf16[3,2,80,640]{3,2,1,0:T(8,128)(2,1)}, bf16[3,2,80,640]{3,2,1,0:T(8,128)(2,1)}, u32[]{:S(2)}, u32[]{:S(2)}) collective-permute-start(bf16[3,2,80,640]{3,2,1,0:T(8,128)(2,1)} %get-tuple-element.165), channel_id=1, source_target_pairs={{0,16},{1,17},{2,18},{3,19},{4,20},{5,21},{6,22},{7,23},{8,24},{9,... | collective-permute-start | bytes 1843208 | tf_op jit(solution)/shard_map/ppermute | solution.py:55
  317.3 34.3 %collective-permute-start.51 = (bf16[4,2,80,483]{3,2,1,0:T(8,128)(2,1)S(1)}, bf16[4,2,80,483]{3,2,1,0:T(8,128)(2,1)S(1)}, u32[]{:S(2)}, u32[]{:S(2)}) collective-permute-start(bf16[4,2,80,483]{3,2,1,0:T(8,128)(2,1)S(1)} %get-tuple-element.176), channel_id=1, source_target_pairs={{0,16},{1,17},{2,18},{3,19},{4,20},{5,21},{6,22},{7,23},{8,24},{9,... | collective-permute-start | bytes 1854728 | tf_op jit(solution)/shard_map/ppermute | solution.py:55
  321.0 23.3 %collective-permute-start.45 = (bf16[3,80,640]{2,1,0:T(8,128)(2,1)S(1)}, bf16[3,80,640]{2,1,0:T(8,128)(2,1)S(1)}, u32[]{:S(2)}, u32[]{:S(2)}) collective-permute-start(bf16[3,80,640]{2,1,0:T(8,128)(2,1)S(1)} %get-tuple-element.171), channel_id=1, source_target_pairs={{0,2},{1,3},{2,4},{3,5},{4,6},{5,7},{6,0},{7,1},{8,10},{9,11},{10,... | collective-permute-start | bytes 921608 | tf_op jit(solution)/shard_map/ppermute | solution.py:55
  321.0 24.9 %collective-permute-start.46 = (bf16[3,80,640]{2,1,0:T(8,128)(2,1)S(1)}, bf16[3,80,640]{2,1,0:T(8,128)(2,1)S(1)}, u32[]{:S(2)}, u32[]{:S(2)}) collective-permute-start(bf16[3,80,640]{2,1,0:T(8,128)(2,1)S(1)} %get-tuple-element.172), channel_id=1, source_target_pairs={{0,4},{1,5},{2,6},{3,7},{4,0},{5,1},{6,2},{7,3},{8,12},{9,13},{10,... | collective-permute-start | bytes 921608 | tf_op jit(solution)/shard_map/ppermute | solution.py:55
  322.6 27.5 %collective-permute-start.47 = (bf16[3,80,640]{2,1,0:T(8,128)(2,1)S(1)}, bf16[3,80,640]{2,1,0:T(8,128)(2,1)S(1)}, u32[]{:S(2)}, u32[]{:S(2)}) collective-permute-start(bf16[3,80,640]{2,1,0:T(8,128)(2,1)S(1)} %get-tuple-element.173), channel_id=1, source_target_pairs={{0,6},{1,7},{2,0},{3,1},{4,2},{5,3},{6,4},{7,5},{8,14},{9,15},{10,... | collective-permute-start | bytes 921608 | tf_op jit(solution)/shard_map/ppermute | solution.py:55
  357.4 20.5 %collective-permute-start.52 = (bf16[2,2,128,1280]{3,2,1,0:T(8,128)(2,1)}, bf16[2,2,128,1280]{3,2,1,0:T(8,128)(2,1)}, u32[]{:S(2)}, u32[]{:S(2)}) collective-permute-start(bf16[2,2,128,1280]{3,2,1,0:T(8,128)(2,1)} %back_project.4.refs_3_), channel_id=1, source_target_pairs={{0,8},{1,9},{2,10},{3,11},{4,12},{5,13},{6,14},{7,15},{8,0},{9,1},... | collective-permute-start | bytes 3932168 | tf_op jit(solution)/shard_map/ppermute | solution.py:55
  359.1 17.1 %collective-permute-start.48 = (bf16[3,80,640]{2,1,0:T(8,128)(2,1)}, bf16[3,80,640]{2,1,0:T(8,128)(2,1)}, u32[]{:S(2)}, u32[]{:S(2)}) collective-permute-start(bf16[3,80,640]{2,1,0:T(8,128)(2,1)} %add_blocks.7.refs_8_.refs_0_), channel_id=1, source_target_pairs={{0,16},{1,17},{2,18},{3,19},{4,20},{5,21},{6,22},{7,23},{8,24},{9,... | collective-permute-start | bytes 921608 | tf_op jit(solution)/shard_map/ppermute | solution.py:55
  359.3 14.5 %collective-permute-start.54 = (bf16[2,80,483]{2,1,0:T(8,128)(2,1)}, bf16[2,80,483]{2,1,0:T(8,128)(2,1)}, u32[]{:S(2)}, u32[]{:S(2)}) collective-permute-start(bf16[2,80,483]{2,1,0:T(8,128)(2,1)} %copy-done.103), channel_id=1, source_target_pairs={{0,4},{1,5},{2,6},{3,7},{4,0},{5,1},{6,2},{7,3},{8,12},{9,13},{10,... | collective-permute-start | bytes 463688 | tf_op jit(solution)/shard_map/ppermute | solution.py:55
  360.7 15.5 %collective-permute-start.55 = (bf16[2,80,483]{2,1,0:T(8,128)(2,1)}, bf16[2,80,483]{2,1,0:T(8,128)(2,1)}, u32[]{:S(2)}, u32[]{:S(2)}) collective-permute-start(bf16[2,80,483]{2,1,0:T(8,128)(2,1)} %copy-done.102), channel_id=1, source_target_pairs={{0,6},{1,7},{2,0},{3,1},{4,2},{5,3},{6,4},{7,5},{8,14},{9,15},{10,... | collective-permute-start | bytes 463688 | tf_op jit(solution)/shard_map/ppermute | solution.py:55
  386.3 18.2 %collective-permute-start.40 = (bf16[2,128,1280]{2,1,0:T(8,128)(2,1)}, bf16[2,128,1280]{2,1,0:T(8,128)(2,1)}, u32[]{:S(2)}, u32[]{:S(2)}) collective-permute-start(bf16[2,128,1280]{2,1,0:T(8,128)(2,1)} %get-tuple-element.158), channel_id=1, source_target_pairs={{0,8},{1,9},{2,10},{3,11},{4,12},{5,13},{6,14},{7,15},{8,0},{9,1},... | collective-permute-start | bytes 1966088 | tf_op jit(solution)/shard_map/ppermute | solution.py:55
  386.4 22.0 %collective-permute-start.58 = (bf16[4,2,80,483]{3,2,1,0:T(8,128)(2,1)}, bf16[4,2,80,483]{3,2,1,0:T(8,128)(2,1)}, u32[]{:S(2)}, u32[]{:S(2)}) collective-permute-start(bf16[4,2,80,483]{3,2,1,0:T(8,128)(2,1)} %get-tuple-element.190), channel_id=1, source_target_pairs={{0,16},{1,17},{2,18},{3,19},{4,20},{5,21},{6,22},{7,23},{8,24},{9,... | collective-permute-start | bytes 1854728 | tf_op jit(solution)/shard_map/ppermute | solution.py:55
  387.0 25.0 %collective-permute-start.57 = (bf16[2,128,1280]{2,1,0:T(8,128)(2,1)}, bf16[2,128,1280]{2,1,0:T(8,128)(2,1)}, u32[]{:S(2)}, u32[]{:S(2)}) collective-permute-start(bf16[2,128,1280]{2,1,0:T(8,128)(2,1)} %get-tuple-element.188), channel_id=1, source_target_pairs={{0,1},{1,0},{2,3},{3,2},{4,5},{5,4},{6,7},{7,6},{8,9},{9,8},{10,11... | collective-permute-start | bytes 1966088 | tf_op jit(solution)/shard_map/ppermute | solution.py:55
  398.2 45.5 %collective-permute-start.61 = (bf16[2,128,1280]{2,1,0:T(8,128)(2,1)}, bf16[2,128,1280]{2,1,0:T(8,128)(2,1)S(1)}, u32[]{:S(2)}, u32[]{:S(2)}) collective-permute-start(bf16[2,128,1280]{2,1,0:T(8,128)(2,1)} %get-tuple-element.194), channel_id=1, source_target_pairs={{0,1},{1,0},{2,3},{3,2},{4,5},{5,4},{6,7},{7,6},{8,9},{9,8},{10,11... | collective-permute-start | bytes 1966088 | tf_op jit(solution)/shard_map/ppermute | solution.py:55
  414.3 30.0 %collective-permute-start.59 = (bf16[128,1280]{1,0:T(8,128)(2,1)S(1)}, bf16[128,1280]{1,0:T(8,128)(2,1)S(1)}, u32[]{:S(2)}, u32[]{:S(2)}) collective-permute-start(bf16[128,1280]{1,0:T(8,128)(2,1)S(1)} %get-tuple-element.192.refs_8_), channel_id=1, source_target_pairs={{0,0},{1,1},{2,2},{3,3},{8,4},{9,5},{10,6},{11,7},{4,8},{5,9},{6,1... | collective-permute-start | bytes 983048 | tf_op jit(solution)/shard_map/ppermute | solution.py:107
  418.5 25.8 %collective-permute-start.60 = (bf16[128,1280]{1,0:T(8,128)(2,1)S(1)}, bf16[128,1280]{1,0:T(8,128)(2,1)S(1)}, u32[]{:S(2)}, u32[]{:S(2)}) collective-permute-start(bf16[128,1280]{1,0:T(8,128)(2,1)S(1)} %get-tuple-element.193), channel_id=1, source_target_pairs={{2,0},{3,1},{0,2},{1,3},{10,4},{11,5},{8,6},{9,7},{6,8},{7,9},{4,1... | collective-permute-start | bytes 983048 | tf_op jit(solution)/shard_map/ppermute | solution.py:107
  419.3 24.3 %collective-permute-start.63 = (bf16[2,80,483]{2,1,0:T(8,128)(2,1)S(1)}, bf16[2,80,483]{2,1,0:T(8,128)(2,1)S(1)}, u32[]{:S(2)}, u32[]{:S(2)}) collective-permute-start(bf16[2,80,483]{2,1,0:T(8,128)(2,1)S(1)} %get-tuple-element.196), channel_id=1, source_target_pairs={{0,4},{1,5},{2,6},{3,7},{4,0},{5,1},{6,2},{7,3},{8,12},{9,13},{10,... | collective-permute-start | bytes 463688 | tf_op jit(solution)/shard_map/ppermute | solution.py:55
  419.3 24.3 %collective-permute-start.64 = (bf16[2,80,483]{2,1,0:T(8,128)(2,1)S(1)}, bf16[2,80,483]{2,1,0:T(8,128)(2,1)S(1)}, u32[]{:S(2)}, u32[]{:S(2)}) collective-permute-start(bf16[2,80,483]{2,1,0:T(8,128)(2,1)S(1)} %get-tuple-element.197), channel_id=1, source_target_pairs={{0,6},{1,7},{2,0},{3,1},{4,2},{5,3},{6,4},{7,5},{8,14},{9,15},{10,... | collective-permute-start | bytes 463688 | tf_op jit(solution)/shard_map/ppermute | solution.py:55
  458.6 16.4 %collective-permute-start.70 = (bf16[4,2,80,483]{3,2,1,0:T(8,128)(2,1)}, bf16[4,2,80,483]{3,2,1,0:T(8,128)(2,1)}, u32[]{:S(2)}, u32[]{:S(2)}) collective-permute-start(bf16[4,2,80,483]{3,2,1,0:T(8,128)(2,1)} %pad_maximum_fusion), channel_id=1, source_target_pairs={{0,16},{1,17},{2,18},{3,19},{4,20},{5,21},{6,22},{7,23},{8,24},{9,... | collective-permute-start | bytes 1854728 | tf_op jit(solution)/shard_map/ppermute | solution.py:55
  460.4 21.9 %collective-permute-start.65 = (bf16[128,1280]{1,0:T(8,128)(2,1)}, bf16[128,1280]{1,0:T(8,128)(2,1)S(1)}, u32[]{:S(2)}, u32[]{:S(2)}) collective-permute-start(bf16[128,1280]{1,0:T(8,128)(2,1)} %get-tuple-element.199.refs_4_), channel_id=1, source_target_pairs={{8,0},{9,1},{10,2},{11,3},{0,4},{1,5},{2,6},{3,7},{12,8},{13,9},{1... | collective-permute-start | bytes 983048 | tf_op jit(solution)/shard_map/ppermute | solution.py:107
  461.0 21.4 %collective-permute-start.66 = (bf16[128,1280]{1,0:T(8,128)(2,1)}, bf16[128,1280]{1,0:T(8,128)(2,1)S(1)}, u32[]{:S(2)}, u32[]{:S(2)}) collective-permute-start(bf16[128,1280]{1,0:T(8,128)(2,1)} %copy-done.99), channel_id=1, source_target_pairs={{10,0},{11,1},{8,2},{9,3},{2,4},{3,5},{0,6},{1,7},{14,8},{15,9},{1... | collective-permute-start | bytes 983048 | tf_op jit(solution)/shard_map/ppermute | solution.py:107
  (139 other events, 934.5 us)

commit v5 on v3

--- a/solution.py
+++ b/solution.py
@@ -81,7 +81,7 @@
             moves += [(0, (i, self.c), 0, i), (0, (i, 1 - self.c), 1, i)]
         own, give = shuffle([halves], [(shape, BF16)] * 2, moves, after)
         got = self.send(give, dc=1)
-        after = yield
+        after = yield got
         parts = route_parts(self, own, got, after or ())
         received = [parts[0]] + [self.send(parts[d], da=d) for d in range(1, self.a_size)]
         moves = [(d, None, 0, (self.a - d) % self.a_size) for d in range(self.a_size)]
@@ -1244,15 +1244,17 @@
         near = at.send(chunks, db=db) if db else chunks
         ready = later(near, *early) if db else near
         parts += [near, at.send(ready, dc=1)]
-    stage = at.to_cluster(cotangent, sources[at.a_size : at.a_size + 1])
-    next(stage)
+    stage = at.to_cluster(cotangent)
+    soon = [next(stage), at.send(doc_lengths, dc=1)]
     quarter = quarter_of(at, (out_weight, up_weight, down_weight), sources[1 : at.a_size])
     pieces = [quarter] + [at.send(quarter, da=d) for d in range(1, at.a_size)]
-    *w_heads, w_pad, vectors = pad_weights(at, sources, heads, groups, parts[1:])
+    *w_heads, w_pad, vectors = pad_weights(
+        at, sources, heads, groups, [*parts[1:], *soon]
+    )
     vectors = vectors.T.astype(F32)
     g_attn, g_mlp, b_query, b_value = vectors[0], vectors[1], vectors[2], vectors[3]
 
-    other_lengths = at.send(doc_lengths, dc=1)
+    other_lengths = soon[1]
     lengths = pick(jnp.where(at.c == at.a // seqs, doc_lengths, other_lengths), at.a % seqs)
     ends = jnp.cumsum(lengths)
     places = jnp.arange(length, dtype=jnp.int32)
@@ -1381,13 +1383,13 @@
     keep(1, give(1))
     reduce_second.over_a()
     back(0)
-    parts = to_peers(at, [first, reduce_second.by_b()])
+    parts = to_peers(at, [first, reduce_second.by_b(keeps[1][1:])])
     back(1)
     *grads_full, grad_gain_mlp = finish_full(at, full_parts, up_weight, gain_mlp, [])
     output = next(stage)
-    input_grad = at.place_back(received)
     weights = (query_weight, key_weight, value_weight)
     *grads_heads, grad_gain_attn, few = finish_heads(at, parts, weights, gain_attn, 3)
+    input_grad = at.place_back(received)
     grad_scale = few[:HEAD_DIM, 2] / scale_dim * (LOG_BASE / math.sqrt(HEAD_DIM))
     grad_scale = grad_scale * jax.nn.sigmoid(dim_scale)
     return (

time: 492 us -> 482 us (0.980)
  starting transfers between devices: 69.8 us -> 62.2 us
    ppermute x4, waiting for transfers between devices: 13 us -> 4.43 us  [send_back(): lax.ppermute(part, AXES, [(j, i) for i, j in self.route(self._match(m))])]
    ppermute x67, starting transfers between devices: 62.8 us -> 55.7 us  [send(): lax.ppermute(value, AXES, self.route(lambda x, c, a, b: ((x + dx) % self....]
    ppermute x67, waiting for transfers between devices: 132 us -> 137 us  [send(): lax.ppermute(value, AXES, self.route(lambda x, c, a, b: ((x + dx) % self....]
    unnamed x265 -> x251, local copies, waits for them, and re-layouts: 62.4 us -> 60.1 us
  transfers between devices with their start and end apart: 71 -> 71, of which waited for: 31 -> 31; matrix products, arithmetic and copies ran while one was open for 2% -> 3% of each run, Pallas kernels for 26% -> 27%
where the time goes in v5:
time: 482 us; the launch traced here: 473 us
  Pallas kernels  193 us (40%)
  waiting for transfers between devices  142 us (29%)
  local copies, waits for them, and re-layouts  68.6 us (14%)
  starting transfers between devices  62.2 us (13%)
    pallas_call x41, Pallas kernels, call(): pl.pallas_call(run, out_shape=[jax.ShapeDtypeStruct(shape, kind) for shap...  193 us
    ppermute x67, waiting for transfers between devices, send(): lax.ppermute(value, AXES, self.route(lambda x, c, a, b: ((x + dx) % self....  137 us
    unnamed x251, local copies, waits for them, and re-layouts  60.1 us
    ppermute x67, starting transfers between devices, send(): lax.ppermute(value, AXES, self.route(lambda x, c, a, b: ((x + dx) % self....  55.7 us
  transfers between devices with their start and end apart: 71, of which 31 were waited for; matrix products, arithmetic and copies ran while one was open for 3% of the time, Pallas kernels for 27%

profile of v5, /device:TPU:9, one launch (start us, length us, event | category | flops | bytes accessed | tf_op | source)
XLA Modules:
  0.0 472.9 jit_solution(385336158214227606)
XLA Ops:
  13.0 3.1 collective-permute-done.5.refs_1_
  17.2 20.0 %collective-permute-done.3.refs_2_ = bf16[128,1280]{1,0:T(8,128)(2,1)S(1)} collective-permute-done((bf16[128,1280]{1,0:T(8,128)(2,1)S(1)}, bf16[128,1280]{1,0:T(8,128)(2,1)S(1)}, u32[]{:S(2)}, u32[]{:S(2)}) %collective-permute-start.3) | collective-permute-done | bytes 327712 | tf_op jit(solution)/shard_map/ppermute | solution.py:55
  37.2 2.5 collective-permute-done.4.refs_3_
  44.1 6.5 %collective-permute-done.9.refs_4_.refs_1_ = bf16[2,80,964]{2,1,0:T(8,128)(2,1)S(1)} collective-permute-done((bf16[2,80,964]{2,1,0:T(8,128)(2,1)S(1)}, bf16[2,80,964]{2,1,0:T(8,128)(2,1)S(1)}, u32[]{:S(2)}, u32[]{:S(2)}) %collective-permute-start.9) | collective-permute-done | bytes 308512 | tf_op jit(solution)/shard_map/ppermute | solution.py:55
  51.8 7.7 %collective-permute-done.11.refs_6_.refs_3_ = bf16[2,80,964]{2,1,0:T(8,128)(2,1)S(1)} collective-permute-done((bf16[2,80,964]{2,1,0:T(8,128)(2,1)S(1)}, bf16[2,80,964]{2,1,0:T(8,128)(2,1)S(1)}, u32[]{:S(2)}, u32[]{:S(2)}) %collective-permute-start.11) | collective-permute-done | bytes 308512 | tf_op jit(solution)/shard_map/ppermute | solution.py:55
  61.6 8.0 %collective-permute-done.8.refs_5_.refs_2_ = bf16[2,80,964]{2,1,0:T(8,128)(2,1)} collective-permute-done((bf16[2,80,964]{2,1,0:T(8,128)(2,1)S(1)}, bf16[2,80,964]{2,1,0:T(8,128)(2,1)}, u32[]{:S(2)}, u32[]{:S(2)}) %collective-permute-start.8) | collective-permute-done | bytes 308512 | tf_op jit(solution)/shard_map/ppermute | solution.py:55
  84.7 6.4 %collective-permute-done.15.refs_6_ = bf16[2,80,964]{2,1,0:T(8,128)(2,1)} collective-permute-done((bf16[2,80,964]{2,1,0:T(8,128)(2,1)}, bf16[2,80,964]{2,1,0:T(8,128)(2,1)}, u32[]{:S(2)}, u32[]{:S(2)}) %collective-permute-start.15) | collective-permute-done | bytes 308512 | tf_op jit(solution)/shard_map/ppermute | solution.py:55
  91.2 3.2 collective-permute-start.18
  96.4 4.5 pad_weights.1
  106.5 13.0 %project.1 = (bf16[2048,1536]{1,0:T(8,128)(2,1)S(1)}, bf16[2048,1280]{1,0:T(8,128)(2,1)S(1)}) custom-call(s32[4]{0:T(128)S(1)} %pad_add_fusion.2.spots, bf16[4,128,1280]{2,1,0:T(8,128)(2,1)S(1)} %shuffle.11.refs_1_.refs_0_.refs_2_, bf16[4,128,1280]{2,1,0:T(8,128)(2,1)} %collective-permute-done.6.refs_9_.refs_1_, ...), custom_call_target="tpu_custom_call" | custom-call | flops 3987500032 | bytes 11962500 | tf_op jit(solution)/shard_map/project/pallas_call | solution.py:167
  121.9 4.3 shuffle.13.refs_2_.refs_4_
  136.7 2.8 copy-done.1
  139.5 21.2 %attend_forward.1 = (bf16[2,2,4,128,320]{4,3,2,1,0:T(8,128)(2,1)S(1)}, bf16[2048,512]{1,0:T(8,128)(2,1)S(1)}) custom-call(s32[10]{0:T(128)S(1)} %pad_add_fusion.1.spots, s32[2048,128]{1,0:T(8,128)S(1)} %broadcast_in_dim.58.refs_0_, bf16[2048,1536]{1,0:T(8,128)(2,1)S(1)} %copy-done.1, bf16[2048,1536]{1,0:T(8,128)(2,1)S(1)} %copy-done.1, ...), custom_call_target="tpu_custom_call" | custom-call | flops 3300000000 | bytes 9900000 | tf_op jit(solution)/shard_map/attend_forward/pallas_call | solution.py:167
  167.7 8.7 %collective-permute-done.26.refs_3_ = bf16[512,320]{1,0:T(8,128)(2,1)S(1)} collective-permute-done((bf16[512,320]{1,0:T(8,128)(2,1)S(1)}, bf16[512,320]{1,0:T(8,128)(2,1)S(1)}, u32[]{:S(2)}, u32[]{:S(2)}) %collective-permute-start.26) | collective-permute-done | bytes 327712 | tf_op jit(solution)/shard_map/ppermute | solution.py:55
  176.4 9.0 %collective-permute-done.25.refs_2_ = bf16[512,320]{1,0:T(8,128)(2,1)S(1)} collective-permute-done((bf16[512,320]{1,0:T(8,128)(2,1)S(1)}, bf16[512,320]{1,0:T(8,128)(2,1)S(1)}, u32[]{:S(2)}, u32[]{:S(2)}) %collective-permute-start.25) | collective-permute-done | bytes 327712 | tf_op jit(solution)/shard_map/ppermute | solution.py:55
  187.3 4.2 collective-permute-done.29.refs_8_
  196.3 20.0 %middle.1 = (bf16[512,1280]{1,0:T(8,128)(2,1)}, f32[512,1280]{1,0:T(8,128)}, bf16[512,1280]{1,0:T(8,128)(2,1)}, bf16[512,1280]{1,0:T(8,128)(2,1)}, bf16[512,1280...) custom-call(s32[192]{0:T(256)S(1)} %stack.264.spots, ...), custom_call_target="tpu_custom_call" | custom-call | flops 5500000256 | bytes 16500000 | tf_op jit(solution)/shard_map/middle/pallas_call | solution.py:167
  217.0 8.5 %outer_give.1.refs_7_ = bf16[3,1280,640]{2,1,0:T(8,128)(2,1)} custom-call(s32[7]{0:T(128)} %stack.289.spots, bf16[512,1280]{1,0:T(8,128)(2,1)} %copy-done.22, bf16[512,1280]{1,0:T(8,128)(2,1)} %get-tuple-element.142.refs_1_, bf16[512,1280]{1,0:T(8,128)(2,1)} %get-tuple-element.143.refs_2_, bf16[512,1280]{1,0:T(8,128)(2,1)} %get-tuple-element.144.refs_3_, ...), custom_call_target="tpu_custom_call" | custom-call | flops 27500000 | bytes 82500 | tf_op jit(solution)/shard_map/outer_give/pallas_call | solution.py:167
  231.3 5.3 %collective-permute-done.35 = bf16[512,320]{1,0:T(8,128)(2,1)S(1)} collective-permute-done((bf16[512,320]{1,0:T(8,128)(2,1)}, bf16[512,320]{1,0:T(8,128)(2,1)S(1)}, u32[]{:S(2)}, u32[]{:S(2)}) %collective-permute-start.35) | collective-permute-done | bytes 327712 | tf_op jit(solution)/shard_map/ppermute | solution.py:55
  236.6 8.9 %collective-permute-done.36 = bf16[512,320]{1,0:T(8,128)(2,1)S(1)} collective-permute-done((bf16[512,320]{1,0:T(8,128)(2,1)S(1)}, bf16[512,320]{1,0:T(8,128)(2,1)S(1)}, u32[]{:S(2)}, u32[]{:S(2)}) %collective-permute-start.36) | collective-permute-done | bytes 327712 | tf_op jit(solution)/shard_map/ppermute | solution.py:55
  246.3 9.9 %outer.1 = (bf16[3,2,2,80,640]{4,3,2,1,0:T(8,128)(2,1)}, bf16[3,2,2,80,640]{4,3,2,1,0:T(8,128)(2,1)}, bf16[3,2,2,80,640]{4,3,2,1,0:T(8,128)(2,1)}, bf16[3,2,2,80,640]{4,3,2,1,0:T(8,128)(2,1)}) custom-call(s32[7]{0:T(128)} %stack.288.spots, bf16[512,1280]{1,0:T(8,128)(2,1)} %copy-done.22, bf16[512,1280]{1,0:T(8,128)(2,1)} %get-tuple-element.142.refs_1_, ...), custom_call_target="tpu_custom_call" | custom-call | flops 1924999936 | bytes 5775000 | tf_op jit(solution)/shard_map/outer/pallas_call | solution.py:167
  263.5 2.8 copy-done.2
  269.8 20.6 %attend_backward.2 = (bf16[2048,480]{1,0:T(8,128)(2,1)S(1)}, f32[8,128]{1,0:T(8,128)S(1)}, f32[8,768]{1,0:T(8,128)S(1)}) custom-call(s32[10]{0:T(128)S(1)} %pad_add_fusion.1.spots, s32[8,2048]{1,0:T(8,128)S(1)} %broadcast_in_dim.61.refs_0_, f32[8,256]{1,0:T(8,128)S(1)} %broadcast_in_dim.63.refs_1_, bf16[2048,512]{1,0:T(8,128)(2,1)S(1)} %copy-done.103, ...), custom_call_target="tpu_custom_call" | custom-call | flops 6874999808 | bytes 20625000 | tf_op jit(solution)/shard_map/attend_backward/pallas_call | solution.py:167
  293.0 2.9 route_back.1
  295.9 3.6 add_blocks.6
  306.7 2.5 copy-done.16
  311.3 4.8 %heads_outer.2 = (bf16[4,2,80,483]{3,2,1,0:T(8,128)(2,1)S(1)}, bf16[4,2,80,483]{3,2,1,0:T(8,128)(2,1)S(1)}) custom-call(s32[1]{0:T(128)} %bitcast.54.spots, bf16[2048,1280]{1,0:T(8,128)(2,1)S(1)} %copy-done.16, bf16[2048,480]{1,0:T(8,128)(2,1)S(1)} %copy-done.4, bf16[1280,3]{1,0:T(8,128)(2,1)S(1)} %copy-done.51, bf16[3,2,80,640]{3,2,1,0:T(8,128)(2,1)S(1)} %copy-done.45), custom_call_target="tpu_custom_call" | custom-call | flops 1512499968 | bytes 4537500 | tf_op jit(solution)/shard_map/heads_outer/pallas_call | solution.py:167
  321.4 21.6 %attend_backward.3 = (bf16[2048,480]{1,0:T(8,128)(2,1)S(1)}, f32[8,128]{1,0:T(8,128)S(1)}, f32[8,768]{1,0:T(8,128)S(1)}) custom-call(s32[10]{0:T(128)S(1)} %pad_add_fusion.1.spots, s32[8,2048]{1,0:T(8,128)S(1)} %broadcast_in_dim.61.refs_0_, f32[8,256]{1,0:T(8,128)S(1)} %broadcast_in_dim.63.refs_1_, bf16[2048,512]{1,0:T(8,128)(2,1)S(1)} %copy-done.104, ...), custom_call_target="tpu_custom_call" | custom-call | flops 6874999808 | bytes 20625000 | tf_op jit(solution)/shard_map/attend_backward/pallas_call | solution.py:167
  344.7 4.0 collective-permute-done.47
  352.9 3.2 back_project.4.refs_3_
  363.5 2.5 copy-done.17
  367.0 4.8 %heads_outer.3 = (bf16[4,2,80,483]{3,2,1,0:T(8,128)(2,1)S(1)}, bf16[4,2,80,483]{3,2,1,0:T(8,128)(2,1)S(1)}) custom-call(s32[1]{0:T(128)} %bitcast.54.spots, bf16[2048,1280]{1,0:T(8,128)(2,1)S(1)} %copy-done.17, bf16[2048,480]{1,0:T(8,128)(2,1)S(1)} %copy-done.7, bf16[1280,3]{1,0:T(8,128)(2,1)S(1)} %copy-done.52, bf16[2,2,128,1280]{3,2,1,0:T(8,128)(2,1)} %back_project.4.refs_3_), custom_call_target="tpu_custom_call" | custom-call | flops 1512499968 | bytes 4537500 | tf_op jit(solution)/shard_map/heads_outer/pallas_call | solution.py:167
  372.5 2.5 collective-permute-done.55.refs_3_.refs_7_
  377.4 3.8 back_project.5
  381.3 3.2 back_project.6.refs_5_
  390.8 4.4 back_project.7
  396.6 4.9 %collective-permute-done.58.refs_1_.refs_3_.refs_5_.refs_7_ = bf16[4,2,80,483]{3,2,1,0:T(8,128)(2,1)} collective-permute-done((bf16[4,2,80,483]{3,2,1,0:T(8,128)(2,1)}, bf16[4,2,80,483]{3,2,1,0:T(8,128)(2,1)}, u32[]{:S(2)}, u32[]{:S(2)}) %collective-permute-start.58) | collective-permute-done | bytes 618272 | tf_op jit(solution)/shard_map/ppermute | solution.py:55
  408.6 2.9 norm_back.2
  411.4 8.2 %collective-permute-done.60.refs_2_.refs_6_ = bf16[2,80,483]{2,1,0:T(8,128)(2,1)S(1)} collective-permute-done((bf16[2,80,483]{2,1,0:T(8,128)(2,1)S(1)}, bf16[2,80,483]{2,1,0:T(8,128)(2,1)S(1)}, u32[]{:S(2)}, u32[]{:S(2)}) %collective-permute-start.60) | collective-permute-done | bytes 154592 | tf_op jit(solution)/shard_map/ppermute | solution.py:55
  419.6 2.6 collective-permute-done.61.refs_3_.refs_7_
  425.4 3.9 collective-permute-done.68.refs_2_
  429.3 3.7 collective-permute-done.69.refs_3_
  436.9 3.2 collective-permute-start.63
  445.6 3.4 finish_full.1
  452.9 2.7 shuffle.16.refs_9_
  457.0 5.1 %finish_heads.1 = (f32[160,1280]{1,0:T(8,128)}, f32[160,1280]{1,0:T(8,128)}, f32[160,1280]{1,0:T(8,128)}, f32[160,1]{1,0:T(8,128)S(1)}, f32[160,3]{1,0:T(8,128)S(1)}) custom-call(s32[5]{0:T(128)S(1)} %stack.317.spots, bf16[2,80,483]{2,1,0:T(8,128)(2,1)S(1)} %get-tuple-element.199.refs_5_.refs_0_, bf16[2,80,483]{2,1,0:T(8,128)(2,1)S(1)} %copy-done.95, ...), custom_call_target="tpu_custom_call" | custom-call | flops 1100000000 | bytes 3300000 | tf_op jit(solution)/shard_map/finish_heads/pallas_call | solution.py:167
  464.3 4.4 collective-permute-done.66.refs_3_
  469.8 2.6 shuffle.17
  (487 shorter events, 157.8 us)
Async XLA Ops:
  9.2 28.0 %collective-permute-start.3 = (bf16[128,1280]{1,0:T(8,128)(2,1)S(1)}, bf16[128,1280]{1,0:T(8,128)(2,1)S(1)}, u32[]{:S(2)}, u32[]{:S(2)}) collective-permute-start(bf16[128,1280]{1,0:T(8,128)(2,1)S(1)} %get-tuple-element.118), channel_id=1, source_target_pairs={{0,4},{1,5},{2,6},{3,7},{4,0},{5,1},{6,2},{7,3},{8,12},{9,13},{10,... | collective-permute-start | bytes 983048 | tf_op jit(solution)/shard_map/ppermute | solution.py:55
  10.2 29.5 %collective-permute-start.4 = (bf16[128,1280]{1,0:T(8,128)(2,1)S(1)}, bf16[128,1280]{1,0:T(8,128)(2,1)S(1)}, u32[]{:S(2)}, u32[]{:S(2)}) collective-permute-start(bf16[128,1280]{1,0:T(8,128)(2,1)S(1)} %get-tuple-element.119), channel_id=1, source_target_pairs={{0,6},{1,7},{2,0},{3,1},{4,2},{5,3},{6,4},{7,5},{8,14},{9,15},{10,... | collective-permute-start | bytes 983048 | tf_op jit(solution)/shard_map/ppermute | solution.py:55
  40.7 30.4 %collective-permute-start.7 = (bf16[4,128,1280]{2,1,0:T(8,128)(2,1)S(1)}, bf16[4,128,1280]{2,1,0:T(8,128)(2,1)}, u32[]{:S(2)}, u32[]{:S(2)}) collective-permute-start(bf16[4,128,1280]{2,1,0:T(8,128)(2,1)S(1)} %shuffle.11.refs_1_.refs_0_.refs_2_), channel_id=1, source_target_pairs={{0,1},{1,0},{2,3},{3,2},{4,5},{5,4},{6,7},{7,6},{8,9},{9,8},{10,11... | collective-permute-start | bytes 3932168 | tf_op jit(solution)/shard_map/ppermute | solution.py:55
  42.0 17.5 %collective-permute-start.11 = (bf16[2,80,964]{2,1,0:T(8,128)(2,1)S(1)}, bf16[2,80,964]{2,1,0:T(8,128)(2,1)S(1)}, u32[]{:S(2)}, u32[]{:S(2)}) collective-permute-start(bf16[2,80,964]{2,1,0:T(8,128)(2,1)S(1)} %shuffle.10.refs_4_.refs_0_), channel_id=1, source_target_pairs={{0,6},{1,7},{2,0},{3,1},{4,2},{5,3},{6,4},{7,5},{8,14},{9,15},{10,... | collective-permute-start | bytes 925448 | tf_op jit(solution)/shard_map/ppermute | solution.py:55
  43.4 26.2 %collective-permute-start.8 = (bf16[2,80,964]{2,1,0:T(8,128)(2,1)S(1)}, bf16[2,80,964]{2,1,0:T(8,128)(2,1)}, u32[]{:S(2)}, u32[]{:S(2)}) collective-permute-start(bf16[2,80,964]{2,1,0:T(8,128)(2,1)S(1)} %shuffle.10.refs_4_.refs_0_), channel_id=1, source_target_pairs={{0,4},{1,5},{2,6},{3,7},{4,0},{5,1},{6,2},{7,3},{8,12},{9,13},{10,... | collective-permute-start | bytes 925448 | tf_op jit(solution)/shard_map/ppermute | solution.py:55
  50.6 19.1 %collective-permute-start.10 = (bf16[2,80,964]{2,1,0:T(8,128)(2,1)S(1)}, bf16[2,80,964]{2,1,0:T(8,128)(2,1)S(1)}, u32[]{:S(2)}, u32[]{:S(2)}) collective-permute-start(bf16[2,80,964]{2,1,0:T(8,128)(2,1)S(1)} %collective-permute-done.9.refs_4_.refs_1_), channel_id=1, source_target_pairs={{0,16},{1,17},{2,18},{3,19},{4,20},{5,21},{6,22},{7,23},{8,24},{9,... | collective-permute-start | bytes 925448 | tf_op jit(solution)/shard_map/ppermute | solution.py:55
  60.7 34.5 %collective-permute-start.6 = (bf16[4,128,1280]{2,1,0:T(8,128)(2,1)S(1)}, bf16[4,128,1280]{2,1,0:T(8,128)(2,1)}, u32[]{:S(2)}, u32[]{:S(2)}) collective-permute-start(bf16[4,128,1280]{2,1,0:T(8,128)(2,1)S(1)} %shuffle.11.refs_1_.refs_0_.refs_2_), channel_id=1, source_target_pairs={{0,8},{1,9},{2,10},{3,11},{4,12},{5,13},{6,14},{7,15},{8,0},{9,1},... | collective-permute-start | bytes 3932168 | tf_op jit(solution)/shard_map/ppermute | solution.py:55
  71.1 24.1 %collective-permute-start.13 = (bf16[4,128,1280]{2,1,0:T(8,128)(2,1)}, bf16[4,128,1280]{2,1,0:T(8,128)(2,1)}, u32[]{:S(2)}, u32[]{:S(2)}) collective-permute-start(bf16[4,128,1280]{2,1,0:T(8,128)(2,1)} %collective-permute-done.7.refs_10_.refs_2_), channel_id=1, source_target_pairs={{0,8},{1,9},{2,10},{3,11},{4,12},{5,13},{6,14},{7,15},{8,0},{9,1},... | collective-permute-start | bytes 3932168 | tf_op jit(solution)/shard_map/ppermute | solution.py:55
  74.2 20.2 %collective-permute-start.16 = (bf16[2,128,1280]{2,1,0:T(8,128)(2,1)}, bf16[2,128,1280]{2,1,0:T(8,128)(2,1)S(1)}, u32[]{:S(2)}, u32[]{:S(2)}) collective-permute-start(bf16[2,128,1280]{2,1,0:T(8,128)(2,1)} %get-tuple-element.123), channel_id=1, source_target_pairs={{0,8},{1,9},{2,10},{3,11},{4,12},{5,13},{6,14},{7,15},{8,0},{9,1},... | collective-permute-start | bytes 1966088 | tf_op jit(solution)/shard_map/ppermute | solution.py:55
  76.0 15.2 %collective-permute-start.15 = (bf16[2,80,964]{2,1,0:T(8,128)(2,1)}, bf16[2,80,964]{2,1,0:T(8,128)(2,1)}, u32[]{:S(2)}, u32[]{:S(2)}) collective-permute-start(bf16[2,80,964]{2,1,0:T(8,128)(2,1)} %collective-permute-done.8.refs_5_.refs_2_), channel_id=1, source_target_pairs={{0,16},{1,17},{2,18},{3,19},{4,20},{5,21},{6,22},{7,23},{8,24},{9,... | collective-permute-start | bytes 925448 | tf_op jit(solution)/shard_map/ppermute | solution.py:55
  84.1 37.7 %collective-permute-start.17 = (bf16[3,80,640]{2,1,0:T(8,128)(2,1)S(1)}, bf16[3,80,640]{2,1,0:T(8,128)(2,1)}, u32[]{:S(2)}, u32[]{:S(2)}) collective-permute-start(bf16[3,80,640]{2,1,0:T(8,128)(2,1)S(1)} %quarter.1.refs_8_.refs_0_), channel_id=1, source_target_pairs={{0,2},{1,3},{2,4},{3,5},{4,6},{5,7},{6,0},{7,1},{8,10},{9,11},{10,... | collective-permute-start | bytes 921608 | tf_op jit(solution)/shard_map/ppermute | solution.py:55
  91.2 30.7 %collective-permute-start.18 = (bf16[3,80,640]{2,1,0:T(8,128)(2,1)S(1)}, bf16[3,80,640]{2,1,0:T(8,128)(2,1)}, u32[]{:S(2)}, u32[]{:S(2)}) collective-permute-start(bf16[3,80,640]{2,1,0:T(8,128)(2,1)S(1)} %quarter.1.refs_8_.refs_0_), channel_id=1, source_target_pairs={{0,4},{1,5},{2,6},{3,7},{4,0},{5,1},{6,2},{7,3},{8,12},{9,13},{10,... | collective-permute-start | bytes 921608 | tf_op jit(solution)/shard_map/ppermute | solution.py:55
  95.2 26.7 %collective-permute-start.19 = (bf16[3,80,640]{2,1,0:T(8,128)(2,1)S(1)}, bf16[3,80,640]{2,1,0:T(8,128)(2,1)}, u32[]{:S(2)}, u32[]{:S(2)}) collective-permute-start(bf16[3,80,640]{2,1,0:T(8,128)(2,1)S(1)} %quarter.1.refs_8_.refs_0_), channel_id=1, source_target_pairs={{0,6},{1,7},{2,0},{3,1},{4,2},{5,3},{6,4},{7,5},{8,14},{9,15},{10,... | collective-permute-start | bytes 921608 | tf_op jit(solution)/shard_map/ppermute | solution.py:55
  127.4 36.1 %collective-permute-start.27 = (bf16[4,3,80,640]{3,2,1,0:T(8,128)(2,1)}, bf16[4,3,80,640]{3,2,1,0:T(8,128)(2,1)}, u32[]{:S(2)}, u32[]{:S(2)}) collective-permute-start(bf16[4,3,80,640]{3,2,1,0:T(8,128)(2,1)} %shuffle.13.refs_2_.refs_4_), channel_id=1, source_target_pairs={{0,1},{1,0},{2,3},{3,2},{4,5},{5,4},{6,7},{7,6},{8,9},{9,8},{10,11... | collective-permute-start | bytes 3686408 | tf_op jit(solution)/shard_map/ppermute | solution.py:55
  131.1 29.7 %collective-permute-start.21 = (bf16[128,1280]{1,0:T(8,128)(2,1)S(1)}, bf16[128,1280]{1,0:T(8,128)(2,1)S(1)}, u32[]{:S(2)}, u32[]{:S(2)}) collective-permute-start(bf16[128,1280]{1,0:T(8,128)(2,1)S(1)} %get-tuple-element.130), channel_id=1, source_target_pairs={{0,2},{1,3},{2,4},{3,5},{4,6},{5,7},{6,0},{7,1},{8,10},{9,11},{10,... | collective-permute-start | bytes 983048 | tf_op jit(solution)/shard_map/ppermute | solution.py:55
  132.9 27.9 %collective-permute-start.22 = (bf16[128,1280]{1,0:T(8,128)(2,1)S(1)}, bf16[128,1280]{1,0:T(8,128)(2,1)S(1)}, u32[]{:S(2)}, u32[]{:S(2)}) collective-permute-start(bf16[128,1280]{1,0:T(8,128)(2,1)S(1)} %get-tuple-element.131), channel_id=1, source_target_pairs={{0,4},{1,5},{2,6},{3,7},{4,0},{5,1},{6,2},{7,3},{8,12},{9,13},{10,... | collective-permute-start | bytes 983048 | tf_op jit(solution)/shard_map/ppermute | solution.py:55
  134.4 28.2 %collective-permute-start.23 = (bf16[128,1280]{1,0:T(8,128)(2,1)S(1)}, bf16[128,1280]{1,0:T(8,128)(2,1)S(1)}, u32[]{:S(2)}, u32[]{:S(2)}) collective-permute-start(bf16[128,1280]{1,0:T(8,128)(2,1)S(1)} %get-tuple-element.132), channel_id=1, source_target_pairs={{0,6},{1,7},{2,0},{3,1},{4,2},{5,3},{6,4},{7,5},{8,14},{9,15},{10,... | collective-permute-start | bytes 983048 | tf_op jit(solution)/shard_map/ppermute | solution.py:55
  135.1 51.6 %collective-permute-start.28 = (bf16[4,3,80,640]{3,2,1,0:T(8,128)(2,1)}, bf16[4,3,80,640]{3,2,1,0:T(8,128)(2,1)}, u32[]{:S(2)}, u32[]{:S(2)}) collective-permute-start(bf16[4,3,80,640]{3,2,1,0:T(8,128)(2,1)} %shuffle.13.refs_2_.refs_4_), channel_id=1, source_target_pairs={{0,16},{1,17},{2,18},{3,19},{4,20},{5,21},{6,22},{7,23},{8,24},{9,... | collective-permute-start | bytes 3686408 | tf_op jit(solution)/shard_map/ppermute | solution.py:55
  163.6 27.9 %collective-permute-start.29 = (bf16[4,3,80,640]{3,2,1,0:T(8,128)(2,1)}, bf16[4,3,80,640]{3,2,1,0:T(8,128)(2,1)}, u32[]{:S(2)}, u32[]{:S(2)}) collective-permute-start(bf16[4,3,80,640]{3,2,1,0:T(8,128)(2,1)} %collective-permute-done.27.refs_6_), channel_id=1, source_target_pairs={{0,16},{1,17},{2,18},{3,19},{4,20},{5,21},{6,22},{7,23},{8,24},{9,... | collective-permute-start | bytes 3686408 | tf_op jit(solution)/shard_map/ppermute | solution.py:55
  166.5 18.9 %collective-permute-start.25 = (bf16[512,320]{1,0:T(8,128)(2,1)S(1)}, bf16[512,320]{1,0:T(8,128)(2,1)S(1)}, u32[]{:S(2)}, u32[]{:S(2)}) collective-permute-start(bf16[512,320]{1,0:T(8,128)(2,1)S(1)} %bitcast.162), channel_id=1, source_target_pairs={{0,1},{1,0},{2,3},{3,2},{4,5},{5,4},{6,7},{7,6},{8,9},{9,8},{10,11... | collective-permute-start | bytes 983048 | tf_op jit(solution)/shard_map/ppermute | solution.py:55
  167.7 17.6 %collective-permute-start.24 = (bf16[512,320]{1,0:T(8,128)(2,1)S(1)}, bf16[512,320]{1,0:T(8,128)(2,1)S(1)}, u32[]{:S(2)}, u32[]{:S(2)}) collective-permute-start(bf16[512,320]{1,0:T(8,128)(2,1)S(1)} %bitcast.161), channel_id=1, source_target_pairs={{0,8},{1,9},{2,10},{3,11},{4,12},{5,13},{6,14},{7,15},{8,0},{9,1},... | collective-permute-start | bytes 983048 | tf_op jit(solution)/shard_map/ppermute | solution.py:55
  225.5 20.0 %collective-permute-start.33 = (bf16[3,1280,640]{2,1,0:T(8,128)(2,1)}, bf16[3,1280,640]{2,1,0:T(8,128)(2,1)}, u32[]{:S(2)}, u32[]{:S(2)}) collective-permute-start(bf16[3,1280,640]{2,1,0:T(8,128)(2,1)} %outer_give.1.refs_7_), channel_id=1, source_target_pairs={{0,8},{1,9},{2,10},{3,11},{4,12},{5,13},{6,14},{7,15},{8,0},{9,1},... | collective-permute-start | bytes 14745608 | tf_op jit(solution)/shard_map/ppermute | solution.py:55
  226.2 19.3 %collective-permute-start.36 = (bf16[512,320]{1,0:T(8,128)(2,1)S(1)}, bf16[512,320]{1,0:T(8,128)(2,1)S(1)}, u32[]{:S(2)}, u32[]{:S(2)}) collective-permute-start(bf16[512,320]{1,0:T(8,128)(2,1)S(1)} %get-tuple-element.149), channel_id=1, source_target_pairs={{0,9},{1,8},{2,11},{3,10},{4,13},{5,12},{6,15},{7,14},{8,1},{9,0},... | collective-permute-start | bytes 983048 | tf_op jit(solution)/shard_map/ppermute | solution.py:55
  256.2 39.7 %collective-permute-start.41 = (bf16[3,2,2,80,640]{4,3,2,1,0:T(8,128)(2,1)}, bf16[3,2,2,80,640]{4,3,2,1,0:T(8,128)(2,1)}, u32[]{:S(2)}, u32[]{:S(2)}) collective-permute-start(bf16[3,2,2,80,640]{4,3,2,1,0:T(8,128)(2,1)} %get-tuple-element.159), channel_id=1, source_target_pairs={{0,16},{1,17},{2,18},{3,19},{4,20},{5,21},{6,22},{7,23},{8,24},{9,... | collective-permute-start | bytes 3686408 | tf_op jit(solution)/shard_map/ppermute | solution.py:55
  257.4 38.5 %collective-permute-start.42 = (bf16[3,2,2,80,640]{4,3,2,1,0:T(8,128)(2,1)}, bf16[3,2,2,80,640]{4,3,2,1,0:T(8,128)(2,1)}, u32[]{:S(2)}, u32[]{:S(2)}) collective-permute-start(bf16[3,2,2,80,640]{4,3,2,1,0:T(8,128)(2,1)} %get-tuple-element.161), channel_id=1, source_target_pairs={{0,1},{1,0},{2,3},{3,2},{4,5},{5,4},{6,7},{7,6},{8,9},{9,8},{10,11... | collective-permute-start | bytes 3686408 | tf_op jit(solution)/shard_map/ppermute | solution.py:55
  260.6 30.0 %collective-permute-start.37 = (bf16[128,1280]{1,0:T(8,128)(2,1)}, bf16[128,1280]{1,0:T(8,128)(2,1)}, u32[]{:S(2)}, u32[]{:S(2)}) collective-permute-start(bf16[128,1280]{1,0:T(8,128)(2,1)} %get-tuple-element.152), channel_id=1, source_target_pairs={{0,2},{1,3},{2,4},{3,5},{4,6},{5,7},{6,0},{7,1},{8,10},{9,11},{10,... | collective-permute-start | bytes 983048 | tf_op jit(solution)/shard_map/ppermute | solution.py:55
  260.7 29.9 %collective-permute-start.38 = (bf16[128,1280]{1,0:T(8,128)(2,1)}, bf16[128,1280]{1,0:T(8,128)(2,1)}, u32[]{:S(2)}, u32[]{:S(2)}) collective-permute-start(bf16[128,1280]{1,0:T(8,128)(2,1)} %get-tuple-element.153), channel_id=1, source_target_pairs={{0,4},{1,5},{2,6},{3,7},{4,0},{5,1},{6,2},{7,3},{8,12},{9,13},{10,... | collective-permute-start | bytes 983048 | tf_op jit(solution)/shard_map/ppermute | solution.py:55
  262.4 29.6 %collective-permute-start.39 = (bf16[128,1280]{1,0:T(8,128)(2,1)}, bf16[128,1280]{1,0:T(8,128)(2,1)}, u32[]{:S(2)}, u32[]{:S(2)}) collective-permute-start(bf16[128,1280]{1,0:T(8,128)(2,1)} %get-tuple-element.154), channel_id=1, source_target_pairs={{0,6},{1,7},{2,0},{3,1},{4,2},{5,3},{6,4},{7,5},{8,14},{9,15},{10,... | collective-permute-start | bytes 983048 | tf_op jit(solution)/shard_map/ppermute | solution.py:55
  301.2 15.6 %collective-permute-start.43 = (bf16[3,2,80,640]{3,2,1,0:T(8,128)(2,1)}, bf16[3,2,80,640]{3,2,1,0:T(8,128)(2,1)}, u32[]{:S(2)}, u32[]{:S(2)}) collective-permute-start(bf16[3,2,80,640]{3,2,1,0:T(8,128)(2,1)} %get-tuple-element.163), channel_id=1, source_target_pairs={{0,1},{1,0},{2,3},{3,2},{4,5},{5,4},{6,7},{7,6},{8,9},{9,8},{10,11... | collective-permute-start | bytes 1843208 | tf_op jit(solution)/shard_map/ppermute | solution.py:55
  302.5 14.9 %collective-permute-start.44 = (bf16[3,2,80,640]{3,2,1,0:T(8,128)(2,1)}, bf16[3,2,80,640]{3,2,1,0:T(8,128)(2,1)}, u32[]{:S(2)}, u32[]{:S(2)}) collective-permute-start(bf16[3,2,80,640]{3,2,1,0:T(8,128)(2,1)} %get-tuple-element.165), channel_id=1, source_target_pairs={{0,16},{1,17},{2,18},{3,19},{4,20},{5,21},{6,22},{7,23},{8,24},{9,... | collective-permute-start | bytes 1843208 | tf_op jit(solution)/shard_map/ppermute | solution.py:55
  316.1 34.1 %collective-permute-start.51 = (bf16[4,2,80,483]{3,2,1,0:T(8,128)(2,1)S(1)}, bf16[4,2,80,483]{3,2,1,0:T(8,128)(2,1)S(1)}, u32[]{:S(2)}, u32[]{:S(2)}) collective-permute-start(bf16[4,2,80,483]{3,2,1,0:T(8,128)(2,1)S(1)} %get-tuple-element.176), channel_id=1, source_target_pairs={{0,16},{1,17},{2,18},{3,19},{4,20},{5,21},{6,22},{7,23},{8,24},{9,... | collective-permute-start | bytes 1854728 | tf_op jit(solution)/shard_map/ppermute | solution.py:55
  319.8 23.2 %collective-permute-start.45 = (bf16[3,80,640]{2,1,0:T(8,128)(2,1)S(1)}, bf16[3,80,640]{2,1,0:T(8,128)(2,1)S(1)}, u32[]{:S(2)}, u32[]{:S(2)}) collective-permute-start(bf16[3,80,640]{2,1,0:T(8,128)(2,1)S(1)} %get-tuple-element.171), channel_id=1, source_target_pairs={{0,2},{1,3},{2,4},{3,5},{4,6},{5,7},{6,0},{7,1},{8,10},{9,11},{10,... | collective-permute-start | bytes 921608 | tf_op jit(solution)/shard_map/ppermute | solution.py:55
  319.8 24.9 %collective-permute-start.46 = (bf16[3,80,640]{2,1,0:T(8,128)(2,1)S(1)}, bf16[3,80,640]{2,1,0:T(8,128)(2,1)S(1)}, u32[]{:S(2)}, u32[]{:S(2)}) collective-permute-start(bf16[3,80,640]{2,1,0:T(8,128)(2,1)S(1)} %get-tuple-element.172), channel_id=1, source_target_pairs={{0,4},{1,5},{2,6},{3,7},{4,0},{5,1},{6,2},{7,3},{8,12},{9,13},{10,... | collective-permute-start | bytes 921608 | tf_op jit(solution)/shard_map/ppermute | solution.py:55
  321.2 27.5 %collective-permute-start.47 = (bf16[3,80,640]{2,1,0:T(8,128)(2,1)S(1)}, bf16[3,80,640]{2,1,0:T(8,128)(2,1)S(1)}, u32[]{:S(2)}, u32[]{:S(2)}) collective-permute-start(bf16[3,80,640]{2,1,0:T(8,128)(2,1)S(1)} %get-tuple-element.173), channel_id=1, source_target_pairs={{0,6},{1,7},{2,0},{3,1},{4,2},{5,3},{6,4},{7,5},{8,14},{9,15},{10,... | collective-permute-start | bytes 921608 | tf_op jit(solution)/shard_map/ppermute | solution.py:55
  356.1 21.3 %collective-permute-start.52 = (bf16[2,2,128,1280]{3,2,1,0:T(8,128)(2,1)}, bf16[2,2,128,1280]{3,2,1,0:T(8,128)(2,1)}, u32[]{:S(2)}, u32[]{:S(2)}) collective-permute-start(bf16[2,2,128,1280]{3,2,1,0:T(8,128)(2,1)} %back_project.4.refs_3_), channel_id=1, source_target_pairs={{0,8},{1,9},{2,10},{3,11},{4,12},{5,13},{6,14},{7,15},{8,0},{9,1},... | collective-permute-start | bytes 3932168 | tf_op jit(solution)/shard_map/ppermute | solution.py:55
  357.7 17.3 %collective-permute-start.48 = (bf16[3,80,640]{2,1,0:T(8,128)(2,1)}, bf16[3,80,640]{2,1,0:T(8,128)(2,1)}, u32[]{:S(2)}, u32[]{:S(2)}) collective-permute-start(bf16[3,80,640]{2,1,0:T(8,128)(2,1)} %add_blocks.7.refs_8_.refs_0_), channel_id=1, source_target_pairs={{0,16},{1,17},{2,18},{3,19},{4,20},{5,21},{6,22},{7,23},{8,24},{9,... | collective-permute-start | bytes 921608 | tf_op jit(solution)/shard_map/ppermute | solution.py:55
  358.1 14.5 %collective-permute-start.54 = (bf16[2,80,483]{2,1,0:T(8,128)(2,1)}, bf16[2,80,483]{2,1,0:T(8,128)(2,1)}, u32[]{:S(2)}, u32[]{:S(2)}) collective-permute-start(bf16[2,80,483]{2,1,0:T(8,128)(2,1)} %copy-done.111), channel_id=1, source_target_pairs={{0,4},{1,5},{2,6},{3,7},{4,0},{5,1},{6,2},{7,3},{8,12},{9,13},{10,... | collective-permute-start | bytes 463688 | tf_op jit(solution)/shard_map/ppermute | solution.py:55
  359.5 15.5 %collective-permute-start.55 = (bf16[2,80,483]{2,1,0:T(8,128)(2,1)}, bf16[2,80,483]{2,1,0:T(8,128)(2,1)}, u32[]{:S(2)}, u32[]{:S(2)}) collective-permute-start(bf16[2,80,483]{2,1,0:T(8,128)(2,1)} %copy-done.110), channel_id=1, source_target_pairs={{0,6},{1,7},{2,0},{3,1},{4,2},{5,3},{6,4},{7,5},{8,14},{9,15},{10,... | collective-permute-start | bytes 463688 | tf_op jit(solution)/shard_map/ppermute | solution.py:55
  384.9 16.6 %collective-permute-start.58 = (bf16[4,2,80,483]{3,2,1,0:T(8,128)(2,1)}, bf16[4,2,80,483]{3,2,1,0:T(8,128)(2,1)}, u32[]{:S(2)}, u32[]{:S(2)}) collective-permute-start(bf16[4,2,80,483]{3,2,1,0:T(8,128)(2,1)} %copy-done.106), channel_id=1, source_target_pairs={{0,16},{1,17},{2,18},{3,19},{4,20},{5,21},{6,22},{7,23},{8,24},{9,... | collective-permute-start | bytes 1854728 | tf_op jit(solution)/shard_map/ppermute | solution.py:55
  385.7 22.9 %collective-permute-start.62 = (bf16[2,128,1280]{2,1,0:T(8,128)(2,1)}, bf16[2,128,1280]{2,1,0:T(8,128)(2,1)}, u32[]{:S(2)}, u32[]{:S(2)}) collective-permute-start(bf16[2,128,1280]{2,1,0:T(8,128)(2,1)} %copy-done.107), channel_id=1, source_target_pairs={{0,1},{1,0},{2,3},{3,2},{4,5},{5,4},{6,7},{7,6},{8,9},{9,8},{10,11... | collective-permute-start | bytes 1966088 | tf_op jit(solution)/shard_map/ppermute | solution.py:55
  396.3 25.9 %collective-permute-start.57 = (bf16[2,128,1280]{2,1,0:T(8,128)(2,1)}, bf16[2,128,1280]{2,1,0:T(8,128)(2,1)S(1)}, u32[]{:S(2)}, u32[]{:S(2)}) collective-permute-start(bf16[2,128,1280]{2,1,0:T(8,128)(2,1)} %get-tuple-element.187), channel_id=1, source_target_pairs={{0,1},{1,0},{2,3},{3,2},{4,5},{5,4},{6,7},{7,6},{8,9},{9,8},{10,11... | collective-permute-start | bytes 1966088 | tf_op jit(solution)/shard_map/ppermute | solution.py:55
  407.1 15.1 %collective-permute-start.61 = (bf16[2,80,483]{2,1,0:T(8,128)(2,1)S(1)}, bf16[2,80,483]{2,1,0:T(8,128)(2,1)S(1)}, u32[]{:S(2)}, u32[]{:S(2)}) collective-permute-start(bf16[2,80,483]{2,1,0:T(8,128)(2,1)S(1)} %get-tuple-element.193), channel_id=1, source_target_pairs={{0,6},{1,7},{2,0},{3,1},{4,2},{5,3},{6,4},{7,5},{8,14},{9,15},{10,... | collective-permute-start | bytes 463688 | tf_op jit(solution)/shard_map/ppermute | solution.py:55
  425.2 24.5 %collective-permute-start.40 = (bf16[2,128,1280]{2,1,0:T(8,128)(2,1)}, bf16[2,128,1280]{2,1,0:T(8,128)(2,1)}, u32[]{:S(2)}, u32[]{:S(2)}) collective-permute-start(bf16[2,128,1280]{2,1,0:T(8,128)(2,1)} %get-tuple-element.158), channel_id=1, source_target_pairs={{0,8},{1,9},{2,10},{3,11},{4,12},{5,13},{6,14},{7,15},{8,0},{9,1},... | collective-permute-start | bytes 1966088 | tf_op jit(solution)/shard_map/ppermute | solution.py:55
  434.5 21.0 %collective-permute-start.70 = (bf16[4,2,80,483]{3,2,1,0:T(8,128)(2,1)}, bf16[4,2,80,483]{3,2,1,0:T(8,128)(2,1)}, u32[]{:S(2)}, u32[]{:S(2)}) collective-permute-start(bf16[4,2,80,483]{3,2,1,0:T(8,128)(2,1)} %pad_maximum_fusion), channel_id=1, source_target_pairs={{0,16},{1,17},{2,18},{3,19},{4,20},{5,21},{6,22},{7,23},{8,24},{9,... | collective-permute-start | bytes 1854728 | tf_op jit(solution)/shard_map/ppermute | solution.py:55
  436.9 27.3 %collective-permute-start.63 = (bf16[128,1280]{1,0:T(8,128)(2,1)}, bf16[128,1280]{1,0:T(8,128)(2,1)}, u32[]{:S(2)}, u32[]{:S(2)}) collective-permute-start(bf16[128,1280]{1,0:T(8,128)(2,1)} %copy-done.91), channel_id=1, source_target_pairs={{0,0},{1,1},{2,2},{3,3},{8,4},{9,5},{10,6},{11,7},{4,8},{5,9},{6,1... | collective-permute-start | bytes 983048 | tf_op jit(solution)/shard_map/ppermute | solution.py:107
  444.4 19.8 %collective-permute-start.64 = (bf16[128,1280]{1,0:T(8,128)(2,1)}, bf16[128,1280]{1,0:T(8,128)(2,1)S(1)}, u32[]{:S(2)}, u32[]{:S(2)}) collective-permute-start(bf16[128,1280]{1,0:T(8,128)(2,1)} %get-tuple-element.202), channel_id=1, source_target_pairs={{2,0},{3,1},{0,2},{1,3},{10,4},{11,5},{8,6},{9,7},{6,8},{7,9},{4,1... | collective-permute-start | bytes 983048 | tf_op jit(solution)/shard_map/ppermute | solution.py:107
  444.4 19.8 %collective-permute-start.65 = (bf16[128,1280]{1,0:T(8,128)(2,1)}, bf16[128,1280]{1,0:T(8,128)(2,1)S(1)}, u32[]{:S(2)}, u32[]{:S(2)}) collective-permute-start(bf16[128,1280]{1,0:T(8,128)(2,1)} %get-tuple-element.200.refs_6_), channel_id=1, source_target_pairs={{8,0},{9,1},{10,2},{11,3},{0,4},{1,5},{2,6},{3,7},{12,8},{13,9},{1... | collective-permute-start | bytes 983048 | tf_op jit(solution)/shard_map/ppermute | solution.py:107
  449.7 19.0 %collective-permute-start.66 = (bf16[128,1280]{1,0:T(8,128)(2,1)S(1)}, bf16[128,1280]{1,0:T(8,128)(2,1)S(1)}, u32[]{:S(2)}, u32[]{:S(2)}) collective-permute-start(bf16[128,1280]{1,0:T(8,128)(2,1)S(1)} %copy-done.109), channel_id=1, source_target_pairs={{10,0},{11,1},{8,2},{9,3},{2,4},{3,5},{0,6},{1,7},{14,8},{15,9},{1... | collective-permute-start | bytes 983048 | tf_op jit(solution)/shard_map/ppermute | solution.py:107
  (148 other events, 1052.7 us)

commit v6 on v5

--- a/solution.py
+++ b/solution.py
@@ -875,7 +875,7 @@
 def give_body(groups, info, *refs):
     grads, weights, out = refs[:groups], refs[groups : 2 * groups], refs[-1]
     value = back_product(grads, weights)
-    out[...] = value.astype(BF16).reshape(out.shape)
+    out[0] = value.astype(BF16).reshape(out.shape[1:])
 
 
 def back_product(grads, weights):
@@ -888,8 +888,8 @@
 def keep_body(groups, info, *refs):
     grads, weights, got = refs[:groups], refs[groups : 2 * groups], refs[2 * groups]
     outs = refs[2 * groups + 1 :]
-    pairs, b_size, half = got.shape[:3]
-    value = back_product(grads, weights).reshape(got.shape) + got[...].astype(F32)
+    b_size = got.shape[2]
+    value = back_product(grads, weights).reshape(got.shape[1:]) + got[0].astype(F32)
     for b in range(b_size):
         for n, out in enumerate(outs):
 
@@ -898,29 +898,39 @@
                 out[...] = value[:, b].astype(out.dtype)
 
 
-def back_project(at, grads, weights, half, which, got=None):
+def back_project_give(at, grads, weights, half):
     model = weights[0].shape[0]
     pair = at.a_size // 2
-    groups = len(grads)
+    width = grads[0].shape[1]
+    shape = (pair, at.b_size, half, model)
+    grads = [g.reshape(at.a_size, at.b_size, CORES, half, width) for g in grads]
+    block = pl.BlockSpec((pair, at.b_size, 1, half, width), lambda i, s: (s[i], 0, s[2], 0, 0))
+    core = 1 - at.c
+    return call(
+        "back_project",
+        functools.partial(give_body, len(grads)),
+        [core, 1 ^ core, core],
+        [(g, block) for g in grads] + [(weight, VMEM) for weight in weights],
+        [((2, *shape), BF16, pl.BlockSpec((1, *shape), lambda i, s: (i, 0, 0, 0, 0)))],
+        grid=(2,),
+    )[0]
+
+
+def back_project_keep(at, grads, weights, half, which, got):
+    model = weights[0].shape[0]
+    pair = at.a_size // 2
     width = grads[0].shape[1]
     shape = (pair, at.b_size, half, model)
     grads = [g.reshape(at.a_size, at.b_size, CORES, half, width) for g in grads]
     block = pl.BlockSpec((pair, at.b_size, 1, half, width), lambda i, s: (s[0], 0, s[1], 0, 0))
-    core = at.c if got is not None else 1 - at.c
-    inputs = [(g, block) for g in grads]
-    inputs += [(weight, VMEM) for weight in weights]
-    if got is None:
-        body, outputs = give_body, [(shape, BF16, VMEM)]
-    else:
-        body = keep_body
-        inputs.append((got, VMEM))
-        outputs = [((pair, half, model), F32 if db == 0 else BF16, VMEM) for db in range(at.b_size)]
     return call(
         "back_project",
-        functools.partial(body, groups),
-        [which ^ core, core, *ahead(at.b, at.b_size)],
-        inputs,
-        outputs,
+        functools.partial(keep_body, len(grads)),
+        [which ^ at.c, at.c, *ahead(at.b, at.b_size)],
+        [(g, block) for g in grads]
+        + [(weight, VMEM) for weight in weights]
+        + [(got, pl.BlockSpec((1, *shape), lambda i, s: (which, 0, 0, 0, 0)))],
+        [((pair, half, model), F32 if db == 0 else BF16, VMEM) for db in range(at.b_size)],
     )
 
 
@@ -1111,9 +1121,7 @@
         [(shape, BF16, VMEM)] * at.b_size,
     )
     parts = [at.send(parts[db], db=db, dc=dc) if db or dc else parts[0] for db, dc in at.peers()]
-    if at.x_split == 1:
-        return [parts]
-    return [parts, at.send(jnp.stack(parts), dx=1)]
+    return parts
 
 
 def in_order(info, refs, split, half, core, spot):
@@ -1364,27 +1372,27 @@
     keeps, received = [], []
     residual_chunks = d_residual.reshape(at.a_size, half, model)
 
-    def give(which):
-        return at.send(back_project(at, d_heads, w_heads, half, which)[0], dc=1)
-
     def keep(which, got):
-        terms = back_project(at, d_heads, w_heads, half, which, got)
+        terms = back_project_keep(at, d_heads, w_heads, half, which, got)
         keeps.append([terms[0]] + [at.send(terms[db], db=db) for db in range(1, at.b_size)])
 
     def back(which):
         sent = norm_back(at, keeps[which], chunks, residual_chunks, g_attn[None], which)
         for k, part in enumerate(sent):
             received.append(at.send_back(part, which * len(sent) + k))
-
-    got = give(0)
+        return sent
+
+    got = at.send(back_project_give(at, d_heads, w_heads, half), dc=1)
     reduce_second = HeadsReduce(at, heads_outer(at, normed, d_second, extra_second))
     first = reduce_first.by_b(full_parts[1:2])
     keep(0, got)
-    keep(1, give(1))
+    keep(1, got)
     reduce_second.over_a()
     back(0)
-    parts = to_peers(at, [first, reduce_second.by_b(keeps[1][1:])])
-    back(1)
+    parts = [to_peers(at, [first, reduce_second.by_b(keeps[1][1:])])]
+    sent = back(1)
+    if at.x_split == 2:
+        parts.append(at.send(later(jnp.stack(parts[0]), sent[0]), dx=1))
     *grads_full, grad_gain_mlp = finish_full(at, full_parts, up_weight, gain_mlp, [])
     output = next(stage)
     weights = (query_weight, key_weight, value_weight)

time: 482 us -> 471 us (0.977)
  waiting for transfers between devices: 142 us -> 136 us
    ppermute x67 -> x66, waiting for transfers between devices: 137 us -> 131 us  [send(): lax.ppermute(value, AXES, self.route(lambda x, c, a, b: ((x + dx) % self....]
    pallas_call x41 -> x40, Pallas kernels: 193 us -> 189 us  [call(): pl.pallas_call(run, out_shape=[jax.ShapeDtypeStruct(shape, kind) for shap...]
    unnamed x251 -> x241, local copies, waits for them, and re-layouts: 60.1 us -> 60.8 us
    ppermute x67 -> x66, starting transfers between devices: 55.7 us -> 56.1 us  [send(): lax.ppermute(value, AXES, self.route(lambda x, c, a, b: ((x + dx) % self....]
  transfers between devices with their start and end apart: 71 -> 70, of which waited for: 31 -> 31; matrix products, arithmetic and copies ran while one was open for 3% -> 3% of each run, Pallas kernels for 27% -> 28%
where the time goes in v6:
time: 471 us; the launch traced here: 462 us
  Pallas kernels  189 us (40%)
  waiting for transfers between devices  136 us (29%)
  local copies, waits for them, and re-layouts  69.2 us (15%)
  starting transfers between devices  59.7 us (13%)
  other arithmetic  5.09 us (1%)
    pallas_call x40, Pallas kernels, call(): pl.pallas_call(run, out_shape=[jax.ShapeDtypeStruct(shape, kind) for shap...  189 us
    ppermute x66, waiting for transfers between devices, send(): lax.ppermute(value, AXES, self.route(lambda x, c, a, b: ((x + dx) % self....  131 us
    unnamed x241, local copies, waits for them, and re-layouts  60.8 us
    ppermute x66, starting transfers between devices, send(): lax.ppermute(value, AXES, self.route(lambda x, c, a, b: ((x + dx) % self....  56.1 us
  transfers between devices with their start and end apart: 70, of which 31 were waited for; matrix products, arithmetic and copies ran while one was open for 3% of the time, Pallas kernels for 28%

profile of v6, /device:TPU:9, one launch (start us, length us, event | category | flops | bytes accessed | tf_op | source)
XLA Modules:
  0.0 461.8 jit_solution(8712070716121896063)
XLA Ops:
  13.2 3.4 collective-permute-done.5.refs_1_
  17.6 19.8 %collective-permute-done.3.refs_2_ = bf16[128,1280]{1,0:T(8,128)(2,1)S(1)} collective-permute-done((bf16[128,1280]{1,0:T(8,128)(2,1)S(1)}, bf16[128,1280]{1,0:T(8,128)(2,1)S(1)}, u32[]{:S(2)}, u32[]{:S(2)}) %collective-permute-start.3) | collective-permute-done | bytes 327712 | tf_op jit(solution)/shard_map/ppermute | solution.py:55
  37.4 2.4 collective-permute-done.4.refs_3_
  44.3 6.4 %collective-permute-done.9.refs_4_.refs_1_ = bf16[2,80,964]{2,1,0:T(8,128)(2,1)S(1)} collective-permute-done((bf16[2,80,964]{2,1,0:T(8,128)(2,1)S(1)}, bf16[2,80,964]{2,1,0:T(8,128)(2,1)S(1)}, u32[]{:S(2)}, u32[]{:S(2)}) %collective-permute-start.9) | collective-permute-done | bytes 308512 | tf_op jit(solution)/shard_map/ppermute | solution.py:55
  52.6 7.0 %collective-permute-done.11.refs_6_.refs_3_ = bf16[2,80,964]{2,1,0:T(8,128)(2,1)S(1)} collective-permute-done((bf16[2,80,964]{2,1,0:T(8,128)(2,1)S(1)}, bf16[2,80,964]{2,1,0:T(8,128)(2,1)S(1)}, u32[]{:S(2)}, u32[]{:S(2)}) %collective-permute-start.11) | collective-permute-done | bytes 308512 | tf_op jit(solution)/shard_map/ppermute | solution.py:55
  62.5 7.3 %collective-permute-done.8.refs_5_.refs_2_ = bf16[2,80,964]{2,1,0:T(8,128)(2,1)} collective-permute-done((bf16[2,80,964]{2,1,0:T(8,128)(2,1)S(1)}, bf16[2,80,964]{2,1,0:T(8,128)(2,1)}, u32[]{:S(2)}, u32[]{:S(2)}) %collective-permute-start.8) | collective-permute-done | bytes 308512 | tf_op jit(solution)/shard_map/ppermute | solution.py:55
  85.0 6.3 %collective-permute-done.15.refs_6_ = bf16[2,80,964]{2,1,0:T(8,128)(2,1)} collective-permute-done((bf16[2,80,964]{2,1,0:T(8,128)(2,1)}, bf16[2,80,964]{2,1,0:T(8,128)(2,1)}, u32[]{:S(2)}, u32[]{:S(2)}) %collective-permute-start.15) | collective-permute-done | bytes 308512 | tf_op jit(solution)/shard_map/ppermute | solution.py:55
  91.3 3.2 collective-permute-start.18
  96.5 4.5 pad_weights.1
  108.5 13.0 %project.1 = (bf16[2048,1536]{1,0:T(8,128)(2,1)S(1)}, bf16[2048,1280]{1,0:T(8,128)(2,1)S(1)}) custom-call(s32[4]{0:T(128)S(1)} %pad_add_fusion.2.spots, bf16[4,128,1280]{2,1,0:T(8,128)(2,1)S(1)} %shuffle.11.refs_1_.refs_0_.refs_2_, bf16[4,128,1280]{2,1,0:T(8,128)(2,1)} %collective-permute-done.6.refs_9_.refs_1_, ...), custom_call_target="tpu_custom_call" | custom-call | flops 3987500032 | bytes 11962500 | tf_op jit(solution)/shard_map/project/pallas_call | solution.py:167
  121.5 2.4 copy-done.10
  124.0 3.5 shuffle.13.refs_2_.refs_4_
  137.9 2.8 copy-done.1
  140.7 21.2 %attend_forward.1 = (bf16[2,2,4,128,320]{4,3,2,1,0:T(8,128)(2,1)S(1)}, bf16[2048,512]{1,0:T(8,128)(2,1)S(1)}) custom-call(s32[10]{0:T(128)S(1)} %pad_add_fusion.1.spots, s32[2048,128]{1,0:T(8,128)S(1)} %broadcast_in_dim.58.refs_0_, bf16[2048,1536]{1,0:T(8,128)(2,1)S(1)} %copy-done.1, bf16[2048,1536]{1,0:T(8,128)(2,1)S(1)} %copy-done.1, ...), custom_call_target="tpu_custom_call" | custom-call | flops 3300000000 | bytes 9900000 | tf_op jit(solution)/shard_map/attend_forward/pallas_call | solution.py:167
  168.8 8.6 %collective-permute-done.26.refs_3_ = bf16[512,320]{1,0:T(8,128)(2,1)S(1)} collective-permute-done((bf16[512,320]{1,0:T(8,128)(2,1)S(1)}, bf16[512,320]{1,0:T(8,128)(2,1)S(1)}, u32[]{:S(2)}, u32[]{:S(2)}) %collective-permute-start.26) | collective-permute-done | bytes 327712 | tf_op jit(solution)/shard_map/ppermute | solution.py:55
  177.4 9.0 %collective-permute-done.25.refs_2_ = bf16[512,320]{1,0:T(8,128)(2,1)S(1)} collective-permute-done((bf16[512,320]{1,0:T(8,128)(2,1)S(1)}, bf16[512,320]{1,0:T(8,128)(2,1)S(1)}, u32[]{:S(2)}, u32[]{:S(2)}) %collective-permute-start.25) | collective-permute-done | bytes 327712 | tf_op jit(solution)/shard_map/ppermute | solution.py:55
  188.3 4.2 collective-permute-done.29.refs_8_
  197.3 19.7 %middle.1 = (bf16[512,1280]{1,0:T(8,128)(2,1)}, f32[512,1280]{1,0:T(8,128)}, bf16[512,1280]{1,0:T(8,128)(2,1)}, bf16[512,1280]{1,0:T(8,128)(2,1)}, bf16[512,1280...) custom-call(s32[192]{0:T(256)S(1)} %stack.262.spots, ...), custom_call_target="tpu_custom_call" | custom-call | flops 5500000256 | bytes 16500000 | tf_op jit(solution)/shard_map/middle/pallas_call | solution.py:167
  217.8 8.5 %outer_give.1.refs_7_ = bf16[3,1280,640]{2,1,0:T(8,128)(2,1)} custom-call(s32[7]{0:T(128)} %stack.287.spots, bf16[512,1280]{1,0:T(8,128)(2,1)} %copy-done.15, bf16[512,1280]{1,0:T(8,128)(2,1)} %get-tuple-element.143.refs_1_, bf16[512,1280]{1,0:T(8,128)(2,1)} %get-tuple-element.144.refs_2_, bf16[512,1280]{1,0:T(8,128)(2,1)} %get-tuple-element.145.refs_3_, ...), custom_call_target="tpu_custom_call" | custom-call | flops 27500000 | bytes 82500 | tf_op jit(solution)/shard_map/outer_give/pallas_call | solution.py:167
  229.7 2.6 collective-permute-done.34
  232.4 4.7 %collective-permute-done.35 = bf16[512,320]{1,0:T(8,128)(2,1)S(1)} collective-permute-done((bf16[512,320]{1,0:T(8,128)(2,1)S(1)}, bf16[512,320]{1,0:T(8,128)(2,1)S(1)}, u32[]{:S(2)}, u32[]{:S(2)}) %collective-permute-start.35) | collective-permute-done | bytes 327712 | tf_op jit(solution)/shard_map/ppermute | solution.py:55
  237.1 9.0 %collective-permute-done.36 = bf16[512,320]{1,0:T(8,128)(2,1)S(1)} collective-permute-done((bf16[512,320]{1,0:T(8,128)(2,1)S(1)}, bf16[512,320]{1,0:T(8,128)(2,1)S(1)}, u32[]{:S(2)}, u32[]{:S(2)}) %collective-permute-start.36) | collective-permute-done | bytes 327712 | tf_op jit(solution)/shard_map/ppermute | solution.py:55
  246.8 9.9 %outer.1 = (bf16[3,2,2,80,640]{4,3,2,1,0:T(8,128)(2,1)}, bf16[3,2,2,80,640]{4,3,2,1,0:T(8,128)(2,1)}, bf16[3,2,2,80,640]{4,3,2,1,0:T(8,128)(2,1)}, bf16[3,2,2,80,640]{4,3,2,1,0:T(8,128)(2,1)}) custom-call(s32[7]{0:T(128)} %stack.286.spots, bf16[512,1280]{1,0:T(8,128)(2,1)} %copy-done.15, bf16[512,1280]{1,0:T(8,128)(2,1)} %get-tuple-element.143.refs_1_, ...), custom_call_target="tpu_custom_call" | custom-call | flops 1924999936 | bytes 5775000 | tf_op jit(solution)/shard_map/outer/pallas_call | solution.py:167
  264.0 2.8 copy-done.2
  270.3 20.5 %attend_backward.2 = (bf16[2048,480]{1,0:T(8,128)(2,1)S(1)}, f32[8,128]{1,0:T(8,128)S(1)}, f32[8,768]{1,0:T(8,128)S(1)}) custom-call(s32[10]{0:T(128)S(1)} %pad_add_fusion.1.spots, s32[8,2048]{1,0:T(8,128)S(1)} %broadcast_in_dim.61.refs_0_, f32[8,256]{1,0:T(8,128)S(1)} %broadcast_in_dim.63.refs_1_, bf16[2048,512]{1,0:T(8,128)(2,1)S(1)} %copy-done.100, ...), custom_call_target="tpu_custom_call" | custom-call | flops 6874999808 | bytes 20625000 | tf_op jit(solution)/shard_map/attend_backward/pallas_call | solution.py:167
  293.3 2.9 route_back.1
  296.3 3.3 add_blocks.6
  306.3 2.5 copy-done.11
  309.9 4.8 %heads_outer.2 = (bf16[4,2,80,483]{3,2,1,0:T(8,128)(2,1)S(1)}, bf16[4,2,80,483]{3,2,1,0:T(8,128)(2,1)S(1)}) custom-call(s32[1]{0:T(128)} %bitcast.54.spots, bf16[2048,1280]{1,0:T(8,128)(2,1)S(1)} %copy-done.11, bf16[2048,480]{1,0:T(8,128)(2,1)S(1)} %copy-done.4, bf16[1280,3]{1,0:T(8,128)(2,1)S(1)} %copy.53.refs_2_, bf16[3,2,80,640]{3,2,1,0:T(8,128)(2,1)S(1)} %copy-done.45), custom_call_target="tpu_custom_call" | custom-call | flops 1512499968 | bytes 4537500 | tf_op jit(solution)/shard_map/heads_outer/pallas_call | solution.py:167
  321.3 21.5 %attend_backward.3 = (bf16[2048,480]{1,0:T(8,128)(2,1)S(1)}, f32[8,128]{1,0:T(8,128)S(1)}, f32[8,768]{1,0:T(8,128)S(1)}) custom-call(s32[10]{0:T(128)S(1)} %pad_add_fusion.1.spots, s32[8,2048]{1,0:T(8,128)S(1)} %broadcast_in_dim.61.refs_0_, f32[8,256]{1,0:T(8,128)S(1)} %broadcast_in_dim.63.refs_1_, bf16[2048,512]{1,0:T(8,128)(2,1)S(1)} %copy-done.101, ...), custom_call_target="tpu_custom_call" | custom-call | flops 6874999808 | bytes 20625000 | tf_op jit(solution)/shard_map/attend_backward/pallas_call | solution.py:167
  343.5 5.2 %collective-permute-done.47 = bf16[3,80,640]{2,1,0:T(8,128)(2,1)S(1)} collective-permute-done((bf16[3,80,640]{2,1,0:T(8,128)(2,1)S(1)}, bf16[3,80,640]{2,1,0:T(8,128)(2,1)S(1)}, u32[]{:S(2)}, u32[]{:S(2)}) %collective-permute-start.47) | collective-permute-done | bytes 307232 | tf_op jit(solution)/shard_map/ppermute | solution.py:55
  352.8 5.0 %back_project.3.refs_3_ = bf16[2,2,2,128,1280]{4,3,2,1,0:T(8,128)(2,1)} custom-call(s32[3]{0:T(128)S(1)} %pad_add_fusion.7.spots, bf16[4,2,2,128,480]{4,3,2,1,0:T(8,128)(2,1)S(1)} %bitcast.121, bf16[4,2,2,128,480]{4,3,2,1,0:T(8,128)(2,1)S(1)} %bitcast.124, bf16[1280,480]{1,0:T(8,128)(2,1)S(1)} %copy-done.17, bf16[1280,480]{1,0:T(8,128)(2,1)S(1)} %copy-done.20, ...), custom_call_target="tpu_custom_call" | custom-call | flops 962499968 | bytes 2887500 | tf_op jit(solution)/shard_map/back_project/pallas_call | solution.py:167
  364.6 2.5 copy-done.12
  367.1 5.6 %heads_outer.3 = (bf16[4,2,80,483]{3,2,1,0:T(8,128)(2,1)S(1)}, bf16[4,2,80,483]{3,2,1,0:T(8,128)(2,1)}) custom-call(s32[1]{0:T(128)} %bitcast.54.spots, bf16[2048,1280]{1,0:T(8,128)(2,1)S(1)} %copy-done.12, bf16[2048,480]{1,0:T(8,128)(2,1)S(1)} %copy-done.7, bf16[1280,3]{1,0:T(8,128)(2,1)S(1)} %copy.54.refs_2_, bf16[2,2,2,128,1280]{4,3,2,1,0:T(8,128)(2,1)} %back_project.3.refs_3_), custom_call_target="tpu_custom_call" | custom-call | flops 1512499968 | bytes 4537500 | tf_op jit(solution)/shard_map/heads_outer/pallas_call | solution.py:167
  373.9 3.2 collective-permute-done.55.refs_3_.refs_7_
  380.3 4.7 %back_project.4 = (f32[2,128,1280]{2,1,0:T(8,128)S(1)}, bf16[2,128,1280]{2,1,0:T(8,128)(2,1)}) custom-call(s32[4]{0:T(128)S(1)} %add_add_fusion.2.spots, bf16[4,2,2,128,480]{4,3,2,1,0:T(8,128)(2,1)S(1)} %bitcast.122, bf16[4,2,2,128,480]{4,3,2,1,0:T(8,128)(2,1)S(1)} %bitcast.125, bf16[1280,480]{1,0:T(8,128)(2,1)S(1)} %copy-done.18, ...), custom_call_target="tpu_custom_call" | custom-call | flops 962499968 | bytes 2887500 | tf_op jit(solution)/shard_map/back_project/pallas_call | solution.py:167
  385.2 4.4 back_project.5
  395.6 5.5 %collective-permute-done.61.refs_1_ = bf16[2,128,1280]{2,1,0:T(8,128)(2,1)} collective-permute-done((bf16[2,128,1280]{2,1,0:T(8,128)(2,1)}, bf16[2,128,1280]{2,1,0:T(8,128)(2,1)}, u32[]{:S(2)}, u32[]{:S(2)}) %collective-permute-start.61) | collective-permute-done | bytes 655392 | tf_op jit(solution)/shard_map/ppermute | solution.py:55
  401.2 2.3 norm_back.2
  403.5 3.9 collective-permute-done.59.refs_2_.refs_6_
  407.4 2.6 collective-permute-done.60.refs_3_.refs_7_
  410.0 5.1 %collective-permute-done.56.refs_9_.refs_1_ = bf16[2,128,1280]{2,1,0:T(8,128)(2,1)S(1)} collective-permute-done((bf16[2,128,1280]{2,1,0:T(8,128)(2,1)}, bf16[2,128,1280]{2,1,0:T(8,128)(2,1)S(1)}, u32[]{:S(2)}, u32[]{:S(2)}) %collective-permute-start.56) | collective-permute-done | bytes 655392 | tf_op jit(solution)/shard_map/ppermute | solution.py:55
  416.0 2.8 collective-permute-start.68
  421.9 3.4 collective-permute-done.68.refs_3_
  429.8 2.7 collective-permute-start.62
  436.0 3.2 finish_full.1
  446.4 5.1 %finish_heads.1 = (f32[160,1280]{1,0:T(8,128)}, f32[160,1280]{1,0:T(8,128)}, f32[160,1280]{1,0:T(8,128)}, f32[160,1]{1,0:T(8,128)S(1)}, f32[160,3]{1,0:T(8,128)S(1)}) custom-call(s32[5]{0:T(128)S(1)} %stack.314.spots, bf16[2,80,483]{2,1,0:T(8,128)(2,1)S(1)} %get-tuple-element.200.refs_5_.refs_0_, bf16[2,80,483]{2,1,0:T(8,128)(2,1)S(1)} %copy-done.93, ...), custom_call_target="tpu_custom_call" | custom-call | flops 1100000000 | bytes 3300000 | tf_op jit(solution)/shard_map/finish_heads/pallas_call | solution.py:167
  454.4 4.2 collective-permute-done.63.refs_1_
  (473 shorter events, 150.1 us)
Async XLA Ops:
  9.3 28.1 %collective-permute-start.3 = (bf16[128,1280]{1,0:T(8,128)(2,1)S(1)}, bf16[128,1280]{1,0:T(8,128)(2,1)S(1)}, u32[]{:S(2)}, u32[]{:S(2)}) collective-permute-start(bf16[128,1280]{1,0:T(8,128)(2,1)S(1)} %get-tuple-element.119), channel_id=1, source_target_pairs={{0,4},{1,5},{2,6},{3,7},{4,0},{5,1},{6,2},{7,3},{8,12},{9,13},{10,... | collective-permute-start | bytes 983048 | tf_op jit(solution)/shard_map/ppermute | solution.py:55
  10.3 29.5 %collective-permute-start.4 = (bf16[128,1280]{1,0:T(8,128)(2,1)S(1)}, bf16[128,1280]{1,0:T(8,128)(2,1)S(1)}, u32[]{:S(2)}, u32[]{:S(2)}) collective-permute-start(bf16[128,1280]{1,0:T(8,128)(2,1)S(1)} %get-tuple-element.120), channel_id=1, source_target_pairs={{0,6},{1,7},{2,0},{3,1},{4,2},{5,3},{6,4},{7,5},{8,14},{9,15},{10,... | collective-permute-start | bytes 983048 | tf_op jit(solution)/shard_map/ppermute | solution.py:55
  40.8 30.4 %collective-permute-start.7 = (bf16[4,128,1280]{2,1,0:T(8,128)(2,1)S(1)}, bf16[4,128,1280]{2,1,0:T(8,128)(2,1)}, u32[]{:S(2)}, u32[]{:S(2)}) collective-permute-start(bf16[4,128,1280]{2,1,0:T(8,128)(2,1)S(1)} %shuffle.11.refs_1_.refs_0_.refs_2_), channel_id=1, source_target_pairs={{0,1},{1,0},{2,3},{3,2},{4,5},{5,4},{6,7},{7,6},{8,9},{9,8},{10,11... | collective-permute-start | bytes 3932168 | tf_op jit(solution)/shard_map/ppermute | solution.py:55
  42.1 17.5 %collective-permute-start.11 = (bf16[2,80,964]{2,1,0:T(8,128)(2,1)S(1)}, bf16[2,80,964]{2,1,0:T(8,128)(2,1)S(1)}, u32[]{:S(2)}, u32[]{:S(2)}) collective-permute-start(bf16[2,80,964]{2,1,0:T(8,128)(2,1)S(1)} %shuffle.10.refs_4_.refs_0_), channel_id=1, source_target_pairs={{0,6},{1,7},{2,0},{3,1},{4,2},{5,3},{6,4},{7,5},{8,14},{9,15},{10,... | collective-permute-start | bytes 925448 | tf_op jit(solution)/shard_map/ppermute | solution.py:55
  43.6 26.2 %collective-permute-start.8 = (bf16[2,80,964]{2,1,0:T(8,128)(2,1)S(1)}, bf16[2,80,964]{2,1,0:T(8,128)(2,1)}, u32[]{:S(2)}, u32[]{:S(2)}) collective-permute-start(bf16[2,80,964]{2,1,0:T(8,128)(2,1)S(1)} %shuffle.10.refs_4_.refs_0_), channel_id=1, source_target_pairs={{0,4},{1,5},{2,6},{3,7},{4,0},{5,1},{6,2},{7,3},{8,12},{9,13},{10,... | collective-permute-start | bytes 925448 | tf_op jit(solution)/shard_map/ppermute | solution.py:55
  50.7 19.1 %collective-permute-start.10 = (bf16[2,80,964]{2,1,0:T(8,128)(2,1)S(1)}, bf16[2,80,964]{2,1,0:T(8,128)(2,1)S(1)}, u32[]{:S(2)}, u32[]{:S(2)}) collective-permute-start(bf16[2,80,964]{2,1,0:T(8,128)(2,1)S(1)} %collective-permute-done.9.refs_4_.refs_1_), channel_id=1, source_target_pairs={{0,16},{1,17},{2,18},{3,19},{4,20},{5,21},{6,22},{7,23},{8,24},{9,... | collective-permute-start | bytes 925448 | tf_op jit(solution)/shard_map/ppermute | solution.py:55
  61.5 33.8 %collective-permute-start.6 = (bf16[4,128,1280]{2,1,0:T(8,128)(2,1)S(1)}, bf16[4,128,1280]{2,1,0:T(8,128)(2,1)}, u32[]{:S(2)}, u32[]{:S(2)}) collective-permute-start(bf16[4,128,1280]{2,1,0:T(8,128)(2,1)S(1)} %shuffle.11.refs_1_.refs_0_.refs_2_), channel_id=1, source_target_pairs={{0,8},{1,9},{2,10},{3,11},{4,12},{5,13},{6,14},{7,15},{8,0},{9,1},... | collective-permute-start | bytes 3932168 | tf_op jit(solution)/shard_map/ppermute | solution.py:55
  71.3 24.1 %collective-permute-start.13 = (bf16[4,128,1280]{2,1,0:T(8,128)(2,1)}, bf16[4,128,1280]{2,1,0:T(8,128)(2,1)}, u32[]{:S(2)}, u32[]{:S(2)}) collective-permute-start(bf16[4,128,1280]{2,1,0:T(8,128)(2,1)} %collective-permute-done.7.refs_10_.refs_2_), channel_id=1, source_target_pairs={{0,8},{1,9},{2,10},{3,11},{4,12},{5,13},{6,14},{7,15},{8,0},{9,1},... | collective-permute-start | bytes 3932168 | tf_op jit(solution)/shard_map/ppermute | solution.py:55
  74.3 20.2 %collective-permute-start.16 = (bf16[2,128,1280]{2,1,0:T(8,128)(2,1)}, bf16[2,128,1280]{2,1,0:T(8,128)(2,1)S(1)}, u32[]{:S(2)}, u32[]{:S(2)}) collective-permute-start(bf16[2,128,1280]{2,1,0:T(8,128)(2,1)} %get-tuple-element.124), channel_id=1, source_target_pairs={{0,8},{1,9},{2,10},{3,11},{4,12},{5,13},{6,14},{7,15},{8,0},{9,1},... | collective-permute-start | bytes 1966088 | tf_op jit(solution)/shard_map/ppermute | solution.py:55
  76.1 15.2 %collective-permute-start.15 = (bf16[2,80,964]{2,1,0:T(8,128)(2,1)}, bf16[2,80,964]{2,1,0:T(8,128)(2,1)}, u32[]{:S(2)}, u32[]{:S(2)}) collective-permute-start(bf16[2,80,964]{2,1,0:T(8,128)(2,1)} %collective-permute-done.8.refs_5_.refs_2_), channel_id=1, source_target_pairs={{0,16},{1,17},{2,18},{3,19},{4,20},{5,21},{6,22},{7,23},{8,24},{9,... | collective-permute-start | bytes 925448 | tf_op jit(solution)/shard_map/ppermute | solution.py:55
  84.3 39.7 %collective-permute-start.17 = (bf16[3,80,640]{2,1,0:T(8,128)(2,1)S(1)}, bf16[3,80,640]{2,1,0:T(8,128)(2,1)}, u32[]{:S(2)}, u32[]{:S(2)}) collective-permute-start(bf16[3,80,640]{2,1,0:T(8,128)(2,1)S(1)} %quarter.1.refs_8_.refs_0_), channel_id=1, source_target_pairs={{0,2},{1,3},{2,4},{3,5},{4,6},{5,7},{6,0},{7,1},{8,10},{9,11},{10,... | collective-permute-start | bytes 921608 | tf_op jit(solution)/shard_map/ppermute | solution.py:55
  91.3 32.6 %collective-permute-start.18 = (bf16[3,80,640]{2,1,0:T(8,128)(2,1)S(1)}, bf16[3,80,640]{2,1,0:T(8,128)(2,1)}, u32[]{:S(2)}, u32[]{:S(2)}) collective-permute-start(bf16[3,80,640]{2,1,0:T(8,128)(2,1)S(1)} %quarter.1.refs_8_.refs_0_), channel_id=1, source_target_pairs={{0,4},{1,5},{2,6},{3,7},{4,0},{5,1},{6,2},{7,3},{8,12},{9,13},{10,... | collective-permute-start | bytes 921608 | tf_op jit(solution)/shard_map/ppermute | solution.py:55
  95.3 28.6 %collective-permute-start.19 = (bf16[3,80,640]{2,1,0:T(8,128)(2,1)S(1)}, bf16[3,80,640]{2,1,0:T(8,128)(2,1)}, u32[]{:S(2)}, u32[]{:S(2)}) collective-permute-start(bf16[3,80,640]{2,1,0:T(8,128)(2,1)S(1)} %quarter.1.refs_8_.refs_0_), channel_id=1, source_target_pairs={{0,6},{1,7},{2,0},{3,1},{4,2},{5,3},{6,4},{7,5},{8,14},{9,15},{10,... | collective-permute-start | bytes 921608 | tf_op jit(solution)/shard_map/ppermute | solution.py:55
  128.7 35.9 %collective-permute-start.27 = (bf16[4,3,80,640]{3,2,1,0:T(8,128)(2,1)S(1)}, bf16[4,3,80,640]{3,2,1,0:T(8,128)(2,1)}, u32[]{:S(2)}, u32[]{:S(2)}) collective-permute-start(bf16[4,3,80,640]{3,2,1,0:T(8,128)(2,1)S(1)} %shuffle.13.refs_2_.refs_4_), channel_id=1, source_target_pairs={{0,1},{1,0},{2,3},{3,2},{4,5},{5,4},{6,7},{7,6},{8,9},{9,8},{10,11... | collective-permute-start | bytes 3686408 | tf_op jit(solution)/shard_map/ppermute | solution.py:55
  132.1 29.8 %collective-permute-start.21 = (bf16[128,1280]{1,0:T(8,128)(2,1)S(1)}, bf16[128,1280]{1,0:T(8,128)(2,1)S(1)}, u32[]{:S(2)}, u32[]{:S(2)}) collective-permute-start(bf16[128,1280]{1,0:T(8,128)(2,1)S(1)} %get-tuple-element.131), channel_id=1, source_target_pairs={{0,2},{1,3},{2,4},{3,5},{4,6},{5,7},{6,0},{7,1},{8,10},{9,11},{10,... | collective-permute-start | bytes 983048 | tf_op jit(solution)/shard_map/ppermute | solution.py:55
  133.9 28.1 %collective-permute-start.22 = (bf16[128,1280]{1,0:T(8,128)(2,1)S(1)}, bf16[128,1280]{1,0:T(8,128)(2,1)S(1)}, u32[]{:S(2)}, u32[]{:S(2)}) collective-permute-start(bf16[128,1280]{1,0:T(8,128)(2,1)S(1)} %get-tuple-element.132), channel_id=1, source_target_pairs={{0,4},{1,5},{2,6},{3,7},{4,0},{5,1},{6,2},{7,3},{8,12},{9,13},{10,... | collective-permute-start | bytes 983048 | tf_op jit(solution)/shard_map/ppermute | solution.py:55
  135.4 28.1 %collective-permute-start.23 = (bf16[128,1280]{1,0:T(8,128)(2,1)S(1)}, bf16[128,1280]{1,0:T(8,128)(2,1)S(1)}, u32[]{:S(2)}, u32[]{:S(2)}) collective-permute-start(bf16[128,1280]{1,0:T(8,128)(2,1)S(1)} %get-tuple-element.133), channel_id=1, source_target_pairs={{0,6},{1,7},{2,0},{3,1},{4,2},{5,3},{6,4},{7,5},{8,14},{9,15},{10,... | collective-permute-start | bytes 983048 | tf_op jit(solution)/shard_map/ppermute | solution.py:55
  136.4 51.4 %collective-permute-start.28 = (bf16[4,3,80,640]{3,2,1,0:T(8,128)(2,1)S(1)}, bf16[4,3,80,640]{3,2,1,0:T(8,128)(2,1)}, u32[]{:S(2)}, u32[]{:S(2)}) collective-permute-start(bf16[4,3,80,640]{3,2,1,0:T(8,128)(2,1)S(1)} %shuffle.13.refs_2_.refs_4_), channel_id=1, source_target_pairs={{0,16},{1,17},{2,18},{3,19},{4,20},{5,21},{6,22},{7,23},{8,24},{9,... | collective-permute-start | bytes 3686408 | tf_op jit(solution)/shard_map/ppermute | solution.py:55
  164.6 27.9 %collective-permute-start.29 = (bf16[4,3,80,640]{3,2,1,0:T(8,128)(2,1)}, bf16[4,3,80,640]{3,2,1,0:T(8,128)(2,1)}, u32[]{:S(2)}, u32[]{:S(2)}) collective-permute-start(bf16[4,3,80,640]{3,2,1,0:T(8,128)(2,1)} %collective-permute-done.27.refs_6_), channel_id=1, source_target_pairs={{0,16},{1,17},{2,18},{3,19},{4,20},{5,21},{6,22},{7,23},{8,24},{9,... | collective-permute-start | bytes 3686408 | tf_op jit(solution)/shard_map/ppermute | solution.py:55
  167.5 18.9 %collective-permute-start.25 = (bf16[512,320]{1,0:T(8,128)(2,1)S(1)}, bf16[512,320]{1,0:T(8,128)(2,1)S(1)}, u32[]{:S(2)}, u32[]{:S(2)}) collective-permute-start(bf16[512,320]{1,0:T(8,128)(2,1)S(1)} %bitcast.160), channel_id=1, source_target_pairs={{0,1},{1,0},{2,3},{3,2},{4,5},{5,4},{6,7},{7,6},{8,9},{9,8},{10,11... | collective-permute-start | bytes 983048 | tf_op jit(solution)/shard_map/ppermute | solution.py:55
  168.8 17.6 %collective-permute-start.24 = (bf16[512,320]{1,0:T(8,128)(2,1)S(1)}, bf16[512,320]{1,0:T(8,128)(2,1)S(1)}, u32[]{:S(2)}, u32[]{:S(2)}) collective-permute-start(bf16[512,320]{1,0:T(8,128)(2,1)S(1)} %bitcast.159), channel_id=1, source_target_pairs={{0,8},{1,9},{2,10},{3,11},{4,12},{5,13},{6,14},{7,15},{8,0},{9,1},... | collective-permute-start | bytes 983048 | tf_op jit(solution)/shard_map/ppermute | solution.py:55
  226.3 19.8 %collective-permute-start.33 = (bf16[3,1280,640]{2,1,0:T(8,128)(2,1)}, bf16[3,1280,640]{2,1,0:T(8,128)(2,1)}, u32[]{:S(2)}, u32[]{:S(2)}) collective-permute-start(bf16[3,1280,640]{2,1,0:T(8,128)(2,1)} %outer_give.1.refs_7_), channel_id=1, source_target_pairs={{0,8},{1,9},{2,10},{3,11},{4,12},{5,13},{6,14},{7,15},{8,0},{9,1},... | collective-permute-start | bytes 14745608 | tf_op jit(solution)/shard_map/ppermute | solution.py:55
  226.9 19.1 %collective-permute-start.36 = (bf16[512,320]{1,0:T(8,128)(2,1)S(1)}, bf16[512,320]{1,0:T(8,128)(2,1)S(1)}, u32[]{:S(2)}, u32[]{:S(2)}) collective-permute-start(bf16[512,320]{1,0:T(8,128)(2,1)S(1)} %get-tuple-element.150), channel_id=1, source_target_pairs={{0,9},{1,8},{2,11},{3,10},{4,13},{5,12},{6,15},{7,14},{8,1},{9,0},... | collective-permute-start | bytes 983048 | tf_op jit(solution)/shard_map/ppermute | solution.py:55
  256.7 39.5 %collective-permute-start.41 = (bf16[3,2,2,80,640]{4,3,2,1,0:T(8,128)(2,1)}, bf16[3,2,2,80,640]{4,3,2,1,0:T(8,128)(2,1)S(1)}, u32[]{:S(2)}, u32[]{:S(2)}) collective-permute-start(bf16[3,2,2,80,640]{4,3,2,1,0:T(8,128)(2,1)} %get-tuple-element.160), channel_id=1, source_target_pairs={{0,16},{1,17},{2,18},{3,19},{4,20},{5,21},{6,22},{7,23},{8,24},{9,... | collective-permute-start | bytes 3686408 | tf_op jit(solution)/shard_map/ppermute | solution.py:55
  258.0 38.3 %collective-permute-start.42 = (bf16[3,2,2,80,640]{4,3,2,1,0:T(8,128)(2,1)}, bf16[3,2,2,80,640]{4,3,2,1,0:T(8,128)(2,1)}, u32[]{:S(2)}, u32[]{:S(2)}) collective-permute-start(bf16[3,2,2,80,640]{4,3,2,1,0:T(8,128)(2,1)} %get-tuple-element.162), channel_id=1, source_target_pairs={{0,1},{1,0},{2,3},{3,2},{4,5},{5,4},{6,7},{7,6},{8,9},{9,8},{10,11... | collective-permute-start | bytes 3686408 | tf_op jit(solution)/shard_map/ppermute | solution.py:55
  261.1 29.9 %collective-permute-start.37 = (bf16[128,1280]{1,0:T(8,128)(2,1)}, bf16[128,1280]{1,0:T(8,128)(2,1)}, u32[]{:S(2)}, u32[]{:S(2)}) collective-permute-start(bf16[128,1280]{1,0:T(8,128)(2,1)} %get-tuple-element.153), channel_id=1, source_target_pairs={{0,2},{1,3},{2,4},{3,5},{4,6},{5,7},{6,0},{7,1},{8,10},{9,11},{10,... | collective-permute-start | bytes 983048 | tf_op jit(solution)/shard_map/ppermute | solution.py:55
  261.2 29.9 %collective-permute-start.38 = (bf16[128,1280]{1,0:T(8,128)(2,1)}, bf16[128,1280]{1,0:T(8,128)(2,1)}, u32[]{:S(2)}, u32[]{:S(2)}) collective-permute-start(bf16[128,1280]{1,0:T(8,128)(2,1)} %get-tuple-element.154), channel_id=1, source_target_pairs={{0,4},{1,5},{2,6},{3,7},{4,0},{5,1},{6,2},{7,3},{8,12},{9,13},{10,... | collective-permute-start | bytes 983048 | tf_op jit(solution)/shard_map/ppermute | solution.py:55
  262.8 29.6 %collective-permute-start.39 = (bf16[128,1280]{1,0:T(8,128)(2,1)}, bf16[128,1280]{1,0:T(8,128)(2,1)}, u32[]{:S(2)}, u32[]{:S(2)}) collective-permute-start(bf16[128,1280]{1,0:T(8,128)(2,1)} %get-tuple-element.155), channel_id=1, source_target_pairs={{0,6},{1,7},{2,0},{3,1},{4,2},{5,3},{6,4},{7,5},{8,14},{9,15},{10,... | collective-permute-start | bytes 983048 | tf_op jit(solution)/shard_map/ppermute | solution.py:55
  301.2 15.2 %collective-permute-start.43 = (bf16[3,2,80,640]{3,2,1,0:T(8,128)(2,1)}, bf16[3,2,80,640]{3,2,1,0:T(8,128)(2,1)S(1)}, u32[]{:S(2)}, u32[]{:S(2)}) collective-permute-start(bf16[3,2,80,640]{3,2,1,0:T(8,128)(2,1)} %get-tuple-element.164), channel_id=1, source_target_pairs={{0,1},{1,0},{2,3},{3,2},{4,5},{5,4},{6,7},{7,6},{8,9},{9,8},{10,11... | collective-permute-start | bytes 1843208 | tf_op jit(solution)/shard_map/ppermute | solution.py:55
  302.5 14.8 %collective-permute-start.44 = (bf16[3,2,80,640]{3,2,1,0:T(8,128)(2,1)}, bf16[3,2,80,640]{3,2,1,0:T(8,128)(2,1)}, u32[]{:S(2)}, u32[]{:S(2)}) collective-permute-start(bf16[3,2,80,640]{3,2,1,0:T(8,128)(2,1)} %get-tuple-element.166), channel_id=1, source_target_pairs={{0,16},{1,17},{2,18},{3,19},{4,20},{5,21},{6,22},{7,23},{8,24},{9,... | collective-permute-start | bytes 1843208 | tf_op jit(solution)/shard_map/ppermute | solution.py:55
  314.7 35.5 %collective-permute-start.51 = (bf16[4,2,80,483]{3,2,1,0:T(8,128)(2,1)S(1)}, bf16[4,2,80,483]{3,2,1,0:T(8,128)(2,1)S(1)}, u32[]{:S(2)}, u32[]{:S(2)}) collective-permute-start(bf16[4,2,80,483]{3,2,1,0:T(8,128)(2,1)S(1)} %get-tuple-element.177), channel_id=1, source_target_pairs={{0,16},{1,17},{2,18},{3,19},{4,20},{5,21},{6,22},{7,23},{8,24},{9,... | collective-permute-start | bytes 1854728 | tf_op jit(solution)/shard_map/ppermute | solution.py:55
  319.6 23.2 %collective-permute-start.45 = (bf16[3,80,640]{2,1,0:T(8,128)(2,1)S(1)}, bf16[3,80,640]{2,1,0:T(8,128)(2,1)S(1)}, u32[]{:S(2)}, u32[]{:S(2)}) collective-permute-start(bf16[3,80,640]{2,1,0:T(8,128)(2,1)S(1)} %get-tuple-element.172), channel_id=1, source_target_pairs={{0,2},{1,3},{2,4},{3,5},{4,6},{5,7},{6,0},{7,1},{8,10},{9,11},{10,... | collective-permute-start | bytes 921608 | tf_op jit(solution)/shard_map/ppermute | solution.py:55
  319.7 23.9 %collective-permute-start.46 = (bf16[3,80,640]{2,1,0:T(8,128)(2,1)S(1)}, bf16[3,80,640]{2,1,0:T(8,128)(2,1)S(1)}, u32[]{:S(2)}, u32[]{:S(2)}) collective-permute-start(bf16[3,80,640]{2,1,0:T(8,128)(2,1)S(1)} %get-tuple-element.173), channel_id=1, source_target_pairs={{0,4},{1,5},{2,6},{3,7},{4,0},{5,1},{6,2},{7,3},{8,12},{9,13},{10,... | collective-permute-start | bytes 921608 | tf_op jit(solution)/shard_map/ppermute | solution.py:55
  321.2 27.6 %collective-permute-start.47 = (bf16[3,80,640]{2,1,0:T(8,128)(2,1)S(1)}, bf16[3,80,640]{2,1,0:T(8,128)(2,1)S(1)}, u32[]{:S(2)}, u32[]{:S(2)}) collective-permute-start(bf16[3,80,640]{2,1,0:T(8,128)(2,1)S(1)} %get-tuple-element.174), channel_id=1, source_target_pairs={{0,6},{1,7},{2,0},{3,1},{4,2},{5,3},{6,4},{7,5},{8,14},{9,15},{10,... | collective-permute-start | bytes 921608 | tf_op jit(solution)/shard_map/ppermute | solution.py:55
  357.7 22.6 %collective-permute-start.52 = (bf16[2,2,2,128,1280]{4,3,2,1,0:T(8,128)(2,1)}, bf16[2,2,2,128,1280]{4,3,2,1,0:T(8,128)(2,1)}, u32[]{:S(2)}, u32[]{:S(2)}) collective-permute-start(bf16[2,2,2,128,1280]{4,3,2,1,0:T(8,128)(2,1)} %back_project.3.refs_3_), channel_id=1, source_target_pairs={{0,8},{1,9},{2,10},{3,11},{4,12},{5,13},{6,14},{7,15},{8,0},{9,1},... | collective-permute-start | bytes 7864328 | tf_op jit(solution)/shard_map/ppermute | solution.py:55
  359.4 17.7 %collective-permute-start.48 = (bf16[3,80,640]{2,1,0:T(8,128)(2,1)}, bf16[3,80,640]{2,1,0:T(8,128)(2,1)}, u32[]{:S(2)}, u32[]{:S(2)}) collective-permute-start(bf16[3,80,640]{2,1,0:T(8,128)(2,1)} %add_blocks.7.refs_8_.refs_0_), channel_id=1, source_target_pairs={{0,16},{1,17},{2,18},{3,19},{4,20},{5,21},{6,22},{7,23},{8,24},{9,... | collective-permute-start | bytes 921608 | tf_op jit(solution)/shard_map/ppermute | solution.py:55
  359.6 14.3 %collective-permute-start.54 = (bf16[2,80,483]{2,1,0:T(8,128)(2,1)}, bf16[2,80,483]{2,1,0:T(8,128)(2,1)}, u32[]{:S(2)}, u32[]{:S(2)}) collective-permute-start(bf16[2,80,483]{2,1,0:T(8,128)(2,1)} %get-tuple-element.180), channel_id=1, source_target_pairs={{0,4},{1,5},{2,6},{3,7},{4,0},{5,1},{6,2},{7,3},{8,12},{9,13},{10,... | collective-permute-start | bytes 463688 | tf_op jit(solution)/shard_map/ppermute | solution.py:55
  361.8 15.3 %collective-permute-start.55 = (bf16[2,80,483]{2,1,0:T(8,128)(2,1)}, bf16[2,80,483]{2,1,0:T(8,128)(2,1)}, u32[]{:S(2)}, u32[]{:S(2)}) collective-permute-start(bf16[2,80,483]{2,1,0:T(8,128)(2,1)} %get-tuple-element.181), channel_id=1, source_target_pairs={{0,6},{1,7},{2,0},{3,1},{4,2},{5,3},{6,4},{7,5},{8,14},{9,15},{10,... | collective-permute-start | bytes 463688 | tf_op jit(solution)/shard_map/ppermute | solution.py:55
  373.4 18.6 %collective-permute-start.57 = (bf16[4,2,80,483]{3,2,1,0:T(8,128)(2,1)}, bf16[4,2,80,483]{3,2,1,0:T(8,128)(2,1)S(1)}, u32[]{:S(2)}, u32[]{:S(2)}) collective-permute-start(bf16[4,2,80,483]{3,2,1,0:T(8,128)(2,1)} %get-tuple-element.190), channel_id=1, source_target_pairs={{0,16},{1,17},{2,18},{3,19},{4,20},{5,21},{6,22},{7,23},{8,24},{9,... | collective-permute-start | bytes 1854728 | tf_op jit(solution)/shard_map/ppermute | solution.py:55
  385.0 16.1 %collective-permute-start.61 = (bf16[2,128,1280]{2,1,0:T(8,128)(2,1)}, bf16[2,128,1280]{2,1,0:T(8,128)(2,1)}, u32[]{:S(2)}, u32[]{:S(2)}) collective-permute-start(bf16[2,128,1280]{2,1,0:T(8,128)(2,1)} %get-tuple-element.195), channel_id=1, source_target_pairs={{0,1},{1,0},{2,3},{3,2},{4,5},{5,4},{6,7},{7,6},{8,9},{9,8},{10,11... | collective-permute-start | bytes 1966088 | tf_op jit(solution)/shard_map/ppermute | solution.py:55
  390.7 24.4 %collective-permute-start.56 = (bf16[2,128,1280]{2,1,0:T(8,128)(2,1)}, bf16[2,128,1280]{2,1,0:T(8,128)(2,1)S(1)}, u32[]{:S(2)}, u32[]{:S(2)}) collective-permute-start(bf16[2,128,1280]{2,1,0:T(8,128)(2,1)} %get-tuple-element.188), channel_id=1, source_target_pairs={{0,1},{1,0},{2,3},{3,2},{4,5},{5,4},{6,7},{7,6},{8,9},{9,8},{10,11... | collective-permute-start | bytes 1966088 | tf_op jit(solution)/shard_map/ppermute | solution.py:55
  394.2 15.8 %collective-permute-start.60 = (bf16[2,80,483]{2,1,0:T(8,128)(2,1)S(1)}, bf16[2,80,483]{2,1,0:T(8,128)(2,1)S(1)}, u32[]{:S(2)}, u32[]{:S(2)}) collective-permute-start(bf16[2,80,483]{2,1,0:T(8,128)(2,1)S(1)} %get-tuple-element.194), channel_id=1, source_target_pairs={{0,6},{1,7},{2,0},{3,1},{4,2},{5,3},{6,4},{7,5},{8,14},{9,15},{10,... | collective-permute-start | bytes 463688 | tf_op jit(solution)/shard_map/ppermute | solution.py:55
  418.9 22.5 %collective-permute-start.40 = (bf16[2,128,1280]{2,1,0:T(8,128)(2,1)}, bf16[2,128,1280]{2,1,0:T(8,128)(2,1)S(1)}, u32[]{:S(2)}, u32[]{:S(2)}) collective-permute-start(bf16[2,128,1280]{2,1,0:T(8,128)(2,1)} %get-tuple-element.159), channel_id=1, source_target_pairs={{0,8},{1,9},{2,10},{3,11},{4,12},{5,13},{6,14},{7,15},{8,0},{9,1},... | collective-permute-start | bytes 1966088 | tf_op jit(solution)/shard_map/ppermute | solution.py:55
  426.2 18.7 %collective-permute-start.69 = (bf16[4,2,80,483]{3,2,1,0:T(8,128)(2,1)}, bf16[4,2,80,483]{3,2,1,0:T(8,128)(2,1)}, u32[]{:S(2)}, u32[]{:S(2)}) collective-permute-start(bf16[4,2,80,483]{3,2,1,0:T(8,128)(2,1)} %pad_maximum_fusion), channel_id=1, source_target_pairs={{0,16},{1,17},{2,18},{3,19},{4,20},{5,21},{6,22},{7,23},{8,24},{9,... | collective-permute-start | bytes 1854728 | tf_op jit(solution)/shard_map/ppermute | solution.py:55
  429.0 24.6 %collective-permute-start.64 = (bf16[128,1280]{1,0:T(8,128)(2,1)}, bf16[128,1280]{1,0:T(8,128)(2,1)S(1)}, u32[]{:S(2)}, u32[]{:S(2)}) collective-permute-start(bf16[128,1280]{1,0:T(8,128)(2,1)} %get-tuple-element.201.refs_6_), channel_id=1, source_target_pairs={{8,0},{9,1},{10,2},{11,3},{0,4},{1,5},{2,6},{3,7},{12,8},{13,9},{1... | collective-permute-start | bytes 983048 | tf_op jit(solution)/shard_map/ppermute | solution.py:107
  429.8 24.6 %collective-permute-start.62 = (bf16[128,1280]{1,0:T(8,128)(2,1)S(1)}, bf16[128,1280]{1,0:T(8,128)(2,1)S(1)}, u32[]{:S(2)}, u32[]{:S(2)}) collective-permute-start(bf16[128,1280]{1,0:T(8,128)(2,1)S(1)} %get-tuple-element.196.refs_8_), channel_id=1, source_target_pairs={{0,0},{1,1},{2,2},{3,3},{8,4},{9,5},{10,6},{11,7},{4,8},{5,9},{6,1... | collective-permute-start | bytes 983048 | tf_op jit(solution)/shard_map/ppermute | solution.py:107
  433.2 21.1 %collective-permute-start.65 = (bf16[128,1280]{1,0:T(8,128)(2,1)}, bf16[128,1280]{1,0:T(8,128)(2,1)S(1)}, u32[]{:S(2)}, u32[]{:S(2)}) collective-permute-start(bf16[128,1280]{1,0:T(8,128)(2,1)} %copy-done.104), channel_id=1, source_target_pairs={{10,0},{11,1},{8,2},{9,3},{2,4},{3,5},{0,6},{1,7},{14,8},{15,9},{1... | collective-permute-start | bytes 983048 | tf_op jit(solution)/shard_map/ppermute | solution.py:107
  441.4 17.2 %collective-permute-start.63 = (bf16[128,1280]{1,0:T(8,128)(2,1)}, bf16[128,1280]{1,0:T(8,128)(2,1)S(1)}, u32[]{:S(2)}, u32[]{:S(2)}) collective-permute-start(bf16[128,1280]{1,0:T(8,128)(2,1)} %copy-done.103), channel_id=1, source_target_pairs={{2,0},{3,1},{0,2},{1,3},{10,4},{11,5},{8,6},{9,7},{6,8},{7,9},{4,1... | collective-permute-start | bytes 983048 | tf_op jit(solution)/shard_map/ppermute | solution.py:107
  (142 other events, 975.3 us)

commit v7 on v6

--- a/solution.py
+++ b/solution.py
@@ -99,7 +99,7 @@
         moves = []
         for i in range(self.seqs):
             moves += [(0, i, 0, i * CORES + self.c), (1, i, 0, i * CORES + 1 - self.c)]
-        yield
+        yield got
         whole = shuffle([own, got], [((self.a_size, half, width), BF16)], moves)[0]
         yield whole.reshape(self.seqs, CORES * half, width)
 
@@ -1090,9 +1090,10 @@
         if at.x_split == 2:
             self.got.append(at.send(parts[1], dx=1))
 
-    def over_a(self):
+    def over_a(self, after=()):
         at = self.at
-        parts = add_blocks([[(t, 0, a) for t in self.got] for a in ahead(at.a, at.a_size)])
+        groups = [[(t, 0, a) for t in self.got] for a in ahead(at.a, at.a_size)]
+        parts = add_blocks(groups, after)
         self.got = [parts[0]] + [at.send(parts[d], da=d) for d in range(1, at.a_size)]
         return parts
 
@@ -1360,7 +1361,7 @@
     stage = at.from_cluster(output.reshape(at.a_size, half, model))
     next(stage)
     d_first, extra_first = backward(0)
-    next(stage)
+    output_got = next(stage)
     full.next()
     reduce_first = HeadsReduce(at, heads_outer(at, normed, d_first, extra_first))
     full.over_a()
@@ -1384,10 +1385,10 @@
 
     got = at.send(back_project_give(at, d_heads, w_heads, half), dc=1)
     reduce_second = HeadsReduce(at, heads_outer(at, normed, d_second, extra_second))
-    first = reduce_first.by_b(full_parts[1:2])
+    first = reduce_first.by_b([full_parts[1], output_got])
     keep(0, got)
     keep(1, got)
-    reduce_second.over_a()
+    reduce_second.over_a(full_parts[2:])
     back(0)
     parts = [to_peers(at, [first, reduce_second.by_b(keeps[1][1:])])]
     sent = back(1)

time: 471 us -> 471 us (level)
    unnamed x241 -> x253, local copies, waits for them, and re-layouts: 60.8 us -> 58.9 us
  transfers between devices with their start and end apart: 70 -> 70, of which waited for: 31 -> 32; matrix products, arithmetic and copies ran while one was open for 3% -> 3% of each run, Pallas kernels for 28% -> 28%
where the time goes in v7:
time: 471 us; the launch traced here: 463 us
  Pallas kernels  189 us (40%)
  waiting for transfers between devices  136 us (29%)
  local copies, waits for them, and re-layouts  67.3 us (14%)
  starting transfers between devices  62.3 us (13%)
  other arithmetic  5.09 us (1%)
    pallas_call x40, Pallas kernels, call(): pl.pallas_call(run, out_shape=[jax.ShapeDtypeStruct(shape, kind) for shap...  189 us
    ppermute x66, waiting for transfers between devices, send(): lax.ppermute(value, AXES, self.route(lambda x, c, a, b: ((x + dx) % self....  129 us
    unnamed x253, local copies, waits for them, and re-layouts  58.9 us
    ppermute x66, starting transfers between devices, send(): lax.ppermute(value, AXES, self.route(lambda x, c, a, b: ((x + dx) % self....  57.8 us
  transfers between devices with their start and end apart: 70, of which 32 were waited for; matrix products, arithmetic and copies ran while one was open for 3% of the time, Pallas kernels for 28%

profile of v7, /device:TPU:9, one launch (start us, length us, event | category | flops | bytes accessed | tf_op | source)
XLA Modules:
  0.0 462.8 jit_solution(2996028607602196611)
XLA Ops:
  13.2 3.4 collective-permute-done.5.refs_1_
  17.6 19.8 %collective-permute-done.3.refs_2_ = bf16[128,1280]{1,0:T(8,128)(2,1)S(1)} collective-permute-done((bf16[128,1280]{1,0:T(8,128)(2,1)S(1)}, bf16[128,1280]{1,0:T(8,128)(2,1)S(1)}, u32[]{:S(2)}, u32[]{:S(2)}) %collective-permute-start.3) | collective-permute-done | bytes 327712 | tf_op jit(solution)/shard_map/ppermute | solution.py:55
  37.4 2.4 collective-permute-done.4.refs_3_
  44.3 6.4 %collective-permute-done.9.refs_4_.refs_1_ = bf16[2,80,964]{2,1,0:T(8,128)(2,1)S(1)} collective-permute-done((bf16[2,80,964]{2,1,0:T(8,128)(2,1)S(1)}, bf16[2,80,964]{2,1,0:T(8,128)(2,1)S(1)}, u32[]{:S(2)}, u32[]{:S(2)}) %collective-permute-start.9) | collective-permute-done | bytes 308512 | tf_op jit(solution)/shard_map/ppermute | solution.py:55
  52.6 7.0 %collective-permute-done.11.refs_6_.refs_3_ = bf16[2,80,964]{2,1,0:T(8,128)(2,1)S(1)} collective-permute-done((bf16[2,80,964]{2,1,0:T(8,128)(2,1)S(1)}, bf16[2,80,964]{2,1,0:T(8,128)(2,1)S(1)}, u32[]{:S(2)}, u32[]{:S(2)}) %collective-permute-start.11) | collective-permute-done | bytes 308512 | tf_op jit(solution)/shard_map/ppermute | solution.py:55
  62.5 7.3 %collective-permute-done.8.refs_5_.refs_2_ = bf16[2,80,964]{2,1,0:T(8,128)(2,1)} collective-permute-done((bf16[2,80,964]{2,1,0:T(8,128)(2,1)S(1)}, bf16[2,80,964]{2,1,0:T(8,128)(2,1)}, u32[]{:S(2)}, u32[]{:S(2)}) %collective-permute-start.8) | collective-permute-done | bytes 308512 | tf_op jit(solution)/shard_map/ppermute | solution.py:55
  85.0 6.3 %collective-permute-done.15.refs_6_ = bf16[2,80,964]{2,1,0:T(8,128)(2,1)} collective-permute-done((bf16[2,80,964]{2,1,0:T(8,128)(2,1)}, bf16[2,80,964]{2,1,0:T(8,128)(2,1)}, u32[]{:S(2)}, u32[]{:S(2)}) %collective-permute-start.15) | collective-permute-done | bytes 308512 | tf_op jit(solution)/shard_map/ppermute | solution.py:55
  91.3 3.2 collective-permute-start.18
  96.5 4.5 pad_weights.1
  108.5 13.0 %project.1 = (bf16[2048,1536]{1,0:T(8,128)(2,1)S(1)}, bf16[2048,1280]{1,0:T(8,128)(2,1)S(1)}) custom-call(s32[4]{0:T(128)S(1)} %pad_add_fusion.2.spots, bf16[4,128,1280]{2,1,0:T(8,128)(2,1)S(1)} %shuffle.11.refs_1_.refs_0_.refs_2_, bf16[4,128,1280]{2,1,0:T(8,128)(2,1)} %collective-permute-done.6.refs_9_.refs_1_, ...), custom_call_target="tpu_custom_call" | custom-call | flops 3987500032 | bytes 11962500 | tf_op jit(solution)/shard_map/project/pallas_call | solution.py:167
  121.5 2.4 copy-done.10
  124.0 3.5 shuffle.13.refs_2_.refs_4_
  137.9 2.8 copy-done.1
  140.7 21.2 %attend_forward.1 = (bf16[2,2,4,128,320]{4,3,2,1,0:T(8,128)(2,1)S(1)}, bf16[2048,512]{1,0:T(8,128)(2,1)S(1)}) custom-call(s32[10]{0:T(128)S(1)} %pad_add_fusion.1.spots, s32[2048,128]{1,0:T(8,128)S(1)} %broadcast_in_dim.58.refs_0_, bf16[2048,1536]{1,0:T(8,128)(2,1)S(1)} %copy-done.1, bf16[2048,1536]{1,0:T(8,128)(2,1)S(1)} %copy-done.1, ...), custom_call_target="tpu_custom_call" | custom-call | flops 3300000000 | bytes 9900000 | tf_op jit(solution)/shard_map/attend_forward/pallas_call | solution.py:167
  168.8 8.6 %collective-permute-done.26.refs_3_ = bf16[512,320]{1,0:T(8,128)(2,1)S(1)} collective-permute-done((bf16[512,320]{1,0:T(8,128)(2,1)S(1)}, bf16[512,320]{1,0:T(8,128)(2,1)S(1)}, u32[]{:S(2)}, u32[]{:S(2)}) %collective-permute-start.26) | collective-permute-done | bytes 327712 | tf_op jit(solution)/shard_map/ppermute | solution.py:55
  177.4 9.0 %collective-permute-done.25.refs_2_ = bf16[512,320]{1,0:T(8,128)(2,1)S(1)} collective-permute-done((bf16[512,320]{1,0:T(8,128)(2,1)S(1)}, bf16[512,320]{1,0:T(8,128)(2,1)S(1)}, u32[]{:S(2)}, u32[]{:S(2)}) %collective-permute-start.25) | collective-permute-done | bytes 327712 | tf_op jit(solution)/shard_map/ppermute | solution.py:55
  188.3 4.2 collective-permute-done.29.refs_8_
  197.3 19.7 %middle.1 = (bf16[512,1280]{1,0:T(8,128)(2,1)}, f32[512,1280]{1,0:T(8,128)}, bf16[512,1280]{1,0:T(8,128)(2,1)}, bf16[512,1280]{1,0:T(8,128)(2,1)}, bf16[512,1280...) custom-call(s32[192]{0:T(256)S(1)} %stack.262.spots, ...), custom_call_target="tpu_custom_call" | custom-call | flops 5500000256 | bytes 16500000 | tf_op jit(solution)/shard_map/middle/pallas_call | solution.py:167
  217.7 8.5 %outer_give.1.refs_7_ = bf16[3,1280,640]{2,1,0:T(8,128)(2,1)} custom-call(s32[7]{0:T(128)} %stack.287.spots, bf16[512,1280]{1,0:T(8,128)(2,1)} %copy-done.15, bf16[512,1280]{1,0:T(8,128)(2,1)} %get-tuple-element.143.refs_1_, bf16[512,1280]{1,0:T(8,128)(2,1)} %get-tuple-element.144.refs_2_, bf16[512,1280]{1,0:T(8,128)(2,1)} %get-tuple-element.145.refs_3_, ...), custom_call_target="tpu_custom_call" | custom-call | flops 27500000 | bytes 82500 | tf_op jit(solution)/shard_map/outer_give/pallas_call | solution.py:167
  229.6 2.6 collective-permute-done.34
  232.2 4.8 %collective-permute-done.35 = bf16[512,320]{1,0:T(8,128)(2,1)S(1)} collective-permute-done((bf16[512,320]{1,0:T(8,128)(2,1)S(1)}, bf16[512,320]{1,0:T(8,128)(2,1)S(1)}, u32[]{:S(2)}, u32[]{:S(2)}) %collective-permute-start.35) | collective-permute-done | bytes 327712 | tf_op jit(solution)/shard_map/ppermute | solution.py:55
  237.0 8.9 %collective-permute-done.36 = bf16[512,320]{1,0:T(8,128)(2,1)S(1)} collective-permute-done((bf16[512,320]{1,0:T(8,128)(2,1)S(1)}, bf16[512,320]{1,0:T(8,128)(2,1)S(1)}, u32[]{:S(2)}, u32[]{:S(2)}) %collective-permute-start.36) | collective-permute-done | bytes 327712 | tf_op jit(solution)/shard_map/ppermute | solution.py:55
  246.7 10.0 %outer.1 = (bf16[3,2,2,80,640]{4,3,2,1,0:T(8,128)(2,1)}, bf16[3,2,2,80,640]{4,3,2,1,0:T(8,128)(2,1)}, bf16[3,2,2,80,640]{4,3,2,1,0:T(8,128)(2,1)}, bf16[3,2,2,80,640]{4,3,2,1,0:T(8,128)(2,1)}) custom-call(s32[7]{0:T(128)} %stack.286.spots, bf16[512,1280]{1,0:T(8,128)(2,1)} %copy-done.15, bf16[512,1280]{1,0:T(8,128)(2,1)} %get-tuple-element.143.refs_1_, ...), custom_call_target="tpu_custom_call" | custom-call | flops 1924999936 | bytes 5775000 | tf_op jit(solution)/shard_map/outer/pallas_call | solution.py:167
  263.9 2.8 copy-done.2
  270.3 20.5 %attend_backward.2 = (bf16[2048,480]{1,0:T(8,128)(2,1)S(1)}, f32[8,128]{1,0:T(8,128)S(1)}, f32[8,768]{1,0:T(8,128)S(1)}) custom-call(s32[10]{0:T(128)S(1)} %pad_add_fusion.1.spots, s32[8,2048]{1,0:T(8,128)S(1)} %broadcast_in_dim.61.refs_0_, f32[8,256]{1,0:T(8,128)S(1)} %broadcast_in_dim.63.refs_1_, bf16[2048,512]{1,0:T(8,128)(2,1)S(1)} %copy-done.111, ...), custom_call_target="tpu_custom_call" | custom-call | flops 6874999808 | bytes 20625000 | tf_op jit(solution)/shard_map/attend_backward/pallas_call | solution.py:167
  293.3 2.9 route_back.1
  296.2 3.3 add_blocks.6
  306.3 2.5 copy-done.11
  309.8 4.8 %heads_outer.2 = (bf16[4,2,80,483]{3,2,1,0:T(8,128)(2,1)S(1)}, bf16[4,2,80,483]{3,2,1,0:T(8,128)(2,1)S(1)}) custom-call(s32[1]{0:T(128)} %bitcast.54.spots, bf16[2048,1280]{1,0:T(8,128)(2,1)S(1)} %copy-done.11, bf16[2048,480]{1,0:T(8,128)(2,1)S(1)} %copy-done.4, bf16[1280,3]{1,0:T(8,128)(2,1)S(1)} %copy.53.refs_2_, bf16[3,2,80,640]{3,2,1,0:T(8,128)(2,1)S(1)} %copy-done.48), custom_call_target="tpu_custom_call" | custom-call | flops 1512499968 | bytes 4537500 | tf_op jit(solution)/shard_map/heads_outer/pallas_call | solution.py:167
  317.3 2.2 cat.1
  321.3 21.5 %attend_backward.3 = (bf16[2048,480]{1,0:T(8,128)(2,1)S(1)}, f32[8,128]{1,0:T(8,128)S(1)}, f32[8,768]{1,0:T(8,128)S(1)}) custom-call(s32[10]{0:T(128)S(1)} %pad_add_fusion.1.spots, s32[8,2048]{1,0:T(8,128)S(1)} %broadcast_in_dim.61.refs_0_, f32[8,256]{1,0:T(8,128)S(1)} %broadcast_in_dim.63.refs_1_, bf16[2048,512]{1,0:T(8,128)(2,1)S(1)} %copy-done.112, ...), custom_call_target="tpu_custom_call" | custom-call | flops 6874999808 | bytes 20625000 | tf_op jit(solution)/shard_map/attend_backward/pallas_call | solution.py:167
  343.4 5.3 %collective-permute-done.47 = bf16[3,80,640]{2,1,0:T(8,128)(2,1)S(1)} collective-permute-done((bf16[3,80,640]{2,1,0:T(8,128)(2,1)S(1)}, bf16[3,80,640]{2,1,0:T(8,128)(2,1)S(1)}, u32[]{:S(2)}, u32[]{:S(2)}) %collective-permute-start.47) | collective-permute-done | bytes 307232 | tf_op jit(solution)/shard_map/ppermute | solution.py:55
  352.8 5.0 %back_project.3.refs_3_ = bf16[2,2,2,128,1280]{4,3,2,1,0:T(8,128)(2,1)} custom-call(s32[3]{0:T(128)S(1)} %pad_add_fusion.7.spots, bf16[4,2,2,128,480]{4,3,2,1,0:T(8,128)(2,1)S(1)} %bitcast.121, bf16[4,2,2,128,480]{4,3,2,1,0:T(8,128)(2,1)S(1)} %bitcast.124, bf16[1280,480]{1,0:T(8,128)(2,1)S(1)} %copy-done.17, bf16[1280,480]{1,0:T(8,128)(2,1)S(1)} %copy-done.20, ...), custom_call_target="tpu_custom_call" | custom-call | flops 962499968 | bytes 2887500 | tf_op jit(solution)/shard_map/back_project/pallas_call | solution.py:167
  361.3 2.5 collective-permute-done.40.refs_10_.refs_1_
  366.5 2.5 copy-done.12
  369.0 5.7 %heads_outer.3 = (bf16[4,2,80,483]{3,2,1,0:T(8,128)(2,1)S(1)}, bf16[4,2,80,483]{3,2,1,0:T(8,128)(2,1)}) custom-call(s32[1]{0:T(128)} %bitcast.54.spots, bf16[2048,1280]{1,0:T(8,128)(2,1)S(1)} %copy-done.12, bf16[2048,480]{1,0:T(8,128)(2,1)S(1)} %copy-done.7, bf16[1280,3]{1,0:T(8,128)(2,1)S(1)} %copy.54.refs_2_, bf16[2,2,2,128,1280]{4,3,2,1,0:T(8,128)(2,1)} %back_project.3.refs_3_), custom_call_target="tpu_custom_call" | custom-call | flops 1512499968 | bytes 4537500 | tf_op jit(solution)/shard_map/heads_outer/pallas_call | solution.py:167
  379.3 4.7 %back_project.4 = (f32[2,128,1280]{2,1,0:T(8,128)S(1)}, bf16[2,128,1280]{2,1,0:T(8,128)(2,1)}) custom-call(s32[4]{0:T(128)S(1)} %add_add_fusion.2.spots, bf16[4,2,2,128,480]{4,3,2,1,0:T(8,128)(2,1)S(1)} %bitcast.122, bf16[4,2,2,128,480]{4,3,2,1,0:T(8,128)(2,1)S(1)} %bitcast.125, bf16[1280,480]{1,0:T(8,128)(2,1)S(1)} %copy-done.18, ...), custom_call_target="tpu_custom_call" | custom-call | flops 962499968 | bytes 2887500 | tf_op jit(solution)/shard_map/back_project/pallas_call | solution.py:167
  384.3 4.4 back_project.5
  396.8 3.3 collective-permute-start.59
  400.2 2.3 norm_back.2
  402.5 8.1 %collective-permute-done.59.refs_2_.refs_6_ = bf16[2,80,483]{2,1,0:T(8,128)(2,1)S(1)} collective-permute-done((bf16[2,80,483]{2,1,0:T(8,128)(2,1)S(1)}, bf16[2,80,483]{2,1,0:T(8,128)(2,1)S(1)}, u32[]{:S(2)}, u32[]{:S(2)}) %collective-permute-start.59) | collective-permute-done | bytes 154592 | tf_op jit(solution)/shard_map/ppermute | solution.py:55
  410.6 3.2 collective-permute-done.60.refs_3_.refs_7_
  415.1 2.7 collective-permute-start.68
  419.8 4.5 collective-permute-done.68.refs_3_
  428.1 2.4 collective-permute-start.62
  435.3 3.2 finish_full.1
  445.0 5.1 %finish_heads.1 = (f32[160,1280]{1,0:T(8,128)}, f32[160,1280]{1,0:T(8,128)}, f32[160,1280]{1,0:T(8,128)}, f32[160,1]{1,0:T(8,128)S(1)}, f32[160,3]{1,0:T(8,128)S(1)}) custom-call(s32[5]{0:T(128)S(1)} %stack.314.spots, bf16[2,80,483]{2,1,0:T(8,128)(2,1)S(1)} %get-tuple-element.200.refs_5_.refs_0_, bf16[2,80,483]{2,1,0:T(8,128)(2,1)S(1)} %copy-done.104, ...), custom_call_target="tpu_custom_call" | custom-call | flops 1100000000 | bytes 3300000 | tf_op jit(solution)/shard_map/finish_heads/pallas_call | solution.py:167
  452.2 7.0 %collective-permute-done.65.refs_3_ = bf16[128,1280]{1,0:T(8,128)(2,1)S(1)} collective-permute-done((bf16[128,1280]{1,0:T(8,128)(2,1)}, bf16[128,1280]{1,0:T(8,128)(2,1)S(1)}, u32[]{:S(2)}, u32[]{:S(2)}) %collective-permute-start.65) | collective-permute-done | bytes 327712 | tf_op jit(solution)/shard_map/ppermute | solution.py:107
  (485 shorter events, 148.4 us)
Async XLA Ops:
  9.3 28.1 %collective-permute-start.3 = (bf16[128,1280]{1,0:T(8,128)(2,1)S(1)}, bf16[128,1280]{1,0:T(8,128)(2,1)S(1)}, u32[]{:S(2)}, u32[]{:S(2)}) collective-permute-start(bf16[128,1280]{1,0:T(8,128)(2,1)S(1)} %get-tuple-element.119), channel_id=1, source_target_pairs={{0,4},{1,5},{2,6},{3,7},{4,0},{5,1},{6,2},{7,3},{8,12},{9,13},{10,... | collective-permute-start | bytes 983048 | tf_op jit(solution)/shard_map/ppermute | solution.py:55
  10.3 29.5 %collective-permute-start.4 = (bf16[128,1280]{1,0:T(8,128)(2,1)S(1)}, bf16[128,1280]{1,0:T(8,128)(2,1)S(1)}, u32[]{:S(2)}, u32[]{:S(2)}) collective-permute-start(bf16[128,1280]{1,0:T(8,128)(2,1)S(1)} %get-tuple-element.120), channel_id=1, source_target_pairs={{0,6},{1,7},{2,0},{3,1},{4,2},{5,3},{6,4},{7,5},{8,14},{9,15},{10,... | collective-permute-start | bytes 983048 | tf_op jit(solution)/shard_map/ppermute | solution.py:55
  40.8 30.4 %collective-permute-start.7 = (bf16[4,128,1280]{2,1,0:T(8,128)(2,1)S(1)}, bf16[4,128,1280]{2,1,0:T(8,128)(2,1)}, u32[]{:S(2)}, u32[]{:S(2)}) collective-permute-start(bf16[4,128,1280]{2,1,0:T(8,128)(2,1)S(1)} %shuffle.11.refs_1_.refs_0_.refs_2_), channel_id=1, source_target_pairs={{0,1},{1,0},{2,3},{3,2},{4,5},{5,4},{6,7},{7,6},{8,9},{9,8},{10,11... | collective-permute-start | bytes 3932168 | tf_op jit(solution)/shard_map/ppermute | solution.py:55
  42.1 17.5 %collective-permute-start.11 = (bf16[2,80,964]{2,1,0:T(8,128)(2,1)S(1)}, bf16[2,80,964]{2,1,0:T(8,128)(2,1)S(1)}, u32[]{:S(2)}, u32[]{:S(2)}) collective-permute-start(bf16[2,80,964]{2,1,0:T(8,128)(2,1)S(1)} %shuffle.10.refs_4_.refs_0_), channel_id=1, source_target_pairs={{0,6},{1,7},{2,0},{3,1},{4,2},{5,3},{6,4},{7,5},{8,14},{9,15},{10,... | collective-permute-start | bytes 925448 | tf_op jit(solution)/shard_map/ppermute | solution.py:55
  43.6 26.2 %collective-permute-start.8 = (bf16[2,80,964]{2,1,0:T(8,128)(2,1)S(1)}, bf16[2,80,964]{2,1,0:T(8,128)(2,1)}, u32[]{:S(2)}, u32[]{:S(2)}) collective-permute-start(bf16[2,80,964]{2,1,0:T(8,128)(2,1)S(1)} %shuffle.10.refs_4_.refs_0_), channel_id=1, source_target_pairs={{0,4},{1,5},{2,6},{3,7},{4,0},{5,1},{6,2},{7,3},{8,12},{9,13},{10,... | collective-permute-start | bytes 925448 | tf_op jit(solution)/shard_map/ppermute | solution.py:55
  50.7 19.1 %collective-permute-start.10 = (bf16[2,80,964]{2,1,0:T(8,128)(2,1)S(1)}, bf16[2,80,964]{2,1,0:T(8,128)(2,1)S(1)}, u32[]{:S(2)}, u32[]{:S(2)}) collective-permute-start(bf16[2,80,964]{2,1,0:T(8,128)(2,1)S(1)} %collective-permute-done.9.refs_4_.refs_1_), channel_id=1, source_target_pairs={{0,16},{1,17},{2,18},{3,19},{4,20},{5,21},{6,22},{7,23},{8,24},{9,... | collective-permute-start | bytes 925448 | tf_op jit(solution)/shard_map/ppermute | solution.py:55
  61.5 33.8 %collective-permute-start.6 = (bf16[4,128,1280]{2,1,0:T(8,128)(2,1)S(1)}, bf16[4,128,1280]{2,1,0:T(8,128)(2,1)}, u32[]{:S(2)}, u32[]{:S(2)}) collective-permute-start(bf16[4,128,1280]{2,1,0:T(8,128)(2,1)S(1)} %shuffle.11.refs_1_.refs_0_.refs_2_), channel_id=1, source_target_pairs={{0,8},{1,9},{2,10},{3,11},{4,12},{5,13},{6,14},{7,15},{8,0},{9,1},... | collective-permute-start | bytes 3932168 | tf_op jit(solution)/shard_map/ppermute | solution.py:55
  71.3 24.1 %collective-permute-start.13 = (bf16[4,128,1280]{2,1,0:T(8,128)(2,1)}, bf16[4,128,1280]{2,1,0:T(8,128)(2,1)}, u32[]{:S(2)}, u32[]{:S(2)}) collective-permute-start(bf16[4,128,1280]{2,1,0:T(8,128)(2,1)} %collective-permute-done.7.refs_10_.refs_2_), channel_id=1, source_target_pairs={{0,8},{1,9},{2,10},{3,11},{4,12},{5,13},{6,14},{7,15},{8,0},{9,1},... | collective-permute-start | bytes 3932168 | tf_op jit(solution)/shard_map/ppermute | solution.py:55
  74.3 20.2 %collective-permute-start.16 = (bf16[2,128,1280]{2,1,0:T(8,128)(2,1)}, bf16[2,128,1280]{2,1,0:T(8,128)(2,1)S(1)}, u32[]{:S(2)}, u32[]{:S(2)}) collective-permute-start(bf16[2,128,1280]{2,1,0:T(8,128)(2,1)} %get-tuple-element.124), channel_id=1, source_target_pairs={{0,8},{1,9},{2,10},{3,11},{4,12},{5,13},{6,14},{7,15},{8,0},{9,1},... | collective-permute-start | bytes 1966088 | tf_op jit(solution)/shard_map/ppermute | solution.py:55
  76.1 15.2 %collective-permute-start.15 = (bf16[2,80,964]{2,1,0:T(8,128)(2,1)}, bf16[2,80,964]{2,1,0:T(8,128)(2,1)}, u32[]{:S(2)}, u32[]{:S(2)}) collective-permute-start(bf16[2,80,964]{2,1,0:T(8,128)(2,1)} %collective-permute-done.8.refs_5_.refs_2_), channel_id=1, source_target_pairs={{0,16},{1,17},{2,18},{3,19},{4,20},{5,21},{6,22},{7,23},{8,24},{9,... | collective-permute-start | bytes 925448 | tf_op jit(solution)/shard_map/ppermute | solution.py:55
  84.3 39.6 %collective-permute-start.17 = (bf16[3,80,640]{2,1,0:T(8,128)(2,1)S(1)}, bf16[3,80,640]{2,1,0:T(8,128)(2,1)}, u32[]{:S(2)}, u32[]{:S(2)}) collective-permute-start(bf16[3,80,640]{2,1,0:T(8,128)(2,1)S(1)} %quarter.1.refs_8_.refs_0_), channel_id=1, source_target_pairs={{0,2},{1,3},{2,4},{3,5},{4,6},{5,7},{6,0},{7,1},{8,10},{9,11},{10,... | collective-permute-start | bytes 921608 | tf_op jit(solution)/shard_map/ppermute | solution.py:55
  91.3 32.6 %collective-permute-start.18 = (bf16[3,80,640]{2,1,0:T(8,128)(2,1)S(1)}, bf16[3,80,640]{2,1,0:T(8,128)(2,1)}, u32[]{:S(2)}, u32[]{:S(2)}) collective-permute-start(bf16[3,80,640]{2,1,0:T(8,128)(2,1)S(1)} %quarter.1.refs_8_.refs_0_), channel_id=1, source_target_pairs={{0,4},{1,5},{2,6},{3,7},{4,0},{5,1},{6,2},{7,3},{8,12},{9,13},{10,... | collective-permute-start | bytes 921608 | tf_op jit(solution)/shard_map/ppermute | solution.py:55
  95.3 28.6 %collective-permute-start.19 = (bf16[3,80,640]{2,1,0:T(8,128)(2,1)S(1)}, bf16[3,80,640]{2,1,0:T(8,128)(2,1)}, u32[]{:S(2)}, u32[]{:S(2)}) collective-permute-start(bf16[3,80,640]{2,1,0:T(8,128)(2,1)S(1)} %quarter.1.refs_8_.refs_0_), channel_id=1, source_target_pairs={{0,6},{1,7},{2,0},{3,1},{4,2},{5,3},{6,4},{7,5},{8,14},{9,15},{10,... | collective-permute-start | bytes 921608 | tf_op jit(solution)/shard_map/ppermute | solution.py:55
  128.7 35.9 %collective-permute-start.27 = (bf16[4,3,80,640]{3,2,1,0:T(8,128)(2,1)S(1)}, bf16[4,3,80,640]{3,2,1,0:T(8,128)(2,1)}, u32[]{:S(2)}, u32[]{:S(2)}) collective-permute-start(bf16[4,3,80,640]{3,2,1,0:T(8,128)(2,1)S(1)} %shuffle.13.refs_2_.refs_4_), channel_id=1, source_target_pairs={{0,1},{1,0},{2,3},{3,2},{4,5},{5,4},{6,7},{7,6},{8,9},{9,8},{10,11... | collective-permute-start | bytes 3686408 | tf_op jit(solution)/shard_map/ppermute | solution.py:55
  132.1 29.8 %collective-permute-start.21 = (bf16[128,1280]{1,0:T(8,128)(2,1)S(1)}, bf16[128,1280]{1,0:T(8,128)(2,1)S(1)}, u32[]{:S(2)}, u32[]{:S(2)}) collective-permute-start(bf16[128,1280]{1,0:T(8,128)(2,1)S(1)} %get-tuple-element.131), channel_id=1, source_target_pairs={{0,2},{1,3},{2,4},{3,5},{4,6},{5,7},{6,0},{7,1},{8,10},{9,11},{10,... | collective-permute-start | bytes 983048 | tf_op jit(solution)/shard_map/ppermute | solution.py:55
  133.9 28.0 %collective-permute-start.22 = (bf16[128,1280]{1,0:T(8,128)(2,1)S(1)}, bf16[128,1280]{1,0:T(8,128)(2,1)S(1)}, u32[]{:S(2)}, u32[]{:S(2)}) collective-permute-start(bf16[128,1280]{1,0:T(8,128)(2,1)S(1)} %get-tuple-element.132), channel_id=1, source_target_pairs={{0,4},{1,5},{2,6},{3,7},{4,0},{5,1},{6,2},{7,3},{8,12},{9,13},{10,... | collective-permute-start | bytes 983048 | tf_op jit(solution)/shard_map/ppermute | solution.py:55
  135.4 28.2 %collective-permute-start.23 = (bf16[128,1280]{1,0:T(8,128)(2,1)S(1)}, bf16[128,1280]{1,0:T(8,128)(2,1)S(1)}, u32[]{:S(2)}, u32[]{:S(2)}) collective-permute-start(bf16[128,1280]{1,0:T(8,128)(2,1)S(1)} %get-tuple-element.133), channel_id=1, source_target_pairs={{0,6},{1,7},{2,0},{3,1},{4,2},{5,3},{6,4},{7,5},{8,14},{9,15},{10,... | collective-permute-start | bytes 983048 | tf_op jit(solution)/shard_map/ppermute | solution.py:55
  136.4 51.4 %collective-permute-start.28 = (bf16[4,3,80,640]{3,2,1,0:T(8,128)(2,1)S(1)}, bf16[4,3,80,640]{3,2,1,0:T(8,128)(2,1)}, u32[]{:S(2)}, u32[]{:S(2)}) collective-permute-start(bf16[4,3,80,640]{3,2,1,0:T(8,128)(2,1)S(1)} %shuffle.13.refs_2_.refs_4_), channel_id=1, source_target_pairs={{0,16},{1,17},{2,18},{3,19},{4,20},{5,21},{6,22},{7,23},{8,24},{9,... | collective-permute-start | bytes 3686408 | tf_op jit(solution)/shard_map/ppermute | solution.py:55
  164.6 27.9 %collective-permute-start.29 = (bf16[4,3,80,640]{3,2,1,0:T(8,128)(2,1)}, bf16[4,3,80,640]{3,2,1,0:T(8,128)(2,1)}, u32[]{:S(2)}, u32[]{:S(2)}) collective-permute-start(bf16[4,3,80,640]{3,2,1,0:T(8,128)(2,1)} %collective-permute-done.27.refs_6_), channel_id=1, source_target_pairs={{0,16},{1,17},{2,18},{3,19},{4,20},{5,21},{6,22},{7,23},{8,24},{9,... | collective-permute-start | bytes 3686408 | tf_op jit(solution)/shard_map/ppermute | solution.py:55
  167.5 18.9 %collective-permute-start.25 = (bf16[512,320]{1,0:T(8,128)(2,1)S(1)}, bf16[512,320]{1,0:T(8,128)(2,1)S(1)}, u32[]{:S(2)}, u32[]{:S(2)}) collective-permute-start(bf16[512,320]{1,0:T(8,128)(2,1)S(1)} %bitcast.160), channel_id=1, source_target_pairs={{0,1},{1,0},{2,3},{3,2},{4,5},{5,4},{6,7},{7,6},{8,9},{9,8},{10,11... | collective-permute-start | bytes 983048 | tf_op jit(solution)/shard_map/ppermute | solution.py:55
  168.8 17.6 %collective-permute-start.24 = (bf16[512,320]{1,0:T(8,128)(2,1)S(1)}, bf16[512,320]{1,0:T(8,128)(2,1)S(1)}, u32[]{:S(2)}, u32[]{:S(2)}) collective-permute-start(bf16[512,320]{1,0:T(8,128)(2,1)S(1)} %bitcast.159), channel_id=1, source_target_pairs={{0,8},{1,9},{2,10},{3,11},{4,12},{5,13},{6,14},{7,15},{8,0},{9,1},... | collective-permute-start | bytes 983048 | tf_op jit(solution)/shard_map/ppermute | solution.py:55
  226.2 19.8 %collective-permute-start.33 = (bf16[3,1280,640]{2,1,0:T(8,128)(2,1)}, bf16[3,1280,640]{2,1,0:T(8,128)(2,1)}, u32[]{:S(2)}, u32[]{:S(2)}) collective-permute-start(bf16[3,1280,640]{2,1,0:T(8,128)(2,1)} %outer_give.1.refs_7_), channel_id=1, source_target_pairs={{0,8},{1,9},{2,10},{3,11},{4,12},{5,13},{6,14},{7,15},{8,0},{9,1},... | collective-permute-start | bytes 14745608 | tf_op jit(solution)/shard_map/ppermute | solution.py:55
  226.9 19.1 %collective-permute-start.36 = (bf16[512,320]{1,0:T(8,128)(2,1)S(1)}, bf16[512,320]{1,0:T(8,128)(2,1)S(1)}, u32[]{:S(2)}, u32[]{:S(2)}) collective-permute-start(bf16[512,320]{1,0:T(8,128)(2,1)S(1)} %get-tuple-element.150), channel_id=1, source_target_pairs={{0,9},{1,8},{2,11},{3,10},{4,13},{5,12},{6,15},{7,14},{8,1},{9,0},... | collective-permute-start | bytes 983048 | tf_op jit(solution)/shard_map/ppermute | solution.py:55
  256.7 39.5 %collective-permute-start.41 = (bf16[3,2,2,80,640]{4,3,2,1,0:T(8,128)(2,1)}, bf16[3,2,2,80,640]{4,3,2,1,0:T(8,128)(2,1)S(1)}, u32[]{:S(2)}, u32[]{:S(2)}) collective-permute-start(bf16[3,2,2,80,640]{4,3,2,1,0:T(8,128)(2,1)} %get-tuple-element.160), channel_id=1, source_target_pairs={{0,16},{1,17},{2,18},{3,19},{4,20},{5,21},{6,22},{7,23},{8,24},{9,... | collective-permute-start | bytes 3686408 | tf_op jit(solution)/shard_map/ppermute | solution.py:55
  257.9 38.3 %collective-permute-start.42 = (bf16[3,2,2,80,640]{4,3,2,1,0:T(8,128)(2,1)}, bf16[3,2,2,80,640]{4,3,2,1,0:T(8,128)(2,1)}, u32[]{:S(2)}, u32[]{:S(2)}) collective-permute-start(bf16[3,2,2,80,640]{4,3,2,1,0:T(8,128)(2,1)} %get-tuple-element.162), channel_id=1, source_target_pairs={{0,1},{1,0},{2,3},{3,2},{4,5},{5,4},{6,7},{7,6},{8,9},{9,8},{10,11... | collective-permute-start | bytes 3686408 | tf_op jit(solution)/shard_map/ppermute | solution.py:55
  261.1 30.0 %collective-permute-start.37 = (bf16[128,1280]{1,0:T(8,128)(2,1)}, bf16[128,1280]{1,0:T(8,128)(2,1)}, u32[]{:S(2)}, u32[]{:S(2)}) collective-permute-start(bf16[128,1280]{1,0:T(8,128)(2,1)} %get-tuple-element.153), channel_id=1, source_target_pairs={{0,2},{1,3},{2,4},{3,5},{4,6},{5,7},{6,0},{7,1},{8,10},{9,11},{10,... | collective-permute-start | bytes 983048 | tf_op jit(solution)/shard_map/ppermute | solution.py:55
  261.1 29.9 %collective-permute-start.38 = (bf16[128,1280]{1,0:T(8,128)(2,1)}, bf16[128,1280]{1,0:T(8,128)(2,1)}, u32[]{:S(2)}, u32[]{:S(2)}) collective-permute-start(bf16[128,1280]{1,0:T(8,128)(2,1)} %get-tuple-element.154), channel_id=1, source_target_pairs={{0,4},{1,5},{2,6},{3,7},{4,0},{5,1},{6,2},{7,3},{8,12},{9,13},{10,... | collective-permute-start | bytes 983048 | tf_op jit(solution)/shard_map/ppermute | solution.py:55
  262.7 29.6 %collective-permute-start.39 = (bf16[128,1280]{1,0:T(8,128)(2,1)}, bf16[128,1280]{1,0:T(8,128)(2,1)}, u32[]{:S(2)}, u32[]{:S(2)}) collective-permute-start(bf16[128,1280]{1,0:T(8,128)(2,1)} %get-tuple-element.155), channel_id=1, source_target_pairs={{0,6},{1,7},{2,0},{3,1},{4,2},{5,3},{6,4},{7,5},{8,14},{9,15},{10,... | collective-permute-start | bytes 983048 | tf_op jit(solution)/shard_map/ppermute | solution.py:55
  301.1 15.2 %collective-permute-start.43 = (bf16[3,2,80,640]{3,2,1,0:T(8,128)(2,1)}, bf16[3,2,80,640]{3,2,1,0:T(8,128)(2,1)S(1)}, u32[]{:S(2)}, u32[]{:S(2)}) collective-permute-start(bf16[3,2,80,640]{3,2,1,0:T(8,128)(2,1)} %get-tuple-element.164), channel_id=1, source_target_pairs={{0,1},{1,0},{2,3},{3,2},{4,5},{5,4},{6,7},{7,6},{8,9},{9,8},{10,11... | collective-permute-start | bytes 1843208 | tf_op jit(solution)/shard_map/ppermute | solution.py:55
  302.4 14.8 %collective-permute-start.44 = (bf16[3,2,80,640]{3,2,1,0:T(8,128)(2,1)}, bf16[3,2,80,640]{3,2,1,0:T(8,128)(2,1)}, u32[]{:S(2)}, u32[]{:S(2)}) collective-permute-start(bf16[3,2,80,640]{3,2,1,0:T(8,128)(2,1)} %get-tuple-element.166), channel_id=1, source_target_pairs={{0,16},{1,17},{2,18},{3,19},{4,20},{5,21},{6,22},{7,23},{8,24},{9,... | collective-permute-start | bytes 1843208 | tf_op jit(solution)/shard_map/ppermute | solution.py:55
  314.7 35.5 %collective-permute-start.51 = (bf16[4,2,80,483]{3,2,1,0:T(8,128)(2,1)S(1)}, bf16[4,2,80,483]{3,2,1,0:T(8,128)(2,1)S(1)}, u32[]{:S(2)}, u32[]{:S(2)}) collective-permute-start(bf16[4,2,80,483]{3,2,1,0:T(8,128)(2,1)S(1)} %get-tuple-element.177), channel_id=1, source_target_pairs={{0,16},{1,17},{2,18},{3,19},{4,20},{5,21},{6,22},{7,23},{8,24},{9,... | collective-permute-start | bytes 1854728 | tf_op jit(solution)/shard_map/ppermute | solution.py:55
  319.5 23.3 %collective-permute-start.45 = (bf16[3,80,640]{2,1,0:T(8,128)(2,1)S(1)}, bf16[3,80,640]{2,1,0:T(8,128)(2,1)S(1)}, u32[]{:S(2)}, u32[]{:S(2)}) collective-permute-start(bf16[3,80,640]{2,1,0:T(8,128)(2,1)S(1)} %get-tuple-element.172), channel_id=1, source_target_pairs={{0,2},{1,3},{2,4},{3,5},{4,6},{5,7},{6,0},{7,1},{8,10},{9,11},{10,... | collective-permute-start | bytes 921608 | tf_op jit(solution)/shard_map/ppermute | solution.py:55
  319.6 23.8 %collective-permute-start.46 = (bf16[3,80,640]{2,1,0:T(8,128)(2,1)S(1)}, bf16[3,80,640]{2,1,0:T(8,128)(2,1)S(1)}, u32[]{:S(2)}, u32[]{:S(2)}) collective-permute-start(bf16[3,80,640]{2,1,0:T(8,128)(2,1)S(1)} %get-tuple-element.173), channel_id=1, source_target_pairs={{0,4},{1,5},{2,6},{3,7},{4,0},{5,1},{6,2},{7,3},{8,12},{9,13},{10,... | collective-permute-start | bytes 921608 | tf_op jit(solution)/shard_map/ppermute | solution.py:55
  321.2 27.6 %collective-permute-start.47 = (bf16[3,80,640]{2,1,0:T(8,128)(2,1)S(1)}, bf16[3,80,640]{2,1,0:T(8,128)(2,1)S(1)}, u32[]{:S(2)}, u32[]{:S(2)}) collective-permute-start(bf16[3,80,640]{2,1,0:T(8,128)(2,1)S(1)} %get-tuple-element.174), channel_id=1, source_target_pairs={{0,6},{1,7},{2,0},{3,1},{4,2},{5,3},{6,4},{7,5},{8,14},{9,15},{10,... | collective-permute-start | bytes 921608 | tf_op jit(solution)/shard_map/ppermute | solution.py:55
  357.7 21.5 %collective-permute-start.52 = (bf16[2,2,2,128,1280]{4,3,2,1,0:T(8,128)(2,1)}, bf16[2,2,2,128,1280]{4,3,2,1,0:T(8,128)(2,1)}, u32[]{:S(2)}, u32[]{:S(2)}) collective-permute-start(bf16[2,2,2,128,1280]{4,3,2,1,0:T(8,128)(2,1)} %back_project.3.refs_3_), channel_id=1, source_target_pairs={{0,8},{1,9},{2,10},{3,11},{4,12},{5,13},{6,14},{7,15},{8,0},{9,1},... | collective-permute-start | bytes 7864328 | tf_op jit(solution)/shard_map/ppermute | solution.py:55
  359.4 17.2 %collective-permute-start.48 = (bf16[3,80,640]{2,1,0:T(8,128)(2,1)}, bf16[3,80,640]{2,1,0:T(8,128)(2,1)}, u32[]{:S(2)}, u32[]{:S(2)}) collective-permute-start(bf16[3,80,640]{2,1,0:T(8,128)(2,1)} %add_blocks.7.refs_8_.refs_0_), channel_id=1, source_target_pairs={{0,16},{1,17},{2,18},{3,19},{4,20},{5,21},{6,22},{7,23},{8,24},{9,... | collective-permute-start | bytes 921608 | tf_op jit(solution)/shard_map/ppermute | solution.py:55
  359.7 15.0 %collective-permute-start.53 = (bf16[2,80,483]{2,1,0:T(8,128)(2,1)S(1)}, bf16[2,80,483]{2,1,0:T(8,128)(2,1)S(1)}, u32[]{:S(2)}, u32[]{:S(2)}) collective-permute-start(bf16[2,80,483]{2,1,0:T(8,128)(2,1)S(1)} %get-tuple-element.179), channel_id=1, source_target_pairs={{0,2},{1,3},{2,4},{3,5},{4,6},{5,7},{6,0},{7,1},{8,10},{9,11},{10,... | collective-permute-start | bytes 463688 | tf_op jit(solution)/shard_map/ppermute | solution.py:55
  359.7 15.9 %collective-permute-start.54 = (bf16[2,80,483]{2,1,0:T(8,128)(2,1)}, bf16[2,80,483]{2,1,0:T(8,128)(2,1)}, u32[]{:S(2)}, u32[]{:S(2)}) collective-permute-start(bf16[2,80,483]{2,1,0:T(8,128)(2,1)} %get-tuple-element.180), channel_id=1, source_target_pairs={{0,4},{1,5},{2,6},{3,7},{4,0},{5,1},{6,2},{7,3},{8,12},{9,13},{10,... | collective-permute-start | bytes 463688 | tf_op jit(solution)/shard_map/ppermute | solution.py:55
  375.3 18.6 %collective-permute-start.57 = (bf16[4,2,80,483]{3,2,1,0:T(8,128)(2,1)}, bf16[4,2,80,483]{3,2,1,0:T(8,128)(2,1)S(1)}, u32[]{:S(2)}, u32[]{:S(2)}) collective-permute-start(bf16[4,2,80,483]{3,2,1,0:T(8,128)(2,1)} %get-tuple-element.190), channel_id=1, source_target_pairs={{0,16},{1,17},{2,18},{3,19},{4,20},{5,21},{6,22},{7,23},{8,24},{9,... | collective-permute-start | bytes 1854728 | tf_op jit(solution)/shard_map/ppermute | solution.py:55
  384.0 16.2 %collective-permute-start.61 = (bf16[2,128,1280]{2,1,0:T(8,128)(2,1)}, bf16[2,128,1280]{2,1,0:T(8,128)(2,1)}, u32[]{:S(2)}, u32[]{:S(2)}) collective-permute-start(bf16[2,128,1280]{2,1,0:T(8,128)(2,1)} %get-tuple-element.195), channel_id=1, source_target_pairs={{0,1},{1,0},{2,3},{3,2},{4,5},{5,4},{6,7},{7,6},{8,9},{9,8},{10,11... | collective-permute-start | bytes 1966088 | tf_op jit(solution)/shard_map/ppermute | solution.py:55
  389.8 24.3 %collective-permute-start.56 = (bf16[2,128,1280]{2,1,0:T(8,128)(2,1)}, bf16[2,128,1280]{2,1,0:T(8,128)(2,1)S(1)}, u32[]{:S(2)}, u32[]{:S(2)}) collective-permute-start(bf16[2,128,1280]{2,1,0:T(8,128)(2,1)} %get-tuple-element.188), channel_id=1, source_target_pairs={{0,1},{1,0},{2,3},{3,2},{4,5},{5,4},{6,7},{7,6},{8,9},{9,8},{10,11... | collective-permute-start | bytes 1966088 | tf_op jit(solution)/shard_map/ppermute | solution.py:55
  396.8 13.8 %collective-permute-start.59 = (bf16[2,80,483]{2,1,0:T(8,128)(2,1)S(1)}, bf16[2,80,483]{2,1,0:T(8,128)(2,1)S(1)}, u32[]{:S(2)}, u32[]{:S(2)}) collective-permute-start(bf16[2,80,483]{2,1,0:T(8,128)(2,1)S(1)} %get-tuple-element.193), channel_id=1, source_target_pairs={{0,4},{1,5},{2,6},{3,7},{4,0},{5,1},{6,2},{7,3},{8,12},{9,13},{10,... | collective-permute-start | bytes 463688 | tf_op jit(solution)/shard_map/ppermute | solution.py:55
  400.1 13.7 %collective-permute-start.60 = (bf16[2,80,483]{2,1,0:T(8,128)(2,1)S(1)}, bf16[2,80,483]{2,1,0:T(8,128)(2,1)S(1)}, u32[]{:S(2)}, u32[]{:S(2)}) collective-permute-start(bf16[2,80,483]{2,1,0:T(8,128)(2,1)S(1)} %get-tuple-element.194), channel_id=1, source_target_pairs={{0,6},{1,7},{2,0},{3,1},{4,2},{5,3},{6,4},{7,5},{8,14},{9,15},{10,... | collective-permute-start | bytes 463688 | tf_op jit(solution)/shard_map/ppermute | solution.py:55
  425.2 18.3 %collective-permute-start.69 = (bf16[4,2,80,483]{3,2,1,0:T(8,128)(2,1)}, bf16[4,2,80,483]{3,2,1,0:T(8,128)(2,1)}, u32[]{:S(2)}, u32[]{:S(2)}) collective-permute-start(bf16[4,2,80,483]{3,2,1,0:T(8,128)(2,1)} %pad_maximum_fusion), channel_id=1, source_target_pairs={{0,16},{1,17},{2,18},{3,19},{4,20},{5,21},{6,22},{7,23},{8,24},{9,... | collective-permute-start | bytes 1854728 | tf_op jit(solution)/shard_map/ppermute | solution.py:55
  428.1 24.2 %collective-permute-start.64 = (bf16[128,1280]{1,0:T(8,128)(2,1)}, bf16[128,1280]{1,0:T(8,128)(2,1)S(1)}, u32[]{:S(2)}, u32[]{:S(2)}) collective-permute-start(bf16[128,1280]{1,0:T(8,128)(2,1)} %get-tuple-element.201.refs_6_), channel_id=1, source_target_pairs={{8,0},{9,1},{10,2},{11,3},{0,4},{1,5},{2,6},{3,7},{12,8},{13,9},{1... | collective-permute-start | bytes 983048 | tf_op jit(solution)/shard_map/ppermute | solution.py:107
  428.1 31.1 %collective-permute-start.62 = (bf16[128,1280]{1,0:T(8,128)(2,1)S(1)}, bf16[128,1280]{1,0:T(8,128)(2,1)S(1)}, u32[]{:S(2)}, u32[]{:S(2)}) collective-permute-start(bf16[128,1280]{1,0:T(8,128)(2,1)S(1)} %get-tuple-element.196.refs_8_), channel_id=1, source_target_pairs={{0,0},{1,1},{2,2},{3,3},{8,4},{9,5},{10,6},{11,7},{4,8},{5,9},{6,1... | collective-permute-start | bytes 983048 | tf_op jit(solution)/shard_map/ppermute | solution.py:107
  430.5 28.7 %collective-permute-start.65 = (bf16[128,1280]{1,0:T(8,128)(2,1)}, bf16[128,1280]{1,0:T(8,128)(2,1)S(1)}, u32[]{:S(2)}, u32[]{:S(2)}) collective-permute-start(bf16[128,1280]{1,0:T(8,128)(2,1)} %get-tuple-element.204), channel_id=1, source_target_pairs={{10,0},{11,1},{8,2},{9,3},{2,4},{3,5},{0,6},{1,7},{14,8},{15,9},{1... | collective-permute-start | bytes 983048 | tf_op jit(solution)/shard_map/ppermute | solution.py:107
  430.6 28.9 %collective-permute-start.63 = (bf16[128,1280]{1,0:T(8,128)(2,1)}, bf16[128,1280]{1,0:T(8,128)(2,1)S(1)}, u32[]{:S(2)}, u32[]{:S(2)}) collective-permute-start(bf16[128,1280]{1,0:T(8,128)(2,1)} %copy-done.114), channel_id=1, source_target_pairs={{2,0},{3,1},{0,2},{1,3},{10,4},{11,5},{8,6},{9,7},{6,8},{7,9},{4,1... | collective-permute-start | bytes 983048 | tf_op jit(solution)/shard_map/ppermute | solution.py:107
  (148 other events, 986.9 us)

commit v8 on v6

--- a/solution.py
+++ b/solution.py
@@ -131,11 +131,11 @@
 SCALE = 0.25
 SIZE = {
     "project": 28,
-    "attend_forward": 24,
+    "attend_forward": 60,
     "middle": 48,
     "outer": 60,
     "outer_give": 60,
-    "attend_backward": 24,
+    "attend_backward": 60,
     "heads_outer": 24,
     "back_project": 20,
     "finish_heads": 16,

time: 471 us -> 490 us (1.040)
  Pallas kernels: 189 us -> 202 us
  starting transfers between devices: 59.7 us -> 65.9 us
  waiting for transfers between devices: 136 us -> 130 us
  local copies, waits for them, and re-layouts: 69.2 us -> 75.1 us
    pallas_call x40, Pallas kernels: 189 us -> 202 us  [call(): pl.pallas_call(run, out_shape=[jax.ShapeDtypeStruct(shape, kind) for shap...]
    ppermute x66, waiting for transfers between devices: 131 us -> 125 us  [send(): lax.ppermute(value, AXES, self.route(lambda x, c, a, b: ((x + dx) % self....]
    ppermute x66, starting transfers between devices: 56.1 us -> 62.4 us  [send(): lax.ppermute(value, AXES, self.route(lambda x, c, a, b: ((x + dx) % self....]
    unnamed x241 -> x247, local copies, waits for them, and re-layouts: 60.8 us -> 61.1 us
  transfers between devices with their start and end apart: 70 -> 70, of which waited for: 31 -> 29; matrix products, arithmetic and copies ran while one was open for 3% -> 4% of each run, Pallas kernels for 28% -> 30%
where the time goes in v8:
time: 490 us; the launch traced here: 481 us
  Pallas kernels  202 us (41%)
  waiting for transfers between devices  130 us (27%)
  local copies, waits for them, and re-layouts  75.1 us (15%)
  starting transfers between devices  65.9 us (13%)
  other arithmetic  5.59 us (1%)
    pallas_call x40, Pallas kernels, call(): pl.pallas_call(run, out_shape=[jax.ShapeDtypeStruct(shape, kind) for shap...  202 us
    ppermute x66, waiting for transfers between devices, send(): lax.ppermute(value, AXES, self.route(lambda x, c, a, b: ((x + dx) % self....  125 us
    ppermute x66, starting transfers between devices, send(): lax.ppermute(value, AXES, self.route(lambda x, c, a, b: ((x + dx) % self....  62.4 us
    unnamed x247, local copies, waits for them, and re-layouts  61.1 us
  transfers between devices with their start and end apart: 70, of which 29 were waited for; matrix products, arithmetic and copies ran while one was open for 4% of the time, Pallas kernels for 30%

profile of v8, /device:TPU:9, one launch (start us, length us, event | category | flops | bytes accessed | tf_op | source)
XLA Modules:
  0.0 481.0 jit_solution(16745662701693278918)
XLA Ops:
  13.7 3.5 collective-permute-done.5.refs_1_
  18.3 19.8 %collective-permute-done.3.refs_2_ = bf16[128,1280]{1,0:T(8,128)(2,1)S(1)} collective-permute-done((bf16[128,1280]{1,0:T(8,128)(2,1)S(1)}, bf16[128,1280]{1,0:T(8,128)(2,1)S(1)}, u32[]{:S(2)}, u32[]{:S(2)}) %collective-permute-start.3) | collective-permute-done | bytes 327712 | tf_op jit(solution)/shard_map/ppermute | solution.py:55
  45.0 6.3 %collective-permute-done.9.refs_4_.refs_1_ = bf16[2,80,964]{2,1,0:T(8,128)(2,1)S(1)} collective-permute-done((bf16[2,80,964]{2,1,0:T(8,128)(2,1)S(1)}, bf16[2,80,964]{2,1,0:T(8,128)(2,1)S(1)}, u32[]{:S(2)}, u32[]{:S(2)}) %collective-permute-start.9) | collective-permute-done | bytes 308512 | tf_op jit(solution)/shard_map/ppermute | solution.py:55
  53.2 6.9 %collective-permute-done.11.refs_6_.refs_3_ = bf16[2,80,964]{2,1,0:T(8,128)(2,1)S(1)} collective-permute-done((bf16[2,80,964]{2,1,0:T(8,128)(2,1)S(1)}, bf16[2,80,964]{2,1,0:T(8,128)(2,1)S(1)}, u32[]{:S(2)}, u32[]{:S(2)}) %collective-permute-start.11) | collective-permute-done | bytes 308512 | tf_op jit(solution)/shard_map/ppermute | solution.py:55
  63.0 7.4 %collective-permute-done.8.refs_5_.refs_2_ = bf16[2,80,964]{2,1,0:T(8,128)(2,1)} collective-permute-done((bf16[2,80,964]{2,1,0:T(8,128)(2,1)S(1)}, bf16[2,80,964]{2,1,0:T(8,128)(2,1)}, u32[]{:S(2)}, u32[]{:S(2)}) %collective-permute-start.8) | collective-permute-done | bytes 308512 | tf_op jit(solution)/shard_map/ppermute | solution.py:55
  85.7 6.2 %collective-permute-done.15.refs_6_ = bf16[2,80,964]{2,1,0:T(8,128)(2,1)} collective-permute-done((bf16[2,80,964]{2,1,0:T(8,128)(2,1)}, bf16[2,80,964]{2,1,0:T(8,128)(2,1)}, u32[]{:S(2)}, u32[]{:S(2)}) %collective-permute-start.15) | collective-permute-done | bytes 308512 | tf_op jit(solution)/shard_map/ppermute | solution.py:55
  91.8 3.2 collective-permute-start.18
  97.0 4.5 pad_weights.1
  109.7 13.0 %project.1 = (bf16[2048,1536]{1,0:T(8,128)(2,1)S(1)}, bf16[2048,1280]{1,0:T(8,128)(2,1)S(1)}) custom-call(s32[4]{0:T(128)S(1)} %pad_add_fusion.2.spots, bf16[4,128,1280]{2,1,0:T(8,128)(2,1)S(1)} %shuffle.11.refs_1_.refs_0_.refs_2_, bf16[4,128,1280]{2,1,0:T(8,128)(2,1)} %collective-permute-done.6.refs_9_.refs_1_, ...), custom_call_target="tpu_custom_call" | custom-call | flops 3987500032 | bytes 11962500 | tf_op jit(solution)/shard_map/project/pallas_call | solution.py:167
  122.7 2.4 copy-done.8
  125.1 4.3 shuffle.13.refs_2_.refs_4_
  142.9 24.2 %attend_forward.1 = (bf16[2,2,4,128,320]{4,3,2,1,0:T(8,128)(2,1)}, bf16[2048,512]{1,0:T(8,128)(2,1)}) custom-call(s32[10]{0:T(128)} %pad_add_fusion.1.spots, s32[2048,128]{1,0:T(8,128)} %broadcast_in_dim.58.refs_0_, bf16[2048,1536]{1,0:T(8,128)(2,1)} %copy-done, bf16[2048,1536]{1,0:T(8,128)(2,1)} %copy-done, bf16[2048,1536]{1,0:T(8,128)(2,1)} %copy-done, ...), custom_call_target="tpu_custom_call" | custom-call | flops 3300000000 | bytes 9900000 | tf_op jit(solution)/shard_map/attend_forward/pallas_call | solution.py:167
  175.6 8.6 %collective-permute-done.26.refs_3_ = bf16[512,320]{1,0:T(8,128)(2,1)S(1)} collective-permute-done((bf16[512,320]{1,0:T(8,128)(2,1)S(1)}, bf16[512,320]{1,0:T(8,128)(2,1)S(1)}, u32[]{:S(2)}, u32[]{:S(2)}) %collective-permute-start.26) | collective-permute-done | bytes 327712 | tf_op jit(solution)/shard_map/ppermute | solution.py:55
  184.2 9.0 %collective-permute-done.25.refs_2_ = bf16[512,320]{1,0:T(8,128)(2,1)S(1)} collective-permute-done((bf16[512,320]{1,0:T(8,128)(2,1)S(1)}, bf16[512,320]{1,0:T(8,128)(2,1)S(1)}, u32[]{:S(2)}, u32[]{:S(2)}) %collective-permute-start.25) | collective-permute-done | bytes 327712 | tf_op jit(solution)/shard_map/ppermute | solution.py:55
  195.1 3.8 collective-permute-done.29.refs_8_
  204.1 19.9 %middle.1 = (bf16[512,1280]{1,0:T(8,128)(2,1)}, f32[512,1280]{1,0:T(8,128)}, bf16[512,1280]{1,0:T(8,128)(2,1)}, bf16[512,1280]{1,0:T(8,128)(2,1)}, bf16[512,1280...) custom-call(s32[192]{0:T(256)S(1)} %stack.262.spots, ...), custom_call_target="tpu_custom_call" | custom-call | flops 5500000256 | bytes 16500000 | tf_op jit(solution)/shard_map/middle/pallas_call | solution.py:167
  224.8 8.5 %outer_give.1.refs_7_ = bf16[3,1280,640]{2,1,0:T(8,128)(2,1)} custom-call(s32[7]{0:T(128)} %stack.287.spots, bf16[512,1280]{1,0:T(8,128)(2,1)} %copy-done.13, bf16[512,1280]{1,0:T(8,128)(2,1)} %get-tuple-element.143.refs_1_, bf16[512,1280]{1,0:T(8,128)(2,1)} %get-tuple-element.144.refs_2_, bf16[512,1280]{1,0:T(8,128)(2,1)} %get-tuple-element.145.refs_3_, ...), custom_call_target="tpu_custom_call" | custom-call | flops 27500000 | bytes 82500 | tf_op jit(solution)/shard_map/outer_give/pallas_call | solution.py:167
  236.7 2.8 collective-permute-done.34
  239.5 4.6 collective-permute-done.35
  244.1 9.0 %collective-permute-done.36 = bf16[512,320]{1,0:T(8,128)(2,1)S(1)} collective-permute-done((bf16[512,320]{1,0:T(8,128)(2,1)S(1)}, bf16[512,320]{1,0:T(8,128)(2,1)S(1)}, u32[]{:S(2)}, u32[]{:S(2)}) %collective-permute-start.36) | collective-permute-done | bytes 327712 | tf_op jit(solution)/shard_map/ppermute | solution.py:55
  253.8 9.9 %outer.1 = (bf16[3,2,2,80,640]{4,3,2,1,0:T(8,128)(2,1)}, bf16[3,2,2,80,640]{4,3,2,1,0:T(8,128)(2,1)}, bf16[3,2,2,80,640]{4,3,2,1,0:T(8,128)(2,1)}, bf16[3,2,2,80,640]{4,3,2,1,0:T(8,128)(2,1)}) custom-call(s32[7]{0:T(128)} %stack.286.spots, bf16[512,1280]{1,0:T(8,128)(2,1)} %copy-done.13, bf16[512,1280]{1,0:T(8,128)(2,1)} %get-tuple-element.143.refs_1_, ...), custom_call_target="tpu_custom_call" | custom-call | flops 1924999936 | bytes 5775000 | tf_op jit(solution)/shard_map/outer/pallas_call | solution.py:167
  269.0 2.6 collective-permute-start.38
  272.9 23.7 %attend_backward.2 = (bf16[2048,480]{1,0:T(8,128)(2,1)}, f32[8,128]{1,0:T(8,128)}, f32[8,768]{1,0:T(8,128)}) custom-call(s32[10]{0:T(128)} %pad_add_fusion.1.spots, s32[8,2048]{1,0:T(8,128)} %broadcast_in_dim.61.refs_0_, f32[8,256]{1,0:T(8,128)} %broadcast_in_dim.63.refs_1_, bf16[2048,512]{1,0:T(8,128)(2,1)} %get-tuple-element.156.refs_2_, ...), custom_call_target="tpu_custom_call" | custom-call | flops 6874999808 | bytes 20625000 | tf_op jit(solution)/shard_map/attend_backward/pallas_call | solution.py:167
  297.6 3.6 collective-permute-done.39.refs_3_
  302.7 2.8 route_back.1
  307.9 2.8 add_blocks.6
  316.4 2.5 copy-done.9
  320.0 5.6 %heads_outer.2 = (bf16[4,2,80,483]{3,2,1,0:T(8,128)(2,1)S(1)}, bf16[4,2,80,483]{3,2,1,0:T(8,128)(2,1)}) custom-call(s32[1]{0:T(128)} %bitcast.54.spots, bf16[2048,1280]{1,0:T(8,128)(2,1)S(1)} %copy-done.9, bf16[2048,480]{1,0:T(8,128)(2,1)S(1)} %copy-done.2, bf16[1280,3]{1,0:T(8,128)(2,1)S(1)} %copy.53.refs_2_, bf16[3,2,80,640]{3,2,1,0:T(8,128)(2,1)S(1)} %copy-done.42), custom_call_target="tpu_custom_call" | custom-call | flops 1512499968 | bytes 4537500 | tf_op jit(solution)/shard_map/heads_outer/pallas_call | solution.py:167
  329.4 3.1 cat.1
  334.7 24.7 %attend_backward.3 = (bf16[2048,480]{1,0:T(8,128)(2,1)}, f32[8,128]{1,0:T(8,128)}, f32[8,768]{1,0:T(8,128)}) custom-call(s32[10]{0:T(128)} %pad_add_fusion.1.spots, s32[8,2048]{1,0:T(8,128)} %broadcast_in_dim.61.refs_0_, f32[8,256]{1,0:T(8,128)} %broadcast_in_dim.63.refs_1_, bf16[2048,512]{1,0:T(8,128)(2,1)} %get-tuple-element.156.refs_2_, ...), custom_call_target="tpu_custom_call" | custom-call | flops 6874999808 | bytes 20625000 | tf_op jit(solution)/shard_map/attend_backward/pallas_call | solution.py:167
  361.6 2.6 add_blocks.7.refs_8_.refs_0_
  366.8 5.0 %back_project.3.refs_3_ = bf16[2,2,2,128,1280]{4,3,2,1,0:T(8,128)(2,1)} custom-call(s32[3]{0:T(128)S(1)} %pad_add_fusion.7.spots, bf16[4,2,2,128,480]{4,3,2,1,0:T(8,128)(2,1)S(1)} %bitcast.119, bf16[4,2,2,128,480]{4,3,2,1,0:T(8,128)(2,1)S(1)} %bitcast.122, bf16[1280,480]{1,0:T(8,128)(2,1)S(1)} %copy-done.15, bf16[1280,480]{1,0:T(8,128)(2,1)S(1)} %copy-done.18, ...), custom_call_target="tpu_custom_call" | custom-call | flops 962499968 | bytes 2887500 | tf_op jit(solution)/shard_map/back_project/pallas_call | solution.py:167
  371.8 2.9 collective-permute-start.52
  378.8 2.7 collective-permute-start.54
  383.4 2.5 copy-done.10
  385.9 5.6 %heads_outer.3 = (bf16[4,2,80,483]{3,2,1,0:T(8,128)(2,1)S(1)}, bf16[4,2,80,483]{3,2,1,0:T(8,128)(2,1)}) custom-call(s32[1]{0:T(128)} %bitcast.54.spots, bf16[2048,1280]{1,0:T(8,128)(2,1)S(1)} %copy-done.10, bf16[2048,480]{1,0:T(8,128)(2,1)S(1)} %copy-done.5, bf16[1280,3]{1,0:T(8,128)(2,1)S(1)} %copy.54.refs_2_, bf16[2,2,2,128,1280]{4,3,2,1,0:T(8,128)(2,1)} %back_project.3.refs_3_), custom_call_target="tpu_custom_call" | custom-call | flops 1512499968 | bytes 4537500 | tf_op jit(solution)/shard_map/heads_outer/pallas_call | solution.py:167
  399.0 4.7 back_project.4
  403.9 4.4 back_project.5
  414.6 4.7 collective-permute-done.61.refs_1_
  421.6 3.8 collective-permute-done.59.refs_2_.refs_6_
  425.4 3.7 collective-permute-done.60.refs_3_.refs_7_
  429.1 4.1 collective-permute-done.56.refs_9_.refs_1_
  434.2 3.3 collective-permute-start.68
  440.6 3.3 collective-permute-done.68.refs_3_
  448.9 2.6 collective-permute-start.62
  455.0 3.2 finish_full.1
  465.5 5.1 %finish_heads.1 = (f32[160,1280]{1,0:T(8,128)}, f32[160,1280]{1,0:T(8,128)}, f32[160,1280]{1,0:T(8,128)}, f32[160,1]{1,0:T(8,128)S(1)}, f32[160,3]{1,0:T(8,128)S(1)}) custom-call(s32[5]{0:T(128)S(1)} %stack.314.spots, bf16[2,80,483]{2,1,0:T(8,128)(2,1)S(1)} %get-tuple-element.200.refs_5_.refs_0_, bf16[2,80,483]{2,1,0:T(8,128)(2,1)S(1)} %copy-done.86, ...), custom_call_target="tpu_custom_call" | custom-call | flops 1100000000 | bytes 3300000 | tf_op jit(solution)/shard_map/finish_heads/pallas_call | solution.py:167
  473.6 4.2 collective-permute-done.63.refs_1_
  (478 shorter events, 161.2 us)
Async XLA Ops:
  9.8 28.2 %collective-permute-start.3 = (bf16[128,1280]{1,0:T(8,128)(2,1)S(1)}, bf16[128,1280]{1,0:T(8,128)(2,1)S(1)}, u32[]{:S(2)}, u32[]{:S(2)}) collective-permute-start(bf16[128,1280]{1,0:T(8,128)(2,1)S(1)} %get-tuple-element.119), channel_id=1, source_target_pairs={{0,4},{1,5},{2,6},{3,7},{4,0},{5,1},{6,2},{7,3},{8,12},{9,13},{10,... | collective-permute-start | bytes 983048 | tf_op jit(solution)/shard_map/ppermute | solution.py:55
  10.8 29.5 %collective-permute-start.4 = (bf16[128,1280]{1,0:T(8,128)(2,1)S(1)}, bf16[128,1280]{1,0:T(8,128)(2,1)S(1)}, u32[]{:S(2)}, u32[]{:S(2)}) collective-permute-start(bf16[128,1280]{1,0:T(8,128)(2,1)S(1)} %get-tuple-element.120), channel_id=1, source_target_pairs={{0,6},{1,7},{2,0},{3,1},{4,2},{5,3},{6,4},{7,5},{8,14},{9,15},{10,... | collective-permute-start | bytes 983048 | tf_op jit(solution)/shard_map/ppermute | solution.py:55
  41.4 30.4 %collective-permute-start.7 = (bf16[4,128,1280]{2,1,0:T(8,128)(2,1)S(1)}, bf16[4,128,1280]{2,1,0:T(8,128)(2,1)}, u32[]{:S(2)}, u32[]{:S(2)}) collective-permute-start(bf16[4,128,1280]{2,1,0:T(8,128)(2,1)S(1)} %shuffle.11.refs_1_.refs_0_.refs_2_), channel_id=1, source_target_pairs={{0,1},{1,0},{2,3},{3,2},{4,5},{5,4},{6,7},{7,6},{8,9},{9,8},{10,11... | collective-permute-start | bytes 3932168 | tf_op jit(solution)/shard_map/ppermute | solution.py:55
  42.7 17.5 %collective-permute-start.11 = (bf16[2,80,964]{2,1,0:T(8,128)(2,1)S(1)}, bf16[2,80,964]{2,1,0:T(8,128)(2,1)S(1)}, u32[]{:S(2)}, u32[]{:S(2)}) collective-permute-start(bf16[2,80,964]{2,1,0:T(8,128)(2,1)S(1)} %shuffle.10.refs_4_.refs_0_), channel_id=1, source_target_pairs={{0,6},{1,7},{2,0},{3,1},{4,2},{5,3},{6,4},{7,5},{8,14},{9,15},{10,... | collective-permute-start | bytes 925448 | tf_op jit(solution)/shard_map/ppermute | solution.py:55
  44.1 26.2 %collective-permute-start.8 = (bf16[2,80,964]{2,1,0:T(8,128)(2,1)S(1)}, bf16[2,80,964]{2,1,0:T(8,128)(2,1)}, u32[]{:S(2)}, u32[]{:S(2)}) collective-permute-start(bf16[2,80,964]{2,1,0:T(8,128)(2,1)S(1)} %shuffle.10.refs_4_.refs_0_), channel_id=1, source_target_pairs={{0,4},{1,5},{2,6},{3,7},{4,0},{5,1},{6,2},{7,3},{8,12},{9,13},{10,... | collective-permute-start | bytes 925448 | tf_op jit(solution)/shard_map/ppermute | solution.py:55
  51.3 19.1 %collective-permute-start.10 = (bf16[2,80,964]{2,1,0:T(8,128)(2,1)S(1)}, bf16[2,80,964]{2,1,0:T(8,128)(2,1)S(1)}, u32[]{:S(2)}, u32[]{:S(2)}) collective-permute-start(bf16[2,80,964]{2,1,0:T(8,128)(2,1)S(1)} %collective-permute-done.9.refs_4_.refs_1_), channel_id=1, source_target_pairs={{0,16},{1,17},{2,18},{3,19},{4,20},{5,21},{6,22},{7,23},{8,24},{9,... | collective-permute-start | bytes 925448 | tf_op jit(solution)/shard_map/ppermute | solution.py:55
  62.1 33.8 %collective-permute-start.6 = (bf16[4,128,1280]{2,1,0:T(8,128)(2,1)S(1)}, bf16[4,128,1280]{2,1,0:T(8,128)(2,1)}, u32[]{:S(2)}, u32[]{:S(2)}) collective-permute-start(bf16[4,128,1280]{2,1,0:T(8,128)(2,1)S(1)} %shuffle.11.refs_1_.refs_0_.refs_2_), channel_id=1, source_target_pairs={{0,8},{1,9},{2,10},{3,11},{4,12},{5,13},{6,14},{7,15},{8,0},{9,1},... | collective-permute-start | bytes 3932168 | tf_op jit(solution)/shard_map/ppermute | solution.py:55
  71.8 24.1 %collective-permute-start.13 = (bf16[4,128,1280]{2,1,0:T(8,128)(2,1)}, bf16[4,128,1280]{2,1,0:T(8,128)(2,1)}, u32[]{:S(2)}, u32[]{:S(2)}) collective-permute-start(bf16[4,128,1280]{2,1,0:T(8,128)(2,1)} %collective-permute-done.7.refs_10_.refs_2_), channel_id=1, source_target_pairs={{0,8},{1,9},{2,10},{3,11},{4,12},{5,13},{6,14},{7,15},{8,0},{9,1},... | collective-permute-start | bytes 3932168 | tf_op jit(solution)/shard_map/ppermute | solution.py:55
  74.8 20.2 %collective-permute-start.16 = (bf16[2,128,1280]{2,1,0:T(8,128)(2,1)}, bf16[2,128,1280]{2,1,0:T(8,128)(2,1)S(1)}, u32[]{:S(2)}, u32[]{:S(2)}) collective-permute-start(bf16[2,128,1280]{2,1,0:T(8,128)(2,1)} %get-tuple-element.124), channel_id=1, source_target_pairs={{0,8},{1,9},{2,10},{3,11},{4,12},{5,13},{6,14},{7,15},{8,0},{9,1},... | collective-permute-start | bytes 1966088 | tf_op jit(solution)/shard_map/ppermute | solution.py:55
  76.7 15.2 %collective-permute-start.15 = (bf16[2,80,964]{2,1,0:T(8,128)(2,1)}, bf16[2,80,964]{2,1,0:T(8,128)(2,1)}, u32[]{:S(2)}, u32[]{:S(2)}) collective-permute-start(bf16[2,80,964]{2,1,0:T(8,128)(2,1)} %collective-permute-done.8.refs_5_.refs_2_), channel_id=1, source_target_pairs={{0,16},{1,17},{2,18},{3,19},{4,20},{5,21},{6,22},{7,23},{8,24},{9,... | collective-permute-start | bytes 925448 | tf_op jit(solution)/shard_map/ppermute | solution.py:55
  84.8 40.2 %collective-permute-start.17 = (bf16[3,80,640]{2,1,0:T(8,128)(2,1)S(1)}, bf16[3,80,640]{2,1,0:T(8,128)(2,1)}, u32[]{:S(2)}, u32[]{:S(2)}) collective-permute-start(bf16[3,80,640]{2,1,0:T(8,128)(2,1)S(1)} %quarter.1.refs_8_.refs_0_), channel_id=1, source_target_pairs={{0,2},{1,3},{2,4},{3,5},{4,6},{5,7},{6,0},{7,1},{8,10},{9,11},{10,... | collective-permute-start | bytes 921608 | tf_op jit(solution)/shard_map/ppermute | solution.py:55
  91.8 33.2 %collective-permute-start.18 = (bf16[3,80,640]{2,1,0:T(8,128)(2,1)S(1)}, bf16[3,80,640]{2,1,0:T(8,128)(2,1)}, u32[]{:S(2)}, u32[]{:S(2)}) collective-permute-start(bf16[3,80,640]{2,1,0:T(8,128)(2,1)S(1)} %quarter.1.refs_8_.refs_0_), channel_id=1, source_target_pairs={{0,4},{1,5},{2,6},{3,7},{4,0},{5,1},{6,2},{7,3},{8,12},{9,13},{10,... | collective-permute-start | bytes 921608 | tf_op jit(solution)/shard_map/ppermute | solution.py:55
  95.9 29.2 %collective-permute-start.19 = (bf16[3,80,640]{2,1,0:T(8,128)(2,1)S(1)}, bf16[3,80,640]{2,1,0:T(8,128)(2,1)}, u32[]{:S(2)}, u32[]{:S(2)}) collective-permute-start(bf16[3,80,640]{2,1,0:T(8,128)(2,1)S(1)} %quarter.1.refs_8_.refs_0_), channel_id=1, source_target_pairs={{0,6},{1,7},{2,0},{3,1},{4,2},{5,3},{6,4},{7,5},{8,14},{9,15},{10,... | collective-permute-start | bytes 921608 | tf_op jit(solution)/shard_map/ppermute | solution.py:55
  130.6 40.8 %collective-permute-start.27 = (bf16[4,3,80,640]{3,2,1,0:T(8,128)(2,1)}, bf16[4,3,80,640]{3,2,1,0:T(8,128)(2,1)}, u32[]{:S(2)}, u32[]{:S(2)}) collective-permute-start(bf16[4,3,80,640]{3,2,1,0:T(8,128)(2,1)} %shuffle.13.refs_2_.refs_4_), channel_id=1, source_target_pairs={{0,1},{1,0},{2,3},{3,2},{4,5},{5,4},{6,7},{7,6},{8,9},{9,8},{10,11... | collective-permute-start | bytes 3686408 | tf_op jit(solution)/shard_map/ppermute | solution.py:55
  135.6 31.5 %collective-permute-start.21 = (bf16[128,1280]{1,0:T(8,128)(2,1)}, bf16[128,1280]{1,0:T(8,128)(2,1)S(1)}, u32[]{:S(2)}, u32[]{:S(2)}) collective-permute-start(bf16[128,1280]{1,0:T(8,128)(2,1)} %get-tuple-element.131), channel_id=1, source_target_pairs={{0,2},{1,3},{2,4},{3,5},{4,6},{5,7},{6,0},{7,1},{8,10},{9,11},{10,... | collective-permute-start | bytes 983048 | tf_op jit(solution)/shard_map/ppermute | solution.py:55
  137.4 29.8 %collective-permute-start.22 = (bf16[128,1280]{1,0:T(8,128)(2,1)}, bf16[128,1280]{1,0:T(8,128)(2,1)S(1)}, u32[]{:S(2)}, u32[]{:S(2)}) collective-permute-start(bf16[128,1280]{1,0:T(8,128)(2,1)} %get-tuple-element.132), channel_id=1, source_target_pairs={{0,4},{1,5},{2,6},{3,7},{4,0},{5,1},{6,2},{7,3},{8,12},{9,13},{10,... | collective-permute-start | bytes 983048 | tf_op jit(solution)/shard_map/ppermute | solution.py:55
  138.9 28.4 %collective-permute-start.23 = (bf16[128,1280]{1,0:T(8,128)(2,1)S(1)}, bf16[128,1280]{1,0:T(8,128)(2,1)S(1)}, u32[]{:S(2)}, u32[]{:S(2)}) collective-permute-start(bf16[128,1280]{1,0:T(8,128)(2,1)S(1)} %get-tuple-element.133), channel_id=1, source_target_pairs={{0,6},{1,7},{2,0},{3,1},{4,2},{5,3},{6,4},{7,5},{8,14},{9,15},{10,... | collective-permute-start | bytes 983048 | tf_op jit(solution)/shard_map/ppermute | solution.py:55
  140.4 54.2 %collective-permute-start.28 = (bf16[4,3,80,640]{3,2,1,0:T(8,128)(2,1)}, bf16[4,3,80,640]{3,2,1,0:T(8,128)(2,1)}, u32[]{:S(2)}, u32[]{:S(2)}) collective-permute-start(bf16[4,3,80,640]{3,2,1,0:T(8,128)(2,1)} %shuffle.13.refs_2_.refs_4_), channel_id=1, source_target_pairs={{0,16},{1,17},{2,18},{3,19},{4,20},{5,21},{6,22},{7,23},{8,24},{9,... | collective-permute-start | bytes 3686408 | tf_op jit(solution)/shard_map/ppermute | solution.py:55
  171.4 27.5 %collective-permute-start.29 = (bf16[4,3,80,640]{3,2,1,0:T(8,128)(2,1)}, bf16[4,3,80,640]{3,2,1,0:T(8,128)(2,1)}, u32[]{:S(2)}, u32[]{:S(2)}) collective-permute-start(bf16[4,3,80,640]{3,2,1,0:T(8,128)(2,1)} %collective-permute-done.27.refs_6_), channel_id=1, source_target_pairs={{0,16},{1,17},{2,18},{3,19},{4,20},{5,21},{6,22},{7,23},{8,24},{9,... | collective-permute-start | bytes 3686408 | tf_op jit(solution)/shard_map/ppermute | solution.py:55
  174.3 18.9 %collective-permute-start.25 = (bf16[512,320]{1,0:T(8,128)(2,1)S(1)}, bf16[512,320]{1,0:T(8,128)(2,1)S(1)}, u32[]{:S(2)}, u32[]{:S(2)}) collective-permute-start(bf16[512,320]{1,0:T(8,128)(2,1)S(1)} %bitcast.146), channel_id=1, source_target_pairs={{0,1},{1,0},{2,3},{3,2},{4,5},{5,4},{6,7},{7,6},{8,9},{9,8},{10,11... | collective-permute-start | bytes 983048 | tf_op jit(solution)/shard_map/ppermute | solution.py:55
  175.6 17.6 %collective-permute-start.24 = (bf16[512,320]{1,0:T(8,128)(2,1)S(1)}, bf16[512,320]{1,0:T(8,128)(2,1)S(1)}, u32[]{:S(2)}, u32[]{:S(2)}) collective-permute-start(bf16[512,320]{1,0:T(8,128)(2,1)S(1)} %bitcast.145), channel_id=1, source_target_pairs={{0,8},{1,9},{2,10},{3,11},{4,12},{5,13},{6,14},{7,15},{8,0},{9,1},... | collective-permute-start | bytes 983048 | tf_op jit(solution)/shard_map/ppermute | solution.py:55
  233.3 19.8 %collective-permute-start.33 = (bf16[3,1280,640]{2,1,0:T(8,128)(2,1)}, bf16[3,1280,640]{2,1,0:T(8,128)(2,1)}, u32[]{:S(2)}, u32[]{:S(2)}) collective-permute-start(bf16[3,1280,640]{2,1,0:T(8,128)(2,1)} %outer_give.1.refs_7_), channel_id=1, source_target_pairs={{0,8},{1,9},{2,10},{3,11},{4,12},{5,13},{6,14},{7,15},{8,0},{9,1},... | collective-permute-start | bytes 14745608 | tf_op jit(solution)/shard_map/ppermute | solution.py:55
  233.9 19.1 %collective-permute-start.36 = (bf16[512,320]{1,0:T(8,128)(2,1)S(1)}, bf16[512,320]{1,0:T(8,128)(2,1)S(1)}, u32[]{:S(2)}, u32[]{:S(2)}) collective-permute-start(bf16[512,320]{1,0:T(8,128)(2,1)S(1)} %get-tuple-element.150), channel_id=1, source_target_pairs={{0,9},{1,8},{2,11},{3,10},{4,13},{5,12},{6,15},{7,14},{8,1},{9,0},... | collective-permute-start | bytes 983048 | tf_op jit(solution)/shard_map/ppermute | solution.py:55
  263.7 41.8 %collective-permute-start.41 = (bf16[3,2,2,80,640]{4,3,2,1,0:T(8,128)(2,1)}, bf16[3,2,2,80,640]{4,3,2,1,0:T(8,128)(2,1)S(1)}, u32[]{:S(2)}, u32[]{:S(2)}) collective-permute-start(bf16[3,2,2,80,640]{4,3,2,1,0:T(8,128)(2,1)} %get-tuple-element.160), channel_id=1, source_target_pairs={{0,16},{1,17},{2,18},{3,19},{4,20},{5,21},{6,22},{7,23},{8,24},{9,... | collective-permute-start | bytes 3686408 | tf_op jit(solution)/shard_map/ppermute | solution.py:55
  265.0 40.5 %collective-permute-start.42 = (bf16[3,2,2,80,640]{4,3,2,1,0:T(8,128)(2,1)}, bf16[3,2,2,80,640]{4,3,2,1,0:T(8,128)(2,1)S(1)}, u32[]{:S(2)}, u32[]{:S(2)}) collective-permute-start(bf16[3,2,2,80,640]{4,3,2,1,0:T(8,128)(2,1)} %get-tuple-element.162), channel_id=1, source_target_pairs={{0,1},{1,0},{2,3},{3,2},{4,5},{5,4},{6,7},{7,6},{8,9},{9,8},{10,11... | collective-permute-start | bytes 3686408 | tf_op jit(solution)/shard_map/ppermute | solution.py:55
  268.9 28.7 %collective-permute-start.37 = (bf16[128,1280]{1,0:T(8,128)(2,1)}, bf16[128,1280]{1,0:T(8,128)(2,1)S(1)}, u32[]{:S(2)}, u32[]{:S(2)}) collective-permute-start(bf16[128,1280]{1,0:T(8,128)(2,1)} %get-tuple-element.153), channel_id=1, source_target_pairs={{0,2},{1,3},{2,4},{3,5},{4,6},{5,7},{6,0},{7,1},{8,10},{9,11},{10,... | collective-permute-start | bytes 983048 | tf_op jit(solution)/shard_map/ppermute | solution.py:55
  269.0 28.6 %collective-permute-start.38 = (bf16[128,1280]{1,0:T(8,128)(2,1)}, bf16[128,1280]{1,0:T(8,128)(2,1)}, u32[]{:S(2)}, u32[]{:S(2)}) collective-permute-start(bf16[128,1280]{1,0:T(8,128)(2,1)} %get-tuple-element.154), channel_id=1, source_target_pairs={{0,4},{1,5},{2,6},{3,7},{4,0},{5,1},{6,2},{7,3},{8,12},{9,13},{10,... | collective-permute-start | bytes 983048 | tf_op jit(solution)/shard_map/ppermute | solution.py:55
  271.6 29.6 %collective-permute-start.39 = (bf16[128,1280]{1,0:T(8,128)(2,1)}, bf16[128,1280]{1,0:T(8,128)(2,1)}, u32[]{:S(2)}, u32[]{:S(2)}) collective-permute-start(bf16[128,1280]{1,0:T(8,128)(2,1)} %get-tuple-element.155), channel_id=1, source_target_pairs={{0,6},{1,7},{2,0},{3,1},{4,2},{5,3},{6,4},{7,5},{8,14},{9,15},{10,... | collective-permute-start | bytes 983048 | tf_op jit(solution)/shard_map/ppermute | solution.py:55
  313.2 15.2 %collective-permute-start.43 = (bf16[3,2,80,640]{3,2,1,0:T(8,128)(2,1)}, bf16[3,2,80,640]{3,2,1,0:T(8,128)(2,1)}, u32[]{:S(2)}, u32[]{:S(2)}) collective-permute-start(bf16[3,2,80,640]{3,2,1,0:T(8,128)(2,1)} %get-tuple-element.164), channel_id=1, source_target_pairs={{0,1},{1,0},{2,3},{3,2},{4,5},{5,4},{6,7},{7,6},{8,9},{9,8},{10,11... | collective-permute-start | bytes 1843208 | tf_op jit(solution)/shard_map/ppermute | solution.py:55
  314.5 14.9 %collective-permute-start.44 = (bf16[3,2,80,640]{3,2,1,0:T(8,128)(2,1)}, bf16[3,2,80,640]{3,2,1,0:T(8,128)(2,1)}, u32[]{:S(2)}, u32[]{:S(2)}) collective-permute-start(bf16[3,2,80,640]{3,2,1,0:T(8,128)(2,1)} %get-tuple-element.166), channel_id=1, source_target_pairs={{0,16},{1,17},{2,18},{3,19},{4,20},{5,21},{6,22},{7,23},{8,24},{9,... | collective-permute-start | bytes 1843208 | tf_op jit(solution)/shard_map/ppermute | solution.py:55
  325.6 38.6 %collective-permute-start.51 = (bf16[4,2,80,483]{3,2,1,0:T(8,128)(2,1)}, bf16[4,2,80,483]{3,2,1,0:T(8,128)(2,1)S(1)}, u32[]{:S(2)}, u32[]{:S(2)}) collective-permute-start(bf16[4,2,80,483]{3,2,1,0:T(8,128)(2,1)} %get-tuple-element.177), channel_id=1, source_target_pairs={{0,16},{1,17},{2,18},{3,19},{4,20},{5,21},{6,22},{7,23},{8,24},{9,... | collective-permute-start | bytes 1854728 | tf_op jit(solution)/shard_map/ppermute | solution.py:55
  333.2 26.2 %collective-permute-start.45 = (bf16[3,80,640]{2,1,0:T(8,128)(2,1)}, bf16[3,80,640]{2,1,0:T(8,128)(2,1)}, u32[]{:S(2)}, u32[]{:S(2)}) collective-permute-start(bf16[3,80,640]{2,1,0:T(8,128)(2,1)} %get-tuple-element.172), channel_id=1, source_target_pairs={{0,2},{1,3},{2,4},{3,5},{4,6},{5,7},{6,0},{7,1},{8,10},{9,11},{10,... | collective-permute-start | bytes 921608 | tf_op jit(solution)/shard_map/ppermute | solution.py:55
  333.2 26.2 %collective-permute-start.46 = (bf16[3,80,640]{2,1,0:T(8,128)(2,1)}, bf16[3,80,640]{2,1,0:T(8,128)(2,1)}, u32[]{:S(2)}, u32[]{:S(2)}) collective-permute-start(bf16[3,80,640]{2,1,0:T(8,128)(2,1)} %get-tuple-element.173), channel_id=1, source_target_pairs={{0,4},{1,5},{2,6},{3,7},{4,0},{5,1},{6,2},{7,3},{8,12},{9,13},{10,... | collective-permute-start | bytes 921608 | tf_op jit(solution)/shard_map/ppermute | solution.py:55
  333.2 26.9 %collective-permute-start.47 = (bf16[3,80,640]{2,1,0:T(8,128)(2,1)}, bf16[3,80,640]{2,1,0:T(8,128)(2,1)}, u32[]{:S(2)}, u32[]{:S(2)}) collective-permute-start(bf16[3,80,640]{2,1,0:T(8,128)(2,1)} %get-tuple-element.174), channel_id=1, source_target_pairs={{0,6},{1,7},{2,0},{3,1},{4,2},{5,3},{6,4},{7,5},{8,14},{9,15},{10,... | collective-permute-start | bytes 921608 | tf_op jit(solution)/shard_map/ppermute | solution.py:55
  371.8 27.2 %collective-permute-start.52 = (bf16[2,2,2,128,1280]{4,3,2,1,0:T(8,128)(2,1)}, bf16[2,2,2,128,1280]{4,3,2,1,0:T(8,128)(2,1)}, u32[]{:S(2)}, u32[]{:S(2)}) collective-permute-start(bf16[2,2,2,128,1280]{4,3,2,1,0:T(8,128)(2,1)} %back_project.3.refs_3_), channel_id=1, source_target_pairs={{0,8},{1,9},{2,10},{3,11},{4,12},{5,13},{6,14},{7,15},{8,0},{9,1},... | collective-permute-start | bytes 7864328 | tf_op jit(solution)/shard_map/ppermute | solution.py:55
  377.2 18.6 %collective-permute-start.48 = (bf16[3,80,640]{2,1,0:T(8,128)(2,1)}, bf16[3,80,640]{2,1,0:T(8,128)(2,1)}, u32[]{:S(2)}, u32[]{:S(2)}) collective-permute-start(bf16[3,80,640]{2,1,0:T(8,128)(2,1)} %add_blocks.7.refs_8_.refs_0_), channel_id=1, source_target_pairs={{0,16},{1,17},{2,18},{3,19},{4,20},{5,21},{6,22},{7,23},{8,24},{9,... | collective-permute-start | bytes 921608 | tf_op jit(solution)/shard_map/ppermute | solution.py:55
  378.8 14.8 %collective-permute-start.54 = (bf16[2,80,483]{2,1,0:T(8,128)(2,1)}, bf16[2,80,483]{2,1,0:T(8,128)(2,1)}, u32[]{:S(2)}, u32[]{:S(2)}) collective-permute-start(bf16[2,80,483]{2,1,0:T(8,128)(2,1)} %get-tuple-element.180), channel_id=1, source_target_pairs={{0,4},{1,5},{2,6},{3,7},{4,0},{5,1},{6,2},{7,3},{8,12},{9,13},{10,... | collective-permute-start | bytes 463688 | tf_op jit(solution)/shard_map/ppermute | solution.py:55
  381.5 14.3 %collective-permute-start.55 = (bf16[2,80,483]{2,1,0:T(8,128)(2,1)}, bf16[2,80,483]{2,1,0:T(8,128)(2,1)}, u32[]{:S(2)}, u32[]{:S(2)}) collective-permute-start(bf16[2,80,483]{2,1,0:T(8,128)(2,1)} %get-tuple-element.181), channel_id=1, source_target_pairs={{0,6},{1,7},{2,0},{3,1},{4,2},{5,3},{6,4},{7,5},{8,14},{9,15},{10,... | collective-permute-start | bytes 463688 | tf_op jit(solution)/shard_map/ppermute | solution.py:55
  392.2 18.5 %collective-permute-start.57 = (bf16[4,2,80,483]{3,2,1,0:T(8,128)(2,1)}, bf16[4,2,80,483]{3,2,1,0:T(8,128)(2,1)S(1)}, u32[]{:S(2)}, u32[]{:S(2)}) collective-permute-start(bf16[4,2,80,483]{3,2,1,0:T(8,128)(2,1)} %get-tuple-element.190), channel_id=1, source_target_pairs={{0,16},{1,17},{2,18},{3,19},{4,20},{5,21},{6,22},{7,23},{8,24},{9,... | collective-permute-start | bytes 1854728 | tf_op jit(solution)/shard_map/ppermute | solution.py:55
  403.7 15.5 %collective-permute-start.61 = (bf16[2,128,1280]{2,1,0:T(8,128)(2,1)}, bf16[2,128,1280]{2,1,0:T(8,128)(2,1)}, u32[]{:S(2)}, u32[]{:S(2)}) collective-permute-start(bf16[2,128,1280]{2,1,0:T(8,128)(2,1)} %get-tuple-element.195), channel_id=1, source_target_pairs={{0,1},{1,0},{2,3},{3,2},{4,5},{5,4},{6,7},{7,6},{8,9},{9,8},{10,11... | collective-permute-start | bytes 1966088 | tf_op jit(solution)/shard_map/ppermute | solution.py:55
  409.4 23.8 %collective-permute-start.56 = (bf16[2,128,1280]{2,1,0:T(8,128)(2,1)}, bf16[2,128,1280]{2,1,0:T(8,128)(2,1)S(1)}, u32[]{:S(2)}, u32[]{:S(2)}) collective-permute-start(bf16[2,128,1280]{2,1,0:T(8,128)(2,1)} %get-tuple-element.188), channel_id=1, source_target_pairs={{0,1},{1,0},{2,3},{3,2},{4,5},{5,4},{6,7},{7,6},{8,9},{9,8},{10,11... | collective-permute-start | bytes 1966088 | tf_op jit(solution)/shard_map/ppermute | solution.py:55
  413.9 15.2 %collective-permute-start.60 = (bf16[2,80,483]{2,1,0:T(8,128)(2,1)S(1)}, bf16[2,80,483]{2,1,0:T(8,128)(2,1)S(1)}, u32[]{:S(2)}, u32[]{:S(2)}) collective-permute-start(bf16[2,80,483]{2,1,0:T(8,128)(2,1)S(1)} %get-tuple-element.194), channel_id=1, source_target_pairs={{0,6},{1,7},{2,0},{3,1},{4,2},{5,3},{6,4},{7,5},{8,14},{9,15},{10,... | collective-permute-start | bytes 463688 | tf_op jit(solution)/shard_map/ppermute | solution.py:55
  437.6 22.8 %collective-permute-start.40 = (bf16[2,128,1280]{2,1,0:T(8,128)(2,1)}, bf16[2,128,1280]{2,1,0:T(8,128)(2,1)S(1)}, u32[]{:S(2)}, u32[]{:S(2)}) collective-permute-start(bf16[2,128,1280]{2,1,0:T(8,128)(2,1)} %get-tuple-element.159), channel_id=1, source_target_pairs={{0,8},{1,9},{2,10},{3,11},{4,12},{5,13},{6,14},{7,15},{8,0},{9,1},... | collective-permute-start | bytes 1966088 | tf_op jit(solution)/shard_map/ppermute | solution.py:55
  444.9 19.3 %collective-permute-start.69 = (bf16[4,2,80,483]{3,2,1,0:T(8,128)(2,1)}, bf16[4,2,80,483]{3,2,1,0:T(8,128)(2,1)}, u32[]{:S(2)}, u32[]{:S(2)}) collective-permute-start(bf16[4,2,80,483]{3,2,1,0:T(8,128)(2,1)} %pad_maximum_fusion), channel_id=1, source_target_pairs={{0,16},{1,17},{2,18},{3,19},{4,20},{5,21},{6,22},{7,23},{8,24},{9,... | collective-permute-start | bytes 1854728 | tf_op jit(solution)/shard_map/ppermute | solution.py:55
  448.2 24.6 %collective-permute-start.64 = (bf16[128,1280]{1,0:T(8,128)(2,1)}, bf16[128,1280]{1,0:T(8,128)(2,1)S(1)}, u32[]{:S(2)}, u32[]{:S(2)}) collective-permute-start(bf16[128,1280]{1,0:T(8,128)(2,1)} %get-tuple-element.201.refs_6_), channel_id=1, source_target_pairs={{8,0},{9,1},{10,2},{11,3},{0,4},{1,5},{2,6},{3,7},{12,8},{13,9},{1... | collective-permute-start | bytes 983048 | tf_op jit(solution)/shard_map/ppermute | solution.py:107
  448.9 24.6 %collective-permute-start.62 = (bf16[128,1280]{1,0:T(8,128)(2,1)S(1)}, bf16[128,1280]{1,0:T(8,128)(2,1)S(1)}, u32[]{:S(2)}, u32[]{:S(2)}) collective-permute-start(bf16[128,1280]{1,0:T(8,128)(2,1)S(1)} %get-tuple-element.196.refs_8_), channel_id=1, source_target_pairs={{0,0},{1,1},{2,2},{3,3},{8,4},{9,5},{10,6},{11,7},{4,8},{5,9},{6,1... | collective-permute-start | bytes 983048 | tf_op jit(solution)/shard_map/ppermute | solution.py:107
  452.2 21.3 %collective-permute-start.65 = (bf16[128,1280]{1,0:T(8,128)(2,1)}, bf16[128,1280]{1,0:T(8,128)(2,1)S(1)}, u32[]{:S(2)}, u32[]{:S(2)}) collective-permute-start(bf16[128,1280]{1,0:T(8,128)(2,1)} %copy-done.95), channel_id=1, source_target_pairs={{10,0},{11,1},{8,2},{9,3},{2,4},{3,5},{0,6},{1,7},{14,8},{15,9},{1... | collective-permute-start | bytes 983048 | tf_op jit(solution)/shard_map/ppermute | solution.py:107
  460.4 17.4 %collective-permute-start.63 = (bf16[128,1280]{1,0:T(8,128)(2,1)}, bf16[128,1280]{1,0:T(8,128)(2,1)S(1)}, u32[]{:S(2)}, u32[]{:S(2)}) collective-permute-start(bf16[128,1280]{1,0:T(8,128)(2,1)} %copy-done.94), channel_id=1, source_target_pairs={{2,0},{3,1},{0,2},{1,3},{10,4},{11,5},{8,6},{9,7},{6,8},{7,9},{4,1... | collective-permute-start | bytes 983048 | tf_op jit(solution)/shard_map/ppermute | solution.py:107
  (145 other events, 975.4 us)
